TPU v7x, 32 devices: a whole 2x2x4 slice. The times are simulated.
32 devices in a mesh: dp: 4 (over y, x), pipe: 4 (over z), expert: 2 (over core).
Axes of the slice: x: 2, y: 2, z: 4, core: 2. Of those that a mesh axis runs over, the one named last changes fastest.
Arguments:
- tokens: bfloat16 [4, 1024, 5120], P('pipe', ('dp', 'expert')), may hold values from -6 to 6
- cotangent: bfloat16 [4, 1024, 5120], P('pipe', ('dp', 'expert')), may hold values from -6 to 6
- gain: float32 [4, 5120], P('pipe'), may hold values from 0.1 to 1.9
- w_gate: bfloat16 [4, 2, 5120, 768], P('pipe', 'expert', 'dp'), may hold values from -0.078125 to 0.078125
- w_up: bfloat16 [4, 2, 5120, 768], P('pipe', 'expert', 'dp'), may hold values from -0.078125 to 0.078125
- w_down: bfloat16 [4, 2, 768, 5120], P('pipe', 'expert', None, 'dp'), may hold values from -0.21875 to 0.21875
- route: int32 [4, 4, 128, 1], P('pipe', None, ('dp', 'expert')), may hold values from 0 to 1; in each aligned block of 16 rows (0 to 15, 16 to 31, ..., all dimensions but the last counted through in order) at most 12 rows name the same one
Outputs:
- out_tokens: bfloat16 [4, 1024, 5120], P('pipe', ('dp', 'expert'))
- grad_tokens: bfloat16 [4, 1024, 5120], P('pipe', ('dp', 'expert'))
- grad_gain: float32 [4, 5120], P('pipe')
- grad_gate: bfloat16 [4, 2, 5120, 768], P('pipe', 'expert', 'dp')
- grad_up: bfloat16 [4, 2, 5120, 768], P('pipe', 'expert', 'dp')
- grad_down: bfloat16 [4, 2, 768, 5120], P('pipe', 'expert', None, 'dp')
Inputs may be any that keep to these rules, and one draw needn't show every extreme that they name: route[l, m, t, 0] is the expert of tile t at layer l for micro-batch m. Among the 16 tiles of one device for one layer and one micro-batch (aligned blocks), no expert is named more than 12 times; every expert is named somewhere.
All inputs are finite; a program needn't handle non-finite values.
Results may differ from a plain program's by a relative error of at most 0.034.
Values may be sent and summed in bfloat16 or wider, within the bound.
No kernel may reach another device: no remote copies, remote signals or barrier semaphores. Data moves between devices by JAX's collectives and lax.ppermute only.
A program may use at most 128 MiB of HBM per device.

v0:
```python
import jax
import jax.numpy as jnp
from jax import lax
from jax.experimental import pallas as pl
from jax.experimental.pallas import tpu as pltpu
from jax.sharding import PartitionSpec as P

TILE = 8
PASSES = 2
PAIR = 2
COLUMNS = 256
LANES = 128
VMEM_BYTES = 12 * 1024 * 1024


epsilon = 1e-06
bf16 = jnp.bfloat16
f32 = jnp.float32


def dot(former, latter, contract):
    return lax.dot_general(
        former, latter, ((contract[:1], contract[1:]), ((), ())), preferred_element_type=f32
    )


def partner_route(size, step):
    return [(i, i ^ step) for i in range(size)]


def swap(block, axis, step):
    return lax.ppermute(block, axis, partner_route(lax.axis_size(axis), step))


def shifted(block, axis, distance):
    size = lax.axis_size(axis)
    return lax.ppermute(block, axis, [(i, (i + distance) % size) for i in range(size)])


def quarter_of(rows, index, width):
    return lax.dynamic_slice_in_dim(rows, index * width, width, axis=-1)


def to_quarters(rows, dp_count):
    width = rows.shape[-1] // dp_count
    here = lax.axis_index("dp")
    quarters = [quarter_of(rows, here ^ step, width) for step in range(dp_count)]
    return quarters[:1] + [swap(quarters[step], "dp", step) for step in range(1, dp_count)]


def assemble(parts):
    here = lax.axis_index("dp")
    rows, width = parts[0].shape
    whole = jnp.zeros((rows, width * len(parts)), parts[0].dtype)
    for step, part in enumerate(parts):
        whole = lax.dynamic_update_slice_in_dim(whole, part, (here ^ step) * width, axis=1)
    return whole


def from_quarters(parts):
    return assemble(
        [swap(part, "dp", step) if step else part for step, part in enumerate(parts)]
    )


def sum_parts(parts):
    total = parts[0].astype(f32)
    for step in range(1, len(parts)):
        total = total + swap(parts[step], "dp", step).astype(f32)
    return total


def gather_rows(rows, dp_count):
    return [rows] + [swap(rows, "dp", step) for step in range(1, dp_count)]


def after(value, *earlier):
    return lax.optimization_barrier((value,) + earlier)[0]


def columns_of(extent):
    return COLUMNS if extent % COLUMNS == 0 else extent


def kernel_call(body, operands, weights, out_shape, scratch):
    count, kept, made = len(operands), len(weights), len(out_shape)

    def call(*refs):
        operand_refs, refs = refs[:count], refs[count:]
        weight_refs, refs = refs[:kept], refs[kept:]
        body(operand_refs, weight_refs, refs[:made], refs[made:])

    in_vmem = pl.BlockSpec(memory_space=pltpu.VMEM)
    return pl.pallas_call(
        call,
        in_specs=[in_vmem] * (count + kept),
        out_specs=[in_vmem] * made,
        out_shape=out_shape,
        scratch_shapes=scratch,
        compiler_params=pltpu.CompilerParams(vmem_limit_bytes=VMEM_BYTES),
        cost_estimate=pl.CostEstimate(flops=0, bytes_accessed=0, transcendentals=0),
    )(*operands, *weights)


def resident(arrays):
    count = len(arrays)

    def call(*refs):
        arrivals = refs[-1]
        copies = [
            pltpu.make_async_copy(refs[i], refs[count + i], arrivals.at[i]) for i in range(count)
        ]
        for copy in copies:
            copy.start()
        for copy in copies:
            copy.wait()

    return pl.pallas_call(
        call,
        in_specs=[pl.BlockSpec(memory_space=pltpu.HBM)] * count,
        out_specs=[pl.BlockSpec(memory_space=pltpu.VMEM)] * count,
        out_shape=[pltpu.VMEM(a.shape, a.dtype) for a in arrays],
        scratch_shapes=[pltpu.SemaphoreType.DMA((count,))],
        compiler_params=pltpu.CompilerParams(vmem_limit_bytes=VMEM_BYTES),
        cost_estimate=pl.CostEstimate(
            flops=0,
            bytes_accessed=2 * sum(a.size * a.dtype.itemsize for a in arrays),
            transcendentals=0,
        ),
    )(*(pltpu.with_memory_space_constraint(a, pltpu.HBM) for a in arrays))


def store_parts(refs, columns, value):
    size = value.shape[0] // len(refs)
    for index, ref in enumerate(refs):
        ref[:, columns] = value[index * size : (index + 1) * size]


def each_tile(extent, visit):
    tile = columns_of(extent)

    def step(j, carry):
        visit(span(j, tile))
        return carry

    lax.fori_loop(0, extent // tile, step, 0)


def span(tile, size):
    return pl.ds(pl.multiple_of(tile * size, size), size)


def hidden_parts(blocks, part_rows, gain_part, mask, gate_pair, up_pair, expert=None):
    width, units = gate_pair[0].shape
    routed = expert is not None
    block_rows = part_rows if routed else blocks[0].shape[0]
    rows = block_rows * len(blocks)
    parts_count = rows // part_rows
    passes = PASSES if routed else 0

    def body(operand_refs, weight_refs, out_refs, scratch):
        *block_refs, gain_ref, choice_ref = operand_refs
        part_refs, gained_ref = out_refs[:parts_count], out_refs[parts_count]
        mask_ref = out_refs[parts_count + 1] if routed else choice_ref
        for index, ref in enumerate(block_refs):
            place = slice(index * block_rows, (index + 1) * block_rows)
            block = ref[:block_rows]
            gained_ref[place] = (block.astype(f32) * gain_ref[...]).astype(bf16)
            if routed:
                out_refs[-1][place] = block
                tiles = block_rows // TILE
                row = lax.broadcasted_iota(jnp.int32, (block_rows, tiles), 0)
                first = TILE * lax.broadcasted_iota(jnp.int32, (block_rows, tiles), 1)
                chosen = ((row >= first) & (row < first + TILE)).astype(bf16)
                experts = dot(chosen, ref[block_rows:, :LANES], (1, 0)) - choice_ref[...]
                for k in range(passes):
                    near = jnp.abs(experts[:, k : k + 1]) < 0.5
                    out_refs[parts_count + 1 + k][place] = jnp.where(near, 1.0, 0.0)

        for pair in range(2):

            def visit(columns, pair=pair):
                own, other = weight_refs[2 * pair : 2 * pair + 2]
                part = jnp.where(
                    mask_ref[...] > 0.5,
                    dot(gained_ref[...], own[:, columns], (1, 0)),
                    dot(gained_ref[...], other[:, columns], (1, 0)),
                ).astype(bf16)
                store_parts([ref.at[:, pair * units :] for ref in part_refs], columns, part)

            each_tile(units, visit)

    outs = kernel_call(
        body,
        (*blocks, gain_part, expert if routed else mask),
        (*gate_pair, *up_pair),
        [jax.ShapeDtypeStruct((part_rows, 2 * units), bf16)] * parts_count
        + [jax.ShapeDtypeStruct((rows, width), bf16)]
        + [jax.ShapeDtypeStruct((rows, 1), f32)] * passes
        + [jax.ShapeDtypeStruct((rows, width), bf16)] * int(routed),
        [],
    )
    return outs[:parts_count], outs[parts_count], outs[parts_count + 1 :]


def activate(parts, inverse):
    rows, both = parts[0].shape
    units = both // 2

    def body(operand_refs, weight_refs, out_refs, scratch):
        *part_refs, inverse_ref = operand_refs
        total = part_refs[0][...].astype(f32)
        for ref in part_refs[1:]:
            total = total + ref[...].astype(f32)
        total = total * inverse_ref[...]
        gate, up = total[:, :units], total[:, units:]
        out_refs[0][...] = gate
        out_refs[1][...] = up
        out_refs[2][...] = (gate / (1.0 + jnp.exp(-gate)) * up).astype(bf16)

    return kernel_call(
        body,
        (*parts, inverse),
        (),
        [jax.ShapeDtypeStruct((rows, units), f32)] * 2
        + [jax.ShapeDtypeStruct((rows, units), bf16)],
        [],
    )


def join(joined, refs, columns):
    size = refs[0].shape[0]
    for index, ref in enumerate(refs):
        joined[index * size : (index + 1) * size] = ref[:, columns]


def add_down(blocks, mask, down_pair, hidden, in_parts):
    count = len(blocks)
    part_rows, units = blocks[0].shape
    rows = part_rows * count
    width = down_pair[0].shape[1]
    out_count = count if in_parts else 1

    def body(operand_refs, weight_refs, out_refs, scratch):
        *block_refs, mask_ref, hidden_ref = operand_refs
        *row_refs, square_ref = out_refs
        (joined,) = scratch
        join(joined, block_refs, slice(None))
        square_ref[...] = jnp.zeros_like(square_ref)

        own, other = weight_refs

        def visit(columns):
            ffn = jnp.where(
                mask_ref[...] > 0.5,
                dot(joined[...], own[:, columns], (1, 0)),
                dot(joined[...], other[:, columns], (1, 0)),
            ).astype(bf16)
            out = (hidden_ref[:, columns].astype(f32) + ffn.astype(f32)).astype(bf16)
            wide = out.astype(f32)
            square_ref[...] += jnp.sum(wide * wide, axis=-1, keepdims=True)
            store_parts(row_refs, columns, out)

        each_tile(width, visit)

    outs = kernel_call(
        body,
        (*blocks, mask, hidden),
        down_pair,
        [jax.ShapeDtypeStruct((rows // out_count, width), bf16)] * out_count
        + [jax.ShapeDtypeStruct((rows, 1), f32)],
        [pltpu.VMEM((rows, units), bf16)],
    )
    return outs[:out_count], outs[out_count]


def act_grad_parts(blocks, part_rows, mask, down_pair):
    rows = sum(block.shape[0] for block in blocks)
    parts_count = rows // part_rows
    units, width = down_pair[0].shape

    def body(operand_refs, weight_refs, out_refs, scratch):
        *block_refs, mask_ref = operand_refs
        *part_refs, grad_ref = out_refs
        own, other = weight_refs
        join(grad_ref, block_refs, slice(None))

        def visit(columns):
            part = jnp.where(
                mask_ref[...] > 0.5,
                dot(grad_ref[...], own[columns], (1, 1)),
                dot(grad_ref[...], other[columns], (1, 1)),
            ).astype(bf16)
            store_parts(part_refs, columns, part)

        each_tile(units, visit)

    outs = kernel_call(
        body,
        (*blocks, mask),
        down_pair,
        [jax.ShapeDtypeStruct((part_rows, units), bf16)] * parts_count
        + [jax.ShapeDtypeStruct((rows, width), bf16)],
        [],
    )
    return outs[:parts_count], outs[parts_count]


def hidden_grads(parts, gate, up, inverse, features):
    rows, units = gate.shape

    def body(operand_refs, weight_refs, out_refs, scratch):
        *part_refs, gate_ref, up_ref, inverse_ref = operand_refs
        (out_ref,) = out_refs
        grad_act = part_refs[0][...].astype(f32)
        for ref in part_refs[1:]:
            grad_act = grad_act + ref[...].astype(f32)
        gate_now, up_now, scale = gate_ref[...], up_ref[...], inverse_ref[...]
        sigmoid = 1.0 / (1.0 + jnp.exp(-gate_now))
        scaled = grad_act * scale
        gate_grad = scaled * up_now * sigmoid * (1.0 + gate_now * (1.0 - sigmoid))
        up_grad = scaled * (gate_now * sigmoid)
        shrink = jnp.sum(gate_grad * gate_now + up_grad * up_now, axis=-1, keepdims=True) * (
            scale / features
        )
        out_ref[:, :units] = gate_grad.astype(bf16)
        out_ref[:, units : 2 * units] = up_grad.astype(bf16)
        coarse = shrink.astype(bf16).astype(f32)
        lane = lax.broadcasted_iota(jnp.int32, (rows, LANES), 1)
        out_ref[:, 2 * units :] = jnp.where(
            lane == 0, coarse, jnp.where(lane == 1, shrink - coarse, 0.0)
        ).astype(bf16)

    (sent,) = kernel_call(
        body,
        (*parts, gate, up, inverse),
        [],
        [jax.ShapeDtypeStruct((rows, 2 * units + LANES), bf16)],
        [],
    )
    return sent


def input_grad(blocks, mask, gate_pair, up_pair, grad, hidden, gain_part, in_parts):
    count = len(blocks)
    part_rows = blocks[0].shape[0]
    rows = part_rows * count
    width, units = gate_pair[0].shape
    out_count = count if in_parts else 1

    def body(operand_refs, weight_refs, out_refs, scratch):
        *block_refs, mask_ref, grad_ref, hidden_ref, gain_ref = operand_refs
        *row_refs, sum_ref = out_refs
        joined, shrink = scratch
        join(joined, block_refs, slice(0, 2 * units))
        for index, ref in enumerate(block_refs):
            tail = ref[:, 2 * units :].astype(f32)
            shrink[index * part_rows : (index + 1) * part_rows] = jnp.sum(
                tail, axis=-1, keepdims=True
            )

        gate_own, gate_other, up_own, up_other = weight_refs

        def visit(columns):
            def back_of(gate, up):
                return dot(joined[:, :units], gate[columns], (1, 1)) + dot(
                    joined[:, units:], up[columns], (1, 1)
                )

            back = jnp.where(
                mask_ref[...] > 0.5, back_of(gate_own, up_own), back_of(gate_other, up_other)
            )
            wide = hidden_ref[:, columns].astype(f32)
            sum_ref[:, columns] = jnp.sum(back * wide, axis=0, keepdims=True)
            out = (
                grad_ref[:, columns].astype(f32)
                + back * gain_ref[:, columns]
                - wide * shrink[...]
            ).astype(bf16)
            store_parts(row_refs, columns, out)

        each_tile(width, visit)

    outs = kernel_call(
        body,
        (*blocks, mask, grad, hidden, gain_part),
        (*gate_pair, *up_pair),
        [jax.ShapeDtypeStruct((rows // out_count, width), bf16)] * out_count
        + [jax.ShapeDtypeStruct((1, width), f32)],
        [
            pltpu.VMEM((rows, 2 * units), bf16),
            pltpu.VMEM((rows, 1), f32),
        ],
    )
    return outs[:out_count], outs[out_count]


def body(tokens, cotangent, gain, w_gate, w_up, w_down, route):
    pipe_count = lax.axis_size("pipe")
    dp_count = lax.axis_size("dp")
    section = lax.axis_index("pipe")
    expert = lax.axis_index("expert")
    here = lax.axis_index("dp")
    features = tokens.shape[-1]
    width = features // dp_count
    units = w_gate.shape[-1]
    gain_part = lax.dynamic_slice_in_dim(gain, here * width, width, axis=1)

    groups = (slice(0, dp_count - 1), slice(dp_count - 1, dp_count))
    own_tokens = tokens[0]
    rows = own_tokens.shape[0]
    micro = [(section - k + pipe_count) % pipe_count for k in range(PASSES)]
    route_rows = jnp.stack(
        [lax.dynamic_index_in_dim(route[0, :, :, 0], m, 0, keepdims=False) for m in micro], axis=1
    ).astype(bf16)
    route_rows = jnp.pad(route_rows, ((0, 0), (0, width - PASSES)))

    def tokens_quarter(step):
        return jnp.concatenate([quarter_of(own_tokens, here ^ step, width), route_rows])

    def cotangent_quarter(step, *earlier):
        return quarter_of(after(cotangent[0], *earlier), here ^ step, width)

    def sent(parts):
        return [swap(part, "dp", step) if step else part for step, part in enumerate(parts)]

    def moved(pieces, distance):
        return [shifted(piece, "pipe", distance) for piece in pieces]

    def scale_of(square_sum):
        return lax.rsqrt(square_sum / features + epsilon)

    def weight_grad(left, right, mask, wanted):
        return dot(left, jnp.where((mask > 0.5) == wanted, right, jnp.zeros_like(right)), (0, 0))

    quarters = [tokens_quarter(step) for step in range(dp_count)]
    weights = [
        weight
        for own in (w_gate, w_up, w_down)
        for weight in (own[0, 0], swap(own[0, 0], "expert", 1))
    ]
    weights = resident(weights)
    gate_pair, up_pair, down_pair = weights[:2], weights[2:4], weights[4:]
    quarters[-1] = after(quarters[-1], *weights)
    blocks = sent(quarters)
    expert_id = jnp.full((1, LANES), expert, f32)
    wide = own_tokens.astype(f32)
    inverse = scale_of(jnp.sum(wide * wide, axis=-1, keepdims=True))

    parts, gained, masks, hidden = [], [], [], []
    for group in groups:
        made, scaled, (*choices, joined) = hidden_parts(
            blocks[group], rows, gain_part, None, gate_pair, up_pair, expert_id
        )
        parts += made
        gained.append(scaled)
        masks.append(choices)
        hidden.append(joined)
    masks = list(zip(*masks))
    gate, up, activated = activate(sent(parts), inverse)
    kept = [(hidden, gained, inverse, gate, up)]
    first_activated = gather_rows(activated, dp_count)
    next_hidden, squares = [], []
    for group, mask, rows_in in zip(groups, masks[0], hidden):
        (out,), square = add_down(first_activated[group], mask, down_pair, rows_in, False)
        next_hidden.append(out)
        squares += jnp.split(square, square.shape[0] // rows)
    hidden = moved(next_hidden, 1)
    grad_blocks = sent([cotangent_quarter(step, *next_hidden) for step in range(dp_count)])
    inverse = shifted(scale_of(sum_parts(squares)), "pipe", 1)
    act_parts, grad = [], []
    for group, mask in zip(groups, masks[1]):
        made, joined = act_grad_parts(grad_blocks[group], rows, mask, down_pair)
        act_parts += made
        grad.append(joined)
    act_parts = sent(act_parts)
    hidden[0] = after(hidden[0], inverse, *act_parts[1:-1])

    parts, gained = [], []
    for rows_in, mask in zip(hidden, masks[1]):
        made, scaled, _ = hidden_parts([rows_in], rows, gain_part, mask, gate_pair, up_pair)
        parts += made
        gained.append(scaled)
    gate, up, activated = activate(sent(parts), inverse)
    kept.append((hidden, gained, inverse, gate, up))

    gain_sum = jnp.zeros((1, width), f32)
    for k in reversed(range(PASSES)):
        hidden, gained, inverse, gate, up = kept[k]
        gained = jnp.concatenate(gained)
        mask = jnp.concatenate(masks[k])
        payload = hidden_grads(act_parts, gate, up, inverse, features)
        both_grad = gather_rows(payload, dp_count)
        joined = jnp.concatenate(both_grad)
        rights = [joined[:, :units], joined[:, units : 2 * units]]
        if k == 0:
            late_down = jnp.concatenate(first_activated)
            grad_now = jnp.concatenate(grad)
            other_down = swap(
                (
                    weight_grad(late_down, grad_now, mask, False) + early[False][2].astype(f32)
                ).astype(bf16),
                "expert",
                1,
            )
            down_grad = (
                weight_grad(late_down, grad_now, mask, True)
                + early[True][2].astype(f32)
                + other_down.astype(f32)
            ).astype(bf16)
            both_grad[1] = after(both_grad[1], down_grad)
            received = [
                swap(
                    (weight_grad(gained, right, mask, False) + soon.astype(f32)).astype(bf16),
                    "expert",
                    1,
                )
                for right, soon in zip(rights, early[False])
            ]
        else:
            last_activated = gather_rows(after(activated, *both_grad[1:]), dp_count)
        outs = []
        for group, choice, rows_in, grad_in in zip(groups, masks[k], hidden, grad):
            made, gain_term = input_grad(
                both_grad[group], choice, gate_pair, up_pair, grad_in, rows_in, gain_part, k == 0
            )
            outs += made
            gain_sum = gain_sum + gain_term
        if k > 0:
            last_grad = jnp.concatenate(grad)
            grad = moved(outs, -1)
            rights = [after(right, *outs) for right in rights]
            early = {
                wanted: [weight_grad(gained, right, mask, wanted).astype(bf16) for right in rights]
                for wanted in (False, True)
            }
            out_parts = []
            for group, choice, rows_in in zip(groups, masks[1], hidden):
                made, _ = add_down(last_activated[group], choice, down_pair, rows_in, True)
                out_parts += made
            out_rows = from_quarters(out_parts)
            grad[0] = after(grad[0], out_rows, *early[False], *early[True])
            act_parts, joined = [], []
            for rows_in, choice in zip(grad, masks[0]):
                made, copied = act_grad_parts([rows_in], rows, choice, down_pair)
                act_parts += made
                joined.append(copied)
            grad = joined
            last_activated = jnp.concatenate(last_activated)
            for wanted in (False, True):
                early[wanted].append(
                    weight_grad(last_activated, last_grad, mask, wanted).astype(bf16)
                )
            act_parts = sent(act_parts)
            act_parts[1] = after(act_parts[1], early[False][2], early[True][2])

    returned = sent(outs)
    rights = [after(right, *outs) for right in rights]
    gain_rows = jnp.concatenate(gather_rows(after(gain_sum, *received), dp_count))
    gain_rows = gain_rows + swap(gain_rows, "expert", 1)
    gain_all = jnp.zeros((features,), f32)
    for step in range(dp_count):
        gain_all = lax.dynamic_update_slice_in_dim(
            gain_all, gain_rows[step], (here ^ step) * width, axis=0
        )
    grads = [
        (
            weight_grad(gained, right, mask, True) + soon.astype(f32) + other.astype(f32)
        ).astype(bf16)
        for right, soon, other in zip(rights, early[True], received)
    ] + [down_grad]
    returned = list(lax.optimization_barrier((*returned, *grads)))[:dp_count]
    entry = assemble(returned)
    return (
        out_rows[None],
        entry[None],
        gain_all[None],
        grads[0][None, None],
        grads[1][None, None],
        grads[2][None, None],
    )


def start_shifted(block, axis, distance):
    devices = range(lax.axis_size(axis))
    route = [((i - distance) % len(devices), i) for i in devices]
    return lax.ppermute(block, axis, route)


def start_contract_last(former, latter):
    return lax.dot_general(
        former, latter, (((1,), (1,)), ((), ())), preferred_element_type=jnp.float32
    )


def start_contract_first(former, latter):
    return lax.dot_general(
        former, latter, (((0,), (0,)), ((), ())), preferred_element_type=jnp.float32
    )


def start_normalize(hidden, gain_row):
    widened = hidden.astype(jnp.float32)
    inverse = lax.rsqrt(jnp.mean(widened * widened, axis=-1, keepdims=True) + epsilon)
    scaled = widened * inverse
    return ((scaled * gain_row).astype(jnp.bfloat16), scaled, inverse)


def start_slot_matrix(route_now, expert_count, capacity):
    tile_count = route_now.shape[0]
    expert_ids = jnp.arange(expert_count, dtype=jnp.int32)
    member = (route_now[None, :] == expert_ids[:, None]).astype(jnp.int32)
    earlier = jnp.cumsum(member, axis=1) - member
    rank_ids = jnp.arange(capacity, dtype=jnp.int32)
    placed = member[:, None, :] * (earlier[:, None, :] == rank_ids[None, :, None]).astype(jnp.int32)
    return placed.reshape(expert_count * capacity, tile_count)


def start_into_slots(placed, rows, tile_rows, dp_count):
    width = rows.shape[-1]
    tile_blocks = rows.reshape(placed.shape[1], tile_rows, dp_count, width // dp_count)
    return jnp.einsum(
        "st,trqd->qsrd",
        placed.astype(jnp.bfloat16),
        tile_blocks,
        preferred_element_type=jnp.float32,
    ).astype(jnp.bfloat16)


def start_from_slots(placed, slot_rows):
    merged = jnp.einsum(
        "st,qsrd->trqd", placed.astype(jnp.bfloat16), slot_rows, preferred_element_type=jnp.float32
    ).astype(jnp.bfloat16)
    return merged.reshape(merged.shape[0] * merged.shape[1], -1)


def start_send_out(slot_rows):
    quarter = slot_rows.shape[-1]
    flat = slot_rows.reshape((-1,) + slot_rows.shape[2:])
    arrived = lax.all_to_all(flat, ("dp", "expert"), split_axis=0, concat_axis=0, tiled=True)
    return arrived.reshape(-1, quarter)


def start_send_back(part_rows, dp_count, tile_rows):
    quarter = part_rows.shape[-1]
    flat = part_rows.reshape(-1, tile_rows, quarter)
    returned = lax.all_to_all(flat, ("dp", "expert"), split_axis=0, concat_axis=0, tiled=True)
    return returned.reshape(dp_count, -1, tile_rows, quarter)


def start_widen_rounded(values):
    return lax.optimization_barrier(values.astype(jnp.bfloat16)).astype(jnp.float32)


def start_expert_forward(received, gate_weight, up_weight, down_weight):
    gate_terms = start_widen_rounded(jnp.dot(received, gate_weight, preferred_element_type=jnp.float32))
    up_terms = start_widen_rounded(jnp.dot(received, up_weight, preferred_element_type=jnp.float32))
    gate_pre, up_pre = (
        lax.psum(gate_terms.astype(jnp.bfloat16), "dp").astype(jnp.float32),
        lax.psum(up_terms.astype(jnp.bfloat16), "dp").astype(jnp.float32),
    )
    activated = (jax.nn.silu(gate_pre) * up_pre).astype(jnp.bfloat16)
    part_rows = jnp.dot(activated, down_weight, preferred_element_type=jnp.float32).astype(
        jnp.bfloat16
    )
    return (part_rows, (gate_pre, up_pre, activated))


def start_expert_backward(
    received, grad_recv, kept_state, gate_weight, up_weight, down_weight, grad_sums
):
    gate_pre, up_pre, activated = kept_state
    grad_terms = start_widen_rounded(start_contract_last(grad_recv, down_weight))
    grad_act = lax.psum(grad_terms.astype(jnp.bfloat16), "dp").astype(jnp.float32)
    sigmoid_gate = jax.nn.sigmoid(gate_pre)
    silu_gate = gate_pre * sigmoid_gate
    grad_gate_pre = (
        grad_act * up_pre * sigmoid_gate * (1.0 + gate_pre * (1.0 - sigmoid_gate))
    ).astype(jnp.bfloat16)
    grad_up_pre = (grad_act * silu_gate).astype(jnp.bfloat16)
    back_rows = (
        start_contract_last(grad_gate_pre, gate_weight) + start_contract_last(grad_up_pre, up_weight)
    ).astype(jnp.bfloat16)
    grad_gate = grad_sums[0] + start_contract_first(received, grad_gate_pre)
    grad_up = grad_sums[1] + start_contract_first(received, grad_up_pre)
    grad_down = grad_sums[2] + start_contract_first(activated, grad_recv)
    return (back_rows, (grad_gate, grad_up, grad_down))


def start_body(tokens, cotangent, gain, w_gate, w_up, w_down, route):
    pipe_count = lax.axis_size("pipe")
    dp_count = lax.axis_size("dp")
    expert_count = lax.axis_size("expert")
    section_index = lax.axis_index("pipe")
    gain_row = gain[0]
    gate_weight = w_gate[0, 0]
    up_weight = w_up[0, 0]
    down_weight = w_down[0, 0]
    route_table = route[0, :, :, 0]
    tile_count = route_table.shape[1]
    capacity = max(2, 3 * tile_count // (2 * expert_count))
    hidden = tokens[0]
    saved_ticks = []
    out_rows = hidden
    for pass_index in range(PASSES):
        micro_index = (section_index - pass_index + pipe_count) % pipe_count
        route_now = lax.dynamic_index_in_dim(route_table, micro_index, 0, keepdims=False)
        placed = start_slot_matrix(route_now, expert_count, capacity)
        normed, scaled, inverse = start_normalize(hidden, gain_row)
        received = start_send_out(start_into_slots(placed, normed, TILE, dp_count))
        part_rows, kept_state = start_expert_forward(received, gate_weight, up_weight, down_weight)
        ffn_rows = start_from_slots(placed, start_send_back(part_rows, dp_count, TILE))
        new_hidden = (hidden.astype(jnp.float32) + ffn_rows.astype(jnp.float32)).astype(
            jnp.bfloat16
        )
        saved_ticks.append((placed, scaled, inverse, received, kept_state))
        if pass_index + 1 < PASSES:
            hidden = start_shifted(new_hidden, "pipe", 1)
        else:
            out_rows = new_hidden
    grad_rows = cotangent[0]
    grad_sums = (
        jnp.zeros(gate_weight.shape, jnp.float32),
        jnp.zeros(up_weight.shape, jnp.float32),
        jnp.zeros(down_weight.shape, jnp.float32),
    )
    gain_sum = jnp.zeros(gain_row.shape, jnp.float32)
    entry_grad = grad_rows
    for pass_index in reversed(range(PASSES)):
        placed, scaled, inverse, received, kept_state = saved_ticks[pass_index]
        grad_recv = start_send_out(start_into_slots(placed, grad_rows, TILE, dp_count))
        back_rows, grad_sums = start_expert_backward(
            received, grad_recv, kept_state, gate_weight, up_weight, down_weight, grad_sums
        )
        grad_normed = start_from_slots(placed, start_send_back(back_rows, dp_count, TILE)).astype(jnp.float32)
        gain_sum = gain_sum + jnp.sum(grad_normed * scaled, axis=0)
        grad_scaled = grad_normed * gain_row
        grad_wide = inverse * (
            grad_scaled - scaled * jnp.mean(grad_scaled * scaled, axis=-1, keepdims=True)
        )
        grad_in = (grad_rows.astype(jnp.float32) + grad_wide).astype(jnp.bfloat16)
        if pass_index > 0:
            grad_rows = start_shifted(grad_in, "pipe", -1)
        else:
            entry_grad = grad_in
    gain_total = lax.psum(gain_sum, ("dp", "expert"))
    return (
        out_rows[None],
        entry_grad[None],
        gain_total[None],
        grad_sums[0].astype(jnp.bfloat16)[None, None],
        grad_sums[1].astype(jnp.bfloat16)[None, None],
        grad_sums[2].astype(jnp.bfloat16)[None, None],
    )


def start_solution(mesh):
    placed = (
        P("pipe", ("dp", "expert"), None),
        P("pipe", ("dp", "expert"), None),
        P("pipe", None),
        P("pipe", "expert", "dp", None),
        P("pipe", "expert", "dp", None),
        P("pipe", "expert", None, "dp"),
        P("pipe", None, ("dp", "expert"), None),
    )
    return jax.shard_map(
        start_body,
        mesh=mesh,
        in_specs=placed,
        out_specs=(
            P("pipe", ("dp", "expert"), None),
            P("pipe", ("dp", "expert"), None),
            P("pipe", None),
            P("pipe", "expert", "dp", None),
            P("pipe", "expert", "dp", None),
            P("pipe", "expert", None, "dp"),
        ),
        check_vma=False,
    )


def solution(mesh):
    if mesh.shape["expert"] != PAIR:
        return start_solution(mesh)
    placed = (
        P("pipe", ("dp", "expert"), None),
        P("pipe", ("dp", "expert"), None),
        P("pipe", None),
        P("pipe", "expert", "dp", None),
        P("pipe", "expert", "dp", None),
        P("pipe", "expert", None, "dp"),
        P("pipe", None, ("dp", "expert"), None),
    )
    return jax.shard_map(
        body,
        mesh=mesh,
        in_specs=placed,
        out_specs=placed[:2] + (P("pipe", None),) + placed[3:6],
        check_vma=False,
    )
```

profile of v0, /device:TPU:0, one launch (start us, length us, event | category | flops | bytes accessed | tf_op | source)
XLA Modules:
  0.0 255.3 jit_solution(14540002789880070406)
XLA Ops:
  4.8 2.6 %collective-permute-start = (bf16[144,1280]{1,0:T(8,128)(2,1)S(1)}, bf16[144,1280]{1,0:T(8,128)(2,1)S(1)}, u32[]{:S(2)}, u32[]{:S(2)}) collective-permute-start(bf16[144,1280]{1,0:T(8,128)(2,1)S(1)} %get-tuple-element.178), channel_id=1, source_target_pairs={{0,8},{8,0},{16,24},{24,16},{1,9},{9,1},{17,25},{25,17},{2,10},{10... | collective-permute-start | bytes 1105928 | tf_op jit(solution)/shard_map/ppermute | solution.py:32
  10.7 4.5 %shard_map.118 = (bf16[1280,768]{1,0:T(8,128)(2,1)S(1)}, bf16[1280,768]{1,0:T(8,128)(2,1)S(1)}, bf16[1280,768]{1,0:T(8,128)(2,1)S(1)}, bf16[1280,768]{1,0:T(8,12...) custom-call(bf16[1280,768]{1,0:T(8,128)(2,1)} %bitcast.43, ...), custom_call_target="tpu_custom_call" | custom-call | bytes 23592960 | tf_op jit(solution)/shard_map/pallas_call | solution.py:118
  21.6 3.8 %collective-permute-start.7 = (bf16[144,1280]{1,0:T(8,128)(2,1)}, bf16[144,1280]{1,0:T(8,128)(2,1)}, u32[]{:S(2)}, u32[]{:S(2)}) collective-permute-start(bf16[144,1280]{1,0:T(8,128)(2,1)} %get-tuple-element.91), channel_id=1, source_target_pairs={{0,24},{8,16},{16,8},{24,0},{1,25},{9,17},{17,9},{25,1},{2,26},{10... | collective-permute-start | bytes 1105928 | tf_op jit(solution)/shard_map/ppermute | solution.py:32
  35.3 5.5 %shard_map.119 = (bf16[128,1536]{1,0:T(8,128)(2,1)S(1)}, bf16[128,1536]{1,0:T(8,128)(2,1)}, bf16[128,1536]{1,0:T(8,128)(2,1)}, bf16[384,1280]{1,0:T(8,128)(2,1)S...) custom-call(bf16[144,1280]{1,0:T(8,128)(2,1)S(1)} %copy-done.16, ...), custom_call_target="tpu_custom_call" | custom-call | tf_op jit(solution)/shard_map/pallas_call | solution.py:94
  41.3 4.1 %shard_map.120 = (bf16[128,1536]{1,0:T(8,128)(2,1)}, bf16[128,1280]{1,0:T(8,128)(2,1)S(1)}, f32[128,1]{1,0:T(8,128)S(1)}, f32[128,1]{1,0:T(8,128)S(1)}, bf16[128,1280]{1,0:T(8,128)(2,1)S(1)}) custom-call(bf16[144,1280]{1,0:T(8,128)(2,1)} %collective-permute-done.7.refs_0_, f32[1,1280]{1,0:T(1,128)S(1)} %constant_dynamic-slice_fusion.4.refs_3_.refs_1_.refs_6_.refs_4_, ...), custom_call_target="tpu_custom_call" | custom-call | tf_op jit(solution)/shard_map/pallas_call | solution.py:94
  46.2 2.9 %collective-permute-start.8 = (bf16[128,1536]{1,0:T(8,128)(2,1)}, bf16[128,1536]{1,0:T(8,128)(2,1)}, u32[]{:S(2)}, u32[]{:S(2)}) collective-permute-start(bf16[128,1536]{1,0:T(8,128)(2,1)} %get-tuple-element.92), channel_id=1, source_target_pairs={{0,24},{8,16},{16,8},{24,0},{1,25},{9,17},{17,9},{25,1},{2,26},{10... | collective-permute-start | bytes 1179656 | tf_op jit(solution)/shard_map/ppermute | solution.py:32
  50.7 1.9 constant_dynamic-update-slice_fusion.14
  53.1 7.6 %collective-permute-done.6.refs_2_ = bf16[128,1536]{1,0:T(8,128)(2,1)} collective-permute-done((bf16[128,1536]{1,0:T(8,128)(2,1)}, bf16[128,1536]{1,0:T(8,128)(2,1)}, u32[]{:S(2)}, u32[]{:S(2)}) %collective-permute-start.6) | collective-permute-done | bytes 393248 | tf_op jit(solution)/shard_map/ppermute | solution.py:32
  62.5 1.7 shard_map.121
  67.8 5.1 %collective-permute-done.14.refs_0_ = bf16[128,768]{1,0:T(8,128)(2,1)S(1)} collective-permute-done((bf16[128,768]{1,0:T(8,128)(2,1)S(1)}, bf16[128,768]{1,0:T(8,128)(2,1)S(1)}, u32[]{:S(2)}, u32[]{:S(2)}) %collective-permute-start.14) | collective-permute-done | bytes 196640 | tf_op jit(solution)/shard_map/ppermute | solution.py:32
  74.4 1.8 shard_map.123
  79.3 2.9 %shard_map.122 = (bf16[384,1280]{1,0:T(8,128)(2,1)S(1)}, f32[384,1]{1,0:T(8,128)S(1)}) custom-call(bf16[128,768]{1,0:T(8,128)(2,1)S(1)} %get-tuple-element.93.refs_0_, bf16[128,768]{1,0:T(8,128)(2,1)S(1)} %collective-permute-done.9.refs_1_, bf16[128,768]{1,0:T(8,128)(2,1)S(1)} %collective-permute-done.10.refs_2_, ...), custom_call_target="tpu_custom_call" | custom-call | tf_op jit(solution)/shard_map/pallas_call | solution.py:94
  86.1 5.8 %collective-permute-done.18.refs_2_ = bf16[128,1280]{1,0:T(8,128)(2,1)S(1)} collective-permute-done((bf16[128,1280]{1,0:T(8,128)(2,1)S(1)}, bf16[128,1280]{1,0:T(8,128)(2,1)S(1)}, u32[]{:S(2)}, u32[]{:S(2)}) %collective-permute-start.18) | collective-permute-done | bytes 327712 | tf_op jit(solution)/shard_map/ppermute | solution.py:32
  93.9 2.2 shard_map.124
  96.1 1.9 collective-permute-start.25
  101.4 2.2 shard_map.126
  103.5 4.2 %collective-permute-done.25.refs_0_ = bf16[128,1280]{1,0:T(8,128)(2,1)S(1)} collective-permute-done((bf16[128,1280]{1,0:T(8,128)(2,1)S(1)}, bf16[128,1280]{1,0:T(8,128)(2,1)S(1)}, u32[]{:S(2)}, u32[]{:S(2)}) %collective-permute-start.25) | collective-permute-done | bytes 327712 | tf_op jit(solution)/shard_map/ppermute | solution.py:32
  107.7 1.9 collective-permute-start.24
  109.6 1.7 shard_map.128
  112.4 4.2 %shard_map.125 = (bf16[128,1536]{1,0:T(8,128)(2,1)S(1)}, bf16[128,1536]{1,0:T(8,128)(2,1)S(1)}, bf16[128,1536]{1,0:T(8,128)(2,1)S(1)}, bf16[384,1280]{1,0:T(8,128)(2,1)S(1)}) custom-call(bf16[384,1280]{1,0:T(8,128)(2,1)S(1)} %collective-permute-done.11.refs_0_.refs_4_.refs_5_, f32[1,1280]{1,0:T(1,128)S(1)} %constant_dynamic-slice_fusion.4.refs_3_.refs_1_.refs_6_.refs_4_, ...), custom_call_target="tpu_custom_call" | custom-call | tf_op jit(solution)/shard_map/pallas_call | solution.py:94
  117.1 2.0 collective-permute-start.22
  120.3 8.0 %collective-permute-done.21.refs_1_ = bf16[128,1536]{1,0:T(8,128)(2,1)S(1)} collective-permute-done((bf16[128,1536]{1,0:T(8,128)(2,1)S(1)}, bf16[128,1536]{1,0:T(8,128)(2,1)S(1)}, u32[]{:S(2)}, u32[]{:S(2)}) %collective-permute-start.21) | collective-permute-done | bytes 393248 | tf_op jit(solution)/shard_map/ppermute | solution.py:32
  130.1 4.5 %collective-permute-start.28 = (bf16[128,1664]{1,0:T(8,128)(2,1)S(1)}, bf16[128,1664]{1,0:T(8,128)(2,1)S(1)}, u32[]{:S(2)}, u32[]{:S(2)}) collective-permute-start(bf16[128,1664]{1,0:T(8,128)(2,1)S(1)} %shard_map.129.refs_0_), channel_id=1, source_target_pairs={{0,16},{8,24},{16,0},{24,8},{1,17},{9,25},{17,1},{25,9},{2,18},{10... | collective-permute-start | bytes 1277960 | tf_op jit(solution)/shard_map/ppermute | solution.py:32
  136.2 5.3 %collective-permute-done.29.refs_0_ = bf16[128,1664]{1,0:T(8,128)(2,1)S(1)} collective-permute-done((bf16[128,1664]{1,0:T(8,128)(2,1)S(1)}, bf16[128,1664]{1,0:T(8,128)(2,1)S(1)}, u32[]{:S(2)}, u32[]{:S(2)}) %collective-permute-start.29) | collective-permute-done | bytes 426016 | tf_op jit(solution)/shard_map/ppermute | solution.py:32
  141.5 5.0 %collective-permute-done.28.refs_2_ = bf16[128,1664]{1,0:T(8,128)(2,1)S(1)} collective-permute-done((bf16[128,1664]{1,0:T(8,128)(2,1)S(1)}, bf16[128,1664]{1,0:T(8,128)(2,1)S(1)}, u32[]{:S(2)}, u32[]{:S(2)}) %collective-permute-start.28) | collective-permute-done | bytes 426016 | tf_op jit(solution)/shard_map/ppermute | solution.py:32
  146.5 2.2 collective-permute-done.27.refs_1_
  148.8 2.1 collective-permute-start.31
  152.3 3.4 %shard_map.133 = (bf16[128,1280]{1,0:T(8,128)(2,1)S(1)}, f32[1,1280]{1,0:T(1,128)S(1)}) custom-call(bf16[128,1664]{1,0:T(8,128)(2,1)S(1)} %collective-permute-done.29.refs_0_, f32[128,1]{1,0:T(8,128)S(1)} %get-tuple-element.110.refs_2_.refs_1_, bf16[128,1280]{1,0:T(8,128)(2,1)S(1)} %get-tuple-element.126.refs_2_, ...), custom_call_target="tpu_custom_call" | custom-call | tf_op jit(solution)/shard_map/pallas_call | solution.py:94
  155.7 5.6 %collective-permute-start.39 = (bf16[128,1280]{1,0:T(8,128)(2,1)S(1)}, bf16[128,1280]{1,0:T(8,128)(2,1)S(1)}, u32[]{:S(2)}, u32[]{:S(2)}) collective-permute-start(bf16[128,1280]{1,0:T(8,128)(2,1)S(1)} %get-tuple-element.127), channel_id=1, source_target_pairs={{0,6},{2,0},{4,2},{6,4},{1,7},{3,1},{5,3},{7,5},{8,14},{10,8},{12,... | collective-permute-start | bytes 983048 | tf_op jit(solution)/shard_map/ppermute | solution.py:37
  161.3 4.4 %shard_map.132 = (bf16[384,1280]{1,0:T(8,128)(2,1)S(1)}, f32[1,1280]{1,0:T(1,128)S(1)}) custom-call(bf16[128,1664]{1,0:T(8,128)(2,1)S(1)} %shard_map.129.refs_0_, bf16[128,1664]{1,0:T(8,128)(2,1)S(1)} %collective-permute-done.27.refs_1_, bf16[128,1664]{1,0:T(8,128)(2,1)S(1)} %collective-permute-done.28.refs_2_, ...), custom_call_target="tpu_custom_call" | custom-call | tf_op jit(solution)/shard_map/pallas_call | solution.py:94
  171.1 3.5 %shard_map.130 = (bf16[128,1280]{1,0:T(8,128)(2,1)S(1)}, bf16[128,1280]{1,0:T(8,128)(2,1)S(1)}, bf16[128,1280]{1,0:T(8,128)(2,1)S(1)}, f32[384,1]{1,0:T(8,128)}) custom-call(bf16[128,768]{1,0:T(8,128)(2,1)S(1)} %get-tuple-element.117.refs_0_, bf16[128,768]{1,0:T(8,128)(2,1)S(1)} %collective-permute-done.30.refs_1_, ...), custom_call_target="tpu_custom_call" | custom-call | tf_op jit(solution)/shard_map/pallas_call | solution.py:94
  179.4 2.4 shard_map.131
  183.5 1.7 shard_map.135
  186.7 8.7 %collective-permute-done.33 = bf16[128,1280]{1,0:T(8,128)(2,1)S(1)} collective-permute-done((bf16[128,1280]{1,0:T(8,128)(2,1)S(1)}, bf16[128,1280]{1,0:T(8,128)(2,1)S(1)}, u32[]{:S(2)}, u32[]{:S(2)}) %collective-permute-start.33) | collective-permute-done | bytes 327712 | tf_op jit(solution)/shard_map/ppermute | solution.py:32
  195.5 2.2 shard_map.134
  197.7 2.1 collective-permute-start.37
  200.8 4.8 %collective-permute-done.37.refs_1_ = bf16[128,768]{1,0:T(8,128)(2,1)S(1)} collective-permute-done((bf16[128,768]{1,0:T(8,128)(2,1)S(1)}, bf16[128,768]{1,0:T(8,128)(2,1)S(1)}, u32[]{:S(2)}, u32[]{:S(2)}) %collective-permute-start.37) | collective-permute-done | bytes 196640 | tf_op jit(solution)/shard_map/ppermute | solution.py:32
  205.6 3.6 %collective-permute-done.38.refs_2_ = bf16[128,768]{1,0:T(8,128)(2,1)S(1)} collective-permute-done((bf16[128,768]{1,0:T(8,128)(2,1)S(1)}, bf16[128,768]{1,0:T(8,128)(2,1)S(1)}, u32[]{:S(2)}, u32[]{:S(2)}) %collective-permute-start.38) | collective-permute-done | bytes 196640 | tf_op jit(solution)/shard_map/ppermute | solution.py:32
  209.7 2.0 collective-permute-start.46
  215.1 3.9 %collective-permute-done.46.refs_0_ = bf16[128,1664]{1,0:T(8,128)(2,1)S(1)} collective-permute-done((bf16[128,1664]{1,0:T(8,128)(2,1)S(1)}, bf16[128,1664]{1,0:T(8,128)(2,1)S(1)}, u32[]{:S(2)}, u32[]{:S(2)}) %collective-permute-start.46) | collective-permute-done | bytes 426016 | tf_op jit(solution)/shard_map/ppermute | solution.py:32
  218.9 4.5 %collective-permute-done.43.refs_2_ = bf16[128,1664]{1,0:T(8,128)(2,1)S(1)} collective-permute-done((bf16[128,1664]{1,0:T(8,128)(2,1)S(1)}, bf16[128,1664]{1,0:T(8,128)(2,1)S(1)}, u32[]{:S(2)}, u32[]{:S(2)}) %collective-permute-start.43) | collective-permute-done | bytes 426016 | tf_op jit(solution)/shard_map/ppermute | solution.py:32
  227.7 3.4 %shard_map.138 = (bf16[128,1280]{1,0:T(8,128)(2,1)S(1)}, f32[1,1280]{1,0:T(1,128)S(1)}) custom-call(bf16[128,1664]{1,0:T(8,128)(2,1)S(1)} %collective-permute-done.46.refs_0_, f32[128,1]{1,0:T(8,128)S(1)} %get-tuple-element.98.refs_1_, bf16[128,1280]{1,0:T(8,128)(2,1)S(1)} %get-tuple-element.139.refs_2_, bf16[128,1280]{1,0:T(8,128)(2,1)S(1)} %copy-done.18, ...), custom_call_target="tpu_custom_call" | custom-call | tf_op jit(solution)/shard_map/pallas_call | solution.py:94
  232.1 2.7 %fusion.5 = bf16[768,1280]{1,0:T(8,128)(2,1)} fusion(bf16[768,1280]{1,0:T(8,128)(2,1)S(1)} %collective-permute-done.42, bf16[768,1280]{1,0:T(8,128)(2,1)S(1)} %convolution_convert_fusion, bf16[512,768]{1,0:T(8,128)(2,1)S(1)} %constant_dynamic-update-slice_fusion.8, bf16[512,1280]{1,0:T(8,128)(2,1)S(1)} %constant_dynamic-update-slice_fusion.12, ...), kind=kOutput, calls=%fused_computation.11 | convolution fusion | flops 1012203520 | bytes 7995904 | tf_op jit(solution)/shard_map/dot_general | solution.py:22
  234.8 4.6 %shard_map.137 = (bf16[128,1280]{1,0:T(8,128)(2,1)S(1)}, bf16[128,1280]{1,0:T(8,128)(2,1)S(1)}, bf16[128,1280]{1,0:T(8,128)(2,1)S(1)}, f32[1,1280]{1,0:T(1,128)S(1)}) custom-call(bf16[128,1664]{1,0:T(8,128)(2,1)S(1)} %shard_map.136.refs_0_, bf16[128,1664]{1,0:T(8,128)(2,1)S(1)} %collective-permute-done.41.refs_1_, ...), custom_call_target="tpu_custom_call" | custom-call | tf_op jit(solution)/shard_map/pallas_call | solution.py:94
  239.4 1.8 collective-permute-start.44
  244.3 2.7 %fusion.4 = bf16[1280,768]{1,0:T(8,128)(2,1)} fusion(bf16[1280,768]{1,0:T(8,128)(2,1)S(1)} %collective-permute-done.48, bf16[1280,768]{1,0:T(8,128)(2,1)S(1)} %convolution_convert_fusion.3, bf16[512,1280]{1,0:T(8,128)(2,1)S(1)} %copy-done.32, bf16[512,768]{1,0:T(8,128)(2,1)S(1)} %get-tuple-element.147, pred[512]{0:T(512)(128)(4,1)S(1)} %get-tuple-element.159), kind=kOutput, calls=%fused_computation.10 | convolution fusion | flops 1011941376 | bytes 7995904 | tf_op jit(solution)/shard_map/dot_general | solution.py:22
  246.9 2.7 %fusion.3 = bf16[1280,768]{1,0:T(8,128)(2,1)} fusion(bf16[1280,768]{1,0:T(8,128)(2,1)S(1)} %collective-permute-done.49, bf16[1280,768]{1,0:T(8,128)(2,1)S(1)} %convolution_convert_fusion.2, bf16[512,1280]{1,0:T(8,128)(2,1)S(1)} %copy-done.32, bf16[512,768]{1,0:T(8,128)(2,1)S(1)} %get-tuple-element.148, pred[512]{0:T(512)(128)(4,1)S(1)} %get-tuple-element.159), kind=kOutput, calls=%fused_computation.9 | convolution fusion | flops 1011941376 | bytes 7995904 | tf_op jit(solution)/shard_map/dot_general | solution.py:22
  251.3 2.0 collective-permute-done.50
  (216 shorter events, 83.6 us)
Async XLA Ops:
  0.6 8.6 %collective-permute-start.2 = (bf16[1280,768]{1,0:T(8,128)(2,1)}, bf16[1280,768]{1,0:T(8,128)(2,1)}, u32[]{:S(2)}, u32[]{:S(2)}) collective-permute-start(bf16[1280,768]{1,0:T(8,128)(2,1)} %bitcast.42), channel_id=1, source_target_pairs={{0,1},{1,0},{2,3},{3,2},{4,5},{5,4},{6,7},{7,6},{8,9},{9,8},{10,11... | collective-permute-start | bytes 5898248 | tf_op jit(solution)/shard_map/ppermute | solution.py:32
  1.2 8.1 %collective-permute-start.3 = (bf16[1280,768]{1,0:T(8,128)(2,1)}, bf16[1280,768]{1,0:T(8,128)(2,1)}, u32[]{:S(2)}, u32[]{:S(2)}) collective-permute-start(bf16[1280,768]{1,0:T(8,128)(2,1)} %bitcast.44), channel_id=1, source_target_pairs={{0,1},{1,0},{2,3},{3,2},{4,5},{5,4},{6,7},{7,6},{8,9},{9,8},{10,11... | collective-permute-start | bytes 5898248 | tf_op jit(solution)/shard_map/ppermute | solution.py:32
  1.2 9.5 %collective-permute-start.4 = (bf16[768,1280]{1,0:T(8,128)(2,1)}, bf16[768,1280]{1,0:T(8,128)(2,1)}, u32[]{:S(2)}, u32[]{:S(2)}) collective-permute-start(bf16[768,1280]{1,0:T(8,128)(2,1)} %bitcast.46), channel_id=1, source_target_pairs={{0,1},{1,0},{2,3},{3,2},{4,5},{5,4},{6,7},{7,6},{8,9},{9,8},{10,11... | collective-permute-start | bytes 5898248 | tf_op jit(solution)/shard_map/ppermute | solution.py:32
  4.8 21.4 %collective-permute-start = (bf16[144,1280]{1,0:T(8,128)(2,1)S(1)}, bf16[144,1280]{1,0:T(8,128)(2,1)S(1)}, u32[]{:S(2)}, u32[]{:S(2)}) collective-permute-start(bf16[144,1280]{1,0:T(8,128)(2,1)S(1)} %get-tuple-element.178), channel_id=1, source_target_pairs={{0,8},{8,0},{16,24},{24,16},{1,9},{9,1},{17,25},{25,17},{2,10},{10... | collective-permute-start | bytes 1105928 | tf_op jit(solution)/shard_map/ppermute | solution.py:32
  7.4 19.6 %collective-permute-start.1 = (bf16[144,1280]{1,0:T(8,128)(2,1)S(1)}, bf16[144,1280]{1,0:T(8,128)(2,1)S(1)}, u32[]{:S(2)}, u32[]{:S(2)}) collective-permute-start(bf16[144,1280]{1,0:T(8,128)(2,1)S(1)} %get-tuple-element.179), channel_id=1, source_target_pairs={{0,16},{8,24},{16,0},{24,8},{1,17},{9,25},{17,1},{25,9},{2,18},{10... | collective-permute-start | bytes 1105928 | tf_op jit(solution)/shard_map/ppermute | solution.py:32
  21.6 19.7 %collective-permute-start.7 = (bf16[144,1280]{1,0:T(8,128)(2,1)}, bf16[144,1280]{1,0:T(8,128)(2,1)}, u32[]{:S(2)}, u32[]{:S(2)}) collective-permute-start(bf16[144,1280]{1,0:T(8,128)(2,1)} %get-tuple-element.91), channel_id=1, source_target_pairs={{0,24},{8,16},{16,8},{24,0},{1,25},{9,17},{17,9},{25,1},{2,26},{10... | collective-permute-start | bytes 1105928 | tf_op jit(solution)/shard_map/ppermute | solution.py:32
  40.7 12.3 %collective-permute-start.5 = (bf16[128,1536]{1,0:T(8,128)(2,1)}, bf16[128,1536]{1,0:T(8,128)(2,1)}, u32[]{:S(2)}, u32[]{:S(2)}) collective-permute-start(bf16[128,1536]{1,0:T(8,128)(2,1)} %get-tuple-element.87), channel_id=1, source_target_pairs={{0,8},{8,0},{16,24},{24,16},{1,9},{9,1},{17,25},{25,17},{2,10},{10... | collective-permute-start | bytes 1179656 | tf_op jit(solution)/shard_map/ppermute | solution.py:32
  41.3 19.3 %collective-permute-start.6 = (bf16[128,1536]{1,0:T(8,128)(2,1)}, bf16[128,1536]{1,0:T(8,128)(2,1)}, u32[]{:S(2)}, u32[]{:S(2)}) collective-permute-start(bf16[128,1536]{1,0:T(8,128)(2,1)} %get-tuple-element.88), channel_id=1, source_target_pairs={{0,16},{8,24},{16,0},{24,8},{1,17},{9,25},{17,1},{25,9},{2,18},{10... | collective-permute-start | bytes 1179656 | tf_op jit(solution)/shard_map/ppermute | solution.py:32
  46.2 14.4 %collective-permute-start.8 = (bf16[128,1536]{1,0:T(8,128)(2,1)}, bf16[128,1536]{1,0:T(8,128)(2,1)}, u32[]{:S(2)}, u32[]{:S(2)}) collective-permute-start(bf16[128,1536]{1,0:T(8,128)(2,1)} %get-tuple-element.92), channel_id=1, source_target_pairs={{0,24},{8,16},{16,8},{24,0},{1,25},{9,17},{17,9},{25,1},{2,26},{10... | collective-permute-start | bytes 1179656 | tf_op jit(solution)/shard_map/ppermute | solution.py:32
  64.2 8.7 %collective-permute-start.14 = (bf16[128,768]{1,0:T(8,128)(2,1)S(1)}, bf16[128,768]{1,0:T(8,128)(2,1)S(1)}, u32[]{:S(2)}, u32[]{:S(2)}) collective-permute-start(bf16[128,768]{1,0:T(8,128)(2,1)S(1)} %get-tuple-element.93.refs_0_), channel_id=1, source_target_pairs={{0,24},{8,16},{16,8},{24,0},{1,25},{9,17},{17,9},{25,1},{2,26},{10... | collective-permute-start | bytes 589832 | tf_op jit(solution)/shard_map/ppermute | solution.py:32
  65.7 13.6 %collective-permute-start.10 = (bf16[128,768]{1,0:T(8,128)(2,1)S(1)}, bf16[128,768]{1,0:T(8,128)(2,1)S(1)}, u32[]{:S(2)}, u32[]{:S(2)}) collective-permute-start(bf16[128,768]{1,0:T(8,128)(2,1)S(1)} %get-tuple-element.93.refs_0_), channel_id=1, source_target_pairs={{0,16},{8,24},{16,0},{24,8},{1,17},{9,25},{17,1},{25,9},{2,18},{10... | collective-permute-start | bytes 589832 | tf_op jit(solution)/shard_map/ppermute | solution.py:32
  67.2 12.1 %collective-permute-start.9 = (bf16[128,768]{1,0:T(8,128)(2,1)S(1)}, bf16[128,768]{1,0:T(8,128)(2,1)S(1)}, u32[]{:S(2)}, u32[]{:S(2)}) collective-permute-start(bf16[128,768]{1,0:T(8,128)(2,1)S(1)} %get-tuple-element.93.refs_0_), channel_id=1, source_target_pairs={{0,8},{8,0},{16,24},{24,16},{1,9},{9,1},{17,25},{25,17},{2,10},{10... | collective-permute-start | bytes 589832 | tf_op jit(solution)/shard_map/ppermute | solution.py:32
  76.2 19.8 %collective-permute-start.15 = (f32[128,1]{1,0:T(8,128)S(1)}, f32[128,1]{1,0:T(8,128)S(1)}, u32[]{:S(2)}, u32[]{:S(2)}) collective-permute-start(f32[128,1]{1,0:T(8,128)S(1)} %get-tuple-element.100), channel_id=1, source_target_pairs={{0,24},{8,16},{16,8},{24,0},{1,25},{9,17},{17,9},{25,1},{2,26},{10... | collective-permute-start | bytes 1544 | tf_op jit(solution)/shard_map/ppermute | solution.py:32
  77.8 21.9 %collective-permute-start.23 = (bf16[128,1280]{1,0:T(8,128)(2,1)S(1)}, bf16[128,1280]{1,0:T(8,128)(2,1)S(1)}, u32[]{:S(2)}, u32[]{:S(2)}) collective-permute-start(bf16[128,1280]{1,0:T(8,128)(2,1)S(1)} %get-tuple-element.101), channel_id=1, source_target_pairs={{0,2},{2,4},{4,6},{6,0},{1,3},{3,5},{5,7},{7,1},{8,10},{10,12},{12... | collective-permute-start | bytes 983048 | tf_op jit(solution)/shard_map/ppermute | solution.py:37
  82.2 30.2 %collective-permute-start.11 = (bf16[384,1280]{1,0:T(8,128)(2,1)S(1)}, bf16[384,1280]{1,0:T(8,128)(2,1)S(1)}, u32[]{:S(2)}, u32[]{:S(2)}) collective-permute-start(bf16[384,1280]{1,0:T(8,128)(2,1)S(1)} %get-tuple-element.96), channel_id=1, source_target_pairs={{0,2},{2,4},{4,6},{6,0},{1,3},{3,5},{5,7},{7,1},{8,10},{10,12},{12... | collective-permute-start | bytes 2949128 | tf_op jit(solution)/shard_map/ppermute | solution.py:37
  84.9 8.3 %collective-permute-start.17 = (bf16[128,1280]{1,0:T(8,128)(2,1)S(1)}, bf16[128,1280]{1,0:T(8,128)(2,1)S(1)}, u32[]{:S(2)}, u32[]{:S(2)}) collective-permute-start(bf16[128,1280]{1,0:T(8,128)(2,1)S(1)} %get-tuple-element.168), channel_id=1, source_target_pairs={{0,8},{8,0},{16,24},{24,16},{1,9},{9,1},{17,25},{25,17},{2,10},{10... | collective-permute-start | bytes 983048 | tf_op jit(solution)/shard_map/ppermute | solution.py:32
  96.1 11.6 %collective-permute-start.25 = (bf16[128,1280]{1,0:T(8,128)(2,1)S(1)}, bf16[128,1280]{1,0:T(8,128)(2,1)S(1)}, u32[]{:S(2)}, u32[]{:S(2)}) collective-permute-start(bf16[128,1280]{1,0:T(8,128)(2,1)S(1)} %get-tuple-element.166), channel_id=1, source_target_pairs={{0,24},{8,16},{16,8},{24,0},{1,25},{9,17},{17,9},{25,1},{2,26},{10... | collective-permute-start | bytes 983048 | tf_op jit(solution)/shard_map/ppermute | solution.py:32
  98.0 14.4 %collective-permute-start.19 = (bf16[128,768]{1,0:T(8,128)(2,1)S(1)}, bf16[128,768]{1,0:T(8,128)(2,1)S(1)}, u32[]{:S(2)}, u32[]{:S(2)}) collective-permute-start(bf16[128,768]{1,0:T(8,128)(2,1)S(1)} %get-tuple-element.104), channel_id=1, source_target_pairs={{0,8},{8,0},{16,24},{24,16},{1,9},{9,1},{17,25},{25,17},{2,10},{10... | collective-permute-start | bytes 589832 | tf_op jit(solution)/shard_map/ppermute | solution.py:32
  99.0 13.5 %collective-permute-start.20 = (bf16[128,768]{1,0:T(8,128)(2,1)S(1)}, bf16[128,768]{1,0:T(8,128)(2,1)S(1)}, u32[]{:S(2)}, u32[]{:S(2)}) collective-permute-start(bf16[128,768]{1,0:T(8,128)(2,1)S(1)} %get-tuple-element.105), channel_id=1, source_target_pairs={{0,16},{8,24},{16,0},{24,8},{1,17},{9,25},{17,1},{25,9},{2,18},{10... | collective-permute-start | bytes 589832 | tf_op jit(solution)/shard_map/ppermute | solution.py:32
  99.7 11.6 %collective-permute-start.16 = (f32[128,1]{1,0:T(8,128)S(1)}, f32[128,1]{1,0:T(8,128)S(1)}, u32[]{:S(2)}, u32[]{:S(2)}) collective-permute-start(f32[128,1]{1,0:T(8,128)S(1)} %add_rsqrt_fusion), channel_id=1, source_target_pairs={{0,2},{2,4},{4,6},{6,0},{1,3},{3,5},{5,7},{7,1},{8,10},{10,12},{12... | collective-permute-start | bytes 1544 | tf_op jit(solution)/shard_map/ppermute | solution.py:37
  107.7 12.6 %collective-permute-start.24 = (bf16[128,1536]{1,0:T(8,128)(2,1)S(1)}, bf16[128,1536]{1,0:T(8,128)(2,1)S(1)}, u32[]{:S(2)}, u32[]{:S(2)}) collective-permute-start(bf16[128,1536]{1,0:T(8,128)(2,1)S(1)} %get-tuple-element.111), channel_id=1, source_target_pairs={{0,24},{8,16},{16,8},{24,0},{1,25},{9,17},{17,9},{25,1},{2,26},{10... | collective-permute-start | bytes 1179656 | tf_op jit(solution)/shard_map/ppermute | solution.py:32
  111.3 17.5 %collective-permute-start.26 = (bf16[128,768]{1,0:T(8,128)(2,1)S(1)}, bf16[128,768]{1,0:T(8,128)(2,1)S(1)}, u32[]{:S(2)}, u32[]{:S(2)}) collective-permute-start(bf16[128,768]{1,0:T(8,128)(2,1)S(1)} %get-tuple-element.114), channel_id=1, source_target_pairs={{0,24},{8,16},{16,8},{24,0},{1,25},{9,17},{17,9},{25,1},{2,26},{10... | collective-permute-start | bytes 589832 | tf_op jit(solution)/shard_map/ppermute | solution.py:32
  116.7 11.6 %collective-permute-start.21 = (bf16[128,1536]{1,0:T(8,128)(2,1)S(1)}, bf16[128,1536]{1,0:T(8,128)(2,1)S(1)}, u32[]{:S(2)}, u32[]{:S(2)}) collective-permute-start(bf16[128,1536]{1,0:T(8,128)(2,1)S(1)} %get-tuple-element.108), channel_id=1, source_target_pairs={{0,8},{8,0},{16,24},{24,16},{1,9},{9,1},{17,25},{25,17},{2,10},{10... | collective-permute-start | bytes 1179656 | tf_op jit(solution)/shard_map/ppermute | solution.py:32
  117.1 11.1 %collective-permute-start.22 = (bf16[128,1536]{1,0:T(8,128)(2,1)S(1)}, bf16[128,1536]{1,0:T(8,128)(2,1)S(1)}, u32[]{:S(2)}, u32[]{:S(2)}) collective-permute-start(bf16[128,1536]{1,0:T(8,128)(2,1)S(1)} %get-tuple-element.109), channel_id=1, source_target_pairs={{0,16},{8,24},{16,0},{24,8},{1,17},{9,25},{17,1},{25,9},{2,18},{10... | collective-permute-start | bytes 1179656 | tf_op jit(solution)/shard_map/ppermute | solution.py:32
  129.3 12.2 %collective-permute-start.29 = (bf16[128,1664]{1,0:T(8,128)(2,1)S(1)}, bf16[128,1664]{1,0:T(8,128)(2,1)S(1)}, u32[]{:S(2)}, u32[]{:S(2)}) collective-permute-start(bf16[128,1664]{1,0:T(8,128)(2,1)S(1)} %shard_map.129.refs_0_), channel_id=1, source_target_pairs={{0,24},{8,16},{16,8},{24,0},{1,25},{9,17},{17,9},{25,1},{2,26},{10... | collective-permute-start | bytes 1277960 | tf_op jit(solution)/shard_map/ppermute | solution.py:32
  130.1 16.4 %collective-permute-start.28 = (bf16[128,1664]{1,0:T(8,128)(2,1)S(1)}, bf16[128,1664]{1,0:T(8,128)(2,1)S(1)}, u32[]{:S(2)}, u32[]{:S(2)}) collective-permute-start(bf16[128,1664]{1,0:T(8,128)(2,1)S(1)} %shard_map.129.refs_0_), channel_id=1, source_target_pairs={{0,16},{8,24},{16,0},{24,8},{1,17},{9,25},{17,1},{25,9},{2,18},{10... | collective-permute-start | bytes 1277960 | tf_op jit(solution)/shard_map/ppermute | solution.py:32
  134.7 14.1 %collective-permute-start.27 = (bf16[128,1664]{1,0:T(8,128)(2,1)S(1)}, bf16[128,1664]{1,0:T(8,128)(2,1)S(1)}, u32[]{:S(2)}, u32[]{:S(2)}) collective-permute-start(bf16[128,1664]{1,0:T(8,128)(2,1)S(1)} %shard_map.129.refs_0_), channel_id=1, source_target_pairs={{0,8},{8,0},{16,24},{24,16},{1,9},{9,1},{17,25},{25,17},{2,10},{10... | collective-permute-start | bytes 1277960 | tf_op jit(solution)/shard_map/ppermute | solution.py:32
  148.8 26.6 %collective-permute-start.34 = (bf16[128,768]{1,0:T(8,128)(2,1)S(1)}, bf16[128,768]{1,0:T(8,128)(2,1)S(1)}, u32[]{:S(2)}, u32[]{:S(2)}) collective-permute-start(bf16[128,768]{1,0:T(8,128)(2,1)S(1)} %get-tuple-element.117.refs_0_), channel_id=1, source_target_pairs={{0,24},{8,16},{16,8},{24,0},{1,25},{9,17},{17,9},{25,1},{2,26},{10... | collective-permute-start | bytes 589832 | tf_op jit(solution)/shard_map/ppermute | solution.py:32
  148.8 22.3 %collective-permute-start.31 = (bf16[128,768]{1,0:T(8,128)(2,1)S(1)}, bf16[128,768]{1,0:T(8,128)(2,1)S(1)}, u32[]{:S(2)}, u32[]{:S(2)}) collective-permute-start(bf16[128,768]{1,0:T(8,128)(2,1)S(1)} %get-tuple-element.117.refs_0_), channel_id=1, source_target_pairs={{0,16},{8,24},{16,0},{24,8},{1,17},{9,25},{17,1},{25,9},{2,18},{10... | collective-permute-start | bytes 589832 | tf_op jit(solution)/shard_map/ppermute | solution.py:32
  150.8 20.3 %collective-permute-start.30 = (bf16[128,768]{1,0:T(8,128)(2,1)S(1)}, bf16[128,768]{1,0:T(8,128)(2,1)S(1)}, u32[]{:S(2)}, u32[]{:S(2)}) collective-permute-start(bf16[128,768]{1,0:T(8,128)(2,1)S(1)} %get-tuple-element.117.refs_0_), channel_id=1, source_target_pairs={{0,8},{8,0},{16,24},{24,16},{1,9},{9,1},{17,25},{25,17},{2,10},{10... | collective-permute-start | bytes 589832 | tf_op jit(solution)/shard_map/ppermute | solution.py:32
  155.7 27.8 %collective-permute-start.39 = (bf16[128,1280]{1,0:T(8,128)(2,1)S(1)}, bf16[128,1280]{1,0:T(8,128)(2,1)S(1)}, u32[]{:S(2)}, u32[]{:S(2)}) collective-permute-start(bf16[128,1280]{1,0:T(8,128)(2,1)S(1)} %get-tuple-element.127), channel_id=1, source_target_pairs={{0,6},{2,0},{4,2},{6,4},{1,7},{3,1},{5,3},{7,5},{8,14},{10,8},{12,... | collective-permute-start | bytes 983048 | tf_op jit(solution)/shard_map/ppermute | solution.py:37
  165.7 29.8 %collective-permute-start.36 = (bf16[384,1280]{1,0:T(8,128)(2,1)S(1)}, bf16[384,1280]{1,0:T(8,128)(2,1)S(1)}, u32[]{:S(2)}, u32[]{:S(2)}) collective-permute-start(bf16[384,1280]{1,0:T(8,128)(2,1)S(1)} %get-tuple-element.123), channel_id=1, source_target_pairs={{0,6},{2,0},{4,2},{6,4},{1,7},{3,1},{5,3},{7,5},{8,14},{10,8},{12,... | collective-permute-start | bytes 2949128 | tf_op jit(solution)/shard_map/ppermute | solution.py:37
  174.7 12.0 %collective-permute-start.32 = (bf16[128,1280]{1,0:T(8,128)(2,1)S(1)}, bf16[128,1280]{1,0:T(8,128)(2,1)S(1)}, u32[]{:S(2)}, u32[]{:S(2)}) collective-permute-start(bf16[128,1280]{1,0:T(8,128)(2,1)S(1)} %get-tuple-element.119), channel_id=1, source_target_pairs={{0,8},{8,0},{16,24},{24,16},{1,9},{9,1},{17,25},{25,17},{2,10},{10... | collective-permute-start | bytes 983048 | tf_op jit(solution)/shard_map/ppermute | solution.py:32
  178.0 17.4 %collective-permute-start.33 = (bf16[128,1280]{1,0:T(8,128)(2,1)S(1)}, bf16[128,1280]{1,0:T(8,128)(2,1)S(1)}, u32[]{:S(2)}, u32[]{:S(2)}) collective-permute-start(bf16[128,1280]{1,0:T(8,128)(2,1)S(1)} %get-tuple-element.120), channel_id=1, source_target_pairs={{0,16},{8,24},{16,0},{24,8},{1,17},{9,25},{17,1},{25,9},{2,18},{10... | collective-permute-start | bytes 983048 | tf_op jit(solution)/shard_map/ppermute | solution.py:32
  181.8 13.6 %collective-permute-start.35 = (bf16[128,1280]{1,0:T(8,128)(2,1)S(1)}, bf16[128,1280]{1,0:T(8,128)(2,1)S(1)}, u32[]{:S(2)}, u32[]{:S(2)}) collective-permute-start(bf16[128,1280]{1,0:T(8,128)(2,1)S(1)} %get-tuple-element.121), channel_id=1, source_target_pairs={{0,24},{8,16},{16,8},{24,0},{1,25},{9,17},{17,9},{25,1},{2,26},{10... | collective-permute-start | bytes 983048 | tf_op jit(solution)/shard_map/ppermute | solution.py:32
  185.2 20.4 %collective-permute-start.40 = (bf16[128,768]{1,0:T(8,128)(2,1)S(1)}, bf16[128,768]{1,0:T(8,128)(2,1)S(1)}, u32[]{:S(2)}, u32[]{:S(2)}) collective-permute-start(bf16[128,768]{1,0:T(8,128)(2,1)S(1)} %get-tuple-element.135), channel_id=1, source_target_pairs={{0,24},{8,16},{16,8},{24,0},{1,25},{9,17},{17,9},{25,1},{2,26},{10... | collective-permute-start | bytes 589832 | tf_op jit(solution)/shard_map/ppermute | solution.py:32
  199.9 9.4 %collective-permute-start.38 = (bf16[128,768]{1,0:T(8,128)(2,1)S(1)}, bf16[128,768]{1,0:T(8,128)(2,1)S(1)}, u32[]{:S(2)}, u32[]{:S(2)}) collective-permute-start(bf16[128,768]{1,0:T(8,128)(2,1)S(1)} %get-tuple-element.134), channel_id=1, source_target_pairs={{0,16},{8,24},{16,0},{24,8},{1,17},{9,25},{17,1},{25,9},{2,18},{10... | collective-permute-start | bytes 589832 | tf_op jit(solution)/shard_map/ppermute | solution.py:32
  209.7 9.2 %collective-permute-start.46 = (bf16[128,1664]{1,0:T(8,128)(2,1)S(1)}, bf16[128,1664]{1,0:T(8,128)(2,1)S(1)}, u32[]{:S(2)}, u32[]{:S(2)}) collective-permute-start(bf16[128,1664]{1,0:T(8,128)(2,1)S(1)} %shard_map.136.refs_0_), channel_id=1, source_target_pairs={{0,24},{8,16},{16,8},{24,0},{1,25},{9,17},{17,9},{25,1},{2,26},{10... | collective-permute-start | bytes 1277960 | tf_op jit(solution)/shard_map/ppermute | solution.py:32
  211.7 11.7 %collective-permute-start.43 = (bf16[128,1664]{1,0:T(8,128)(2,1)S(1)}, bf16[128,1664]{1,0:T(8,128)(2,1)S(1)}, u32[]{:S(2)}, u32[]{:S(2)}) collective-permute-start(bf16[128,1664]{1,0:T(8,128)(2,1)S(1)} %shard_map.136.refs_0_), channel_id=1, source_target_pairs={{0,16},{8,24},{16,0},{24,8},{1,17},{9,25},{17,1},{25,9},{2,18},{10... | collective-permute-start | bytes 1277960 | tf_op jit(solution)/shard_map/ppermute | solution.py:32
  212.9 11.5 %collective-permute-start.41 = (bf16[128,1664]{1,0:T(8,128)(2,1)S(1)}, bf16[128,1664]{1,0:T(8,128)(2,1)S(1)}, u32[]{:S(2)}, u32[]{:S(2)}) collective-permute-start(bf16[128,1664]{1,0:T(8,128)(2,1)S(1)} %shard_map.136.refs_0_), channel_id=1, source_target_pairs={{0,8},{8,0},{16,24},{24,16},{1,9},{9,1},{17,25},{25,17},{2,10},{10... | collective-permute-start | bytes 1277960 | tf_op jit(solution)/shard_map/ppermute | solution.py:32
  215.0 17.1 %collective-permute-start.42 = (bf16[768,1280]{1,0:T(8,128)(2,1)S(1)}, bf16[768,1280]{1,0:T(8,128)(2,1)S(1)}, u32[]{:S(2)}, u32[]{:S(2)}) collective-permute-start(bf16[768,1280]{1,0:T(8,128)(2,1)S(1)} %fusion.6), channel_id=1, source_target_pairs={{0,1},{1,0},{2,3},{3,2},{4,5},{5,4},{6,7},{7,6},{8,9},{9,8},{10,11... | collective-permute-start | bytes 5898248 | tf_op jit(solution)/shard_map/ppermute | solution.py:32
  227.1 15.0 %collective-permute-start.48 = (bf16[1280,768]{1,0:T(8,128)(2,1)S(1)}, bf16[1280,768]{1,0:T(8,128)(2,1)S(1)}, u32[]{:S(2)}, u32[]{:S(2)}) collective-permute-start(bf16[1280,768]{1,0:T(8,128)(2,1)S(1)} %fusion.7), channel_id=1, source_target_pairs={{0,1},{1,0},{2,3},{3,2},{4,5},{5,4},{6,7},{7,6},{8,9},{9,8},{10,11... | collective-permute-start | bytes 5898248 | tf_op jit(solution)/shard_map/ppermute | solution.py:32
  227.2 14.9 %collective-permute-start.49 = (bf16[1280,768]{1,0:T(8,128)(2,1)S(1)}, bf16[1280,768]{1,0:T(8,128)(2,1)S(1)}, u32[]{:S(2)}, u32[]{:S(2)}) collective-permute-start(bf16[1280,768]{1,0:T(8,128)(2,1)S(1)} %fusion.8), channel_id=1, source_target_pairs={{0,1},{1,0},{2,3},{3,2},{4,5},{5,4},{6,7},{7,6},{8,9},{9,8},{10,11... | collective-permute-start | bytes 5898248 | tf_op jit(solution)/shard_map/ppermute | solution.py:32
  231.1 18.5 %collective-permute-start.47 = (bf16[128,1280]{1,0:T(8,128)(2,1)S(1)}, bf16[128,1280]{1,0:T(8,128)(2,1)S(1)}, u32[]{:S(2)}, u32[]{:S(2)}) collective-permute-start(bf16[128,1280]{1,0:T(8,128)(2,1)S(1)} %get-tuple-element.144), channel_id=1, source_target_pairs={{0,24},{8,16},{16,8},{24,0},{1,25},{9,17},{17,9},{25,1},{2,26},{10... | collective-permute-start | bytes 983048 | tf_op jit(solution)/shard_map/ppermute | solution.py:32
  239.4 11.6 %collective-permute-start.44 = (bf16[128,1280]{1,0:T(8,128)(2,1)S(1)}, bf16[128,1280]{1,0:T(8,128)(2,1)S(1)}, u32[]{:S(2)}, u32[]{:S(2)}) collective-permute-start(bf16[128,1280]{1,0:T(8,128)(2,1)S(1)} %get-tuple-element.142), channel_id=1, source_target_pairs={{0,8},{8,0},{16,24},{24,16},{1,9},{9,1},{17,25},{25,17},{2,10},{10... | collective-permute-start | bytes 983048 | tf_op jit(solution)/shard_map/ppermute | solution.py:32
  241.2 9.7 %collective-permute-start.45 = (bf16[128,1280]{1,0:T(8,128)(2,1)S(1)}, bf16[128,1280]{1,0:T(8,128)(2,1)S(1)}, u32[]{:S(2)}, u32[]{:S(2)}) collective-permute-start(bf16[128,1280]{1,0:T(8,128)(2,1)S(1)} %get-tuple-element.143), channel_id=1, source_target_pairs={{0,16},{8,24},{16,0},{24,8},{1,17},{9,25},{17,1},{25,9},{2,18},{10... | collective-permute-start | bytes 983048 | tf_op jit(solution)/shard_map/ppermute | solution.py:32
  242.1 9.2 %collective-permute-start.52 = (f32[1,1280]{1,0:T(1,128)S(1)}, f32[1,1280]{1,0:T(1,128)S(1)}, u32[]{:S(2)}, u32[]{:S(2)}) collective-permute-start(f32[1,1280]{1,0:T(1,128)S(1)} %add_add_fusion), channel_id=1, source_target_pairs={{0,24},{8,16},{16,8},{24,0},{1,25},{9,17},{17,9},{25,1},{2,26},{10... | collective-permute-start | bytes 15368 | tf_op jit(solution)/shard_map/ppermute | solution.py:32
  243.1 8.2 %collective-permute-start.51 = (f32[1,1280]{1,0:T(1,128)S(1)}, f32[1,1280]{1,0:T(1,128)S(1)}, u32[]{:S(2)}, u32[]{:S(2)}) collective-permute-start(f32[1,1280]{1,0:T(1,128)S(1)} %add_add_fusion), channel_id=1, source_target_pairs={{0,16},{8,24},{16,0},{24,8},{1,17},{9,25},{17,1},{25,9},{2,18},{10... | collective-permute-start | bytes 15368 | tf_op jit(solution)/shard_map/ppermute | solution.py:32
  (40 other events, 202.3 us)
where the time goes:
time: 256 us; the launch traced here: 255 us
  waiting for transfers between devices  75.8 us (30%)
  starting transfers between devices  71.2 us (28%)
  Pallas kernels  58.1 us (23%)
  local copies, waits for them, and re-layouts  26.4 us (10%)
  matrix products  19.6 us (8%)
  other arithmetic  2.82 us (1%)
    ppermute x49, waiting for transfers between devices, swap(): return lax.ppermute(block, axis, partner_route(lax.axis_size(axis), step))  75.8 us
    ppermute x49, starting transfers between devices, swap(): return lax.ppermute(block, axis, partner_route(lax.axis_size(axis), step))  60.7 us
    pallas_call x20, Pallas kernels, kernel_call(): pl.pallas_call(call, in_specs=[in_vmem] * (count + kept), out_specs=[in_v...  53.6 us
    unnamed x78, local copies, waits for them, and re-layouts  21.5 us
    dot_general x12, matrix products, dot(): lax.dot_general(former, latter, ((contract[:1], contract[1:]), ((), ())),...  19.6 us
    ppermute x5, starting transfers between devices, shifted(): lax.ppermute(block, axis, [(i, (i + distance) % size) for i in range(size)])  10.5 us
  transfers between devices with their start and end apart: 54, of which 19 were waited for; matrix products, arithmetic and copies ran while one was open for 11% of the time, Pallas kernels for 22%

commit v1 on v0

--- a/solution.py
+++ b/solution.py
@@ -39,13 +39,6 @@
 
 def quarter_of(rows, index, width):
     return lax.dynamic_slice_in_dim(rows, index * width, width, axis=-1)
-
-
-def to_quarters(rows, dp_count):
-    width = rows.shape[-1] // dp_count
-    here = lax.axis_index("dp")
-    quarters = [quarter_of(rows, here ^ step, width) for step in range(dp_count)]
-    return quarters[:1] + [swap(quarters[step], "dp", step) for step in range(1, dp_count)]
 
 
 def assemble(parts):
@@ -61,13 +54,6 @@
     return assemble(
         [swap(part, "dp", step) if step else part for step, part in enumerate(parts)]
     )
-
-
-def sum_parts(parts):
-    total = parts[0].astype(f32)
-    for step in range(1, len(parts)):
-        total = total + swap(parts[step], "dp", step).astype(f32)
-    return total
 
 
 def gather_rows(rows, dp_count):
@@ -150,6 +136,13 @@
     return pl.ds(pl.multiple_of(tile * size, size), size)
 
 
+def split_rows(rows_ref, mask_ref, other_ref, own_ref):
+    rows = rows_ref[...]
+    chosen = mask_ref[...] > 0.5
+    own_ref[...] = jnp.where(chosen, rows, jnp.zeros_like(rows))
+    other_ref[...] = jnp.where(chosen, jnp.zeros_like(rows), rows)
+
+
 def hidden_parts(blocks, part_rows, gain_part, mask, gate_pair, up_pair, expert=None):
     width, units = gate_pair[0].shape
     routed = expert is not None
@@ -160,8 +153,9 @@
 
     def body(operand_refs, weight_refs, out_refs, scratch):
         *block_refs, gain_ref, choice_ref = operand_refs
-        part_refs, gained_ref = out_refs[:parts_count], out_refs[parts_count]
-        mask_ref = out_refs[parts_count + 1] if routed else choice_ref
+        part_refs, (other_rows, own_rows) = out_refs[:parts_count], out_refs[parts_count:][:2]
+        mask_ref = out_refs[parts_count + 2] if routed else choice_ref
+        (gained_ref,) = scratch
         for index, ref in enumerate(block_refs):
             place = slice(index * block_rows, (index + 1) * block_rows)
             block = ref[:block_rows]
@@ -175,8 +169,9 @@
                 experts = dot(chosen, ref[block_rows:, :LANES], (1, 0)) - choice_ref[...]
                 for k in range(passes):
                     near = jnp.abs(experts[:, k : k + 1]) < 0.5
-                    out_refs[parts_count + 1 + k][place] = jnp.where(near, 1.0, 0.0)
-
+                    out_refs[parts_count + 2 + k][place] = jnp.where(near, 1.0, 0.0)
+
+        split_rows(gained_ref, mask_ref, other_rows, own_rows)
         for pair in range(2):
 
             def visit(columns, pair=pair):
@@ -195,12 +190,28 @@
         (*blocks, gain_part, expert if routed else mask),
         (*gate_pair, *up_pair),
         [jax.ShapeDtypeStruct((part_rows, 2 * units), bf16)] * parts_count
-        + [jax.ShapeDtypeStruct((rows, width), bf16)]
+        + [jax.ShapeDtypeStruct((rows, width), bf16)] * 2
         + [jax.ShapeDtypeStruct((rows, 1), f32)] * passes
         + [jax.ShapeDtypeStruct((rows, width), bf16)] * int(routed),
-        [],
-    )
-    return outs[:parts_count], outs[parts_count], outs[parts_count + 1 :]
+        [pltpu.VMEM((rows, width), bf16)],
+    )
+    return outs[:parts_count], outs[parts_count : parts_count + 2], outs[parts_count + 2 :]
+
+
+def row_scale(blocks, features, summed):
+    rows = blocks[0].shape[0]
+
+    def body(operand_refs, weight_refs, out_refs, scratch):
+        total = jnp.zeros((rows, 1), f32)
+        for ref in operand_refs:
+            wide = ref[...].astype(f32)
+            if not summed:
+                wide = jnp.sum(wide * wide, axis=-1, keepdims=True)
+            total = total + wide
+        out_refs[0][...] = lax.rsqrt(total / features + epsilon)
+
+    (scale,) = kernel_call(body, blocks, (), [jax.ShapeDtypeStruct((rows, 1), f32)], [])
+    return scale
 
 
 def activate(parts, inverse):
@@ -243,11 +254,11 @@
 
     def body(operand_refs, weight_refs, out_refs, scratch):
         *block_refs, mask_ref, hidden_ref = operand_refs
-        *row_refs, square_ref = out_refs
-        (joined,) = scratch
+        row_refs, square_refs = out_refs[:out_count], out_refs[out_count:-2]
+        joined, square_ref = scratch
         join(joined, block_refs, slice(None))
+        split_rows(joined, mask_ref, *out_refs[-2:])
         square_ref[...] = jnp.zeros_like(square_ref)
-
         own, other = weight_refs
 
         def visit(columns):
@@ -262,16 +273,18 @@
             store_parts(row_refs, columns, out)
 
         each_tile(width, visit)
+        store_parts(square_refs, slice(None), square_ref[...])
 
     outs = kernel_call(
         body,
         (*blocks, mask, hidden),
         down_pair,
         [jax.ShapeDtypeStruct((rows // out_count, width), bf16)] * out_count
-        + [jax.ShapeDtypeStruct((rows, 1), f32)],
-        [pltpu.VMEM((rows, units), bf16)],
-    )
-    return outs[:out_count], outs[out_count]
+        + [jax.ShapeDtypeStruct((part_rows, 1), f32)] * count
+        + [jax.ShapeDtypeStruct((rows, units), bf16)] * 2,
+        [pltpu.VMEM((rows, units), bf16), pltpu.VMEM((rows, 1), f32)],
+    )
+    return outs[:out_count], outs[out_count:-2], outs[-2:]
 
 
 def act_grad_parts(blocks, part_rows, mask, down_pair):
@@ -413,7 +426,8 @@
     route_rows = jnp.stack(
         [lax.dynamic_index_in_dim(route[0, :, :, 0], m, 0, keepdims=False) for m in micro], axis=1
     ).astype(bf16)
-    route_rows = jnp.pad(route_rows, ((0, 0), (0, width - PASSES)))
+    expert_id = jnp.full((1, LANES), expert, f32)
+    route_rows = after(jnp.pad(route_rows, ((0, 0), (0, width - PASSES))), expert_id)
 
     def tokens_quarter(step):
         return jnp.concatenate([quarter_of(own_tokens, here ^ step, width), route_rows])
@@ -427,11 +441,11 @@
     def moved(pieces, distance):
         return [shifted(piece, "pipe", distance) for piece in pieces]
 
-    def scale_of(square_sum):
-        return lax.rsqrt(square_sum / features + epsilon)
-
-    def weight_grad(left, right, mask, wanted):
-        return dot(left, jnp.where((mask > 0.5) == wanted, right, jnp.zeros_like(right)), (0, 0))
+    def weight_grad(lefts, right, wanted):
+        return dot(lefts[wanted], right, (0, 0))
+
+    def stacked(pairs):
+        return [jnp.concatenate(pieces) for pieces in zip(*pairs)]
 
     quarters = [tokens_quarter(step) for step in range(dp_count)]
     weights = [
@@ -443,9 +457,7 @@
     gate_pair, up_pair, down_pair = weights[:2], weights[2:4], weights[4:]
     quarters[-1] = after(quarters[-1], *weights)
     blocks = sent(quarters)
-    expert_id = jnp.full((1, LANES), expert, f32)
-    wide = own_tokens.astype(f32)
-    inverse = scale_of(jnp.sum(wide * wide, axis=-1, keepdims=True))
+    inverse = row_scale([own_tokens], features, False)
 
     parts, gained, masks, hidden = [], [], [], []
     for group in groups:
@@ -460,14 +472,17 @@
     gate, up, activated = activate(sent(parts), inverse)
     kept = [(hidden, gained, inverse, gate, up)]
     first_activated = gather_rows(activated, dp_count)
-    next_hidden, squares = [], []
+    next_hidden, squares, first_rows = [], [], []
     for group, mask, rows_in in zip(groups, masks[0], hidden):
-        (out,), square = add_down(first_activated[group], mask, down_pair, rows_in, False)
+        (out,), square, split = add_down(
+            first_activated[group], mask, down_pair, rows_in, False
+        )
         next_hidden.append(out)
-        squares += jnp.split(square, square.shape[0] // rows)
+        squares += square
+        first_rows.append(split)
     hidden = moved(next_hidden, 1)
     grad_blocks = sent([cotangent_quarter(step, *next_hidden) for step in range(dp_count)])
-    inverse = shifted(scale_of(sum_parts(squares)), "pipe", 1)
+    inverse = shifted(row_scale(sent(squares), features, True), "pipe", 1)
     act_parts, grad = [], []
     for group, mask in zip(groups, masks[1]):
         made, joined = act_grad_parts(grad_blocks[group], rows, mask, down_pair)
@@ -487,36 +502,20 @@
     gain_sum = jnp.zeros((1, width), f32)
     for k in reversed(range(PASSES)):
         hidden, gained, inverse, gate, up = kept[k]
-        gained = jnp.concatenate(gained)
-        mask = jnp.concatenate(masks[k])
+        gained = stacked(gained)
         payload = hidden_grads(act_parts, gate, up, inverse, features)
         both_grad = gather_rows(payload, dp_count)
         joined = jnp.concatenate(both_grad)
         rights = [joined[:, :units], joined[:, units : 2 * units]]
         if k == 0:
-            late_down = jnp.concatenate(first_activated)
-            grad_now = jnp.concatenate(grad)
-            other_down = swap(
-                (
-                    weight_grad(late_down, grad_now, mask, False) + early[False][2].astype(f32)
-                ).astype(bf16),
-                "expert",
-                1,
-            )
-            down_grad = (
-                weight_grad(late_down, grad_now, mask, True)
-                + early[True][2].astype(f32)
-                + other_down.astype(f32)
-            ).astype(bf16)
-            both_grad[1] = after(both_grad[1], down_grad)
-            received = [
-                swap(
-                    (weight_grad(gained, right, mask, False) + soon.astype(f32)).astype(bf16),
-                    "expert",
-                    1,
-                )
-                for right, soon in zip(rights, early[False])
+            lefts = [gained, gained, stacked(first_rows)]
+            rights.append(jnp.concatenate(grad))
+            given = [
+                (weight_grad(left, right, False) + soon.astype(f32)).astype(bf16)
+                for left, right, soon in zip(lefts, rights, early[False])
             ]
+            both_grad[1] = after(both_grad[1], given[2])
+            received = [swap(value, "expert", 1) for value in given]
         else:
             last_activated = gather_rows(after(activated, *both_grad[1:]), dp_count)
         outs = []
@@ -531,13 +530,16 @@
             grad = moved(outs, -1)
             rights = [after(right, *outs) for right in rights]
             early = {
-                wanted: [weight_grad(gained, right, mask, wanted).astype(bf16) for right in rights]
+                wanted: [weight_grad(gained, right, wanted).astype(bf16) for right in rights]
                 for wanted in (False, True)
             }
-            out_parts = []
+            out_parts, last_rows = [], []
             for group, choice, rows_in in zip(groups, masks[1], hidden):
-                made, _ = add_down(last_activated[group], choice, down_pair, rows_in, True)
+                made, _, split = add_down(
+                    last_activated[group], choice, down_pair, rows_in, True
+                )
                 out_parts += made
+                last_rows.append(split)
             out_rows = from_quarters(out_parts)
             grad[0] = after(grad[0], out_rows, *early[False], *early[True])
             act_parts, joined = [], []
@@ -546,11 +548,9 @@
                 act_parts += made
                 joined.append(copied)
             grad = joined
-            last_activated = jnp.concatenate(last_activated)
+            last_rows = stacked(last_rows)
             for wanted in (False, True):
-                early[wanted].append(
-                    weight_grad(last_activated, last_grad, mask, wanted).astype(bf16)
-                )
+                early[wanted].append(weight_grad(last_rows, last_grad, wanted).astype(bf16))
             act_parts = sent(act_parts)
             act_parts[1] = after(act_parts[1], early[False][2], early[True][2])
 
@@ -564,11 +564,9 @@
             gain_all, gain_rows[step], (here ^ step) * width, axis=0
         )
     grads = [
-        (
-            weight_grad(gained, right, mask, True) + soon.astype(f32) + other.astype(f32)
-        ).astype(bf16)
-        for right, soon, other in zip(rights, early[True], received)
-    ] + [down_grad]
+        (weight_grad(left, right, True) + soon.astype(f32) + other.astype(f32)).astype(bf16)
+        for left, right, soon, other in zip(lefts, rights, early[True], received)
+    ]
     returned = list(lax.optimization_barrier((*returned, *grads)))[:dp_count]
     entry = assemble(returned)
     return (

time: 256 us -> 241 us (0.941)
  local copies, waits for them, and re-layouts: 26.4 us -> 3.34 us
  waiting for transfers between devices: 75.8 us -> 87.4 us
  Pallas kernels: 58.1 us -> 55.4 us
    unnamed x78 -> x21, local copies, waits for them, and re-layouts: 21.5 us -> 1.02 us
    ppermute x49, waiting for transfers between devices: 75.8 us -> 85.8 us  [swap(): return lax.ppermute(block, axis, partner_route(lax.axis_size(axis), step))]
    pallas_call x20 -> x22, Pallas kernels: 53.6 us -> 50.9 us  [kernel_call(): pl.pallas_call(call, in_specs=[in_vmem] * (count + kept), out_specs=[in_v...]
  transfers between devices with their start and end apart: 54 -> 54, of which waited for: 19 -> 25; matrix products, arithmetic and copies ran while one was open for 11% -> 10% of each run, Pallas kernels for 22% -> 22%
where the time goes in v1:
time: 241 us
  waiting for transfers between devices  87.4 us (36%)
  starting transfers between devices  73.5 us (30%)
  Pallas kernels  55.4 us (23%)
  matrix products  19.3 us (8%)
  local copies, waits for them, and re-layouts  3.34 us (1%)
    ppermute x49, waiting for transfers between devices, swap(): return lax.ppermute(block, axis, partner_route(lax.axis_size(axis), step))  85.8 us
    ppermute x49, starting transfers between devices, swap(): return lax.ppermute(block, axis, partner_route(lax.axis_size(axis), step))  61.4 us
    pallas_call x22, Pallas kernels, kernel_call(): pl.pallas_call(call, in_specs=[in_vmem] * (count + kept), out_specs=[in_v...  50.9 us
    dot_general x12, matrix products, dot(): lax.dot_general(former, latter, ((contract[:1], contract[1:]), ((), ())),...  19.3 us
    ppermute x5, starting transfers between devices, shifted(): lax.ppermute(block, axis, [(i, (i + distance) % size) for i in range(size)])  12.1 us
  transfers between devices with their start and end apart: 54, of which 25 were waited for; matrix products, arithmetic and copies ran while one was open for 10% of the time, Pallas kernels for 22%

profile of v1, /device:TPU:0, one launch (start us, length us, event | category | flops | bytes accessed | tf_op | source)
XLA Modules:
  0.0 241.2 jit_solution(9612714041566316378)
XLA Ops:
  4.0 2.6 %collective-permute-start = (bf16[144,1280]{1,0:T(8,128)(2,1)S(1)}, bf16[144,1280]{1,0:T(8,128)(2,1)S(1)}, u32[]{:S(2)}, u32[]{:S(2)}) collective-permute-start(bf16[144,1280]{1,0:T(8,128)(2,1)S(1)} %get-tuple-element.203), channel_id=1, source_target_pairs={{0,8},{8,0},{16,24},{24,16},{1,9},{9,1},{17,25},{25,17},{2,10},{10... | collective-permute-start | bytes 1105928 | tf_op jit(solution)/shard_map/ppermute | solution.py:32
  8.1 2.6 %collective-permute-done.4.refs_5_ = bf16[768,1280]{1,0:T(8,128)(2,1)} collective-permute-done((bf16[768,1280]{1,0:T(8,128)(2,1)}, bf16[768,1280]{1,0:T(8,128)(2,1)}, u32[]{:S(2)}, u32[]{:S(2)}) %collective-permute-start.4) | collective-permute-done | bytes 1966112 | tf_op jit(solution)/shard_map/ppermute | solution.py:32
  10.7 4.5 %shard_map.118 = (bf16[1280,768]{1,0:T(8,128)(2,1)S(1)}, bf16[1280,768]{1,0:T(8,128)(2,1)S(1)}, bf16[1280,768]{1,0:T(8,128)(2,1)S(1)}, bf16[1280,768]{1,0:T(8,12...) custom-call(bf16[1280,768]{1,0:T(8,128)(2,1)} %bitcast.51, bf16[1280,768]{1,0:T(8,128)(2,1)} %copy-done.3, ...), custom_call_target="tpu_custom_call" | custom-call | bytes 23592960 | tf_op jit(solution)/shard_map/pallas_call | solution.py:104
  15.2 3.9 %collective-permute-start.7 = (bf16[144,1280]{1,0:T(8,128)(2,1)S(1)}, bf16[144,1280]{1,0:T(8,128)(2,1)S(1)}, u32[]{:S(2)}, u32[]{:S(2)}) collective-permute-start(bf16[144,1280]{1,0:T(8,128)(2,1)S(1)} %get-tuple-element.108), channel_id=1, source_target_pairs={{0,24},{8,16},{16,8},{24,0},{1,25},{9,17},{17,9},{25,1},{2,26},{10... | collective-permute-start | bytes 1105928 | tf_op jit(solution)/shard_map/ppermute | solution.py:32
  19.1 4.6 %shard_map.119 = (bf16[128,1536]{1,0:T(8,128)(2,1)S(1)}, bf16[128,1536]{1,0:T(8,128)(2,1)S(1)}, bf16[128,1536]{1,0:T(8,128)(2,1)S(1)}, bf16[384,1280]{1,0:T(8,12...) custom-call(bf16[144,1280]{1,0:T(8,128)(2,1)S(1)} %get-tuple-element, ...), custom_call_target="tpu_custom_call" | custom-call | tf_op jit(solution)/shard_map/pallas_call | solution.py:80
  24.4 4.1 %collective-permute-done.7.refs_0_ = bf16[144,1280]{1,0:T(8,128)(2,1)S(1)} collective-permute-done((bf16[144,1280]{1,0:T(8,128)(2,1)S(1)}, bf16[144,1280]{1,0:T(8,128)(2,1)S(1)}, u32[]{:S(2)}, u32[]{:S(2)}) %collective-permute-start.7) | collective-permute-done | bytes 368672 | tf_op jit(solution)/shard_map/ppermute | solution.py:32
  28.5 2.4 %shard_map.120 = (bf16[128,1536]{1,0:T(8,128)(2,1)S(1)}, bf16[128,1280]{1,0:T(8,128)(2,1)S(1)}, bf16[128,1280]{1,0:T(8,128)(2,1)S(1)}, f32[128,1]{1,0:T(8,128)S(...) custom-call(bf16[144,1280]{1,0:T(8,128)(2,1)S(1)} %collective-permute-done.7.refs_0_, ...), custom_call_target="tpu_custom_call" | custom-call | tf_op jit(solution)/shard_map/pallas_call | solution.py:80
  30.9 3.1 %collective-permute-start.8 = (bf16[128,1536]{1,0:T(8,128)(2,1)S(1)}, bf16[128,1536]{1,0:T(8,128)(2,1)S(1)}, u32[]{:S(2)}, u32[]{:S(2)}) collective-permute-start(bf16[128,1536]{1,0:T(8,128)(2,1)S(1)} %get-tuple-element.109), channel_id=1, source_target_pairs={{0,24},{8,16},{16,8},{24,0},{1,25},{9,17},{17,9},{25,1},{2,26},{10... | collective-permute-start | bytes 1179656 | tf_op jit(solution)/shard_map/ppermute | solution.py:32
  34.3 3.2 %collective-permute-done.5.refs_1_ = bf16[128,1536]{1,0:T(8,128)(2,1)S(1)} collective-permute-done((bf16[128,1536]{1,0:T(8,128)(2,1)S(1)}, bf16[128,1536]{1,0:T(8,128)(2,1)S(1)}, u32[]{:S(2)}, u32[]{:S(2)}) %collective-permute-start.5) | collective-permute-done | bytes 393248 | tf_op jit(solution)/shard_map/ppermute | solution.py:32
  37.5 7.3 %collective-permute-done.8.refs_3_ = bf16[128,1536]{1,0:T(8,128)(2,1)S(1)} collective-permute-done((bf16[128,1536]{1,0:T(8,128)(2,1)S(1)}, bf16[128,1536]{1,0:T(8,128)(2,1)S(1)}, u32[]{:S(2)}, u32[]{:S(2)}) %collective-permute-start.8) | collective-permute-done | bytes 393248 | tf_op jit(solution)/shard_map/ppermute | solution.py:32
  48.9 3.4 %collective-permute-done.10.refs_2_ = bf16[128,768]{1,0:T(8,128)(2,1)S(1)} collective-permute-done((bf16[128,768]{1,0:T(8,128)(2,1)S(1)}, bf16[128,768]{1,0:T(8,128)(2,1)S(1)}, u32[]{:S(2)}, u32[]{:S(2)}) %collective-permute-start.10) | collective-permute-done | bytes 196640 | tf_op jit(solution)/shard_map/ppermute | solution.py:32
  52.4 2.7 %collective-permute-done.9.refs_1_ = bf16[128,768]{1,0:T(8,128)(2,1)S(1)} collective-permute-done((bf16[128,768]{1,0:T(8,128)(2,1)S(1)}, bf16[128,768]{1,0:T(8,128)(2,1)S(1)}, u32[]{:S(2)}, u32[]{:S(2)}) %collective-permute-start.9) | collective-permute-done | bytes 196640 | tf_op jit(solution)/shard_map/ppermute | solution.py:32
  55.0 3.0 %shard_map.123 = (bf16[384,1280]{1,0:T(8,128)(2,1)S(1)}, f32[128,1]{1,0:T(8,128)S(1)}, f32[128,1]{1,0:T(8,128)S(1)}, f32[128,1]{1,0:T(8,128)S(1)}, bf16[384,768]...) custom-call(bf16[128,768]{1,0:T(8,128)(2,1)S(1)} %get-tuple-element.110.refs_0_, ...), custom_call_target="tpu_custom_call" | custom-call | tf_op jit(solution)/shard_map/pallas_call | solution.py:80
  59.7 1.9 shard_map.124
  63.7 2.5 %collective-permute-start.25 = (bf16[128,1280]{1,0:T(8,128)(2,1)S(1)}, bf16[128,1280]{1,0:T(8,128)(2,1)S(1)}, u32[]{:S(2)}, u32[]{:S(2)}) collective-permute-start(bf16[128,1280]{1,0:T(8,128)(2,1)S(1)} %get-tuple-element.194), channel_id=1, source_target_pairs={{0,24},{8,16},{16,8},{24,0},{1,25},{9,17},{17,9},{25,1},{2,26},{10... | collective-permute-start | bytes 983048 | tf_op jit(solution)/shard_map/ppermute | solution.py:32
  69.7 9.8 %collective-permute-done.13.refs_2_ = f32[128,1]{1,0:T(8,128)S(1)} collective-permute-done((f32[128,1]{1,0:T(8,128)S(1)}, f32[128,1]{1,0:T(8,128)S(1)}, u32[]{:S(2)}, u32[]{:S(2)}) %collective-permute-start.13) | collective-permute-done | bytes 544 | tf_op jit(solution)/shard_map/ppermute | solution.py:32
  82.8 2.2 shard_map.126
  91.8 2.3 shard_map.128
  95.9 6.0 %collective-permute-done.20.refs_2_ = bf16[128,768]{1,0:T(8,128)(2,1)S(1)} collective-permute-done((bf16[128,768]{1,0:T(8,128)(2,1)S(1)}, bf16[128,768]{1,0:T(8,128)(2,1)S(1)}, u32[]{:S(2)}, u32[]{:S(2)}) %collective-permute-start.20) | collective-permute-done | bytes 196640 | tf_op jit(solution)/shard_map/ppermute | solution.py:32
  102.0 4.4 %shard_map.127 = (bf16[128,1536]{1,0:T(8,128)(2,1)S(1)}, bf16[128,1536]{1,0:T(8,128)(2,1)S(1)}, bf16[128,1536]{1,0:T(8,128)(2,1)S(1)}, bf16[384,1280]{1,0:T(8,128)(2,1)S(1)}, bf16[384,1280]{1,0:T(8,128)(2,1)S(1)}) custom-call(bf16[384,1280]{1,0:T(8,128)(2,1)S(1)} %collective-permute-done.11.refs_0_.refs_4_.refs_5_, ...), custom_call_target="tpu_custom_call" | custom-call | tf_op jit(solution)/shard_map/pallas_call | solution.py:80
  107.8 6.4 %collective-permute-done.21.refs_1_ = bf16[128,1536]{1,0:T(8,128)(2,1)S(1)} collective-permute-done((bf16[128,1536]{1,0:T(8,128)(2,1)S(1)}, bf16[128,1536]{1,0:T(8,128)(2,1)S(1)}, u32[]{:S(2)}, u32[]{:S(2)}) %collective-permute-start.21) | collective-permute-done | bytes 393248 | tf_op jit(solution)/shard_map/ppermute | solution.py:32
  115.3 6.1 %collective-permute-start.29 = (bf16[128,1664]{1,0:T(8,128)(2,1)S(1)}, bf16[128,1664]{1,0:T(8,128)(2,1)S(1)}, u32[]{:S(2)}, u32[]{:S(2)}) collective-permute-start(bf16[128,1664]{1,0:T(8,128)(2,1)S(1)} %shard_map.131.refs_0_), channel_id=1, source_target_pairs={{0,24},{8,16},{16,8},{24,0},{1,25},{9,17},{17,9},{25,1},{2,26},{10... | collective-permute-start | bytes 1277960 | tf_op jit(solution)/shard_map/ppermute | solution.py:32
  124.0 4.7 %collective-permute-done.29.refs_0_ = bf16[128,1664]{1,0:T(8,128)(2,1)S(1)} collective-permute-done((bf16[128,1664]{1,0:T(8,128)(2,1)S(1)}, bf16[128,1664]{1,0:T(8,128)(2,1)S(1)}, u32[]{:S(2)}, u32[]{:S(2)}) %collective-permute-start.29) | collective-permute-done | bytes 426016 | tf_op jit(solution)/shard_map/ppermute | solution.py:32
  128.7 8.7 %collective-permute-done.27.refs_1_ = bf16[128,1664]{1,0:T(8,128)(2,1)S(1)} collective-permute-done((bf16[128,1664]{1,0:T(8,128)(2,1)S(1)}, bf16[128,1664]{1,0:T(8,128)(2,1)S(1)}, u32[]{:S(2)}, u32[]{:S(2)}) %collective-permute-start.27) | collective-permute-done | bytes 426016 | tf_op jit(solution)/shard_map/ppermute | solution.py:32
  137.4 2.9 %collective-permute-start.34 = (bf16[128,768]{1,0:T(8,128)(2,1)S(1)}, bf16[128,768]{1,0:T(8,128)(2,1)S(1)}, u32[]{:S(2)}, u32[]{:S(2)}) collective-permute-start(bf16[128,768]{1,0:T(8,128)(2,1)S(1)} %get-tuple-element.136.refs_0_), channel_id=1, source_target_pairs={{0,24},{8,16},{16,8},{24,0},{1,25},{9,17},{17,9},{25,1},{2,26},{10... | collective-permute-start | bytes 589832 | tf_op jit(solution)/shard_map/ppermute | solution.py:32
  141.8 3.4 %shard_map.135 = (bf16[128,1280]{1,0:T(8,128)(2,1)S(1)}, f32[1,1280]{1,0:T(1,128)S(1)}) custom-call(bf16[128,1664]{1,0:T(8,128)(2,1)S(1)} %collective-permute-done.29.refs_0_, f32[128,1]{1,0:T(8,128)S(1)} %get-tuple-element.129.refs_2_.refs_1_, bf16[128,1280]{1,0:T(8,128)(2,1)S(1)} %get-tuple-element.145.refs_2_, ...), custom_call_target="tpu_custom_call" | custom-call | tf_op jit(solution)/shard_map/pallas_call | solution.py:80
  145.2 5.3 %collective-permute-start.39 = (bf16[128,1280]{1,0:T(8,128)(2,1)S(1)}, bf16[128,1280]{1,0:T(8,128)(2,1)S(1)}, u32[]{:S(2)}, u32[]{:S(2)}) collective-permute-start(bf16[128,1280]{1,0:T(8,128)(2,1)S(1)} %get-tuple-element.146), channel_id=1, source_target_pairs={{0,6},{2,0},{4,2},{6,4},{1,7},{3,1},{5,3},{7,5},{8,14},{10,8},{12,... | collective-permute-start | bytes 983048 | tf_op jit(solution)/shard_map/ppermute | solution.py:37
  150.5 4.4 %shard_map.134 = (bf16[384,1280]{1,0:T(8,128)(2,1)S(1)}, f32[1,1280]{1,0:T(1,128)S(1)}) custom-call(bf16[128,1664]{1,0:T(8,128)(2,1)S(1)} %shard_map.131.refs_0_, bf16[128,1664]{1,0:T(8,128)(2,1)S(1)} %collective-permute-done.27.refs_1_, bf16[128,1664]{1,0:T(8,128)(2,1)S(1)} %collective-permute-done.28.refs_2_, ...), custom_call_target="tpu_custom_call" | custom-call | tf_op jit(solution)/shard_map/pallas_call | solution.py:80
  154.9 1.9 collective-permute-start.36
  161.8 2.6 %shard_map.133 = (bf16[128,1280]{1,0:T(8,128)(2,1)S(1)}, f32[128,1]{1,0:T(8,128)}, bf16[128,768]{1,0:T(8,128)(2,1)S(1)}, bf16[128,768]{1,0:T(8,128)(2,1)S(1)}) custom-call(bf16[128,768]{1,0:T(8,128)(2,1)S(1)} %collective-permute-done.34.refs_0_, f32[128,1]{1,0:T(8,128)S(1)} %get-tuple-element.129.refs_2_.refs_1_, ...), custom_call_target="tpu_custom_call" | custom-call | tf_op jit(solution)/shard_map/pallas_call | solution.py:80
  164.4 2.0 collective-permute-start.35
  166.4 3.6 %shard_map.132 = (bf16[128,1280]{1,0:T(8,128)(2,1)S(1)}, bf16[128,1280]{1,0:T(8,128)(2,1)S(1)}, bf16[128,1280]{1,0:T(8,128)(2,1)S(1)}, f32[128,1]{1,0:T(8,128)},...) custom-call(bf16[128,768]{1,0:T(8,128)(2,1)S(1)} %get-tuple-element.136.refs_, ...), custom_call_target="tpu_custom_call" | custom-call | tf_op jit(solution)/shard_map/pallas_call | solution.py:80
  175.9 2.0 collective-permute-start.40
  177.9 2.8 %collective-permute-done.32 = bf16[128,1280]{1,0:T(8,128)(2,1)S(1)} collective-permute-done((bf16[128,1280]{1,0:T(8,128)(2,1)S(1)}, bf16[128,1280]{1,0:T(8,128)(2,1)S(1)}, u32[]{:S(2)}, u32[]{:S(2)}) %collective-permute-start.32) | collective-permute-done | bytes 327712 | tf_op jit(solution)/shard_map/ppermute | solution.py:32
  180.7 5.4 %collective-permute-done.33 = bf16[128,1280]{1,0:T(8,128)(2,1)S(1)} collective-permute-done((bf16[128,1280]{1,0:T(8,128)(2,1)S(1)}, bf16[128,1280]{1,0:T(8,128)(2,1)S(1)}, u32[]{:S(2)}, u32[]{:S(2)}) %collective-permute-start.33) | collective-permute-done | bytes 327712 | tf_op jit(solution)/shard_map/ppermute | solution.py:32
  186.2 2.2 shard_map.136
  191.2 2.9 %collective-permute-done.37.refs_1_ = bf16[128,768]{1,0:T(8,128)(2,1)S(1)} collective-permute-done((bf16[128,768]{1,0:T(8,128)(2,1)S(1)}, bf16[128,768]{1,0:T(8,128)(2,1)S(1)}, u32[]{:S(2)}, u32[]{:S(2)}) %collective-permute-start.37) | collective-permute-done | bytes 196640 | tf_op jit(solution)/shard_map/ppermute | solution.py:32
  196.9 1.9 collective-permute-start.41
  200.9 4.3 %collective-permute-done.45.refs_0_ = bf16[128,1664]{1,0:T(8,128)(2,1)S(1)} collective-permute-done((bf16[128,1664]{1,0:T(8,128)(2,1)S(1)}, bf16[128,1664]{1,0:T(8,128)(2,1)S(1)}, u32[]{:S(2)}, u32[]{:S(2)}) %collective-permute-start.45) | collective-permute-done | bytes 426016 | tf_op jit(solution)/shard_map/ppermute | solution.py:32
  205.2 4.3 %collective-permute-done.41.refs_1_ = bf16[128,1664]{1,0:T(8,128)(2,1)S(1)} collective-permute-done((bf16[128,1664]{1,0:T(8,128)(2,1)S(1)}, bf16[128,1664]{1,0:T(8,128)(2,1)S(1)}, u32[]{:S(2)}, u32[]{:S(2)}) %collective-permute-start.41) | collective-permute-done | bytes 426016 | tf_op jit(solution)/shard_map/ppermute | solution.py:32
  213.1 3.4 %shard_map.140 = (bf16[128,1280]{1,0:T(8,128)(2,1)S(1)}, f32[1,1280]{1,0:T(1,128)S(1)}) custom-call(bf16[128,1664]{1,0:T(8,128)(2,1)S(1)} %collective-permute-done.45.refs_0_, f32[128,1]{1,0:T(8,128)S(1)} %get-tuple-element.117.refs_1_, bf16[128,1280]{1,0:T(8,128)(2,1)S(1)} %get-tuple-element.166.refs_2_, ...), custom_call_target="tpu_custom_call" | custom-call | tf_op jit(solution)/shard_map/pallas_call | solution.py:80
  216.5 4.6 %shard_map.139 = (bf16[128,1280]{1,0:T(8,128)(2,1)S(1)}, bf16[128,1280]{1,0:T(8,128)(2,1)S(1)}, bf16[128,1280]{1,0:T(8,128)(2,1)S(1)}, f32[1,1280]{1,0:T(1,128)S(1)}) custom-call(bf16[128,1664]{1,0:T(8,128)(2,1)S(1)} %shard_map.138.refs_0_, bf16[128,1664]{1,0:T(8,128)(2,1)S(1)} %collective-permute-done.41.refs_1_, ...), custom_call_target="tpu_custom_call" | custom-call | tf_op jit(solution)/shard_map/pallas_call | solution.py:80
  222.1 1.9 collective-permute-start.43
  224.8 2.7 %fusion.3 = bf16[768,1280]{1,0:T(8,128)(2,1)} fusion(bf16[768,1280]{1,0:T(8,128)(2,1)S(1)} %collective-permute-done.49, bf16[768,1280]{1,0:T(8,128)(2,1)S(1)} %convolution_convert_fusion, bf16[512,1280]{1,0:T(8,128)(2,1)S(1)} %constant_dynamic-update-slice_fusion.6, bf16[128,768]{1,0:T(8,128)(2,1)S(1)} %get-tuple-element.179, ...), kind=kOutput, calls=%fused_computation.9 | convolution fusion | flops 1013121024 | bytes 7995392 | tf_op jit(solution)/shard_map/dot_general | solution.py:22
  229.0 2.7 %fusion.4 = bf16[1280,768]{1,0:T(8,128)(2,1)} fusion(bf16[1280,768]{1,0:T(8,128)(2,1)S(1)} %collective-permute-done.48, bf16[1280,768]{1,0:T(8,128)(2,1)S(1)} %convolution_convert_fusion.2, bf16[512,1280]{1,0:T(8,128)(2,1)S(1)} %constant_dynamic-update-slice_fusion.8, bf16[512,768]{1,0:T(8,128)(2,1)S(1)} %get-tuple-element.177), kind=kOutput, calls=%fused_computation.10 | convolution fusion | flops 1011548160 | bytes 7995392 | tf_op jit(solution)/shard_map/dot_general | solution.py:22
  231.7 2.7 %fusion.5 = bf16[1280,768]{1,0:T(8,128)(2,1)} fusion(bf16[1280,768]{1,0:T(8,128)(2,1)S(1)} %collective-permute-done.47, bf16[1280,768]{1,0:T(8,128)(2,1)S(1)} %convolution_convert_fusion.3, bf16[512,1280]{1,0:T(8,128)(2,1)S(1)} %constant_dynamic-update-slice_fusion.8, bf16[512,768]{1,0:T(8,128)(2,1)S(1)} %get-tuple-element.174), kind=kOutput, calls=%fused_computation.11 | convolution fusion | flops 1011548160 | bytes 7995392 | tf_op jit(solution)/shard_map/dot_general | solution.py:22
  234.4 2.0 collective-permute-start.52
  236.4 2.3 collective-permute-done.43
  (151 shorter events, 63.1 us)
Async XLA Ops:
  0.6 7.5 %collective-permute-start.2 = (bf16[1280,768]{1,0:T(8,128)(2,1)}, bf16[1280,768]{1,0:T(8,128)(2,1)S(1)}, u32[]{:S(2)}, u32[]{:S(2)}) collective-permute-start(bf16[1280,768]{1,0:T(8,128)(2,1)} %bitcast.50), channel_id=1, source_target_pairs={{0,1},{1,0},{2,3},{3,2},{4,5},{5,4},{6,7},{7,6},{8,9},{9,8},{10,11... | collective-permute-start | bytes 5898248 | tf_op jit(solution)/shard_map/ppermute | solution.py:32
  1.2 7.0 %collective-permute-start.3 = (bf16[1280,768]{1,0:T(8,128)(2,1)}, bf16[1280,768]{1,0:T(8,128)(2,1)}, u32[]{:S(2)}, u32[]{:S(2)}) collective-permute-start(bf16[1280,768]{1,0:T(8,128)(2,1)} %bitcast.52), channel_id=1, source_target_pairs={{0,1},{1,0},{2,3},{3,2},{4,5},{5,4},{6,7},{7,6},{8,9},{9,8},{10,11... | collective-permute-start | bytes 5898248 | tf_op jit(solution)/shard_map/ppermute | solution.py:32
  1.2 9.5 %collective-permute-start.4 = (bf16[768,1280]{1,0:T(8,128)(2,1)}, bf16[768,1280]{1,0:T(8,128)(2,1)}, u32[]{:S(2)}, u32[]{:S(2)}) collective-permute-start(bf16[768,1280]{1,0:T(8,128)(2,1)} %bitcast.54), channel_id=1, source_target_pairs={{0,1},{1,0},{2,3},{3,2},{4,5},{5,4},{6,7},{7,6},{8,9},{9,8},{10,11... | collective-permute-start | bytes 5898248 | tf_op jit(solution)/shard_map/ppermute | solution.py:32
  4.0 15.1 %collective-permute-start = (bf16[144,1280]{1,0:T(8,128)(2,1)S(1)}, bf16[144,1280]{1,0:T(8,128)(2,1)S(1)}, u32[]{:S(2)}, u32[]{:S(2)}) collective-permute-start(bf16[144,1280]{1,0:T(8,128)(2,1)S(1)} %get-tuple-element.203), channel_id=1, source_target_pairs={{0,8},{8,0},{16,24},{24,16},{1,9},{9,1},{17,25},{25,17},{2,10},{10... | collective-permute-start | bytes 1105928 | tf_op jit(solution)/shard_map/ppermute | solution.py:32
  6.6 12.5 %collective-permute-start.1 = (bf16[144,1280]{1,0:T(8,128)(2,1)S(1)}, bf16[144,1280]{1,0:T(8,128)(2,1)S(1)}, u32[]{:S(2)}, u32[]{:S(2)}) collective-permute-start(bf16[144,1280]{1,0:T(8,128)(2,1)S(1)} %get-tuple-element.204), channel_id=1, source_target_pairs={{0,16},{8,24},{16,0},{24,8},{1,17},{9,25},{17,1},{25,9},{2,18},{10... | collective-permute-start | bytes 1105928 | tf_op jit(solution)/shard_map/ppermute | solution.py:32
  15.2 13.3 %collective-permute-start.7 = (bf16[144,1280]{1,0:T(8,128)(2,1)S(1)}, bf16[144,1280]{1,0:T(8,128)(2,1)S(1)}, u32[]{:S(2)}, u32[]{:S(2)}) collective-permute-start(bf16[144,1280]{1,0:T(8,128)(2,1)S(1)} %get-tuple-element.108), channel_id=1, source_target_pairs={{0,24},{8,16},{16,8},{24,0},{1,25},{9,17},{17,9},{25,1},{2,26},{10... | collective-permute-start | bytes 1105928 | tf_op jit(solution)/shard_map/ppermute | solution.py:32
  23.7 13.8 %collective-permute-start.5 = (bf16[128,1536]{1,0:T(8,128)(2,1)S(1)}, bf16[128,1536]{1,0:T(8,128)(2,1)S(1)}, u32[]{:S(2)}, u32[]{:S(2)}) collective-permute-start(bf16[128,1536]{1,0:T(8,128)(2,1)S(1)} %get-tuple-element.104), channel_id=1, source_target_pairs={{0,8},{8,0},{16,24},{24,16},{1,9},{9,1},{17,25},{25,17},{2,10},{10... | collective-permute-start | bytes 1179656 | tf_op jit(solution)/shard_map/ppermute | solution.py:32
  24.3 13.2 %collective-permute-start.6 = (bf16[128,1536]{1,0:T(8,128)(2,1)S(1)}, bf16[128,1536]{1,0:T(8,128)(2,1)S(1)}, u32[]{:S(2)}, u32[]{:S(2)}) collective-permute-start(bf16[128,1536]{1,0:T(8,128)(2,1)S(1)} %get-tuple-element.105), channel_id=1, source_target_pairs={{0,16},{8,24},{16,0},{24,8},{1,17},{9,25},{17,1},{25,9},{2,18},{10... | collective-permute-start | bytes 1179656 | tf_op jit(solution)/shard_map/ppermute | solution.py:32
  30.9 13.9 %collective-permute-start.8 = (bf16[128,1536]{1,0:T(8,128)(2,1)S(1)}, bf16[128,1536]{1,0:T(8,128)(2,1)S(1)}, u32[]{:S(2)}, u32[]{:S(2)}) collective-permute-start(bf16[128,1536]{1,0:T(8,128)(2,1)S(1)} %get-tuple-element.109), channel_id=1, source_target_pairs={{0,24},{8,16},{16,8},{24,0},{1,25},{9,17},{17,9},{25,1},{2,26},{10... | collective-permute-start | bytes 1179656 | tf_op jit(solution)/shard_map/ppermute | solution.py:32
  45.4 7.0 %collective-permute-start.10 = (bf16[128,768]{1,0:T(8,128)(2,1)S(1)}, bf16[128,768]{1,0:T(8,128)(2,1)S(1)}, u32[]{:S(2)}, u32[]{:S(2)}) collective-permute-start(bf16[128,768]{1,0:T(8,128)(2,1)S(1)} %get-tuple-element.110.refs_0_), channel_id=1, source_target_pairs={{0,16},{8,24},{16,0},{24,8},{1,17},{9,25},{17,1},{25,9},{2,18},{10... | collective-permute-start | bytes 589832 | tf_op jit(solution)/shard_map/ppermute | solution.py:32
  47.2 7.8 %collective-permute-start.9 = (bf16[128,768]{1,0:T(8,128)(2,1)S(1)}, bf16[128,768]{1,0:T(8,128)(2,1)S(1)}, u32[]{:S(2)}, u32[]{:S(2)}) collective-permute-start(bf16[128,768]{1,0:T(8,128)(2,1)S(1)} %get-tuple-element.110.refs_0_), channel_id=1, source_target_pairs={{0,8},{8,0},{16,24},{24,16},{1,9},{9,1},{17,25},{25,17},{2,10},{10... | collective-permute-start | bytes 589832 | tf_op jit(solution)/shard_map/ppermute | solution.py:32
  48.7 11.0 %collective-permute-start.14 = (bf16[128,768]{1,0:T(8,128)(2,1)S(1)}, bf16[128,768]{1,0:T(8,128)(2,1)S(1)}, u32[]{:S(2)}, u32[]{:S(2)}) collective-permute-start(bf16[128,768]{1,0:T(8,128)(2,1)S(1)} %get-tuple-element.110.refs_0_), channel_id=1, source_target_pairs={{0,24},{8,16},{16,8},{24,0},{1,25},{9,17},{17,9},{25,1},{2,26},{10... | collective-permute-start | bytes 589832 | tf_op jit(solution)/shard_map/ppermute | solution.py:32
  58.0 43.9 %collective-permute-start.11 = (bf16[384,1280]{1,0:T(8,128)(2,1)S(1)}, bf16[384,1280]{1,0:T(8,128)(2,1)S(1)}, u32[]{:S(2)}, u32[]{:S(2)}) collective-permute-start(bf16[384,1280]{1,0:T(8,128)(2,1)S(1)} %get-tuple-element.113), channel_id=1, source_target_pairs={{0,2},{2,4},{4,6},{6,0},{1,3},{3,5},{5,7},{7,1},{8,10},{10,12},{12... | collective-permute-start | bytes 2949128 | tf_op jit(solution)/shard_map/ppermute | solution.py:37
  63.7 22.8 %collective-permute-start.25 = (bf16[128,1280]{1,0:T(8,128)(2,1)S(1)}, bf16[128,1280]{1,0:T(8,128)(2,1)S(1)}, u32[]{:S(2)}, u32[]{:S(2)}) collective-permute-start(bf16[128,1280]{1,0:T(8,128)(2,1)S(1)} %get-tuple-element.194), channel_id=1, source_target_pairs={{0,24},{8,16},{16,8},{24,0},{1,25},{9,17},{17,9},{25,1},{2,26},{10... | collective-permute-start | bytes 983048 | tf_op jit(solution)/shard_map/ppermute | solution.py:32
  66.2 15.0 %collective-permute-start.17 = (bf16[128,1280]{1,0:T(8,128)(2,1)S(1)}, bf16[128,1280]{1,0:T(8,128)(2,1)S(1)}, u32[]{:S(2)}, u32[]{:S(2)}) collective-permute-start(bf16[128,1280]{1,0:T(8,128)(2,1)S(1)} %get-tuple-element.196), channel_id=1, source_target_pairs={{0,8},{8,0},{16,24},{24,16},{1,9},{9,1},{17,25},{25,17},{2,10},{10... | collective-permute-start | bytes 983048 | tf_op jit(solution)/shard_map/ppermute | solution.py:32
  67.6 15.2 %collective-permute-start.18 = (bf16[128,1280]{1,0:T(8,128)(2,1)S(1)}, bf16[128,1280]{1,0:T(8,128)(2,1)S(1)}, u32[]{:S(2)}, u32[]{:S(2)}) collective-permute-start(bf16[128,1280]{1,0:T(8,128)(2,1)S(1)} %get-tuple-element.195), channel_id=1, source_target_pairs={{0,16},{8,24},{16,0},{24,8},{1,17},{9,25},{17,1},{25,9},{2,18},{10... | collective-permute-start | bytes 983048 | tf_op jit(solution)/shard_map/ppermute | solution.py:32
  68.1 11.4 %collective-permute-start.13 = (f32[128,1]{1,0:T(8,128)S(1)}, f32[128,1]{1,0:T(8,128)S(1)}, u32[]{:S(2)}, u32[]{:S(2)}) collective-permute-start(f32[128,1]{1,0:T(8,128)S(1)} %get-tuple-element.116), channel_id=1, source_target_pairs={{0,16},{8,24},{16,0},{24,8},{1,17},{9,25},{17,1},{25,9},{2,18},{10... | collective-permute-start | bytes 1544 | tf_op jit(solution)/shard_map/ppermute | solution.py:32
  79.6 11.1 %collective-permute-start.23 = (bf16[128,1280]{1,0:T(8,128)(2,1)S(1)}, bf16[128,1280]{1,0:T(8,128)(2,1)S(1)}, u32[]{:S(2)}, u32[]{:S(2)}) collective-permute-start(bf16[128,1280]{1,0:T(8,128)(2,1)S(1)} %get-tuple-element.120), channel_id=1, source_target_pairs={{0,2},{2,4},{4,6},{6,0},{1,3},{3,5},{5,7},{7,1},{8,10},{10,12},{12... | collective-permute-start | bytes 983048 | tf_op jit(solution)/shard_map/ppermute | solution.py:37
  81.2 12.9 %collective-permute-start.16 = (f32[128,1]{1,0:T(8,128)S(1)}, f32[128,1]{1,0:T(8,128)S(1)}, u32[]{:S(2)}, u32[]{:S(2)}) collective-permute-start(f32[128,1]{1,0:T(8,128)S(1)} %shard_map.125), channel_id=1, source_target_pairs={{0,2},{2,4},{4,6},{6,0},{1,3},{3,5},{5,7},{7,1},{8,10},{10,12},{12... | collective-permute-start | bytes 1544 | tf_op jit(solution)/shard_map/ppermute | solution.py:37
  85.0 10.9 %collective-permute-start.19 = (bf16[128,768]{1,0:T(8,128)(2,1)S(1)}, bf16[128,768]{1,0:T(8,128)(2,1)S(1)}, u32[]{:S(2)}, u32[]{:S(2)}) collective-permute-start(bf16[128,768]{1,0:T(8,128)(2,1)S(1)} %get-tuple-element.123), channel_id=1, source_target_pairs={{0,8},{8,0},{16,24},{24,16},{1,9},{9,1},{17,25},{25,17},{2,10},{10... | collective-permute-start | bytes 589832 | tf_op jit(solution)/shard_map/ppermute | solution.py:32
  86.6 15.4 %collective-permute-start.20 = (bf16[128,768]{1,0:T(8,128)(2,1)S(1)}, bf16[128,768]{1,0:T(8,128)(2,1)S(1)}, u32[]{:S(2)}, u32[]{:S(2)}) collective-permute-start(bf16[128,768]{1,0:T(8,128)(2,1)S(1)} %get-tuple-element.124), channel_id=1, source_target_pairs={{0,16},{8,24},{16,0},{24,8},{1,17},{9,25},{17,1},{25,9},{2,18},{10... | collective-permute-start | bytes 589832 | tf_op jit(solution)/shard_map/ppermute | solution.py:32
  90.6 24.2 %collective-permute-start.26 = (bf16[128,768]{1,0:T(8,128)(2,1)S(1)}, bf16[128,768]{1,0:T(8,128)(2,1)S(1)}, u32[]{:S(2)}, u32[]{:S(2)}) collective-permute-start(bf16[128,768]{1,0:T(8,128)(2,1)S(1)} %get-tuple-element.133), channel_id=1, source_target_pairs={{0,24},{8,16},{16,8},{24,0},{1,25},{9,17},{17,9},{25,1},{2,26},{10... | collective-permute-start | bytes 589832 | tf_op jit(solution)/shard_map/ppermute | solution.py:32
  94.1 13.7 %collective-permute-start.24 = (bf16[128,1536]{1,0:T(8,128)(2,1)S(1)}, bf16[128,1536]{1,0:T(8,128)(2,1)S(1)}, u32[]{:S(2)}, u32[]{:S(2)}) collective-permute-start(bf16[128,1536]{1,0:T(8,128)(2,1)S(1)} %get-tuple-element.130), channel_id=1, source_target_pairs={{0,24},{8,16},{16,8},{24,0},{1,25},{9,17},{17,9},{25,1},{2,26},{10... | collective-permute-start | bytes 1179656 | tf_op jit(solution)/shard_map/ppermute | solution.py:32
  106.4 7.8 %collective-permute-start.21 = (bf16[128,1536]{1,0:T(8,128)(2,1)S(1)}, bf16[128,1536]{1,0:T(8,128)(2,1)S(1)}, u32[]{:S(2)}, u32[]{:S(2)}) collective-permute-start(bf16[128,1536]{1,0:T(8,128)(2,1)S(1)} %get-tuple-element.127), channel_id=1, source_target_pairs={{0,8},{8,0},{16,24},{24,16},{1,9},{9,1},{17,25},{25,17},{2,10},{10... | collective-permute-start | bytes 1179656 | tf_op jit(solution)/shard_map/ppermute | solution.py:32
  106.4 7.8 %collective-permute-start.22 = (bf16[128,1536]{1,0:T(8,128)(2,1)S(1)}, bf16[128,1536]{1,0:T(8,128)(2,1)S(1)}, u32[]{:S(2)}, u32[]{:S(2)}) collective-permute-start(bf16[128,1536]{1,0:T(8,128)(2,1)S(1)} %get-tuple-element.128), channel_id=1, source_target_pairs={{0,16},{8,24},{16,0},{24,8},{1,17},{9,25},{17,1},{25,9},{2,18},{10... | collective-permute-start | bytes 1179656 | tf_op jit(solution)/shard_map/ppermute | solution.py:32
  115.3 13.4 %collective-permute-start.29 = (bf16[128,1664]{1,0:T(8,128)(2,1)S(1)}, bf16[128,1664]{1,0:T(8,128)(2,1)S(1)}, u32[]{:S(2)}, u32[]{:S(2)}) collective-permute-start(bf16[128,1664]{1,0:T(8,128)(2,1)S(1)} %shard_map.131.refs_0_), channel_id=1, source_target_pairs={{0,24},{8,16},{16,8},{24,0},{1,25},{9,17},{17,9},{25,1},{2,26},{10... | collective-permute-start | bytes 1277960 | tf_op jit(solution)/shard_map/ppermute | solution.py:32
  121.5 15.9 %collective-permute-start.27 = (bf16[128,1664]{1,0:T(8,128)(2,1)S(1)}, bf16[128,1664]{1,0:T(8,128)(2,1)S(1)}, u32[]{:S(2)}, u32[]{:S(2)}) collective-permute-start(bf16[128,1664]{1,0:T(8,128)(2,1)S(1)} %shard_map.131.refs_0_), channel_id=1, source_target_pairs={{0,8},{8,0},{16,24},{24,16},{1,9},{9,1},{17,25},{25,17},{2,10},{10... | collective-permute-start | bytes 1277960 | tf_op jit(solution)/shard_map/ppermute | solution.py:32
  122.6 14.9 %collective-permute-start.28 = (bf16[128,1664]{1,0:T(8,128)(2,1)S(1)}, bf16[128,1664]{1,0:T(8,128)(2,1)S(1)}, u32[]{:S(2)}, u32[]{:S(2)}) collective-permute-start(bf16[128,1664]{1,0:T(8,128)(2,1)S(1)} %shard_map.131.refs_0_), channel_id=1, source_target_pairs={{0,16},{8,24},{16,0},{24,8},{1,17},{9,25},{17,1},{25,9},{2,18},{10... | collective-permute-start | bytes 1277960 | tf_op jit(solution)/shard_map/ppermute | solution.py:32
  137.4 24.4 %collective-permute-start.34 = (bf16[128,768]{1,0:T(8,128)(2,1)S(1)}, bf16[128,768]{1,0:T(8,128)(2,1)S(1)}, u32[]{:S(2)}, u32[]{:S(2)}) collective-permute-start(bf16[128,768]{1,0:T(8,128)(2,1)S(1)} %get-tuple-element.136.refs_0_), channel_id=1, source_target_pairs={{0,24},{8,16},{16,8},{24,0},{1,25},{9,17},{17,9},{25,1},{2,26},{10... | collective-permute-start | bytes 589832 | tf_op jit(solution)/shard_map/ppermute | solution.py:32
  140.3 26.0 %collective-permute-start.30 = (bf16[128,768]{1,0:T(8,128)(2,1)S(1)}, bf16[128,768]{1,0:T(8,128)(2,1)S(1)}, u32[]{:S(2)}, u32[]{:S(2)}) collective-permute-start(bf16[128,768]{1,0:T(8,128)(2,1)S(1)} %get-tuple-element.136.refs_0_), channel_id=1, source_target_pairs={{0,8},{8,0},{16,24},{24,16},{1,9},{9,1},{17,25},{25,17},{2,10},{10... | collective-permute-start | bytes 589832 | tf_op jit(solution)/shard_map/ppermute | solution.py:32
  140.3 26.0 %collective-permute-start.31 = (bf16[128,768]{1,0:T(8,128)(2,1)S(1)}, bf16[128,768]{1,0:T(8,128)(2,1)S(1)}, u32[]{:S(2)}, u32[]{:S(2)}) collective-permute-start(bf16[128,768]{1,0:T(8,128)(2,1)S(1)} %get-tuple-element.136.refs_0_), channel_id=1, source_target_pairs={{0,16},{8,24},{16,0},{24,8},{1,17},{9,25},{17,1},{25,9},{2,18},{10... | collective-permute-start | bytes 589832 | tf_op jit(solution)/shard_map/ppermute | solution.py:32
  145.2 29.0 %collective-permute-start.39 = (bf16[128,1280]{1,0:T(8,128)(2,1)S(1)}, bf16[128,1280]{1,0:T(8,128)(2,1)S(1)}, u32[]{:S(2)}, u32[]{:S(2)}) collective-permute-start(bf16[128,1280]{1,0:T(8,128)(2,1)S(1)} %get-tuple-element.146), channel_id=1, source_target_pairs={{0,6},{2,0},{4,2},{6,4},{1,7},{3,1},{5,3},{7,5},{8,14},{10,8},{12,... | collective-permute-start | bytes 983048 | tf_op jit(solution)/shard_map/ppermute | solution.py:37
  154.9 31.3 %collective-permute-start.36 = (bf16[384,1280]{1,0:T(8,128)(2,1)S(1)}, bf16[384,1280]{1,0:T(8,128)(2,1)S(1)}, u32[]{:S(2)}, u32[]{:S(2)}) collective-permute-start(bf16[384,1280]{1,0:T(8,128)(2,1)S(1)} %get-tuple-element.142), channel_id=1, source_target_pairs={{0,6},{2,0},{4,2},{6,4},{1,7},{3,1},{5,3},{7,5},{8,14},{10,8},{12,... | collective-permute-start | bytes 2949128 | tf_op jit(solution)/shard_map/ppermute | solution.py:37
  164.4 21.7 %collective-permute-start.35 = (bf16[128,1280]{1,0:T(8,128)(2,1)S(1)}, bf16[128,1280]{1,0:T(8,128)(2,1)S(1)}, u32[]{:S(2)}, u32[]{:S(2)}) collective-permute-start(bf16[128,1280]{1,0:T(8,128)(2,1)S(1)} %get-tuple-element.140), channel_id=1, source_target_pairs={{0,24},{8,16},{16,8},{24,0},{1,25},{9,17},{17,9},{25,1},{2,26},{10... | collective-permute-start | bytes 983048 | tf_op jit(solution)/shard_map/ppermute | solution.py:32
  170.0 10.6 %collective-permute-start.32 = (bf16[128,1280]{1,0:T(8,128)(2,1)S(1)}, bf16[128,1280]{1,0:T(8,128)(2,1)S(1)}, u32[]{:S(2)}, u32[]{:S(2)}) collective-permute-start(bf16[128,1280]{1,0:T(8,128)(2,1)S(1)} %get-tuple-element.138), channel_id=1, source_target_pairs={{0,8},{8,0},{16,24},{24,16},{1,9},{9,1},{17,25},{25,17},{2,10},{10... | collective-permute-start | bytes 983048 | tf_op jit(solution)/shard_map/ppermute | solution.py:32
  170.2 15.8 %collective-permute-start.33 = (bf16[128,1280]{1,0:T(8,128)(2,1)S(1)}, bf16[128,1280]{1,0:T(8,128)(2,1)S(1)}, u32[]{:S(2)}, u32[]{:S(2)}) collective-permute-start(bf16[128,1280]{1,0:T(8,128)(2,1)S(1)} %get-tuple-element.139), channel_id=1, source_target_pairs={{0,16},{8,24},{16,0},{24,8},{1,17},{9,25},{17,1},{25,9},{2,18},{10... | collective-permute-start | bytes 983048 | tf_op jit(solution)/shard_map/ppermute | solution.py:32
  175.9 18.3 %collective-permute-start.40 = (bf16[128,768]{1,0:T(8,128)(2,1)S(1)}, bf16[128,768]{1,0:T(8,128)(2,1)S(1)}, u32[]{:S(2)}, u32[]{:S(2)}) collective-permute-start(bf16[128,768]{1,0:T(8,128)(2,1)S(1)} %get-tuple-element.160), channel_id=1, source_target_pairs={{0,24},{8,16},{16,8},{24,0},{1,25},{9,17},{17,9},{25,1},{2,26},{10... | collective-permute-start | bytes 589832 | tf_op jit(solution)/shard_map/ppermute | solution.py:32
  196.0 9.2 %collective-permute-start.45 = (bf16[128,1664]{1,0:T(8,128)(2,1)S(1)}, bf16[128,1664]{1,0:T(8,128)(2,1)S(1)}, u32[]{:S(2)}, u32[]{:S(2)}) collective-permute-start(bf16[128,1664]{1,0:T(8,128)(2,1)S(1)} %shard_map.138.refs_0_), channel_id=1, source_target_pairs={{0,24},{8,16},{16,8},{24,0},{1,25},{9,17},{17,9},{25,1},{2,26},{10... | collective-permute-start | bytes 1277960 | tf_op jit(solution)/shard_map/ppermute | solution.py:32
  196.9 12.6 %collective-permute-start.41 = (bf16[128,1664]{1,0:T(8,128)(2,1)S(1)}, bf16[128,1664]{1,0:T(8,128)(2,1)S(1)}, u32[]{:S(2)}, u32[]{:S(2)}) collective-permute-start(bf16[128,1664]{1,0:T(8,128)(2,1)S(1)} %shard_map.138.refs_0_), channel_id=1, source_target_pairs={{0,8},{8,0},{16,24},{24,16},{1,9},{9,1},{17,25},{25,17},{2,10},{10... | collective-permute-start | bytes 1277960 | tf_op jit(solution)/shard_map/ppermute | solution.py:32
  198.8 10.8 %collective-permute-start.42 = (bf16[128,1664]{1,0:T(8,128)(2,1)S(1)}, bf16[128,1664]{1,0:T(8,128)(2,1)S(1)}, u32[]{:S(2)}, u32[]{:S(2)}) collective-permute-start(bf16[128,1664]{1,0:T(8,128)(2,1)S(1)} %shard_map.138.refs_0_), channel_id=1, source_target_pairs={{0,16},{8,24},{16,0},{24,8},{1,17},{9,25},{17,1},{25,9},{2,18},{10... | collective-permute-start | bytes 1277960 | tf_op jit(solution)/shard_map/ppermute | solution.py:32
  200.8 23.1 %collective-permute-start.49 = (bf16[768,1280]{1,0:T(8,128)(2,1)S(1)}, bf16[768,1280]{1,0:T(8,128)(2,1)S(1)}, u32[]{:S(2)}, u32[]{:S(2)}) collective-permute-start(bf16[768,1280]{1,0:T(8,128)(2,1)S(1)} %fusion.6), channel_id=1, source_target_pairs={{0,1},{1,0},{2,3},{3,2},{4,5},{5,4},{6,7},{7,6},{8,9},{9,8},{10,11... | collective-permute-start | bytes 5898248 | tf_op jit(solution)/shard_map/ppermute | solution.py:32
  211.0 16.5 %collective-permute-start.48 = (bf16[1280,768]{1,0:T(8,128)(2,1)S(1)}, bf16[1280,768]{1,0:T(8,128)(2,1)S(1)}, u32[]{:S(2)}, u32[]{:S(2)}) collective-permute-start(bf16[1280,768]{1,0:T(8,128)(2,1)S(1)} %fusion.8), channel_id=1, source_target_pairs={{0,1},{1,0},{2,3},{3,2},{4,5},{5,4},{6,7},{7,6},{8,9},{9,8},{10,11... | collective-permute-start | bytes 5898248 | tf_op jit(solution)/shard_map/ppermute | solution.py:32
  212.4 15.1 %collective-permute-start.47 = (bf16[1280,768]{1,0:T(8,128)(2,1)S(1)}, bf16[1280,768]{1,0:T(8,128)(2,1)S(1)}, u32[]{:S(2)}, u32[]{:S(2)}) collective-permute-start(bf16[1280,768]{1,0:T(8,128)(2,1)S(1)} %fusion.7), channel_id=1, source_target_pairs={{0,1},{1,0},{2,3},{3,2},{4,5},{5,4},{6,7},{7,6},{8,9},{9,8},{10,11... | collective-permute-start | bytes 5898248 | tf_op jit(solution)/shard_map/ppermute | solution.py:32
  221.1 13.3 %collective-permute-start.46 = (bf16[128,1280]{1,0:T(8,128)(2,1)S(1)}, bf16[128,1280]{1,0:T(8,128)(2,1)S(1)}, u32[]{:S(2)}, u32[]{:S(2)}) collective-permute-start(bf16[128,1280]{1,0:T(8,128)(2,1)S(1)} %get-tuple-element.171), channel_id=1, source_target_pairs={{0,24},{8,16},{16,8},{24,0},{1,25},{9,17},{17,9},{25,1},{2,26},{10... | collective-permute-start | bytes 983048 | tf_op jit(solution)/shard_map/ppermute | solution.py:32
  222.1 16.7 %collective-permute-start.43 = (bf16[128,1280]{1,0:T(8,128)(2,1)S(1)}, bf16[128,1280]{1,0:T(8,128)(2,1)S(1)}, u32[]{:S(2)}, u32[]{:S(2)}) collective-permute-start(bf16[128,1280]{1,0:T(8,128)(2,1)S(1)} %get-tuple-element.169), channel_id=1, source_target_pairs={{0,8},{8,0},{16,24},{24,16},{1,9},{9,1},{17,25},{25,17},{2,10},{10... | collective-permute-start | bytes 983048 | tf_op jit(solution)/shard_map/ppermute | solution.py:32
  224.0 14.9 %collective-permute-start.44 = (bf16[128,1280]{1,0:T(8,128)(2,1)S(1)}, bf16[128,1280]{1,0:T(8,128)(2,1)S(1)}, u32[]{:S(2)}, u32[]{:S(2)}) collective-permute-start(bf16[128,1280]{1,0:T(8,128)(2,1)S(1)} %get-tuple-element.170), channel_id=1, source_target_pairs={{0,16},{8,24},{16,0},{24,8},{1,17},{9,25},{17,1},{25,9},{2,18},{10... | collective-permute-start | bytes 983048 | tf_op jit(solution)/shard_map/ppermute | solution.py:32
  227.5 11.6 %collective-permute-start.50 = (f32[1,1280]{1,0:T(1,128)S(1)}, f32[1,1280]{1,0:T(1,128)S(1)}, u32[]{:S(2)}, u32[]{:S(2)}) collective-permute-start(f32[1,1280]{1,0:T(1,128)S(1)} %add_add_fusion), channel_id=1, source_target_pairs={{0,8},{8,0},{16,24},{24,16},{1,9},{9,1},{17,25},{25,17},{2,10},{10... | collective-permute-start | bytes 15368 | tf_op jit(solution)/shard_map/ppermute | solution.py:32
  228.2 10.9 %collective-permute-start.51 = (f32[1,1280]{1,0:T(1,128)S(1)}, f32[1,1280]{1,0:T(1,128)S(1)}, u32[]{:S(2)}, u32[]{:S(2)}) collective-permute-start(f32[1,1280]{1,0:T(1,128)S(1)} %add_add_fusion), channel_id=1, source_target_pairs={{0,16},{8,24},{16,0},{24,8},{1,17},{9,25},{17,1},{25,9},{2,18},{10... | collective-permute-start | bytes 15368 | tf_op jit(solution)/shard_map/ppermute | solution.py:32
  (14 other events, 69.6 us)

commit v2 on v1

--- a/solution.py
+++ b/solution.py
@@ -70,6 +70,7 @@
 
 def kernel_call(body, operands, weights, out_shape, scratch):
     count, kept, made = len(operands), len(weights), len(out_shape)
+    rows = max(shape.shape[0] for shape in out_shape)
 
     def call(*refs):
         operand_refs, refs = refs[:count], refs[count:]
@@ -84,7 +85,11 @@
         out_shape=out_shape,
         scratch_shapes=scratch,
         compiler_params=pltpu.CompilerParams(vmem_limit_bytes=VMEM_BYTES),
-        cost_estimate=pl.CostEstimate(flops=0, bytes_accessed=0, transcendentals=0),
+        cost_estimate=pl.CostEstimate(
+            flops=4 * rows * sum(weight.size for weight in weights) // 2,
+            bytes_accessed=0,
+            transcendentals=0,
+        ),
     )(*operands, *weights)
 
 
@@ -481,15 +486,17 @@
         squares += square
         first_rows.append(split)
     hidden = moved(next_hidden, 1)
-    grad_blocks = sent([cotangent_quarter(step, *next_hidden) for step in range(dp_count)])
+    grad_blocks = sent([cotangent_quarter(step, next_hidden[0]) for step in range(dp_count)])
+    squares = [after(square, *grad_blocks[1:-1]) for square in squares]
     inverse = shifted(row_scale(sent(squares), features, True), "pipe", 1)
     act_parts, grad = [], []
     for group, mask in zip(groups, masks[1]):
         made, joined = act_grad_parts(grad_blocks[group], rows, mask, down_pair)
         act_parts += made
         grad.append(joined)
+    act_grads = act_parts
     act_parts = sent(act_parts)
-    hidden[0] = after(hidden[0], inverse, *act_parts[1:-1])
+    hidden[0] = after(hidden[0], inverse, *act_grads)
 
     parts, gained = [], []
     for rows_in, mask in zip(hidden, masks[1]):
@@ -516,8 +523,6 @@
             ]
             both_grad[1] = after(both_grad[1], given[2])
             received = [swap(value, "expert", 1) for value in given]
-        else:
-            last_activated = gather_rows(after(activated, *both_grad[1:]), dp_count)
         outs = []
         for group, choice, rows_in, grad_in in zip(groups, masks[k], hidden, grad):
             made, gain_term = input_grad(
@@ -528,6 +533,7 @@
         if k > 0:
             last_grad = jnp.concatenate(grad)
             grad = moved(outs, -1)
+            last_activated = gather_rows(after(activated, outs[0], grad[1]), dp_count)
             rights = [after(right, *outs) for right in rights]
             early = {
                 wanted: [weight_grad(gained, right, wanted).astype(bf16) for right in rights]

time: 241 us -> 238 us (0.988)
  starting transfers between devices: 73.5 us -> 66 us
  waiting for transfers between devices: 87.4 us -> 90.2 us
    ppermute x5, starting transfers between devices: 12.1 us -> 7.43 us  [shifted(): lax.ppermute(block, axis, [(i, (i + distance) % size) for i in range(size)])]
    ppermute x49, starting transfers between devices: 61.4 us -> 58.5 us  [swap(): return lax.ppermute(block, axis, partner_route(lax.axis_size(axis), step))]
    ppermute x5, waiting for transfers between devices: 1.62 us -> 4.43 us  [shifted(): lax.ppermute(block, axis, [(i, (i + distance) % size) for i in range(size)])]
  transfers between devices with their start and end apart: 54 -> 54, of which waited for: 25 -> 20; matrix products, arithmetic and copies ran while one was open for 10% -> 10% of each run, Pallas kernels for 22% -> 23%
where the time goes in v2:
time: 238 us
  waiting for transfers between devices  90.2 us (38%)
  starting transfers between devices  66 us (28%)
  Pallas kernels  55.3 us (23%)
  matrix products  20.6 us (9%)
  local copies, waits for them, and re-layouts  3.51 us (1%)
    ppermute x49, waiting for transfers between devices, swap(): return lax.ppermute(block, axis, partner_route(lax.axis_size(axis), step))  85.8 us
    ppermute x49, starting transfers between devices, swap(): return lax.ppermute(block, axis, partner_route(lax.axis_size(axis), step))  58.5 us
    pallas_call x22, Pallas kernels, kernel_call(): pl.pallas_call(call, in_specs=[in_vmem] * (count + kept), out_specs=[in_v...  50.9 us
    dot_general x12, matrix products, dot(): lax.dot_general(former, latter, ((contract[:1], contract[1:]), ((), ())),...  20.6 us
    ppermute x5, starting transfers between devices, shifted(): lax.ppermute(block, axis, [(i, (i + distance) % size) for i in range(size)])  7.43 us
  transfers between devices with their start and end apart: 54, of which 20 were waited for; matrix products, arithmetic and copies ran while one was open for 10% of the time, Pallas kernels for 23%

profile of v2, /device:TPU:0, one launch (start us, length us, event | category | flops | bytes accessed | tf_op | source)
XLA Modules:
  0.0 237.9 jit_solution(18076473208636118463)
XLA Ops:
  4.0 2.6 %collective-permute-start = (bf16[144,1280]{1,0:T(8,128)(2,1)S(1)}, bf16[144,1280]{1,0:T(8,128)(2,1)S(1)}, u32[]{:S(2)}, u32[]{:S(2)}) collective-permute-start(bf16[144,1280]{1,0:T(8,128)(2,1)S(1)} %get-tuple-element.211), channel_id=1, source_target_pairs={{0,8},{8,0},{16,24},{24,16},{1,9},{9,1},{17,25},{25,17},{2,10},{10... | collective-permute-start | bytes 1105928 | tf_op jit(solution)/shard_map/ppermute | solution.py:32
  8.1 2.6 %collective-permute-done.4.refs_5_ = bf16[768,1280]{1,0:T(8,128)(2,1)} collective-permute-done((bf16[768,1280]{1,0:T(8,128)(2,1)}, bf16[768,1280]{1,0:T(8,128)(2,1)}, u32[]{:S(2)}, u32[]{:S(2)}) %collective-permute-start.4) | collective-permute-done | bytes 1966112 | tf_op jit(solution)/shard_map/ppermute | solution.py:32
  10.7 4.5 %shard_map.118 = (bf16[1280,768]{1,0:T(8,128)(2,1)S(1)}, bf16[1280,768]{1,0:T(8,128)(2,1)S(1)}, bf16[1280,768]{1,0:T(8,128)(2,1)S(1)}, bf16[1280,768]{1,0:T(8,12...) custom-call(bf16[1280,768]{1,0:T(8,128)(2,1)} %bitcast.51, bf16[1280,768]{1,0:T(8,128)(2,1)} %copy-done.3, ...), custom_call_target="tpu_custom_call" | custom-call | bytes 23592960 | tf_op jit(solution)/shard_map/pallas_call | solution.py:109
  15.2 3.9 %collective-permute-start.7 = (bf16[144,1280]{1,0:T(8,128)(2,1)S(1)}, bf16[144,1280]{1,0:T(8,128)(2,1)S(1)}, u32[]{:S(2)}, u32[]{:S(2)}) collective-permute-start(bf16[144,1280]{1,0:T(8,128)(2,1)S(1)} %get-tuple-element.112), channel_id=1, source_target_pairs={{0,24},{8,16},{16,8},{24,0},{1,25},{9,17},{17,9},{25,1},{2,26},{10... | collective-permute-start | bytes 1105928 | tf_op jit(solution)/shard_map/ppermute | solution.py:32
  19.1 4.6 %shard_map.119 = (bf16[128,1536]{1,0:T(8,128)(2,1)S(1)}, bf16[128,1536]{1,0:T(8,128)(2,1)S(1)}, bf16[128,1536]{1,0:T(8,128)(2,1)S(1)}, bf16[384,1280]{1,0:T(8,12...) custom-call(bf16[144,1280]{1,0:T(8,128)(2,1)S(1)} %get-tuple-element, ...), custom_call_target="tpu_custom_call" | custom-call | flops 3019898880 | tf_op jit(solution)/shard_map/pallas_call | solution.py:81
  24.4 4.1 %collective-permute-done.7.refs_0_ = bf16[144,1280]{1,0:T(8,128)(2,1)S(1)} collective-permute-done((bf16[144,1280]{1,0:T(8,128)(2,1)S(1)}, bf16[144,1280]{1,0:T(8,128)(2,1)S(1)}, u32[]{:S(2)}, u32[]{:S(2)}) %collective-permute-start.7) | collective-permute-done | bytes 368672 | tf_op jit(solution)/shard_map/ppermute | solution.py:32
  28.5 2.4 %shard_map.120 = (bf16[128,1536]{1,0:T(8,128)(2,1)S(1)}, bf16[128,1280]{1,0:T(8,128)(2,1)S(1)}, bf16[128,1280]{1,0:T(8,128)(2,1)S(1)}, f32[128,1]{1,0:T(8,128)S(...) custom-call(bf16[144,1280]{1,0:T(8,128)(2,1)S(1)} %collective-permute-done.7.refs_0_, ...), custom_call_target="tpu_custom_call" | custom-call | flops 1006632960 | tf_op jit(solution)/shard_map/pallas_call | solution.py:81
  30.9 3.1 %collective-permute-start.8 = (bf16[128,1536]{1,0:T(8,128)(2,1)S(1)}, bf16[128,1536]{1,0:T(8,128)(2,1)S(1)}, u32[]{:S(2)}, u32[]{:S(2)}) collective-permute-start(bf16[128,1536]{1,0:T(8,128)(2,1)S(1)} %get-tuple-element.113), channel_id=1, source_target_pairs={{0,24},{8,16},{16,8},{24,0},{1,25},{9,17},{17,9},{25,1},{2,26},{10... | collective-permute-start | bytes 1179656 | tf_op jit(solution)/shard_map/ppermute | solution.py:32
  34.3 3.2 %collective-permute-done.5.refs_1_ = bf16[128,1536]{1,0:T(8,128)(2,1)S(1)} collective-permute-done((bf16[128,1536]{1,0:T(8,128)(2,1)S(1)}, bf16[128,1536]{1,0:T(8,128)(2,1)S(1)}, u32[]{:S(2)}, u32[]{:S(2)}) %collective-permute-start.5) | collective-permute-done | bytes 393248 | tf_op jit(solution)/shard_map/ppermute | solution.py:32
  37.5 7.3 %collective-permute-done.8.refs_3_ = bf16[128,1536]{1,0:T(8,128)(2,1)S(1)} collective-permute-done((bf16[128,1536]{1,0:T(8,128)(2,1)S(1)}, bf16[128,1536]{1,0:T(8,128)(2,1)S(1)}, u32[]{:S(2)}, u32[]{:S(2)}) %collective-permute-start.8) | collective-permute-done | bytes 393248 | tf_op jit(solution)/shard_map/ppermute | solution.py:32
  45.4 2.7 %collective-permute-start.16 = (bf16[128,768]{1,0:T(8,128)(2,1)S(1)}, bf16[128,768]{1,0:T(8,128)(2,1)S(1)}, u32[]{:S(2)}, u32[]{:S(2)}) collective-permute-start(bf16[128,768]{1,0:T(8,128)(2,1)S(1)} %get-tuple-element.114.refs_0_), channel_id=1, source_target_pairs={{0,24},{8,16},{16,8},{24,0},{1,25},{9,17},{17,9},{25,1},{2,26},{10... | collective-permute-start | bytes 589832 | tf_op jit(solution)/shard_map/ppermute | solution.py:32
  49.0 5.2 %collective-permute-done.16.refs_0_ = bf16[128,768]{1,0:T(8,128)(2,1)S(1)} collective-permute-done((bf16[128,768]{1,0:T(8,128)(2,1)S(1)}, bf16[128,768]{1,0:T(8,128)(2,1)S(1)}, u32[]{:S(2)}, u32[]{:S(2)}) %collective-permute-start.16) | collective-permute-done | bytes 196640 | tf_op jit(solution)/shard_map/ppermute | solution.py:32
  54.2 1.9 shard_map.124
  56.1 1.9 collective-permute-start.22
  58.0 3.0 %shard_map.123 = (bf16[384,1280]{1,0:T(8,128)(2,1)S(1)}, f32[128,1]{1,0:T(8,128)S(1)}, f32[128,1]{1,0:T(8,128)S(1)}, f32[128,1]{1,0:T(8,128)S(1)}, bf16[384,768]...) custom-call(bf16[128,768]{1,0:T(8,128)(2,1)S(1)} %get-tuple-element.114.refs_0_, ...), custom_call_target="tpu_custom_call" | custom-call | flops 1509949440 | tf_op jit(solution)/shard_map/pallas_call | solution.py:81
  62.7 2.5 %collective-permute-start.19 = (bf16[128,1280]{1,0:T(8,128)(2,1)S(1)}, bf16[128,1280]{1,0:T(8,128)(2,1)S(1)}, u32[]{:S(2)}, u32[]{:S(2)}) collective-permute-start(bf16[128,1280]{1,0:T(8,128)(2,1)S(1)} %get-tuple-element.202), channel_id=1, source_target_pairs={{0,24},{8,16},{16,8},{24,0},{1,25},{9,17},{17,9},{25,1},{2,26},{10... | collective-permute-start | bytes 983048 | tf_op jit(solution)/shard_map/ppermute | solution.py:32
  66.3 2.2 shard_map.129
  68.6 3.6 %collective-permute-start.23 = (bf16[128,1536]{1,0:T(8,128)(2,1)S(1)}, bf16[128,1536]{1,0:T(8,128)(2,1)S(1)}, u32[]{:S(2)}, u32[]{:S(2)}) collective-permute-start(bf16[128,1536]{1,0:T(8,128)(2,1)S(1)} %get-tuple-element.140), channel_id=1, source_target_pairs={{0,24},{8,16},{16,8},{24,0},{1,25},{9,17},{17,9},{25,1},{2,26},{10... | collective-permute-start | bytes 1179656 | tf_op jit(solution)/shard_map/ppermute | solution.py:32
  72.2 9.3 %collective-permute-done.12.refs_1_ = bf16[128,1280]{1,0:T(8,128)(2,1)S(1)} collective-permute-done((bf16[128,1280]{1,0:T(8,128)(2,1)S(1)}, bf16[128,1280]{1,0:T(8,128)(2,1)S(1)}, u32[]{:S(2)}, u32[]{:S(2)}) %collective-permute-start.12) | collective-permute-done | bytes 327712 | tf_op jit(solution)/shard_map/ppermute | solution.py:32
  81.5 2.3 collective-permute-start.17
  84.4 2.2 shard_map.126
  87.2 1.7 shard_map.127
  89.0 2.4 %collective-permute-start.26 = (bf16[128,768]{1,0:T(8,128)(2,1)S(1)}, bf16[128,768]{1,0:T(8,128)(2,1)S(1)}, u32[]{:S(2)}, u32[]{:S(2)}) collective-permute-start(bf16[128,768]{1,0:T(8,128)(2,1)S(1)} %get-tuple-element.134), channel_id=1, source_target_pairs={{0,24},{8,16},{16,8},{24,0},{1,25},{9,17},{17,9},{25,1},{2,26},{10... | collective-permute-start | bytes 589832 | tf_op jit(solution)/shard_map/ppermute | solution.py:32
  94.1 4.4 %collective-permute-done.18.refs_4_.refs_6_ = f32[128,1]{1,0:T(8,128)S(1)} collective-permute-done((f32[128,1]{1,0:T(8,128)S(1)}, f32[128,1]{1,0:T(8,128)S(1)}, u32[]{:S(2)}, u32[]{:S(2)}) %collective-permute-start.18) | collective-permute-done | bytes 544 | tf_op jit(solution)/shard_map/ppermute | solution.py:37
  98.5 4.4 %shard_map.128 = (bf16[128,1536]{1,0:T(8,128)(2,1)S(1)}, bf16[128,1536]{1,0:T(8,128)(2,1)S(1)}, bf16[128,1536]{1,0:T(8,128)(2,1)S(1)}, bf16[384,1280]{1,0:T(8,128)(2,1)S(1)}, bf16[384,1280]{1,0:T(8,128)(2,1)S(1)}) custom-call(bf16[384,1280]{1,0:T(8,128)(2,1)S(1)} %collective-permute-done.11.refs_0_.refs_5_.refs_4_, ...), custom_call_target="tpu_custom_call" | custom-call | flops 3019898880 | tf_op jit(solution)/shard_map/pallas_call | solution.py:81
  106.3 5.7 %collective-permute-done.20.refs_1_ = bf16[128,1536]{1,0:T(8,128)(2,1)S(1)} collective-permute-done((bf16[128,1536]{1,0:T(8,128)(2,1)S(1)}, bf16[128,1536]{1,0:T(8,128)(2,1)S(1)}, u32[]{:S(2)}, u32[]{:S(2)}) %collective-permute-start.20) | collective-permute-done | bytes 393248 | tf_op jit(solution)/shard_map/ppermute | solution.py:32
  112.0 2.2 collective-permute-done.21.refs_2_
  120.4 10.0 %collective-permute-done.29.refs_0_ = bf16[128,1664]{1,0:T(8,128)(2,1)S(1)} collective-permute-done((bf16[128,1664]{1,0:T(8,128)(2,1)S(1)}, bf16[128,1664]{1,0:T(8,128)(2,1)S(1)}, u32[]{:S(2)}, u32[]{:S(2)}) %collective-permute-start.29) | collective-permute-done | bytes 426016 | tf_op jit(solution)/shard_map/ppermute | solution.py:32
  130.4 3.4 %shard_map.133 = (bf16[128,1280]{1,0:T(8,128)(2,1)S(1)}, f32[1,1280]{1,0:T(1,128)S(1)}) custom-call(bf16[128,1664]{1,0:T(8,128)(2,1)S(1)} %collective-permute-done.29.refs_0_, f32[128,1]{1,0:T(8,128)S(1)} %get-tuple-element.133.refs_1_.refs_2_, bf16[128,1280]{1,0:T(8,128)(2,1)S(1)} %get-tuple-element.146.refs_2_, ...), custom_call_target="tpu_custom_call" | custom-call | flops 1006632960 | tf_op jit(solution)/shard_map/pallas_call | solution.py:81
  135.9 4.4 %shard_map.132 = (bf16[384,1280]{1,0:T(8,128)(2,1)S(1)}, f32[1,1280]{1,0:T(1,128)S(1)}) custom-call(bf16[128,1664]{1,0:T(8,128)(2,1)S(1)} %shard_map.131.refs_0_, bf16[128,1664]{1,0:T(8,128)(2,1)S(1)} %collective-permute-done.27.refs_1_, bf16[128,1664]{1,0:T(8,128)(2,1)S(1)} %collective-permute-done.28.refs_2_, ...), custom_call_target="tpu_custom_call" | custom-call | flops 3019898880 | tf_op jit(solution)/shard_map/pallas_call | solution.py:81
  145.3 1.8 collective-permute-start.31
  147.7 2.5 %convolution_convert_fusion.5 = bf16[1280,768]{1,0:T(8,128)(2,1)} fusion(bf16[512,1280]{1,0:T(8,128)(2,1)S(1)} %constant_dynamic-update-slice_fusion, bf16[512,768]{1,0:T(8,128)(2,1)S(1)} %get-tuple-element.155), kind=kOutput, calls=%fused_computation.20 | convolution fusion | flops 1007616000 | bytes 4063232 | tf_op jit(solution)/shard_map/dot_general | solution.py:22
  151.2 1.7 shard_map.137
  154.3 2.6 %shard_map.135 = (bf16[128,1280]{1,0:T(8,128)(2,1)S(1)}, f32[128,1]{1,0:T(8,128)}, bf16[128,768]{1,0:T(8,128)(2,1)S(1)}, bf16[128,768]{1,0:T(8,128)(2,1)S(1)}) custom-call(bf16[128,768]{1,0:T(8,128)(2,1)S(1)} %collective-permute-done.35.refs_0_, f32[128,1]{1,0:T(8,128)S(1)} %get-tuple-element.133.refs_1_.refs_2_, ...), custom_call_target="tpu_custom_call" | custom-call | flops 503316480 | tf_op jit(solution)/shard_map/pallas_call | solution.py:81
  158.5 3.6 %shard_map.134 = (bf16[128,1280]{1,0:T(8,128)(2,1)S(1)}, bf16[128,1280]{1,0:T(8,128)(2,1)S(1)}, bf16[128,1280]{1,0:T(8,128)(2,1)S(1)}, f32[128,1]{1,0:T(8,128)},...) custom-call(bf16[128,768]{1,0:T(8,128)(2,1)S(1)} %get-tuple-element.148.refs_, ...), custom_call_target="tpu_custom_call" | custom-call | flops 1509949440 | tf_op jit(solution)/shard_map/pallas_call | solution.py:81
  166.6 7.9 %collective-permute-done.33 = bf16[128,1280]{1,0:T(8,128)(2,1)S(1)} collective-permute-done((bf16[128,1280]{1,0:T(8,128)(2,1)S(1)}, bf16[128,1280]{1,0:T(8,128)(2,1)S(1)}, u32[]{:S(2)}, u32[]{:S(2)}) %collective-permute-start.33) | collective-permute-done | bytes 327712 | tf_op jit(solution)/shard_map/ppermute | solution.py:32
  174.6 2.2 shard_map.136
  178.6 4.0 %collective-permute-done.38.refs_1_ = bf16[128,768]{1,0:T(8,128)(2,1)S(1)} collective-permute-done((bf16[128,768]{1,0:T(8,128)(2,1)S(1)}, bf16[128,768]{1,0:T(8,128)(2,1)S(1)}, u32[]{:S(2)}, u32[]{:S(2)}) %collective-permute-start.38) | collective-permute-done | bytes 196640 | tf_op jit(solution)/shard_map/ppermute | solution.py:32
  184.4 2.4 %collective-permute-start.45 = (bf16[128,1664]{1,0:T(8,128)(2,1)S(1)}, bf16[128,1664]{1,0:T(8,128)(2,1)S(1)}, u32[]{:S(2)}, u32[]{:S(2)}) collective-permute-start(bf16[128,1664]{1,0:T(8,128)(2,1)S(1)} %shard_map.138.refs_0_), channel_id=1, source_target_pairs={{0,24},{8,16},{16,8},{24,0},{1,25},{9,17},{17,9},{25,1},{2,26},{10... | collective-permute-start | bytes 1277960 | tf_op jit(solution)/shard_map/ppermute | solution.py:32
  189.4 8.8 %collective-permute-done.45.refs_0_ = bf16[128,1664]{1,0:T(8,128)(2,1)S(1)} collective-permute-done((bf16[128,1664]{1,0:T(8,128)(2,1)S(1)}, bf16[128,1664]{1,0:T(8,128)(2,1)S(1)}, u32[]{:S(2)}, u32[]{:S(2)}) %collective-permute-start.45) | collective-permute-done | bytes 426016 | tf_op jit(solution)/shard_map/ppermute | solution.py:32
  198.2 7.0 %collective-permute-done.41.refs_1_ = bf16[128,1664]{1,0:T(8,128)(2,1)S(1)} collective-permute-done((bf16[128,1664]{1,0:T(8,128)(2,1)S(1)}, bf16[128,1664]{1,0:T(8,128)(2,1)S(1)}, u32[]{:S(2)}, u32[]{:S(2)}) %collective-permute-start.41) | collective-permute-done | bytes 426016 | tf_op jit(solution)/shard_map/ppermute | solution.py:32
  208.6 3.4 %shard_map.140 = (bf16[128,1280]{1,0:T(8,128)(2,1)S(1)}, f32[1,1280]{1,0:T(1,128)S(1)}) custom-call(bf16[128,1664]{1,0:T(8,128)(2,1)S(1)} %collective-permute-done.45.refs_0_, f32[128,1]{1,0:T(8,128)S(1)} %get-tuple-element.125.refs_1_, bf16[128,1280]{1,0:T(8,128)(2,1)S(1)} %get-tuple-element.174.refs_2_, ...), custom_call_target="tpu_custom_call" | custom-call | flops 1006632960 | tf_op jit(solution)/shard_map/pallas_call | solution.py:81
  212.0 4.6 %shard_map.139 = (bf16[128,1280]{1,0:T(8,128)(2,1)S(1)}, bf16[128,1280]{1,0:T(8,128)(2,1)S(1)}, bf16[128,1280]{1,0:T(8,128)(2,1)S(1)}, f32[1,1280]{1,0:T(1,128)S(1)}) custom-call(bf16[128,1664]{1,0:T(8,128)(2,1)S(1)} %shard_map.138.refs_0_, bf16[128,1664]{1,0:T(8,128)(2,1)S(1)} %collective-permute-done.41.refs_1_, ...), custom_call_target="tpu_custom_call" | custom-call | flops 1006632960 | tf_op jit(solution)/shard_map/pallas_call | solution.py:81
  216.7 2.4 collective-permute-start.46
  220.3 2.7 %fusion.3 = bf16[768,1280]{1,0:T(8,128)(2,1)} fusion(bf16[768,1280]{1,0:T(8,128)(2,1)S(1)} %collective-permute-done.49, bf16[768,1280]{1,0:T(8,128)(2,1)S(1)} %convolution_convert_fusion, bf16[512,1280]{1,0:T(8,128)(2,1)S(1)} %constant_dynamic-update-slice_fusion.6, bf16[128,768]{1,0:T(8,128)(2,1)S(1)} %get-tuple-element.187, ...), kind=kOutput, calls=%fused_computation.9 | convolution fusion | flops 1013121024 | bytes 7995392 | tf_op jit(solution)/shard_map/dot_general | solution.py:22
  225.9 2.7 %fusion.4 = bf16[1280,768]{1,0:T(8,128)(2,1)} fusion(bf16[1280,768]{1,0:T(8,128)(2,1)S(1)} %collective-permute-done.48, bf16[1280,768]{1,0:T(8,128)(2,1)S(1)} %convolution_convert_fusion.2, bf16[512,1280]{1,0:T(8,128)(2,1)S(1)} %constant_dynamic-update-slice_fusion.8, bf16[512,768]{1,0:T(8,128)(2,1)S(1)} %get-tuple-element.185), kind=kOutput, calls=%fused_computation.10 | convolution fusion | flops 1011548160 | bytes 7995392 | tf_op jit(solution)/shard_map/dot_general | solution.py:22
  228.6 2.7 %fusion.5 = bf16[1280,768]{1,0:T(8,128)(2,1)} fusion(bf16[1280,768]{1,0:T(8,128)(2,1)S(1)} %collective-permute-done.47, bf16[1280,768]{1,0:T(8,128)(2,1)S(1)} %convolution_convert_fusion.3, bf16[512,1280]{1,0:T(8,128)(2,1)S(1)} %constant_dynamic-update-slice_fusion.8, bf16[512,768]{1,0:T(8,128)(2,1)S(1)} %get-tuple-element.182), kind=kOutput, calls=%fused_computation.11 | convolution fusion | flops 1011548160 | bytes 7995392 | tf_op jit(solution)/shard_map/dot_general | solution.py:22
  232.0 2.6 %collective-permute-done.43 = bf16[128,1280]{1,0:T(8,128)(2,1)S(1)} collective-permute-done((bf16[128,1280]{1,0:T(8,128)(2,1)S(1)}, bf16[128,1280]{1,0:T(8,128)(2,1)S(1)}, u32[]{:S(2)}, u32[]{:S(2)}) %collective-permute-start.43) | collective-permute-done | bytes 327712 | tf_op jit(solution)/shard_map/ppermute | solution.py:32
  (153 shorter events, 57.2 us)
Async XLA Ops:
  0.6 7.5 %collective-permute-start.2 = (bf16[1280,768]{1,0:T(8,128)(2,1)}, bf16[1280,768]{1,0:T(8,128)(2,1)S(1)}, u32[]{:S(2)}, u32[]{:S(2)}) collective-permute-start(bf16[1280,768]{1,0:T(8,128)(2,1)} %bitcast.50), channel_id=1, source_target_pairs={{0,1},{1,0},{2,3},{3,2},{4,5},{5,4},{6,7},{7,6},{8,9},{9,8},{10,11... | collective-permute-start | bytes 5898248 | tf_op jit(solution)/shard_map/ppermute | solution.py:32
  1.2 7.0 %collective-permute-start.3 = (bf16[1280,768]{1,0:T(8,128)(2,1)}, bf16[1280,768]{1,0:T(8,128)(2,1)}, u32[]{:S(2)}, u32[]{:S(2)}) collective-permute-start(bf16[1280,768]{1,0:T(8,128)(2,1)} %bitcast.52), channel_id=1, source_target_pairs={{0,1},{1,0},{2,3},{3,2},{4,5},{5,4},{6,7},{7,6},{8,9},{9,8},{10,11... | collective-permute-start | bytes 5898248 | tf_op jit(solution)/shard_map/ppermute | solution.py:32
  1.2 9.5 %collective-permute-start.4 = (bf16[768,1280]{1,0:T(8,128)(2,1)}, bf16[768,1280]{1,0:T(8,128)(2,1)}, u32[]{:S(2)}, u32[]{:S(2)}) collective-permute-start(bf16[768,1280]{1,0:T(8,128)(2,1)} %bitcast.54), channel_id=1, source_target_pairs={{0,1},{1,0},{2,3},{3,2},{4,5},{5,4},{6,7},{7,6},{8,9},{9,8},{10,11... | collective-permute-start | bytes 5898248 | tf_op jit(solution)/shard_map/ppermute | solution.py:32
  4.0 15.1 %collective-permute-start = (bf16[144,1280]{1,0:T(8,128)(2,1)S(1)}, bf16[144,1280]{1,0:T(8,128)(2,1)S(1)}, u32[]{:S(2)}, u32[]{:S(2)}) collective-permute-start(bf16[144,1280]{1,0:T(8,128)(2,1)S(1)} %get-tuple-element.211), channel_id=1, source_target_pairs={{0,8},{8,0},{16,24},{24,16},{1,9},{9,1},{17,25},{25,17},{2,10},{10... | collective-permute-start | bytes 1105928 | tf_op jit(solution)/shard_map/ppermute | solution.py:32
  6.6 12.5 %collective-permute-start.1 = (bf16[144,1280]{1,0:T(8,128)(2,1)S(1)}, bf16[144,1280]{1,0:T(8,128)(2,1)S(1)}, u32[]{:S(2)}, u32[]{:S(2)}) collective-permute-start(bf16[144,1280]{1,0:T(8,128)(2,1)S(1)} %get-tuple-element.212), channel_id=1, source_target_pairs={{0,16},{8,24},{16,0},{24,8},{1,17},{9,25},{17,1},{25,9},{2,18},{10... | collective-permute-start | bytes 1105928 | tf_op jit(solution)/shard_map/ppermute | solution.py:32
  15.2 13.3 %collective-permute-start.7 = (bf16[144,1280]{1,0:T(8,128)(2,1)S(1)}, bf16[144,1280]{1,0:T(8,128)(2,1)S(1)}, u32[]{:S(2)}, u32[]{:S(2)}) collective-permute-start(bf16[144,1280]{1,0:T(8,128)(2,1)S(1)} %get-tuple-element.112), channel_id=1, source_target_pairs={{0,24},{8,16},{16,8},{24,0},{1,25},{9,17},{17,9},{25,1},{2,26},{10... | collective-permute-start | bytes 1105928 | tf_op jit(solution)/shard_map/ppermute | solution.py:32
  23.7 13.8 %collective-permute-start.5 = (bf16[128,1536]{1,0:T(8,128)(2,1)S(1)}, bf16[128,1536]{1,0:T(8,128)(2,1)S(1)}, u32[]{:S(2)}, u32[]{:S(2)}) collective-permute-start(bf16[128,1536]{1,0:T(8,128)(2,1)S(1)} %get-tuple-element.108), channel_id=1, source_target_pairs={{0,8},{8,0},{16,24},{24,16},{1,9},{9,1},{17,25},{25,17},{2,10},{10... | collective-permute-start | bytes 1179656 | tf_op jit(solution)/shard_map/ppermute | solution.py:32
  24.3 13.2 %collective-permute-start.6 = (bf16[128,1536]{1,0:T(8,128)(2,1)S(1)}, bf16[128,1536]{1,0:T(8,128)(2,1)S(1)}, u32[]{:S(2)}, u32[]{:S(2)}) collective-permute-start(bf16[128,1536]{1,0:T(8,128)(2,1)S(1)} %get-tuple-element.109), channel_id=1, source_target_pairs={{0,16},{8,24},{16,0},{24,8},{1,17},{9,25},{17,1},{25,9},{2,18},{10... | collective-permute-start | bytes 1179656 | tf_op jit(solution)/shard_map/ppermute | solution.py:32
  30.9 13.9 %collective-permute-start.8 = (bf16[128,1536]{1,0:T(8,128)(2,1)S(1)}, bf16[128,1536]{1,0:T(8,128)(2,1)S(1)}, u32[]{:S(2)}, u32[]{:S(2)}) collective-permute-start(bf16[128,1536]{1,0:T(8,128)(2,1)S(1)} %get-tuple-element.113), channel_id=1, source_target_pairs={{0,24},{8,16},{16,8},{24,0},{1,25},{9,17},{17,9},{25,1},{2,26},{10... | collective-permute-start | bytes 1179656 | tf_op jit(solution)/shard_map/ppermute | solution.py:32
  45.4 8.8 %collective-permute-start.16 = (bf16[128,768]{1,0:T(8,128)(2,1)S(1)}, bf16[128,768]{1,0:T(8,128)(2,1)S(1)}, u32[]{:S(2)}, u32[]{:S(2)}) collective-permute-start(bf16[128,768]{1,0:T(8,128)(2,1)S(1)} %get-tuple-element.114.refs_0_), channel_id=1, source_target_pairs={{0,24},{8,16},{16,8},{24,0},{1,25},{9,17},{17,9},{25,1},{2,26},{10... | collective-permute-start | bytes 589832 | tf_op jit(solution)/shard_map/ppermute | solution.py:32
  48.1 9.8 %collective-permute-start.10 = (bf16[128,768]{1,0:T(8,128)(2,1)S(1)}, bf16[128,768]{1,0:T(8,128)(2,1)S(1)}, u32[]{:S(2)}, u32[]{:S(2)}) collective-permute-start(bf16[128,768]{1,0:T(8,128)(2,1)S(1)} %get-tuple-element.114.refs_0_), channel_id=1, source_target_pairs={{0,16},{8,24},{16,0},{24,8},{1,17},{9,25},{17,1},{25,9},{2,18},{10... | collective-permute-start | bytes 589832 | tf_op jit(solution)/shard_map/ppermute | solution.py:32
  48.6 9.4 %collective-permute-start.9 = (bf16[128,768]{1,0:T(8,128)(2,1)S(1)}, bf16[128,768]{1,0:T(8,128)(2,1)S(1)}, u32[]{:S(2)}, u32[]{:S(2)}) collective-permute-start(bf16[128,768]{1,0:T(8,128)(2,1)S(1)} %get-tuple-element.114.refs_0_), channel_id=1, source_target_pairs={{0,8},{8,0},{16,24},{24,16},{1,9},{9,1},{17,25},{25,17},{2,10},{10... | collective-permute-start | bytes 589832 | tf_op jit(solution)/shard_map/ppermute | solution.py:32
  56.1 10.2 %collective-permute-start.22 = (bf16[128,1280]{1,0:T(8,128)(2,1)S(1)}, bf16[128,1280]{1,0:T(8,128)(2,1)S(1)}, u32[]{:S(2)}, u32[]{:S(2)}) collective-permute-start(bf16[128,1280]{1,0:T(8,128)(2,1)S(1)} %get-tuple-element.139), channel_id=1, source_target_pairs={{0,2},{2,4},{4,6},{6,0},{1,3},{3,5},{5,7},{7,1},{8,10},{10,12},{12... | collective-permute-start | bytes 983048 | tf_op jit(solution)/shard_map/ppermute | solution.py:37
  61.0 37.6 %collective-permute-start.11 = (bf16[384,1280]{1,0:T(8,128)(2,1)S(1)}, bf16[384,1280]{1,0:T(8,128)(2,1)S(1)}, u32[]{:S(2)}, u32[]{:S(2)}) collective-permute-start(bf16[384,1280]{1,0:T(8,128)(2,1)S(1)} %get-tuple-element.117), channel_id=1, source_target_pairs={{0,2},{2,4},{4,6},{6,0},{1,3},{3,5},{5,7},{7,1},{8,10},{10,12},{12... | collective-permute-start | bytes 2949128 | tf_op jit(solution)/shard_map/ppermute | solution.py:37
  62.7 23.9 %collective-permute-start.19 = (bf16[128,1280]{1,0:T(8,128)(2,1)S(1)}, bf16[128,1280]{1,0:T(8,128)(2,1)S(1)}, u32[]{:S(2)}, u32[]{:S(2)}) collective-permute-start(bf16[128,1280]{1,0:T(8,128)(2,1)S(1)} %get-tuple-element.202), channel_id=1, source_target_pairs={{0,24},{8,16},{16,8},{24,0},{1,25},{9,17},{17,9},{25,1},{2,26},{10... | collective-permute-start | bytes 983048 | tf_op jit(solution)/shard_map/ppermute | solution.py:32
  65.3 16.2 %collective-permute-start.12 = (bf16[128,1280]{1,0:T(8,128)(2,1)S(1)}, bf16[128,1280]{1,0:T(8,128)(2,1)S(1)}, u32[]{:S(2)}, u32[]{:S(2)}) collective-permute-start(bf16[128,1280]{1,0:T(8,128)(2,1)S(1)} %get-tuple-element.205), channel_id=1, source_target_pairs={{0,8},{8,0},{16,24},{24,16},{1,9},{9,1},{17,25},{25,17},{2,10},{10... | collective-permute-start | bytes 983048 | tf_op jit(solution)/shard_map/ppermute | solution.py:32
  65.8 15.6 %collective-permute-start.13 = (bf16[128,1280]{1,0:T(8,128)(2,1)S(1)}, bf16[128,1280]{1,0:T(8,128)(2,1)S(1)}, u32[]{:S(2)}, u32[]{:S(2)}) collective-permute-start(bf16[128,1280]{1,0:T(8,128)(2,1)S(1)} %get-tuple-element.204), channel_id=1, source_target_pairs={{0,16},{8,24},{16,0},{24,8},{1,17},{9,25},{17,1},{25,9},{2,18},{10... | collective-permute-start | bytes 983048 | tf_op jit(solution)/shard_map/ppermute | solution.py:32
  68.6 36.3 %collective-permute-start.23 = (bf16[128,1536]{1,0:T(8,128)(2,1)S(1)}, bf16[128,1536]{1,0:T(8,128)(2,1)S(1)}, u32[]{:S(2)}, u32[]{:S(2)}) collective-permute-start(bf16[128,1536]{1,0:T(8,128)(2,1)S(1)} %get-tuple-element.140), channel_id=1, source_target_pairs={{0,24},{8,16},{16,8},{24,0},{1,25},{9,17},{17,9},{25,1},{2,26},{10... | collective-permute-start | bytes 1179656 | tf_op jit(solution)/shard_map/ppermute | solution.py:32
  81.5 7.5 %collective-permute-start.17 = (f32[128,1]{1,0:T(8,128)S(1)}, f32[128,1]{1,0:T(8,128)S(1)}, u32[]{:S(2)}, u32[]{:S(2)}) collective-permute-start(f32[128,1]{1,0:T(8,128)S(1)} %get-tuple-element.128), channel_id=1, source_target_pairs={{0,24},{8,16},{16,8},{24,0},{1,25},{9,17},{17,9},{25,1},{2,26},{10... | collective-permute-start | bytes 1544 | tf_op jit(solution)/shard_map/ppermute | solution.py:32
  83.8 7.5 %collective-permute-start.15 = (f32[128,1]{1,0:T(8,128)S(1)}, f32[128,1]{1,0:T(8,128)S(1)}, u32[]{:S(2)}, u32[]{:S(2)}) collective-permute-start(f32[128,1]{1,0:T(8,128)S(1)} %get-tuple-element.124), channel_id=1, source_target_pairs={{0,16},{8,24},{16,0},{24,8},{1,17},{9,25},{17,1},{25,9},{2,18},{10... | collective-permute-start | bytes 1544 | tf_op jit(solution)/shard_map/ppermute | solution.py:32
  89.0 25.7 %collective-permute-start.26 = (bf16[128,768]{1,0:T(8,128)(2,1)S(1)}, bf16[128,768]{1,0:T(8,128)(2,1)S(1)}, u32[]{:S(2)}, u32[]{:S(2)}) collective-permute-start(bf16[128,768]{1,0:T(8,128)(2,1)S(1)} %get-tuple-element.134), channel_id=1, source_target_pairs={{0,24},{8,16},{16,8},{24,0},{1,25},{9,17},{17,9},{25,1},{2,26},{10... | collective-permute-start | bytes 589832 | tf_op jit(solution)/shard_map/ppermute | solution.py:32
  91.4 23.3 %collective-permute-start.24 = (bf16[128,768]{1,0:T(8,128)(2,1)S(1)}, bf16[128,768]{1,0:T(8,128)(2,1)S(1)}, u32[]{:S(2)}, u32[]{:S(2)}) collective-permute-start(bf16[128,768]{1,0:T(8,128)(2,1)S(1)} %get-tuple-element.131), channel_id=1, source_target_pairs={{0,8},{8,0},{16,24},{24,16},{1,9},{9,1},{17,25},{25,17},{2,10},{10... | collective-permute-start | bytes 589832 | tf_op jit(solution)/shard_map/ppermute | solution.py:32
  102.9 9.0 %collective-permute-start.20 = (bf16[128,1536]{1,0:T(8,128)(2,1)S(1)}, bf16[128,1536]{1,0:T(8,128)(2,1)S(1)}, u32[]{:S(2)}, u32[]{:S(2)}) collective-permute-start(bf16[128,1536]{1,0:T(8,128)(2,1)S(1)} %get-tuple-element.137), channel_id=1, source_target_pairs={{0,8},{8,0},{16,24},{24,16},{1,9},{9,1},{17,25},{25,17},{2,10},{10... | collective-permute-start | bytes 1179656 | tf_op jit(solution)/shard_map/ppermute | solution.py:32
  104.0 10.1 %collective-permute-start.21 = (bf16[128,1536]{1,0:T(8,128)(2,1)S(1)}, bf16[128,1536]{1,0:T(8,128)(2,1)S(1)}, u32[]{:S(2)}, u32[]{:S(2)}) collective-permute-start(bf16[128,1536]{1,0:T(8,128)(2,1)S(1)} %get-tuple-element.138), channel_id=1, source_target_pairs={{0,16},{8,24},{16,0},{24,8},{1,17},{9,25},{17,1},{25,9},{2,18},{10... | collective-permute-start | bytes 1179656 | tf_op jit(solution)/shard_map/ppermute | solution.py:32
  104.9 11.4 %collective-permute-start.25 = (bf16[128,768]{1,0:T(8,128)(2,1)S(1)}, bf16[128,768]{1,0:T(8,128)(2,1)S(1)}, u32[]{:S(2)}, u32[]{:S(2)}) collective-permute-start(bf16[128,768]{1,0:T(8,128)(2,1)S(1)} %get-tuple-element.132), channel_id=1, source_target_pairs={{0,16},{8,24},{16,0},{24,8},{1,17},{9,25},{17,1},{25,9},{2,18},{10... | collective-permute-start | bytes 589832 | tf_op jit(solution)/shard_map/ppermute | solution.py:32
  116.8 13.6 %collective-permute-start.29 = (bf16[128,1664]{1,0:T(8,128)(2,1)S(1)}, bf16[128,1664]{1,0:T(8,128)(2,1)S(1)}, u32[]{:S(2)}, u32[]{:S(2)}) collective-permute-start(bf16[128,1664]{1,0:T(8,128)(2,1)S(1)} %shard_map.131.refs_0_), channel_id=1, source_target_pairs={{0,24},{8,16},{16,8},{24,0},{1,25},{9,17},{17,9},{25,1},{2,26},{10... | collective-permute-start | bytes 1277960 | tf_op jit(solution)/shard_map/ppermute | solution.py:32
  118.4 17.6 %collective-permute-start.27 = (bf16[128,1664]{1,0:T(8,128)(2,1)S(1)}, bf16[128,1664]{1,0:T(8,128)(2,1)S(1)}, u32[]{:S(2)}, u32[]{:S(2)}) collective-permute-start(bf16[128,1664]{1,0:T(8,128)(2,1)S(1)} %shard_map.131.refs_0_), channel_id=1, source_target_pairs={{0,8},{8,0},{16,24},{24,16},{1,9},{9,1},{17,25},{25,17},{2,10},{10... | collective-permute-start | bytes 1277960 | tf_op jit(solution)/shard_map/ppermute | solution.py:32
  120.0 15.9 %collective-permute-start.28 = (bf16[128,1664]{1,0:T(8,128)(2,1)S(1)}, bf16[128,1664]{1,0:T(8,128)(2,1)S(1)}, u32[]{:S(2)}, u32[]{:S(2)}) collective-permute-start(bf16[128,1664]{1,0:T(8,128)(2,1)S(1)} %shard_map.131.refs_0_), channel_id=1, source_target_pairs={{0,16},{8,24},{16,0},{24,8},{1,17},{9,25},{17,1},{25,9},{2,18},{10... | collective-permute-start | bytes 1277960 | tf_op jit(solution)/shard_map/ppermute | solution.py:32
  133.8 10.4 %collective-permute-start.30 = (bf16[128,1280]{1,0:T(8,128)(2,1)S(1)}, bf16[128,1280]{1,0:T(8,128)(2,1)S(1)}, u32[]{:S(2)}, u32[]{:S(2)}) collective-permute-start(bf16[128,1280]{1,0:T(8,128)(2,1)S(1)} %get-tuple-element.147), channel_id=1, source_target_pairs={{0,6},{2,0},{4,2},{6,4},{1,7},{3,1},{5,3},{7,5},{8,14},{10,8},{12,... | collective-permute-start | bytes 983048 | tf_op jit(solution)/shard_map/ppermute | solution.py:37
  144.2 10.1 %collective-permute-start.35 = (bf16[128,768]{1,0:T(8,128)(2,1)S(1)}, bf16[128,768]{1,0:T(8,128)(2,1)S(1)}, u32[]{:S(2)}, u32[]{:S(2)}) collective-permute-start(bf16[128,768]{1,0:T(8,128)(2,1)S(1)} %get-tuple-element.148.refs_0_), channel_id=1, source_target_pairs={{0,24},{8,16},{16,8},{24,0},{1,25},{9,17},{17,9},{25,1},{2,26},{10... | collective-permute-start | bytes 589832 | tf_op jit(solution)/shard_map/ppermute | solution.py:32
  145.3 13.1 %collective-permute-start.31 = (bf16[128,768]{1,0:T(8,128)(2,1)S(1)}, bf16[128,768]{1,0:T(8,128)(2,1)S(1)}, u32[]{:S(2)}, u32[]{:S(2)}) collective-permute-start(bf16[128,768]{1,0:T(8,128)(2,1)S(1)} %get-tuple-element.148.refs_0_), channel_id=1, source_target_pairs={{0,8},{8,0},{16,24},{24,16},{1,9},{9,1},{17,25},{25,17},{2,10},{10... | collective-permute-start | bytes 589832 | tf_op jit(solution)/shard_map/ppermute | solution.py:32
  147.1 11.4 %collective-permute-start.32 = (bf16[128,768]{1,0:T(8,128)(2,1)S(1)}, bf16[128,768]{1,0:T(8,128)(2,1)S(1)}, u32[]{:S(2)}, u32[]{:S(2)}) collective-permute-start(bf16[128,768]{1,0:T(8,128)(2,1)S(1)} %get-tuple-element.148.refs_0_), channel_id=1, source_target_pairs={{0,16},{8,24},{16,0},{24,8},{1,17},{9,25},{17,1},{25,9},{2,18},{10... | collective-permute-start | bytes 589832 | tf_op jit(solution)/shard_map/ppermute | solution.py:32
  150.2 24.4 %collective-permute-start.37 = (bf16[384,1280]{1,0:T(8,128)(2,1)S(1)}, bf16[384,1280]{1,0:T(8,128)(2,1)S(1)}, u32[]{:S(2)}, u32[]{:S(2)}) collective-permute-start(bf16[384,1280]{1,0:T(8,128)(2,1)S(1)} %get-tuple-element.145), channel_id=1, source_target_pairs={{0,6},{2,0},{4,2},{6,4},{1,7},{3,1},{5,3},{7,5},{8,14},{10,8},{12,... | collective-permute-start | bytes 2949128 | tf_op jit(solution)/shard_map/ppermute | solution.py:37
  152.9 29.7 %collective-permute-start.40 = (bf16[128,768]{1,0:T(8,128)(2,1)S(1)}, bf16[128,768]{1,0:T(8,128)(2,1)S(1)}, u32[]{:S(2)}, u32[]{:S(2)}) collective-permute-start(bf16[128,768]{1,0:T(8,128)(2,1)S(1)} %get-tuple-element.168), channel_id=1, source_target_pairs={{0,24},{8,16},{16,8},{24,0},{1,25},{9,17},{17,9},{25,1},{2,26},{10... | collective-permute-start | bytes 589832 | tf_op jit(solution)/shard_map/ppermute | solution.py:32
  156.9 17.7 %collective-permute-start.36 = (bf16[128,1280]{1,0:T(8,128)(2,1)S(1)}, bf16[128,1280]{1,0:T(8,128)(2,1)S(1)}, u32[]{:S(2)}, u32[]{:S(2)}) collective-permute-start(bf16[128,1280]{1,0:T(8,128)(2,1)S(1)} %get-tuple-element.152), channel_id=1, source_target_pairs={{0,24},{8,16},{16,8},{24,0},{1,25},{9,17},{17,9},{25,1},{2,26},{10... | collective-permute-start | bytes 983048 | tf_op jit(solution)/shard_map/ppermute | solution.py:32
  162.1 12.4 %collective-permute-start.33 = (bf16[128,1280]{1,0:T(8,128)(2,1)S(1)}, bf16[128,1280]{1,0:T(8,128)(2,1)S(1)}, u32[]{:S(2)}, u32[]{:S(2)}) collective-permute-start(bf16[128,1280]{1,0:T(8,128)(2,1)S(1)} %get-tuple-element.150), channel_id=1, source_target_pairs={{0,8},{8,0},{16,24},{24,16},{1,9},{9,1},{17,25},{25,17},{2,10},{10... | collective-permute-start | bytes 983048 | tf_op jit(solution)/shard_map/ppermute | solution.py:32
  163.6 10.9 %collective-permute-start.34 = (bf16[128,1280]{1,0:T(8,128)(2,1)S(1)}, bf16[128,1280]{1,0:T(8,128)(2,1)S(1)}, u32[]{:S(2)}, u32[]{:S(2)}) collective-permute-start(bf16[128,1280]{1,0:T(8,128)(2,1)S(1)} %get-tuple-element.151), channel_id=1, source_target_pairs={{0,16},{8,24},{16,0},{24,8},{1,17},{9,25},{17,1},{25,9},{2,18},{10... | collective-permute-start | bytes 983048 | tf_op jit(solution)/shard_map/ppermute | solution.py:32
  184.4 13.8 %collective-permute-start.45 = (bf16[128,1664]{1,0:T(8,128)(2,1)S(1)}, bf16[128,1664]{1,0:T(8,128)(2,1)S(1)}, u32[]{:S(2)}, u32[]{:S(2)}) collective-permute-start(bf16[128,1664]{1,0:T(8,128)(2,1)S(1)} %shard_map.138.refs_0_), channel_id=1, source_target_pairs={{0,24},{8,16},{16,8},{24,0},{1,25},{9,17},{17,9},{25,1},{2,26},{10... | collective-permute-start | bytes 1277960 | tf_op jit(solution)/shard_map/ppermute | solution.py:32
  186.8 18.3 %collective-permute-start.41 = (bf16[128,1664]{1,0:T(8,128)(2,1)S(1)}, bf16[128,1664]{1,0:T(8,128)(2,1)S(1)}, u32[]{:S(2)}, u32[]{:S(2)}) collective-permute-start(bf16[128,1664]{1,0:T(8,128)(2,1)S(1)} %shard_map.138.refs_0_), channel_id=1, source_target_pairs={{0,8},{8,0},{16,24},{24,16},{1,9},{9,1},{17,25},{25,17},{2,10},{10... | collective-permute-start | bytes 1277960 | tf_op jit(solution)/shard_map/ppermute | solution.py:32
  187.2 18.0 %collective-permute-start.42 = (bf16[128,1664]{1,0:T(8,128)(2,1)S(1)}, bf16[128,1664]{1,0:T(8,128)(2,1)S(1)}, u32[]{:S(2)}, u32[]{:S(2)}) collective-permute-start(bf16[128,1664]{1,0:T(8,128)(2,1)S(1)} %shard_map.138.refs_0_), channel_id=1, source_target_pairs={{0,16},{8,24},{16,0},{24,8},{1,17},{9,25},{17,1},{25,9},{2,18},{10... | collective-permute-start | bytes 1277960 | tf_op jit(solution)/shard_map/ppermute | solution.py:32
  189.3 30.3 %collective-permute-start.49 = (bf16[768,1280]{1,0:T(8,128)(2,1)S(1)}, bf16[768,1280]{1,0:T(8,128)(2,1)S(1)}, u32[]{:S(2)}, u32[]{:S(2)}) collective-permute-start(bf16[768,1280]{1,0:T(8,128)(2,1)S(1)} %fusion.6), channel_id=1, source_target_pairs={{0,1},{1,0},{2,3},{3,2},{4,5},{5,4},{6,7},{7,6},{8,9},{9,8},{10,11... | collective-permute-start | bytes 5898248 | tf_op jit(solution)/shard_map/ppermute | solution.py:32
  206.6 16.5 %collective-permute-start.48 = (bf16[1280,768]{1,0:T(8,128)(2,1)S(1)}, bf16[1280,768]{1,0:T(8,128)(2,1)S(1)}, u32[]{:S(2)}, u32[]{:S(2)}) collective-permute-start(bf16[1280,768]{1,0:T(8,128)(2,1)S(1)} %fusion.8), channel_id=1, source_target_pairs={{0,1},{1,0},{2,3},{3,2},{4,5},{5,4},{6,7},{7,6},{8,9},{9,8},{10,11... | collective-permute-start | bytes 5898248 | tf_op jit(solution)/shard_map/ppermute | solution.py:32
  208.1 15.0 %collective-permute-start.47 = (bf16[1280,768]{1,0:T(8,128)(2,1)S(1)}, bf16[1280,768]{1,0:T(8,128)(2,1)S(1)}, u32[]{:S(2)}, u32[]{:S(2)}) collective-permute-start(bf16[1280,768]{1,0:T(8,128)(2,1)S(1)} %fusion.7), channel_id=1, source_target_pairs={{0,1},{1,0},{2,3},{3,2},{4,5},{5,4},{6,7},{7,6},{8,9},{9,8},{10,11... | collective-permute-start | bytes 5898248 | tf_op jit(solution)/shard_map/ppermute | solution.py:32
  216.7 14.7 %collective-permute-start.46 = (bf16[128,1280]{1,0:T(8,128)(2,1)S(1)}, bf16[128,1280]{1,0:T(8,128)(2,1)S(1)}, u32[]{:S(2)}, u32[]{:S(2)}) collective-permute-start(bf16[128,1280]{1,0:T(8,128)(2,1)S(1)} %get-tuple-element.179), channel_id=1, source_target_pairs={{0,24},{8,16},{16,8},{24,0},{1,25},{9,17},{17,9},{25,1},{2,26},{10... | collective-permute-start | bytes 983048 | tf_op jit(solution)/shard_map/ppermute | solution.py:32
  219.0 15.5 %collective-permute-start.43 = (bf16[128,1280]{1,0:T(8,128)(2,1)S(1)}, bf16[128,1280]{1,0:T(8,128)(2,1)S(1)}, u32[]{:S(2)}, u32[]{:S(2)}) collective-permute-start(bf16[128,1280]{1,0:T(8,128)(2,1)S(1)} %get-tuple-element.177), channel_id=1, source_target_pairs={{0,8},{8,0},{16,24},{24,16},{1,9},{9,1},{17,25},{25,17},{2,10},{10... | collective-permute-start | bytes 983048 | tf_op jit(solution)/shard_map/ppermute | solution.py:32
  219.6 14.9 %collective-permute-start.44 = (bf16[128,1280]{1,0:T(8,128)(2,1)S(1)}, bf16[128,1280]{1,0:T(8,128)(2,1)S(1)}, u32[]{:S(2)}, u32[]{:S(2)}) collective-permute-start(bf16[128,1280]{1,0:T(8,128)(2,1)S(1)} %get-tuple-element.178), channel_id=1, source_target_pairs={{0,16},{8,24},{16,0},{24,8},{1,17},{9,25},{17,1},{25,9},{2,18},{10... | collective-permute-start | bytes 983048 | tf_op jit(solution)/shard_map/ppermute | solution.py:32
  223.1 11.8 %collective-permute-start.50 = (f32[1,1280]{1,0:T(1,128)S(1)}, f32[1,1280]{1,0:T(1,128)S(1)}, u32[]{:S(2)}, u32[]{:S(2)}) collective-permute-start(f32[1,1280]{1,0:T(1,128)S(1)} %add_add_fusion), channel_id=1, source_target_pairs={{0,8},{8,0},{16,24},{24,16},{1,9},{9,1},{17,25},{25,17},{2,10},{10... | collective-permute-start | bytes 15368 | tf_op jit(solution)/shard_map/ppermute | solution.py:32
  224.5 10.3 %collective-permute-start.51 = (f32[1,1280]{1,0:T(1,128)S(1)}, f32[1,1280]{1,0:T(1,128)S(1)}, u32[]{:S(2)}, u32[]{:S(2)}) collective-permute-start(f32[1,1280]{1,0:T(1,128)S(1)} %add_add_fusion), channel_id=1, source_target_pairs={{0,16},{8,24},{16,0},{24,8},{1,17},{9,25},{17,1},{25,9},{2,18},{10... | collective-permute-start | bytes 15368 | tf_op jit(solution)/shard_map/ppermute | solution.py:32
  (15 other events, 73.9 us)

commit v3 on v2

--- a/solution.py
+++ b/solution.py
@@ -68,7 +68,7 @@
     return COLUMNS if extent % COLUMNS == 0 else extent
 
 
-def kernel_call(body, operands, weights, out_shape, scratch):
+def kernel_call(body, operands, weights, out_shape, scratch, weight_cost=1):
     count, kept, made = len(operands), len(weights), len(out_shape)
     rows = max(shape.shape[0] for shape in out_shape)
 
@@ -86,7 +86,7 @@
         scratch_shapes=scratch,
         compiler_params=pltpu.CompilerParams(vmem_limit_bytes=VMEM_BYTES),
         cost_estimate=pl.CostEstimate(
-            flops=4 * rows * sum(weight.size for weight in weights) // 2,
+            flops=weight_cost * 2 * rows * sum(weight.size for weight in weights),
             bytes_accessed=0,
             transcendentals=0,
         ),
@@ -288,6 +288,7 @@
         + [jax.ShapeDtypeStruct((part_rows, 1), f32)] * count
         + [jax.ShapeDtypeStruct((rows, units), bf16)] * 2,
         [pltpu.VMEM((rows, units), bf16), pltpu.VMEM((rows, 1), f32)],
+        weight_cost=0 if in_parts else 1,
     )
     return outs[:out_count], outs[out_count:-2], outs[-2:]
 
@@ -486,7 +487,8 @@
         squares += square
         first_rows.append(split)
     hidden = moved(next_hidden, 1)
-    grad_blocks = sent([cotangent_quarter(step, next_hidden[0]) for step in range(dp_count)])
+    waited = [first_activated[1:-1]] * (dp_count - 1) + [next_hidden[:1]]
+    grad_blocks = sent([cotangent_quarter(step, *waited[step]) for step in range(dp_count)])
     squares = [after(square, *grad_blocks[1:-1]) for square in squares]
     inverse = shifted(row_scale(sent(squares), features, True), "pipe", 1)
     act_parts, grad = [], []
@@ -496,7 +498,7 @@
         grad.append(joined)
     act_grads = act_parts
     act_parts = sent(act_parts)
-    hidden[0] = after(hidden[0], inverse, *act_grads)
+    hidden[0] = after(hidden[0], act_grads[0])
 
     parts, gained = [], []
     for rows_in, mask in zip(hidden, masks[1]):
@@ -517,24 +519,35 @@
         if k == 0:
             lefts = [gained, gained, stacked(first_rows)]
             rights.append(jnp.concatenate(grad))
-            given = [
-                (weight_grad(left, right, False) + soon.astype(f32)).astype(bf16)
-                for left, right, soon in zip(lefts, rights, early[False])
-            ]
-            both_grad[1] = after(both_grad[1], given[2])
-            received = [swap(value, "expert", 1) for value in given]
         outs = []
-        for group, choice, rows_in, grad_in in zip(groups, masks[k], hidden, grad):
+        for index in reversed(range(len(groups))):
             made, gain_term = input_grad(
-                both_grad[group], choice, gate_pair, up_pair, grad_in, rows_in, gain_part, k == 0
+                both_grad[groups[index]],
+                masks[k][index],
+                gate_pair,
+                up_pair,
+                grad[index],
+                hidden[index],
+                gain_part,
+                k == 0,
             )
-            outs += made
+            outs = list(made) + outs
             gain_sum = gain_sum + gain_term
+            if k == 0 and index > 0:
+                both_grad[1] = after(both_grad[1], *early[False], *early[True])
+                given = [
+                    (weight_grad(left, after(right, made[0]), False) + soon.astype(f32)).astype(
+                        bf16
+                    )
+                    for left, right, soon in zip(lefts, rights, early[False])
+                ]
+                both_grad[1] = after(both_grad[1], *given)
+                received = [swap(value, "expert", 1) for value in given]
         if k > 0:
             last_grad = jnp.concatenate(grad)
             grad = moved(outs, -1)
             last_activated = gather_rows(after(activated, outs[0], grad[1]), dp_count)
-            rights = [after(right, *outs) for right in rights]
+            rights = [after(right, *last_activated[1:]) for right in rights]
             early = {
                 wanted: [weight_grad(gained, right, wanted).astype(bf16) for right in rights]
                 for wanted in (False, True)
@@ -547,7 +560,7 @@
                 out_parts += made
                 last_rows.append(split)
             out_rows = from_quarters(out_parts)
-            grad[0] = after(grad[0], out_rows, *early[False], *early[True])
+            grad[0] = after(grad[0], out_rows)
             act_parts, joined = [], []
             for rows_in, choice in zip(grad, masks[0]):
                 made, copied = act_grad_parts([rows_in], rows, choice, down_pair)
@@ -558,7 +571,6 @@
             for wanted in (False, True):
                 early[wanted].append(weight_grad(last_rows, last_grad, wanted).astype(bf16))
             act_parts = sent(act_parts)
-            act_parts[1] = after(act_parts[1], early[False][2], early[True][2])
 
     returned = sent(outs)
     rights = [after(right, *outs) for right in rights]

time: 238 us -> 245 us (1.029)
  waiting for transfers between devices: 90.2 us -> 102 us
  starting transfers between devices: 66 us -> 61.7 us
    ppermute x5, waiting for transfers between devices: 4.43 us -> 24.5 us  [shifted(): lax.ppermute(block, axis, [(i, (i + distance) % size) for i in range(size)])]
    ppermute x49, waiting for transfers between devices: 85.8 us -> 77.8 us  [swap(): return lax.ppermute(block, axis, partner_route(lax.axis_size(axis), step))]
    ppermute x5, starting transfers between devices: 7.43 us -> 3.99 us  [shifted(): lax.ppermute(block, axis, [(i, (i + distance) % size) for i in range(size)])]
  transfers between devices with their start and end apart: 54 -> 54, of which waited for: 20 -> 22; matrix products, arithmetic and copies ran while one was open for 10% -> 9% of each run, Pallas kernels for 23% -> 22%
where the time goes in v3:
time: 245 us
  waiting for transfers between devices  102 us (42%)
  starting transfers between devices  61.7 us (25%)
  Pallas kernels  55.6 us (23%)
  matrix products  19.3 us (8%)
  local copies, waits for them, and re-layouts  3.43 us (1%)
    ppermute x49, waiting for transfers between devices, swap(): return lax.ppermute(block, axis, partner_route(lax.axis_size(axis), step))  77.8 us
    ppermute x49, starting transfers between devices, swap(): return lax.ppermute(block, axis, partner_route(lax.axis_size(axis), step))  57.7 us
    pallas_call x22, Pallas kernels, kernel_call(): pl.pallas_call(call, in_specs=[in_vmem] * (count + kept), out_specs=[in_v...  51.1 us
    ppermute x5, waiting for transfers between devices, shifted(): lax.ppermute(block, axis, [(i, (i + distance) % size) for i in range(size)])  24.5 us
    dot_general x12, matrix products, dot(): lax.dot_general(former, latter, ((contract[:1], contract[1:]), ((), ())),...  19.3 us
  transfers between devices with their start and end apart: 54, of which 22 were waited for; matrix products, arithmetic and copies ran while one was open for 9% of the time, Pallas kernels for 22%

profile of v3, /device:TPU:0, one launch (start us, length us, event | category | flops | bytes accessed | tf_op | source)
XLA Modules:
  0.0 244.7 jit_solution(14631343729928499458)
XLA Ops:
  4.0 2.6 %collective-permute-start = (bf16[144,1280]{1,0:T(8,128)(2,1)S(1)}, bf16[144,1280]{1,0:T(8,128)(2,1)S(1)}, u32[]{:S(2)}, u32[]{:S(2)}) collective-permute-start(bf16[144,1280]{1,0:T(8,128)(2,1)S(1)} %get-tuple-element.218), channel_id=1, source_target_pairs={{0,8},{8,0},{16,24},{24,16},{1,9},{9,1},{17,25},{25,17},{2,10},{10... | collective-permute-start | bytes 1105928 | tf_op jit(solution)/shard_map/ppermute | solution.py:32
  8.1 2.6 %collective-permute-done.4.refs_5_ = bf16[768,1280]{1,0:T(8,128)(2,1)} collective-permute-done((bf16[768,1280]{1,0:T(8,128)(2,1)}, bf16[768,1280]{1,0:T(8,128)(2,1)}, u32[]{:S(2)}, u32[]{:S(2)}) %collective-permute-start.4) | collective-permute-done | bytes 1966112 | tf_op jit(solution)/shard_map/ppermute | solution.py:32
  10.7 4.5 %shard_map.118 = (bf16[1280,768]{1,0:T(8,128)(2,1)S(1)}, bf16[1280,768]{1,0:T(8,128)(2,1)S(1)}, bf16[1280,768]{1,0:T(8,128)(2,1)S(1)}, bf16[1280,768]{1,0:T(8,12...) custom-call(bf16[1280,768]{1,0:T(8,128)(2,1)} %bitcast.51, bf16[1280,768]{1,0:T(8,128)(2,1)} %copy-done.3, ...), custom_call_target="tpu_custom_call" | custom-call | bytes 23592960 | tf_op jit(solution)/shard_map/pallas_call | solution.py:109
  15.2 3.9 %collective-permute-start.7 = (bf16[144,1280]{1,0:T(8,128)(2,1)S(1)}, bf16[144,1280]{1,0:T(8,128)(2,1)S(1)}, u32[]{:S(2)}, u32[]{:S(2)}) collective-permute-start(bf16[144,1280]{1,0:T(8,128)(2,1)S(1)} %get-tuple-element.116), channel_id=1, source_target_pairs={{0,24},{8,16},{16,8},{24,0},{1,25},{9,17},{17,9},{25,1},{2,26},{10... | collective-permute-start | bytes 1105928 | tf_op jit(solution)/shard_map/ppermute | solution.py:32
  19.1 4.6 %shard_map.119 = (bf16[128,1536]{1,0:T(8,128)(2,1)S(1)}, bf16[128,1536]{1,0:T(8,128)(2,1)S(1)}, bf16[128,1536]{1,0:T(8,128)(2,1)S(1)}, bf16[384,1280]{1,0:T(8,12...) custom-call(bf16[144,1280]{1,0:T(8,128)(2,1)S(1)} %get-tuple-element, ...), custom_call_target="tpu_custom_call" | custom-call | flops 3019898880 | tf_op jit(solution)/shard_map/pallas_call | solution.py:81
  24.4 4.1 %collective-permute-done.7.refs_0_ = bf16[144,1280]{1,0:T(8,128)(2,1)S(1)} collective-permute-done((bf16[144,1280]{1,0:T(8,128)(2,1)S(1)}, bf16[144,1280]{1,0:T(8,128)(2,1)S(1)}, u32[]{:S(2)}, u32[]{:S(2)}) %collective-permute-start.7) | collective-permute-done | bytes 368672 | tf_op jit(solution)/shard_map/ppermute | solution.py:32
  28.5 2.4 shard_map.120
  30.9 3.1 %collective-permute-start.8 = (bf16[128,1536]{1,0:T(8,128)(2,1)S(1)}, bf16[128,1536]{1,0:T(8,128)(2,1)S(1)}, u32[]{:S(2)}, u32[]{:S(2)}) collective-permute-start(bf16[128,1536]{1,0:T(8,128)(2,1)S(1)} %get-tuple-element.117), channel_id=1, source_target_pairs={{0,24},{8,16},{16,8},{24,0},{1,25},{9,17},{17,9},{25,1},{2,26},{10... | collective-permute-start | bytes 1179656 | tf_op jit(solution)/shard_map/ppermute | solution.py:32
  34.3 3.2 %collective-permute-done.5.refs_1_ = bf16[128,1536]{1,0:T(8,128)(2,1)S(1)} collective-permute-done((bf16[128,1536]{1,0:T(8,128)(2,1)S(1)}, bf16[128,1536]{1,0:T(8,128)(2,1)S(1)}, u32[]{:S(2)}, u32[]{:S(2)}) %collective-permute-start.5) | collective-permute-done | bytes 393248 | tf_op jit(solution)/shard_map/ppermute | solution.py:32
  37.5 7.3 %collective-permute-done.8.refs_3_ = bf16[128,1536]{1,0:T(8,128)(2,1)S(1)} collective-permute-done((bf16[128,1536]{1,0:T(8,128)(2,1)S(1)}, bf16[128,1536]{1,0:T(8,128)(2,1)S(1)}, u32[]{:S(2)}, u32[]{:S(2)}) %collective-permute-start.8) | collective-permute-done | bytes 393248 | tf_op jit(solution)/shard_map/ppermute | solution.py:32
  49.1 4.2 %collective-permute-done.9.refs_1_ = bf16[128,768]{1,0:T(8,128)(2,1)S(1)} collective-permute-done((bf16[128,768]{1,0:T(8,128)(2,1)S(1)}, bf16[128,768]{1,0:T(8,128)(2,1)S(1)}, u32[]{:S(2)}, u32[]{:S(2)}) %collective-permute-start.9) | collective-permute-done | bytes 196640 | tf_op jit(solution)/shard_map/ppermute | solution.py:32
  53.3 3.9 %collective-permute-done.10.refs_2_ = bf16[128,768]{1,0:T(8,128)(2,1)S(1)} collective-permute-done((bf16[128,768]{1,0:T(8,128)(2,1)S(1)}, bf16[128,768]{1,0:T(8,128)(2,1)S(1)}, u32[]{:S(2)}, u32[]{:S(2)}) %collective-permute-start.10) | collective-permute-done | bytes 196640 | tf_op jit(solution)/shard_map/ppermute | solution.py:32
  57.2 3.0 %shard_map.123 = (bf16[384,1280]{1,0:T(8,128)(2,1)S(1)}, f32[128,1]{1,0:T(8,128)S(1)}, f32[128,1]{1,0:T(8,128)S(1)}, f32[128,1]{1,0:T(8,128)S(1)}, bf16[384,768]...) custom-call(bf16[128,768]{1,0:T(8,128)(2,1)S(1)} %get-tuple-element.118.refs_0_, ...), custom_call_target="tpu_custom_call" | custom-call | flops 1509949440 | tf_op jit(solution)/shard_map/pallas_call | solution.py:81
  65.6 2.1 collective-permute-start.13
  69.2 17.8 %collective-permute-done.17.refs_0_.refs_3_.refs_2_ = bf16[128,1280]{1,0:T(8,128)(2,1)S(1)} collective-permute-done((bf16[128,1280]{1,0:T(8,128)(2,1)S(1)}, bf16[128,1280]{1,0:T(8,128)(2,1)S(1)}, u32[]{:S(2)}, u32[]{:S(2)}) %collective-permute-start.17) | collective-permute-done | bytes 327712 | tf_op jit(solution)/shard_map/ppermute | solution.py:37
  87.0 2.2 shard_map.127
  90.6 3.2 %collective-permute-start.19 = (f32[128,1]{1,0:T(8,128)S(1)}, f32[128,1]{1,0:T(8,128)S(1)}, u32[]{:S(2)}, u32[]{:S(2)}) collective-permute-start(f32[128,1]{1,0:T(8,128)S(1)} %get-tuple-element.137), channel_id=1, source_target_pairs={{0,8},{8,0},{16,24},{24,16},{1,9},{9,1},{17,25},{25,17},{2,10},{10... | collective-permute-start | bytes 1544 | tf_op jit(solution)/shard_map/ppermute | solution.py:32
  93.8 2.2 shard_map.124
  97.6 4.4 %shard_map.125 = (bf16[128,1536]{1,0:T(8,128)(2,1)S(1)}, bf16[128,1536]{1,0:T(8,128)(2,1)S(1)}, bf16[128,1536]{1,0:T(8,128)(2,1)S(1)}, bf16[384,1280]{1,0:T(8,128)(2,1)S(1)}, bf16[384,1280]{1,0:T(8,128)(2,1)S(1)}) custom-call(bf16[384,1280]{1,0:T(8,128)(2,1)S(1)} %collective-permute-done.11.refs_0_.refs_5_.refs_4_, ...), custom_call_target="tpu_custom_call" | custom-call | flops 3019898880 | tf_op jit(solution)/shard_map/pallas_call | solution.py:81
  102.0 2.0 collective-permute-start.14
  106.6 4.3 %collective-permute-done.22.refs_4_.refs_6_ = f32[128,1]{1,0:T(8,128)S(1)} collective-permute-done((f32[128,1]{1,0:T(8,128)S(1)}, f32[128,1]{1,0:T(8,128)S(1)}, u32[]{:S(2)}, u32[]{:S(2)}) %collective-permute-start.22) | collective-permute-done | bytes 544 | tf_op jit(solution)/shard_map/ppermute | solution.py:37
  115.7 8.2 %collective-permute-done.24.refs_2_ = bf16[128,768]{1,0:T(8,128)(2,1)S(1)} collective-permute-done((bf16[128,768]{1,0:T(8,128)(2,1)S(1)}, bf16[128,768]{1,0:T(8,128)(2,1)S(1)}, u32[]{:S(2)}, u32[]{:S(2)}) %collective-permute-start.24) | collective-permute-done | bytes 196640 | tf_op jit(solution)/shard_map/ppermute | solution.py:32
  124.4 3.3 %collective-permute-start.29 = (bf16[128,1664]{1,0:T(8,128)(2,1)S(1)}, bf16[128,1664]{1,0:T(8,128)(2,1)S(1)}, u32[]{:S(2)}, u32[]{:S(2)}) collective-permute-start(bf16[128,1664]{1,0:T(8,128)(2,1)S(1)} %shard_map.131.refs_0_), channel_id=1, source_target_pairs={{0,24},{8,16},{16,8},{24,0},{1,25},{9,17},{17,9},{25,1},{2,26},{10... | collective-permute-start | bytes 1277960 | tf_op jit(solution)/shard_map/ppermute | solution.py:32
  128.6 5.3 %collective-permute-done.29.refs_0_ = bf16[128,1664]{1,0:T(8,128)(2,1)S(1)} collective-permute-done((bf16[128,1664]{1,0:T(8,128)(2,1)S(1)}, bf16[128,1664]{1,0:T(8,128)(2,1)S(1)}, u32[]{:S(2)}, u32[]{:S(2)}) %collective-permute-start.29) | collective-permute-done | bytes 426016 | tf_op jit(solution)/shard_map/ppermute | solution.py:32
  133.9 3.4 %shard_map.133 = (bf16[128,1280]{1,0:T(8,128)(2,1)S(1)}, f32[1,1280]{1,0:T(1,128)S(1)}) custom-call(bf16[128,1664]{1,0:T(8,128)(2,1)S(1)} %collective-permute-done.29.refs_0_, f32[128,1]{1,0:T(8,128)S(1)} %get-tuple-element.132.refs_2_.refs_1_, bf16[128,1280]{1,0:T(8,128)(2,1)S(1)} %get-tuple-element.151.refs_2_, ...), custom_call_target="tpu_custom_call" | custom-call | flops 1006632960 | tf_op jit(solution)/shard_map/pallas_call | solution.py:81
  138.0 3.5 %collective-permute-done.27.refs_1_ = bf16[128,1664]{1,0:T(8,128)(2,1)S(1)} collective-permute-done((bf16[128,1664]{1,0:T(8,128)(2,1)S(1)}, bf16[128,1664]{1,0:T(8,128)(2,1)S(1)}, u32[]{:S(2)}, u32[]{:S(2)}) %collective-permute-start.27) | collective-permute-done | bytes 426016 | tf_op jit(solution)/shard_map/ppermute | solution.py:32
  141.4 4.4 %shard_map.132 = (bf16[384,1280]{1,0:T(8,128)(2,1)S(1)}, f32[1,1280]{1,0:T(1,128)S(1)}) custom-call(bf16[128,1664]{1,0:T(8,128)(2,1)S(1)} %shard_map.131.refs_0_, bf16[128,1664]{1,0:T(8,128)(2,1)S(1)} %collective-permute-done.27.refs_1_, bf16[128,1664]{1,0:T(8,128)(2,1)S(1)} %collective-permute-done.28.refs_2_, ...), custom_call_target="tpu_custom_call" | custom-call | flops 3019898880 | tf_op jit(solution)/shard_map/pallas_call | solution.py:81
  145.9 2.3 collective-permute-done.30.refs_0_
  149.2 2.5 %collective-permute-start.32 = (bf16[128,768]{1,0:T(8,128)(2,1)S(1)}, bf16[128,768]{1,0:T(8,128)(2,1)S(1)}, u32[]{:S(2)}, u32[]{:S(2)}) collective-permute-start(bf16[128,768]{1,0:T(8,128)(2,1)S(1)} %get-tuple-element.153.refs_0_), channel_id=1, source_target_pairs={{0,16},{8,24},{16,0},{24,8},{1,17},{9,25},{17,1},{25,9},{2,18},{10... | collective-permute-start | bytes 589832 | tf_op jit(solution)/shard_map/ppermute | solution.py:32
  153.5 3.0 %collective-permute-start.40 = (bf16[128,768]{1,0:T(8,128)(2,1)S(1)}, bf16[128,768]{1,0:T(8,128)(2,1)S(1)}, u32[]{:S(2)}, u32[]{:S(2)}) collective-permute-start(bf16[128,768]{1,0:T(8,128)(2,1)S(1)} %get-tuple-element.162), channel_id=1, source_target_pairs={{0,24},{8,16},{16,8},{24,0},{1,25},{9,17},{17,9},{25,1},{2,26},{10... | collective-permute-start | bytes 589832 | tf_op jit(solution)/shard_map/ppermute | solution.py:32
  156.5 6.6 %collective-permute-done.32.refs_2_ = bf16[128,768]{1,0:T(8,128)(2,1)S(1)} collective-permute-done((bf16[128,768]{1,0:T(8,128)(2,1)S(1)}, bf16[128,768]{1,0:T(8,128)(2,1)S(1)}, u32[]{:S(2)}, u32[]{:S(2)}) %collective-permute-start.32) | collective-permute-done | bytes 196640 | tf_op jit(solution)/shard_map/ppermute | solution.py:32
  163.1 3.6 %shard_map.134 = (bf16[128,1280]{1,0:T(8,128)(2,1)S(1)}, bf16[128,1280]{1,0:T(8,128)(2,1)S(1)}, bf16[128,1280]{1,0:T(8,128)(2,1)S(1)}, f32[128,1]{1,0:T(8,128)},...) custom-call(bf16[128,768]{1,0:T(8,128)(2,1)S(1)} %get-tuple-element.153.refs_, ...), custom_call_target="tpu_custom_call" | custom-call | tf_op jit(solution)/shard_map/pallas_call | solution.py:81
  166.7 2.0 collective-permute-start.34
  168.7 2.6 %shard_map.135 = (bf16[128,1280]{1,0:T(8,128)(2,1)S(1)}, f32[128,1]{1,0:T(8,128)}, bf16[128,768]{1,0:T(8,128)(2,1)S(1)}, bf16[128,768]{1,0:T(8,128)(2,1)S(1)}) custom-call(bf16[128,768]{1,0:T(8,128)(2,1)S(1)} %collective-permute-done.35.refs_0_, f32[128,1]{1,0:T(8,128)S(1)} %get-tuple-element.132.refs_2_.refs_1_, ...), custom_call_target="tpu_custom_call" | custom-call | tf_op jit(solution)/shard_map/pallas_call | solution.py:81
  175.9 9.5 %collective-permute-done.36 = bf16[128,1280]{1,0:T(8,128)(2,1)S(1)} collective-permute-done((bf16[128,1280]{1,0:T(8,128)(2,1)S(1)}, bf16[128,1280]{1,0:T(8,128)(2,1)S(1)}, u32[]{:S(2)}, u32[]{:S(2)}) %collective-permute-start.36) | collective-permute-done | bytes 327712 | tf_op jit(solution)/shard_map/ppermute | solution.py:32
  185.5 2.2 shard_map.136
  189.1 4.3 %collective-permute-done.38.refs_1_ = bf16[128,768]{1,0:T(8,128)(2,1)S(1)} collective-permute-done((bf16[128,768]{1,0:T(8,128)(2,1)S(1)}, bf16[128,768]{1,0:T(8,128)(2,1)S(1)}, u32[]{:S(2)}, u32[]{:S(2)}) %collective-permute-start.38) | collective-permute-done | bytes 196640 | tf_op jit(solution)/shard_map/ppermute | solution.py:32
  194.0 2.0 collective-permute-start.41
  197.6 8.7 %collective-permute-done.43.refs_0_ = bf16[128,1664]{1,0:T(8,128)(2,1)S(1)} collective-permute-done((bf16[128,1664]{1,0:T(8,128)(2,1)S(1)}, bf16[128,1664]{1,0:T(8,128)(2,1)S(1)}, u32[]{:S(2)}, u32[]{:S(2)}) %collective-permute-start.43) | collective-permute-done | bytes 426016 | tf_op jit(solution)/shard_map/ppermute | solution.py:32
  206.3 3.6 %shard_map.139 = (bf16[128,1280]{1,0:T(8,128)(2,1)S(1)}, f32[1,1280]{1,0:T(1,128)S(1)}) custom-call(bf16[128,1664]{1,0:T(8,128)(2,1)S(1)} %collective-permute-done.43.refs_0_, f32[128,1]{1,0:T(8,128)S(1)} %get-tuple-element.129.refs_1_, bf16[128,1280]{1,0:T(8,128)(2,1)S(1)} %get-tuple-element.178.refs_2_, ...), custom_call_target="tpu_custom_call" | custom-call | flops 1006632960 | tf_op jit(solution)/shard_map/pallas_call | solution.py:81
  218.4 4.7 %shard_map.140 = (bf16[128,1280]{1,0:T(8,128)(2,1)S(1)}, bf16[128,1280]{1,0:T(8,128)(2,1)S(1)}, bf16[128,1280]{1,0:T(8,128)(2,1)S(1)}, f32[1,1280]{1,0:T(1,128)S(1)}) custom-call(bf16[128,1664]{1,0:T(8,128)(2,1)S(1)} %shard_map.138.refs_0_, bf16[128,1664]{1,0:T(8,128)(2,1)S(1)} %collective-permute-done.41.refs_1_, ...), custom_call_target="tpu_custom_call" | custom-call | flops 1006632960 | tf_op jit(solution)/shard_map/pallas_call | solution.py:81
  223.1 2.0 collective-permute-start.44
  225.1 2.0 collective-permute-start.45
  227.2 2.9 %collective-permute-start.52 = (f32[1,1280]{1,0:T(1,128)S(1)}, f32[1,1280]{1,0:T(1,128)S(1)}, u32[]{:S(2)}, u32[]{:S(2)}) collective-permute-start(f32[1,1280]{1,0:T(1,128)S(1)} %add_add_fusion), channel_id=1, source_target_pairs={{0,24},{8,16},{16,8},{24,0},{1,25},{9,17},{17,9},{25,1},{2,26},{10... | collective-permute-start | bytes 15368 | tf_op jit(solution)/shard_map/ppermute | solution.py:32
  230.1 2.7 %fusion.5 = bf16[1280,768]{1,0:T(8,128)(2,1)} fusion(bf16[1280,768]{1,0:T(8,128)(2,1)S(1)} %collective-permute-done.47, bf16[1280,768]{1,0:T(8,128)(2,1)S(1)} %convolution_convert_fusion.2, bf16[512,1280]{1,0:T(8,128)(2,1)S(1)} %constant_dynamic-update-slice_fusion.10, bf16[512,768]{1,0:T(8,128)(2,1)S(1)} %get-tuple-element.192), kind=kOutput, calls=%fused_computation.11 | convolution fusion | flops 1011548160 | bytes 7995392 | tf_op jit(solution)/shard_map/dot_general | solution.py:22
  232.8 2.7 %fusion.4 = bf16[1280,768]{1,0:T(8,128)(2,1)} fusion(bf16[1280,768]{1,0:T(8,128)(2,1)S(1)} %collective-permute-done.48, bf16[1280,768]{1,0:T(8,128)(2,1)S(1)} %convolution_convert_fusion.1, bf16[512,1280]{1,0:T(8,128)(2,1)S(1)} %constant_dynamic-update-slice_fusion.10, bf16[512,768]{1,0:T(8,128)(2,1)S(1)} %get-tuple-element.193), kind=kOutput, calls=%fused_computation.10 | convolution fusion | flops 1011548160 | bytes 7995392 | tf_op jit(solution)/shard_map/dot_general | solution.py:22
  235.5 2.7 %fusion.3 = bf16[768,1280]{1,0:T(8,128)(2,1)} fusion(bf16[768,1280]{1,0:T(8,128)(2,1)S(1)} %collective-permute-done.49, bf16[768,1280]{1,0:T(8,128)(2,1)S(1)} %convolution_convert_fusion, bf16[512,1280]{1,0:T(8,128)(2,1)S(1)} %constant_dynamic-update-slice_fusion.8, bf16[128,768]{1,0:T(8,128)(2,1)S(1)} %get-tuple-element.195, ...), kind=kOutput, calls=%fused_computation.9 | convolution fusion | flops 1013121024 | bytes 7995392 | tf_op jit(solution)/shard_map/dot_general | solution.py:22
  238.9 3.4 %collective-permute-done.45 = bf16[128,1280]{1,0:T(8,128)(2,1)S(1)} collective-permute-done((bf16[128,1280]{1,0:T(8,128)(2,1)S(1)}, bf16[128,1280]{1,0:T(8,128)(2,1)S(1)}, u32[]{:S(2)}, u32[]{:S(2)}) %collective-permute-start.45) | collective-permute-done | bytes 327712 | tf_op jit(solution)/shard_map/ppermute | solution.py:32
  (152 shorter events, 51.6 us)
Async XLA Ops:
  0.6 7.5 %collective-permute-start.2 = (bf16[1280,768]{1,0:T(8,128)(2,1)}, bf16[1280,768]{1,0:T(8,128)(2,1)S(1)}, u32[]{:S(2)}, u32[]{:S(2)}) collective-permute-start(bf16[1280,768]{1,0:T(8,128)(2,1)} %bitcast.50), channel_id=1, source_target_pairs={{0,1},{1,0},{2,3},{3,2},{4,5},{5,4},{6,7},{7,6},{8,9},{9,8},{10,11... | collective-permute-start | bytes 5898248 | tf_op jit(solution)/shard_map/ppermute | solution.py:32
  1.2 9.5 %collective-permute-start.4 = (bf16[768,1280]{1,0:T(8,128)(2,1)}, bf16[768,1280]{1,0:T(8,128)(2,1)}, u32[]{:S(2)}, u32[]{:S(2)}) collective-permute-start(bf16[768,1280]{1,0:T(8,128)(2,1)} %bitcast.54), channel_id=1, source_target_pairs={{0,1},{1,0},{2,3},{3,2},{4,5},{5,4},{6,7},{7,6},{8,9},{9,8},{10,11... | collective-permute-start | bytes 5898248 | tf_op jit(solution)/shard_map/ppermute | solution.py:32
  4.0 15.1 %collective-permute-start = (bf16[144,1280]{1,0:T(8,128)(2,1)S(1)}, bf16[144,1280]{1,0:T(8,128)(2,1)S(1)}, u32[]{:S(2)}, u32[]{:S(2)}) collective-permute-start(bf16[144,1280]{1,0:T(8,128)(2,1)S(1)} %get-tuple-element.218), channel_id=1, source_target_pairs={{0,8},{8,0},{16,24},{24,16},{1,9},{9,1},{17,25},{25,17},{2,10},{10... | collective-permute-start | bytes 1105928 | tf_op jit(solution)/shard_map/ppermute | solution.py:32
  6.6 12.5 %collective-permute-start.1 = (bf16[144,1280]{1,0:T(8,128)(2,1)S(1)}, bf16[144,1280]{1,0:T(8,128)(2,1)S(1)}, u32[]{:S(2)}, u32[]{:S(2)}) collective-permute-start(bf16[144,1280]{1,0:T(8,128)(2,1)S(1)} %get-tuple-element.219), channel_id=1, source_target_pairs={{0,16},{8,24},{16,0},{24,8},{1,17},{9,25},{17,1},{25,9},{2,18},{10... | collective-permute-start | bytes 1105928 | tf_op jit(solution)/shard_map/ppermute | solution.py:32
  15.2 13.3 %collective-permute-start.7 = (bf16[144,1280]{1,0:T(8,128)(2,1)S(1)}, bf16[144,1280]{1,0:T(8,128)(2,1)S(1)}, u32[]{:S(2)}, u32[]{:S(2)}) collective-permute-start(bf16[144,1280]{1,0:T(8,128)(2,1)S(1)} %get-tuple-element.116), channel_id=1, source_target_pairs={{0,24},{8,16},{16,8},{24,0},{1,25},{9,17},{17,9},{25,1},{2,26},{10... | collective-permute-start | bytes 1105928 | tf_op jit(solution)/shard_map/ppermute | solution.py:32
  23.7 13.8 %collective-permute-start.5 = (bf16[128,1536]{1,0:T(8,128)(2,1)S(1)}, bf16[128,1536]{1,0:T(8,128)(2,1)S(1)}, u32[]{:S(2)}, u32[]{:S(2)}) collective-permute-start(bf16[128,1536]{1,0:T(8,128)(2,1)S(1)} %get-tuple-element.112), channel_id=1, source_target_pairs={{0,8},{8,0},{16,24},{24,16},{1,9},{9,1},{17,25},{25,17},{2,10},{10... | collective-permute-start | bytes 1179656 | tf_op jit(solution)/shard_map/ppermute | solution.py:32
  24.3 13.2 %collective-permute-start.6 = (bf16[128,1536]{1,0:T(8,128)(2,1)S(1)}, bf16[128,1536]{1,0:T(8,128)(2,1)S(1)}, u32[]{:S(2)}, u32[]{:S(2)}) collective-permute-start(bf16[128,1536]{1,0:T(8,128)(2,1)S(1)} %get-tuple-element.113), channel_id=1, source_target_pairs={{0,16},{8,24},{16,0},{24,8},{1,17},{9,25},{17,1},{25,9},{2,18},{10... | collective-permute-start | bytes 1179656 | tf_op jit(solution)/shard_map/ppermute | solution.py:32
  30.9 13.9 %collective-permute-start.8 = (bf16[128,1536]{1,0:T(8,128)(2,1)S(1)}, bf16[128,1536]{1,0:T(8,128)(2,1)S(1)}, u32[]{:S(2)}, u32[]{:S(2)}) collective-permute-start(bf16[128,1536]{1,0:T(8,128)(2,1)S(1)} %get-tuple-element.117), channel_id=1, source_target_pairs={{0,24},{8,16},{16,8},{24,0},{1,25},{9,17},{17,9},{25,1},{2,26},{10... | collective-permute-start | bytes 1179656 | tf_op jit(solution)/shard_map/ppermute | solution.py:32
  45.4 7.9 %collective-permute-start.9 = (bf16[128,768]{1,0:T(8,128)(2,1)S(1)}, bf16[128,768]{1,0:T(8,128)(2,1)S(1)}, u32[]{:S(2)}, u32[]{:S(2)}) collective-permute-start(bf16[128,768]{1,0:T(8,128)(2,1)S(1)} %get-tuple-element.118.refs_0_), channel_id=1, source_target_pairs={{0,8},{8,0},{16,24},{24,16},{1,9},{9,1},{17,25},{25,17},{2,10},{10... | collective-permute-start | bytes 589832 | tf_op jit(solution)/shard_map/ppermute | solution.py:32
  47.1 10.0 %collective-permute-start.10 = (bf16[128,768]{1,0:T(8,128)(2,1)S(1)}, bf16[128,768]{1,0:T(8,128)(2,1)S(1)}, u32[]{:S(2)}, u32[]{:S(2)}) collective-permute-start(bf16[128,768]{1,0:T(8,128)(2,1)S(1)} %get-tuple-element.118.refs_0_), channel_id=1, source_target_pairs={{0,16},{8,24},{16,0},{24,8},{1,17},{9,25},{17,1},{25,9},{2,18},{10... | collective-permute-start | bytes 589832 | tf_op jit(solution)/shard_map/ppermute | solution.py:32
  48.8 13.1 %collective-permute-start.16 = (bf16[128,768]{1,0:T(8,128)(2,1)S(1)}, bf16[128,768]{1,0:T(8,128)(2,1)S(1)}, u32[]{:S(2)}, u32[]{:S(2)}) collective-permute-start(bf16[128,768]{1,0:T(8,128)(2,1)S(1)} %get-tuple-element.118.refs_0_), channel_id=1, source_target_pairs={{0,24},{8,16},{16,8},{24,0},{1,25},{9,17},{17,9},{25,1},{2,26},{10... | collective-permute-start | bytes 589832 | tf_op jit(solution)/shard_map/ppermute | solution.py:32
  60.2 35.8 %collective-permute-start.11 = (bf16[384,1280]{1,0:T(8,128)(2,1)S(1)}, bf16[384,1280]{1,0:T(8,128)(2,1)S(1)}, u32[]{:S(2)}, u32[]{:S(2)}) collective-permute-start(bf16[384,1280]{1,0:T(8,128)(2,1)S(1)} %get-tuple-element.121), channel_id=1, source_target_pairs={{0,2},{2,4},{4,6},{6,0},{1,3},{3,5},{5,7},{7,1},{8,10},{10,12},{12... | collective-permute-start | bytes 2949128 | tf_op jit(solution)/shard_map/ppermute | solution.py:37
  63.8 23.2 %collective-permute-start.17 = (bf16[128,1280]{1,0:T(8,128)(2,1)S(1)}, bf16[128,1280]{1,0:T(8,128)(2,1)S(1)}, u32[]{:S(2)}, u32[]{:S(2)}) collective-permute-start(bf16[128,1280]{1,0:T(8,128)(2,1)S(1)} %get-tuple-element.131), channel_id=1, source_target_pairs={{0,2},{2,4},{4,6},{6,0},{1,3},{3,5},{5,7},{7,1},{8,10},{10,12},{12... | collective-permute-start | bytes 983048 | tf_op jit(solution)/shard_map/ppermute | solution.py:37
  65.5 25.1 %collective-permute-start.12 = (bf16[128,1280]{1,0:T(8,128)(2,1)S(1)}, bf16[128,1280]{1,0:T(8,128)(2,1)S(1)}, u32[]{:S(2)}, u32[]{:S(2)}) collective-permute-start(bf16[128,1280]{1,0:T(8,128)(2,1)S(1)} %get-tuple-element.211), channel_id=1, source_target_pairs={{0,8},{8,0},{16,24},{24,16},{1,9},{9,1},{17,25},{25,17},{2,10},{10... | collective-permute-start | bytes 983048 | tf_op jit(solution)/shard_map/ppermute | solution.py:32
  65.6 25.0 %collective-permute-start.13 = (bf16[128,1280]{1,0:T(8,128)(2,1)S(1)}, bf16[128,1280]{1,0:T(8,128)(2,1)S(1)}, u32[]{:S(2)}, u32[]{:S(2)}) collective-permute-start(bf16[128,1280]{1,0:T(8,128)(2,1)S(1)} %get-tuple-element.210), channel_id=1, source_target_pairs={{0,16},{8,24},{16,0},{24,8},{1,17},{9,25},{17,1},{25,9},{2,18},{10... | collective-permute-start | bytes 983048 | tf_op jit(solution)/shard_map/ppermute | solution.py:32
  67.7 37.1 %collective-permute-start.25 = (bf16[128,1280]{1,0:T(8,128)(2,1)S(1)}, bf16[128,1280]{1,0:T(8,128)(2,1)S(1)}, u32[]{:S(2)}, u32[]{:S(2)}) collective-permute-start(bf16[128,1280]{1,0:T(8,128)(2,1)S(1)} %constant_dynamic-slice_fusion), channel_id=1, source_target_pairs={{0,24},{8,16},{16,8},{24,0},{1,25},{9,17},{17,9},{25,1},{2,26},{10... | collective-permute-start | bytes 983048 | tf_op jit(solution)/shard_map/ppermute | solution.py:32
  89.3 23.1 %collective-permute-start.18 = (bf16[128,1536]{1,0:T(8,128)(2,1)S(1)}, bf16[128,1536]{1,0:T(8,128)(2,1)S(1)}, u32[]{:S(2)}, u32[]{:S(2)}) collective-permute-start(bf16[128,1536]{1,0:T(8,128)(2,1)S(1)} %get-tuple-element.133), channel_id=1, source_target_pairs={{0,24},{8,16},{16,8},{24,0},{1,25},{9,17},{17,9},{25,1},{2,26},{10... | collective-permute-start | bytes 1179656 | tf_op jit(solution)/shard_map/ppermute | solution.py:32
  90.6 11.4 %collective-permute-start.19 = (f32[128,1]{1,0:T(8,128)S(1)}, f32[128,1]{1,0:T(8,128)S(1)}, u32[]{:S(2)}, u32[]{:S(2)}) collective-permute-start(f32[128,1]{1,0:T(8,128)S(1)} %get-tuple-element.137), channel_id=1, source_target_pairs={{0,8},{8,0},{16,24},{24,16},{1,9},{9,1},{17,25},{25,17},{2,10},{10... | collective-permute-start | bytes 1544 | tf_op jit(solution)/shard_map/ppermute | solution.py:32
  93.8 10.2 %collective-permute-start.20 = (f32[128,1]{1,0:T(8,128)S(1)}, f32[128,1]{1,0:T(8,128)S(1)}, u32[]{:S(2)}, u32[]{:S(2)}) collective-permute-start(f32[128,1]{1,0:T(8,128)S(1)} %get-tuple-element.139), channel_id=1, source_target_pairs={{0,16},{8,24},{16,0},{24,8},{1,17},{9,25},{17,1},{25,9},{2,18},{10... | collective-permute-start | bytes 1544 | tf_op jit(solution)/shard_map/ppermute | solution.py:32
  96.0 8.1 %collective-permute-start.21 = (f32[128,1]{1,0:T(8,128)S(1)}, f32[128,1]{1,0:T(8,128)S(1)}, u32[]{:S(2)}, u32[]{:S(2)}) collective-permute-start(f32[128,1]{1,0:T(8,128)S(1)} %get-tuple-element.141), channel_id=1, source_target_pairs={{0,24},{8,16},{16,8},{24,0},{1,25},{9,17},{17,9},{25,1},{2,26},{10... | collective-permute-start | bytes 1544 | tf_op jit(solution)/shard_map/ppermute | solution.py:32
  102.0 11.8 %collective-permute-start.14 = (bf16[128,1536]{1,0:T(8,128)(2,1)S(1)}, bf16[128,1536]{1,0:T(8,128)(2,1)S(1)}, u32[]{:S(2)}, u32[]{:S(2)}) collective-permute-start(bf16[128,1536]{1,0:T(8,128)(2,1)S(1)} %get-tuple-element.127), channel_id=1, source_target_pairs={{0,8},{8,0},{16,24},{24,16},{1,9},{9,1},{17,25},{25,17},{2,10},{10... | collective-permute-start | bytes 1179656 | tf_op jit(solution)/shard_map/ppermute | solution.py:32
  104.0 9.9 %collective-permute-start.15 = (bf16[128,1536]{1,0:T(8,128)(2,1)S(1)}, bf16[128,1536]{1,0:T(8,128)(2,1)S(1)}, u32[]{:S(2)}, u32[]{:S(2)}) collective-permute-start(bf16[128,1536]{1,0:T(8,128)(2,1)S(1)} %get-tuple-element.128), channel_id=1, source_target_pairs={{0,16},{8,24},{16,0},{24,8},{1,17},{9,25},{17,1},{25,9},{2,18},{10... | collective-permute-start | bytes 1179656 | tf_op jit(solution)/shard_map/ppermute | solution.py:32
  104.1 11.6 %collective-permute-start.23 = (bf16[128,768]{1,0:T(8,128)(2,1)S(1)}, bf16[128,768]{1,0:T(8,128)(2,1)S(1)}, u32[]{:S(2)}, u32[]{:S(2)}) collective-permute-start(bf16[128,768]{1,0:T(8,128)(2,1)S(1)} %get-tuple-element.143), channel_id=1, source_target_pairs={{0,8},{8,0},{16,24},{24,16},{1,9},{9,1},{17,25},{25,17},{2,10},{10... | collective-permute-start | bytes 589832 | tf_op jit(solution)/shard_map/ppermute | solution.py:32
  110.9 13.0 %collective-permute-start.24 = (bf16[128,768]{1,0:T(8,128)(2,1)S(1)}, bf16[128,768]{1,0:T(8,128)(2,1)S(1)}, u32[]{:S(2)}, u32[]{:S(2)}) collective-permute-start(bf16[128,768]{1,0:T(8,128)(2,1)S(1)} %get-tuple-element.144), channel_id=1, source_target_pairs={{0,16},{8,24},{16,0},{24,8},{1,17},{9,25},{17,1},{25,9},{2,18},{10... | collective-permute-start | bytes 589832 | tf_op jit(solution)/shard_map/ppermute | solution.py:32
  112.4 11.5 %collective-permute-start.26 = (bf16[128,768]{1,0:T(8,128)(2,1)S(1)}, bf16[128,768]{1,0:T(8,128)(2,1)S(1)}, u32[]{:S(2)}, u32[]{:S(2)}) collective-permute-start(bf16[128,768]{1,0:T(8,128)(2,1)S(1)} %get-tuple-element.146), channel_id=1, source_target_pairs={{0,24},{8,16},{16,8},{24,0},{1,25},{9,17},{17,9},{25,1},{2,26},{10... | collective-permute-start | bytes 589832 | tf_op jit(solution)/shard_map/ppermute | solution.py:32
  124.4 9.5 %collective-permute-start.29 = (bf16[128,1664]{1,0:T(8,128)(2,1)S(1)}, bf16[128,1664]{1,0:T(8,128)(2,1)S(1)}, u32[]{:S(2)}, u32[]{:S(2)}) collective-permute-start(bf16[128,1664]{1,0:T(8,128)(2,1)S(1)} %shard_map.131.refs_0_), channel_id=1, source_target_pairs={{0,24},{8,16},{16,8},{24,0},{1,25},{9,17},{17,9},{25,1},{2,26},{10... | collective-permute-start | bytes 1277960 | tf_op jit(solution)/shard_map/ppermute | solution.py:32
  127.7 13.7 %collective-permute-start.27 = (bf16[128,1664]{1,0:T(8,128)(2,1)S(1)}, bf16[128,1664]{1,0:T(8,128)(2,1)S(1)}, u32[]{:S(2)}, u32[]{:S(2)}) collective-permute-start(bf16[128,1664]{1,0:T(8,128)(2,1)S(1)} %shard_map.131.refs_0_), channel_id=1, source_target_pairs={{0,8},{8,0},{16,24},{24,16},{1,9},{9,1},{17,25},{25,17},{2,10},{10... | collective-permute-start | bytes 1277960 | tf_op jit(solution)/shard_map/ppermute | solution.py:32
  127.8 13.7 %collective-permute-start.28 = (bf16[128,1664]{1,0:T(8,128)(2,1)S(1)}, bf16[128,1664]{1,0:T(8,128)(2,1)S(1)}, u32[]{:S(2)}, u32[]{:S(2)}) collective-permute-start(bf16[128,1664]{1,0:T(8,128)(2,1)S(1)} %shard_map.131.refs_0_), channel_id=1, source_target_pairs={{0,16},{8,24},{16,0},{24,8},{1,17},{9,25},{17,1},{25,9},{2,18},{10... | collective-permute-start | bytes 1277960 | tf_op jit(solution)/shard_map/ppermute | solution.py:32
  137.3 10.9 %collective-permute-start.30 = (bf16[128,1280]{1,0:T(8,128)(2,1)S(1)}, bf16[128,1280]{1,0:T(8,128)(2,1)S(1)}, u32[]{:S(2)}, u32[]{:S(2)}) collective-permute-start(bf16[128,1280]{1,0:T(8,128)(2,1)S(1)} %get-tuple-element.152), channel_id=1, source_target_pairs={{0,6},{2,0},{4,2},{6,4},{1,7},{3,1},{5,3},{7,5},{8,14},{10,8},{12,... | collective-permute-start | bytes 983048 | tf_op jit(solution)/shard_map/ppermute | solution.py:37
  145.9 39.6 %collective-permute-start.37 = (bf16[384,1280]{1,0:T(8,128)(2,1)S(1)}, bf16[384,1280]{1,0:T(8,128)(2,1)S(1)}, u32[]{:S(2)}, u32[]{:S(2)}) collective-permute-start(bf16[384,1280]{1,0:T(8,128)(2,1)S(1)} %get-tuple-element.150), channel_id=1, source_target_pairs={{0,6},{2,0},{4,2},{6,4},{1,7},{3,1},{5,3},{7,5},{8,14},{10,8},{12,... | collective-permute-start | bytes 2949128 | tf_op jit(solution)/shard_map/ppermute | solution.py:37
  148.2 8.3 %collective-permute-start.31 = (bf16[128,768]{1,0:T(8,128)(2,1)S(1)}, bf16[128,768]{1,0:T(8,128)(2,1)S(1)}, u32[]{:S(2)}, u32[]{:S(2)}) collective-permute-start(bf16[128,768]{1,0:T(8,128)(2,1)S(1)} %get-tuple-element.153.refs_0_), channel_id=1, source_target_pairs={{0,8},{8,0},{16,24},{24,16},{1,9},{9,1},{17,25},{25,17},{2,10},{10... | collective-permute-start | bytes 589832 | tf_op jit(solution)/shard_map/ppermute | solution.py:32
  149.2 13.8 %collective-permute-start.32 = (bf16[128,768]{1,0:T(8,128)(2,1)S(1)}, bf16[128,768]{1,0:T(8,128)(2,1)S(1)}, u32[]{:S(2)}, u32[]{:S(2)}) collective-permute-start(bf16[128,768]{1,0:T(8,128)(2,1)S(1)} %get-tuple-element.153.refs_0_), channel_id=1, source_target_pairs={{0,16},{8,24},{16,0},{24,8},{1,17},{9,25},{17,1},{25,9},{2,18},{10... | collective-permute-start | bytes 589832 | tf_op jit(solution)/shard_map/ppermute | solution.py:32
  151.7 17.0 %collective-permute-start.35 = (bf16[128,768]{1,0:T(8,128)(2,1)S(1)}, bf16[128,768]{1,0:T(8,128)(2,1)S(1)}, u32[]{:S(2)}, u32[]{:S(2)}) collective-permute-start(bf16[128,768]{1,0:T(8,128)(2,1)S(1)} %get-tuple-element.153.refs_0_), channel_id=1, source_target_pairs={{0,24},{8,16},{16,8},{24,0},{1,25},{9,17},{17,9},{25,1},{2,26},{10... | collective-permute-start | bytes 589832 | tf_op jit(solution)/shard_map/ppermute | solution.py:32
  153.5 35.5 %collective-permute-start.40 = (bf16[128,768]{1,0:T(8,128)(2,1)S(1)}, bf16[128,768]{1,0:T(8,128)(2,1)S(1)}, u32[]{:S(2)}, u32[]{:S(2)}) collective-permute-start(bf16[128,768]{1,0:T(8,128)(2,1)S(1)} %get-tuple-element.162), channel_id=1, source_target_pairs={{0,24},{8,16},{16,8},{24,0},{1,25},{9,17},{17,9},{25,1},{2,26},{10... | collective-permute-start | bytes 589832 | tf_op jit(solution)/shard_map/ppermute | solution.py:32
  166.7 9.1 %collective-permute-start.33 = (bf16[128,1280]{1,0:T(8,128)(2,1)S(1)}, bf16[128,1280]{1,0:T(8,128)(2,1)S(1)}, u32[]{:S(2)}, u32[]{:S(2)}) collective-permute-start(bf16[128,1280]{1,0:T(8,128)(2,1)S(1)} %get-tuple-element.155), channel_id=1, source_target_pairs={{0,8},{8,0},{16,24},{24,16},{1,9},{9,1},{17,25},{25,17},{2,10},{10... | collective-permute-start | bytes 983048 | tf_op jit(solution)/shard_map/ppermute | solution.py:32
  166.7 9.1 %collective-permute-start.34 = (bf16[128,1280]{1,0:T(8,128)(2,1)S(1)}, bf16[128,1280]{1,0:T(8,128)(2,1)S(1)}, u32[]{:S(2)}, u32[]{:S(2)}) collective-permute-start(bf16[128,1280]{1,0:T(8,128)(2,1)S(1)} %get-tuple-element.156), channel_id=1, source_target_pairs={{0,16},{8,24},{16,0},{24,8},{1,17},{9,25},{17,1},{25,9},{2,18},{10... | collective-permute-start | bytes 983048 | tf_op jit(solution)/shard_map/ppermute | solution.py:32
  171.3 14.1 %collective-permute-start.36 = (bf16[128,1280]{1,0:T(8,128)(2,1)S(1)}, bf16[128,1280]{1,0:T(8,128)(2,1)S(1)}, u32[]{:S(2)}, u32[]{:S(2)}) collective-permute-start(bf16[128,1280]{1,0:T(8,128)(2,1)S(1)} %get-tuple-element.157), channel_id=1, source_target_pairs={{0,24},{8,16},{16,8},{24,0},{1,25},{9,17},{17,9},{25,1},{2,26},{10... | collective-permute-start | bytes 983048 | tf_op jit(solution)/shard_map/ppermute | solution.py:32
  194.0 16.0 %collective-permute-start.41 = (bf16[128,1664]{1,0:T(8,128)(2,1)S(1)}, bf16[128,1664]{1,0:T(8,128)(2,1)S(1)}, u32[]{:S(2)}, u32[]{:S(2)}) collective-permute-start(bf16[128,1664]{1,0:T(8,128)(2,1)S(1)} %shard_map.138.refs_0_), channel_id=1, source_target_pairs={{0,8},{8,0},{16,24},{24,16},{1,9},{9,1},{17,25},{25,17},{2,10},{10... | collective-permute-start | bytes 1277960 | tf_op jit(solution)/shard_map/ppermute | solution.py:32
  196.0 10.3 %collective-permute-start.43 = (bf16[128,1664]{1,0:T(8,128)(2,1)S(1)}, bf16[128,1664]{1,0:T(8,128)(2,1)S(1)}, u32[]{:S(2)}, u32[]{:S(2)}) collective-permute-start(bf16[128,1664]{1,0:T(8,128)(2,1)S(1)} %shard_map.138.refs_0_), channel_id=1, source_target_pairs={{0,24},{8,16},{16,8},{24,0},{1,25},{9,17},{17,9},{25,1},{2,26},{10... | collective-permute-start | bytes 1277960 | tf_op jit(solution)/shard_map/ppermute | solution.py:32
  196.0 14.0 %collective-permute-start.42 = (bf16[128,1664]{1,0:T(8,128)(2,1)S(1)}, bf16[128,1664]{1,0:T(8,128)(2,1)S(1)}, u32[]{:S(2)}, u32[]{:S(2)}) collective-permute-start(bf16[128,1664]{1,0:T(8,128)(2,1)S(1)} %shard_map.138.refs_0_), channel_id=1, source_target_pairs={{0,16},{8,24},{16,0},{24,8},{1,17},{9,25},{17,1},{25,9},{2,18},{10... | collective-permute-start | bytes 1277960 | tf_op jit(solution)/shard_map/ppermute | solution.py:32
  211.4 15.7 %collective-permute-start.47 = (bf16[1280,768]{1,0:T(8,128)(2,1)S(1)}, bf16[1280,768]{1,0:T(8,128)(2,1)S(1)}, u32[]{:S(2)}, u32[]{:S(2)}) collective-permute-start(bf16[1280,768]{1,0:T(8,128)(2,1)S(1)} %fusion.6), channel_id=1, source_target_pairs={{0,1},{1,0},{2,3},{3,2},{4,5},{5,4},{6,7},{7,6},{8,9},{9,8},{10,11... | collective-permute-start | bytes 5898248 | tf_op jit(solution)/shard_map/ppermute | solution.py:32
  212.7 14.5 %collective-permute-start.48 = (bf16[1280,768]{1,0:T(8,128)(2,1)S(1)}, bf16[1280,768]{1,0:T(8,128)(2,1)S(1)}, u32[]{:S(2)}, u32[]{:S(2)}) collective-permute-start(bf16[1280,768]{1,0:T(8,128)(2,1)S(1)} %fusion.7), channel_id=1, source_target_pairs={{0,1},{1,0},{2,3},{3,2},{4,5},{5,4},{6,7},{7,6},{8,9},{9,8},{10,11... | collective-permute-start | bytes 5898248 | tf_op jit(solution)/shard_map/ppermute | solution.py:32
  214.6 12.6 %collective-permute-start.49 = (bf16[768,1280]{1,0:T(8,128)(2,1)S(1)}, bf16[768,1280]{1,0:T(8,128)(2,1)S(1)}, u32[]{:S(2)}, u32[]{:S(2)}) collective-permute-start(bf16[768,1280]{1,0:T(8,128)(2,1)S(1)} %fusion.8), channel_id=1, source_target_pairs={{0,1},{1,0},{2,3},{3,2},{4,5},{5,4},{6,7},{7,6},{8,9},{9,8},{10,11... | collective-permute-start | bytes 5898248 | tf_op jit(solution)/shard_map/ppermute | solution.py:32
  223.1 15.2 %collective-permute-start.44 = (bf16[128,1280]{1,0:T(8,128)(2,1)S(1)}, bf16[128,1280]{1,0:T(8,128)(2,1)S(1)}, u32[]{:S(2)}, u32[]{:S(2)}) collective-permute-start(bf16[128,1280]{1,0:T(8,128)(2,1)S(1)} %get-tuple-element.188), channel_id=1, source_target_pairs={{0,8},{8,0},{16,24},{24,16},{1,9},{9,1},{17,25},{25,17},{2,10},{10... | collective-permute-start | bytes 983048 | tf_op jit(solution)/shard_map/ppermute | solution.py:32
  225.1 17.3 %collective-permute-start.45 = (bf16[128,1280]{1,0:T(8,128)(2,1)S(1)}, bf16[128,1280]{1,0:T(8,128)(2,1)S(1)}, u32[]{:S(2)}, u32[]{:S(2)}) collective-permute-start(bf16[128,1280]{1,0:T(8,128)(2,1)S(1)} %get-tuple-element.189), channel_id=1, source_target_pairs={{0,16},{8,24},{16,0},{24,8},{1,17},{9,25},{17,1},{25,9},{2,18},{10... | collective-permute-start | bytes 983048 | tf_op jit(solution)/shard_map/ppermute | solution.py:32
  227.1 15.3 %collective-permute-start.46 = (bf16[128,1280]{1,0:T(8,128)(2,1)S(1)}, bf16[128,1280]{1,0:T(8,128)(2,1)S(1)}, u32[]{:S(2)}, u32[]{:S(2)}) collective-permute-start(bf16[128,1280]{1,0:T(8,128)(2,1)S(1)} %get-tuple-element.179), channel_id=1, source_target_pairs={{0,24},{8,16},{16,8},{24,0},{1,25},{9,17},{17,9},{25,1},{2,26},{10... | collective-permute-start | bytes 983048 | tf_op jit(solution)/shard_map/ppermute | solution.py:32
  227.2 15.4 %collective-permute-start.52 = (f32[1,1280]{1,0:T(1,128)S(1)}, f32[1,1280]{1,0:T(1,128)S(1)}, u32[]{:S(2)}, u32[]{:S(2)}) collective-permute-start(f32[1,1280]{1,0:T(1,128)S(1)} %add_add_fusion), channel_id=1, source_target_pairs={{0,24},{8,16},{16,8},{24,0},{1,25},{9,17},{17,9},{25,1},{2,26},{10... | collective-permute-start | bytes 15368 | tf_op jit(solution)/shard_map/ppermute | solution.py:32
  230.1 12.5 %collective-permute-start.51 = (f32[1,1280]{1,0:T(1,128)S(1)}, f32[1,1280]{1,0:T(1,128)S(1)}, u32[]{:S(2)}, u32[]{:S(2)}) collective-permute-start(f32[1,1280]{1,0:T(1,128)S(1)} %add_add_fusion), channel_id=1, source_target_pairs={{0,16},{8,24},{16,0},{24,8},{1,17},{9,25},{17,1},{25,9},{2,18},{10... | collective-permute-start | bytes 15368 | tf_op jit(solution)/shard_map/ppermute | solution.py:32
  (14 other events, 70.9 us)

commit v4 on v3

--- a/solution.py
+++ b/solution.py
@@ -479,16 +479,16 @@
     kept = [(hidden, gained, inverse, gate, up)]
     first_activated = gather_rows(activated, dp_count)
     next_hidden, squares, first_rows = [], [], []
-    for group, mask, rows_in in zip(groups, masks[0], hidden):
-        (out,), square, split = add_down(
-            first_activated[group], mask, down_pair, rows_in, False
-        )
-        next_hidden.append(out)
-        squares += square
-        first_rows.append(split)
+    for index in reversed(range(len(groups))):
+        near = first_activated[groups[index]]
+        if next_hidden:
+            near = [after(near[0], next_hidden[0]), *near[1:]]
+        (out,), square, split = add_down(near, masks[0][index], down_pair, hidden[index], False)
+        next_hidden.insert(0, out)
+        squares = [*square, *squares]
+        first_rows.insert(0, split)
     hidden = moved(next_hidden, 1)
-    waited = [first_activated[1:-1]] * (dp_count - 1) + [next_hidden[:1]]
-    grad_blocks = sent([cotangent_quarter(step, *waited[step]) for step in range(dp_count)])
+    grad_blocks = sent([cotangent_quarter(step, next_hidden[0]) for step in range(dp_count)])
     squares = [after(square, *grad_blocks[1:-1]) for square in squares]
     inverse = shifted(row_scale(sent(squares), features, True), "pipe", 1)
     act_parts, grad = [], []
@@ -534,19 +534,17 @@
             outs = list(made) + outs
             gain_sum = gain_sum + gain_term
             if k == 0 and index > 0:
-                both_grad[1] = after(both_grad[1], *early[False], *early[True])
+                ready = [after(right, made[0]) for right in rights[:2]] + rights[2:]
                 given = [
-                    (weight_grad(left, after(right, made[0]), False) + soon.astype(f32)).astype(
-                        bf16
-                    )
-                    for left, right, soon in zip(lefts, rights, early[False])
+                    (weight_grad(left, right, False) + soon.astype(f32)).astype(bf16)
+                    for left, right, soon in zip(lefts, ready, early[False])
                 ]
                 both_grad[1] = after(both_grad[1], *given)
                 received = [swap(value, "expert", 1) for value in given]
         if k > 0:
             last_grad = jnp.concatenate(grad)
             grad = moved(outs, -1)
-            last_activated = gather_rows(after(activated, outs[0], grad[1]), dp_count)
+            last_activated = gather_rows(after(activated, both_grad[-1]), dp_count)
             rights = [after(right, *last_activated[1:]) for right in rights]
             early = {
                 wanted: [weight_grad(gained, right, wanted).astype(bf16) for right in rights]
@@ -560,7 +558,7 @@
                 out_parts += made
                 last_rows.append(split)
             out_rows = from_quarters(out_parts)
-            grad[0] = after(grad[0], out_rows)
+            grad[0] = after(grad[0], *out_parts, *early[False], *early[True])
             act_parts, joined = [], []
             for rows_in, choice in zip(grad, masks[0]):
                 made, copied = act_grad_parts([rows_in], rows, choice, down_pair)
@@ -571,11 +569,12 @@
             for wanted in (False, True):
                 early[wanted].append(weight_grad(last_rows, last_grad, wanted).astype(bf16))
             act_parts = sent(act_parts)
+            act_parts[1] = after(act_parts[1], early[False][2], early[True][2])
 
     returned = sent(outs)
     rights = [after(right, *outs) for right in rights]
+    gain_sum = gain_sum + swap(gain_sum, "expert", 1)
     gain_rows = jnp.concatenate(gather_rows(after(gain_sum, *received), dp_count))
-    gain_rows = gain_rows + swap(gain_rows, "expert", 1)
     gain_all = jnp.zeros((features,), f32)
     for step in range(dp_count):
         gain_all = lax.dynamic_update_slice_in_dim(

time: 245 us -> 232 us (0.947)
  waiting for transfers between devices: 102 us -> 84.3 us
  starting transfers between devices: 61.7 us -> 64.7 us
  matrix products: 19.3 us -> 22.1 us
    ppermute x5, waiting for transfers between devices: 24.5 us -> 6.59 us  [shifted(): lax.ppermute(block, axis, [(i, (i + distance) % size) for i in range(size)])]
    dot_general x12, matrix products: 19.3 us -> 22.1 us  [dot(): lax.dot_general(former, latter, ((contract[:1], contract[1:]), ((), ())),...]
  transfers between devices with their start and end apart: 54 -> 54, of which waited for: 22 -> 22; matrix products, arithmetic and copies ran while one was open for 9% -> 11% of each run, Pallas kernels for 22% -> 22%
where the time goes in v4:
time: 232 us
  waiting for transfers between devices  84.3 us (36%)
  starting transfers between devices  64.7 us (28%)
  Pallas kernels  55.4 us (24%)
  matrix products  22.1 us (10%)
  local copies, waits for them, and re-layouts  3.35 us (1%)
    ppermute x49, waiting for transfers between devices, swap(): return lax.ppermute(block, axis, partner_route(lax.axis_size(axis), step))  77.7 us
    ppermute x49, starting transfers between devices, swap(): return lax.ppermute(block, axis, partner_route(lax.axis_size(axis), step))  59.2 us
    pallas_call x22, Pallas kernels, kernel_call(): pl.pallas_call(call, in_specs=[in_vmem] * (count + kept), out_specs=[in_v...  50.9 us
    dot_general x12, matrix products, dot(): lax.dot_general(former, latter, ((contract[:1], contract[1:]), ((), ())),...  22.1 us
    ppermute x5, waiting for transfers between devices, shifted(): lax.ppermute(block, axis, [(i, (i + distance) % size) for i in range(size)])  6.59 us
    ppermute x5, starting transfers between devices, shifted(): lax.ppermute(block, axis, [(i, (i + distance) % size) for i in range(size)])  5.42 us
  transfers between devices with their start and end apart: 54, of which 22 were waited for; matrix products, arithmetic and copies ran while one was open for 11% of the time, Pallas kernels for 22%

profile of v4, /device:TPU:0, one launch (start us, length us, event | category | flops | bytes accessed | tf_op | source)
XLA Modules:
  0.0 232.0 jit_solution(6739459729282105943)
XLA Ops:
  4.0 2.6 %collective-permute-start = (bf16[144,1280]{1,0:T(8,128)(2,1)S(1)}, bf16[144,1280]{1,0:T(8,128)(2,1)S(1)}, u32[]{:S(2)}, u32[]{:S(2)}) collective-permute-start(bf16[144,1280]{1,0:T(8,128)(2,1)S(1)} %get-tuple-element.217), channel_id=1, source_target_pairs={{0,8},{8,0},{16,24},{24,16},{1,9},{9,1},{17,25},{25,17},{2,10},{10... | collective-permute-start | bytes 1105928 | tf_op jit(solution)/shard_map/ppermute | solution.py:32
  8.1 2.6 %collective-permute-done.4.refs_5_ = bf16[768,1280]{1,0:T(8,128)(2,1)} collective-permute-done((bf16[768,1280]{1,0:T(8,128)(2,1)}, bf16[768,1280]{1,0:T(8,128)(2,1)}, u32[]{:S(2)}, u32[]{:S(2)}) %collective-permute-start.4) | collective-permute-done | bytes 1966112 | tf_op jit(solution)/shard_map/ppermute | solution.py:32
  10.7 4.5 %shard_map.118 = (bf16[1280,768]{1,0:T(8,128)(2,1)S(1)}, bf16[1280,768]{1,0:T(8,128)(2,1)S(1)}, bf16[1280,768]{1,0:T(8,128)(2,1)S(1)}, bf16[1280,768]{1,0:T(8,12...) custom-call(bf16[1280,768]{1,0:T(8,128)(2,1)} %bitcast.58, bf16[1280,768]{1,0:T(8,128)(2,1)} %copy-done.3, ...), custom_call_target="tpu_custom_call" | custom-call | bytes 23592960 | tf_op jit(solution)/shard_map/pallas_call | solution.py:109
  15.2 3.9 %collective-permute-start.7 = (bf16[144,1280]{1,0:T(8,128)(2,1)S(1)}, bf16[144,1280]{1,0:T(8,128)(2,1)S(1)}, u32[]{:S(2)}, u32[]{:S(2)}) collective-permute-start(bf16[144,1280]{1,0:T(8,128)(2,1)S(1)} %get-tuple-element.115), channel_id=1, source_target_pairs={{0,24},{8,16},{16,8},{24,0},{1,25},{9,17},{17,9},{25,1},{2,26},{10... | collective-permute-start | bytes 1105928 | tf_op jit(solution)/shard_map/ppermute | solution.py:32
  19.1 4.6 %shard_map.119 = (bf16[128,1536]{1,0:T(8,128)(2,1)S(1)}, bf16[128,1536]{1,0:T(8,128)(2,1)S(1)}, bf16[128,1536]{1,0:T(8,128)(2,1)S(1)}, bf16[384,1280]{1,0:T(8,12...) custom-call(bf16[144,1280]{1,0:T(8,128)(2,1)S(1)} %get-tuple-element, ...), custom_call_target="tpu_custom_call" | custom-call | flops 3019898880 | tf_op jit(solution)/shard_map/pallas_call | solution.py:81
  24.4 4.1 %collective-permute-done.7.refs_0_ = bf16[144,1280]{1,0:T(8,128)(2,1)S(1)} collective-permute-done((bf16[144,1280]{1,0:T(8,128)(2,1)S(1)}, bf16[144,1280]{1,0:T(8,128)(2,1)S(1)}, u32[]{:S(2)}, u32[]{:S(2)}) %collective-permute-start.7) | collective-permute-done | bytes 368672 | tf_op jit(solution)/shard_map/ppermute | solution.py:32
  28.5 2.4 %shard_map.120 = (bf16[128,1536]{1,0:T(8,128)(2,1)S(1)}, bf16[128,1280]{1,0:T(8,128)(2,1)S(1)}, bf16[128,1280]{1,0:T(8,128)(2,1)S(1)}, f32[128,1]{1,0:T(8,128)S(...) custom-call(bf16[144,1280]{1,0:T(8,128)(2,1)S(1)} %collective-permute-done.7.refs_0_, ...), custom_call_target="tpu_custom_call" | custom-call | flops 1006632960 | tf_op jit(solution)/shard_map/pallas_call | solution.py:81
  30.9 3.1 %collective-permute-start.8 = (bf16[128,1536]{1,0:T(8,128)(2,1)S(1)}, bf16[128,1536]{1,0:T(8,128)(2,1)S(1)}, u32[]{:S(2)}, u32[]{:S(2)}) collective-permute-start(bf16[128,1536]{1,0:T(8,128)(2,1)S(1)} %get-tuple-element.116), channel_id=1, source_target_pairs={{0,24},{8,16},{16,8},{24,0},{1,25},{9,17},{17,9},{25,1},{2,26},{10... | collective-permute-start | bytes 1179656 | tf_op jit(solution)/shard_map/ppermute | solution.py:32
  34.4 3.1 %collective-permute-done.5.refs_1_ = bf16[128,1536]{1,0:T(8,128)(2,1)S(1)} collective-permute-done((bf16[128,1536]{1,0:T(8,128)(2,1)S(1)}, bf16[128,1536]{1,0:T(8,128)(2,1)S(1)}, u32[]{:S(2)}, u32[]{:S(2)}) %collective-permute-start.5) | collective-permute-done | bytes 393248 | tf_op jit(solution)/shard_map/ppermute | solution.py:32
  37.5 7.3 %collective-permute-done.8.refs_3_ = bf16[128,1536]{1,0:T(8,128)(2,1)S(1)} collective-permute-done((bf16[128,1536]{1,0:T(8,128)(2,1)S(1)}, bf16[128,1536]{1,0:T(8,128)(2,1)S(1)}, u32[]{:S(2)}, u32[]{:S(2)}) %collective-permute-start.8) | collective-permute-done | bytes 393248 | tf_op jit(solution)/shard_map/ppermute | solution.py:32
  45.4 2.7 %collective-permute-start.9 = (bf16[128,768]{1,0:T(8,128)(2,1)S(1)}, bf16[128,768]{1,0:T(8,128)(2,1)S(1)}, u32[]{:S(2)}, u32[]{:S(2)}) collective-permute-start(bf16[128,768]{1,0:T(8,128)(2,1)S(1)} %get-tuple-element.121.refs_0_), channel_id=1, source_target_pairs={{0,24},{8,16},{16,8},{24,0},{1,25},{9,17},{17,9},{25,1},{2,26},{10... | collective-permute-start | bytes 589832 | tf_op jit(solution)/shard_map/ppermute | solution.py:32
  49.0 5.2 %collective-permute-done.9.refs_0_ = bf16[128,768]{1,0:T(8,128)(2,1)S(1)} collective-permute-done((bf16[128,768]{1,0:T(8,128)(2,1)S(1)}, bf16[128,768]{1,0:T(8,128)(2,1)S(1)}, u32[]{:S(2)}, u32[]{:S(2)}) %collective-permute-start.9) | collective-permute-done | bytes 196640 | tf_op jit(solution)/shard_map/ppermute | solution.py:32
  54.2 1.9 shard_map.123
  57.0 3.0 %shard_map.124 = (bf16[384,1280]{1,0:T(8,128)(2,1)S(1)}, f32[128,1]{1,0:T(8,128)S(1)}, f32[128,1]{1,0:T(8,128)S(1)}, f32[128,1]{1,0:T(8,128)S(1)}, bf16[384,768]...) custom-call(bf16[128,768]{1,0:T(8,128)(2,1)S(1)} %get-tuple-element.121.refs_0_, ...), custom_call_target="tpu_custom_call" | custom-call | flops 1509949440 | tf_op jit(solution)/shard_map/pallas_call | solution.py:81
  61.8 2.4 %collective-permute-start.25 = (bf16[128,1280]{1,0:T(8,128)(2,1)S(1)}, bf16[128,1280]{1,0:T(8,128)(2,1)S(1)}, u32[]{:S(2)}, u32[]{:S(2)}) collective-permute-start(bf16[128,1280]{1,0:T(8,128)(2,1)S(1)} %get-tuple-element.208), channel_id=1, source_target_pairs={{0,24},{8,16},{16,8},{24,0},{1,25},{9,17},{17,9},{25,1},{2,26},{10... | collective-permute-start | bytes 983048 | tf_op jit(solution)/shard_map/ppermute | solution.py:32
  67.0 6.4 %collective-permute-done.25.refs_0_ = bf16[128,1280]{1,0:T(8,128)(2,1)S(1)} collective-permute-done((bf16[128,1280]{1,0:T(8,128)(2,1)S(1)}, bf16[128,1280]{1,0:T(8,128)(2,1)S(1)}, u32[]{:S(2)}, u32[]{:S(2)}) %collective-permute-start.25) | collective-permute-done | bytes 327712 | tf_op jit(solution)/shard_map/ppermute | solution.py:32
  75.1 2.3 %collective-permute-start.26 = (bf16[128,768]{1,0:T(8,128)(2,1)S(1)}, bf16[128,768]{1,0:T(8,128)(2,1)S(1)}, u32[]{:S(2)}, u32[]{:S(2)}) collective-permute-start(bf16[128,768]{1,0:T(8,128)(2,1)S(1)} %get-tuple-element.145), channel_id=1, source_target_pairs={{0,24},{8,16},{16,8},{24,0},{1,25},{9,17},{17,9},{25,1},{2,26},{10... | collective-permute-start | bytes 589832 | tf_op jit(solution)/shard_map/ppermute | solution.py:32
  77.5 2.9 %collective-permute-done.13.refs_1_ = bf16[128,1280]{1,0:T(8,128)(2,1)S(1)} collective-permute-done((bf16[128,1280]{1,0:T(8,128)(2,1)S(1)}, bf16[128,1280]{1,0:T(8,128)(2,1)S(1)}, u32[]{:S(2)}, u32[]{:S(2)}) %collective-permute-start.13) | collective-permute-done | bytes 327712 | tf_op jit(solution)/shard_map/ppermute | solution.py:32
  80.4 2.3 collective-permute-start.21
  83.3 2.2 shard_map.125
  85.6 6.6 %collective-permute-done.17.refs_0_.refs_2_.refs_3_ = bf16[128,1280]{1,0:T(8,128)(2,1)S(1)} collective-permute-done((bf16[128,1280]{1,0:T(8,128)(2,1)S(1)}, bf16[128,1280]{1,0:T(8,128)(2,1)S(1)}, u32[]{:S(2)}, u32[]{:S(2)}) %collective-permute-start.17) | collective-permute-done | bytes 327712 | tf_op jit(solution)/shard_map/ppermute | solution.py:37
  93.3 2.2 shard_map.127
  95.6 2.2 collective-permute-start.18
  97.9 4.4 %shard_map.126 = (bf16[128,1536]{1,0:T(8,128)(2,1)S(1)}, bf16[128,1536]{1,0:T(8,128)(2,1)S(1)}, bf16[128,1536]{1,0:T(8,128)(2,1)S(1)}, bf16[384,1280]{1,0:T(8,128)(2,1)S(1)}, bf16[384,1280]{1,0:T(8,128)(2,1)S(1)}) custom-call(bf16[384,1280]{1,0:T(8,128)(2,1)S(1)} %collective-permute-done.12.refs_0_.refs_4_.refs_5_, ...), custom_call_target="tpu_custom_call" | custom-call | flops 3019898880 | tf_op jit(solution)/shard_map/pallas_call | solution.py:81
  105.4 3.2 %collective-permute-done.18.refs_3_ = bf16[128,1536]{1,0:T(8,128)(2,1)S(1)} collective-permute-done((bf16[128,1536]{1,0:T(8,128)(2,1)S(1)}, bf16[128,1536]{1,0:T(8,128)(2,1)S(1)}, u32[]{:S(2)}, u32[]{:S(2)}) %collective-permute-start.18) | collective-permute-done | bytes 393248 | tf_op jit(solution)/shard_map/ppermute | solution.py:32
  108.6 2.2 collective-permute-start.24
  110.9 6.8 %collective-permute-done.15.refs_1_ = bf16[128,1536]{1,0:T(8,128)(2,1)S(1)} collective-permute-done((bf16[128,1536]{1,0:T(8,128)(2,1)S(1)}, bf16[128,1536]{1,0:T(8,128)(2,1)S(1)}, u32[]{:S(2)}, u32[]{:S(2)}) %collective-permute-start.15) | collective-permute-done | bytes 393248 | tf_op jit(solution)/shard_map/ppermute | solution.py:32
  124.0 10.2 %collective-permute-done.27.refs_0_ = bf16[128,1664]{1,0:T(8,128)(2,1)S(1)} collective-permute-done((bf16[128,1664]{1,0:T(8,128)(2,1)S(1)}, bf16[128,1664]{1,0:T(8,128)(2,1)S(1)}, u32[]{:S(2)}, u32[]{:S(2)}) %collective-permute-start.27) | collective-permute-done | bytes 426016 | tf_op jit(solution)/shard_map/ppermute | solution.py:32
  137.6 3.4 %shard_map.136 = (bf16[128,1280]{1,0:T(8,128)(2,1)S(1)}, f32[1,1280]{1,0:T(1,128)S(1)}) custom-call(bf16[128,1664]{1,0:T(8,128)(2,1)S(1)} %collective-permute-done.27.refs_0_, f32[128,1]{1,0:T(8,128)S(1)} %get-tuple-element.132.refs_2_.refs_1_, bf16[128,1280]{1,0:T(8,128)(2,1)S(1)} %get-tuple-element.166.refs_2_, ...), custom_call_target="tpu_custom_call" | custom-call | flops 1006632960 | tf_op jit(solution)/shard_map/pallas_call | solution.py:81
  141.1 2.2 collective-permute-done.34.refs_1_
  144.9 4.4 %shard_map.134 = (bf16[384,1280]{1,0:T(8,128)(2,1)S(1)}, f32[1,1280]{1,0:T(1,128)S(1)}) custom-call(bf16[128,1664]{1,0:T(8,128)(2,1)S(1)} %shard_map.131.refs_0_, bf16[128,1664]{1,0:T(8,128)(2,1)S(1)} %collective-permute-done.34.refs_1_, bf16[128,1664]{1,0:T(8,128)(2,1)S(1)} %collective-permute-done.35.refs_2_, ...), custom_call_target="tpu_custom_call" | custom-call | flops 3019898880 | tf_op jit(solution)/shard_map/pallas_call | solution.py:81
  154.8 2.6 %shard_map.133 = (bf16[128,1280]{1,0:T(8,128)(2,1)S(1)}, f32[128,1]{1,0:T(8,128)}, bf16[128,768]{1,0:T(8,128)(2,1)S(1)}, bf16[128,768]{1,0:T(8,128)(2,1)S(1)}) custom-call(bf16[128,768]{1,0:T(8,128)(2,1)S(1)} %collective-permute-done.32.refs_0_, f32[128,1]{1,0:T(8,128)S(1)} %get-tuple-element.132.refs_2_.refs_1_, ...), custom_call_target="tpu_custom_call" | custom-call | tf_op jit(solution)/shard_map/pallas_call | solution.py:81
  158.8 3.6 %shard_map.132 = (bf16[128,1280]{1,0:T(8,128)(2,1)S(1)}, bf16[128,1280]{1,0:T(8,128)(2,1)S(1)}, bf16[128,1280]{1,0:T(8,128)(2,1)S(1)}, f32[128,1]{1,0:T(8,128)},...) custom-call(bf16[128,768]{1,0:T(8,128)(2,1)S(1)} %get-tuple-element.148.refs_, ...), custom_call_target="tpu_custom_call" | custom-call | tf_op jit(solution)/shard_map/pallas_call | solution.py:81
  165.9 2.5 %convolution_convert_fusion = bf16[768,1280]{1,0:T(8,128)(2,1)} fusion(bf16[512,1280]{1,0:T(8,128)(2,1)S(1)} %constant_dynamic-update-slice_fusion.4, bf16[128,768]{1,0:T(8,128)(2,1)S(1)} %get-tuple-element.168, bf16[384,768]{1,0:T(8,128)(2,1)S(1)} %get-tuple-element.167), kind=kOutput, calls=%fused_computation.15 | convolution fusion | flops 1009188864 | bytes 4063232 | tf_op jit(solution)/shard_map/dot_general | solution.py:22
  168.4 1.7 shard_map.137
  171.6 3.8 %collective-permute-done.30 = bf16[128,1280]{1,0:T(8,128)(2,1)S(1)} collective-permute-done((bf16[128,1280]{1,0:T(8,128)(2,1)S(1)}, bf16[128,1280]{1,0:T(8,128)(2,1)S(1)}, u32[]{:S(2)}, u32[]{:S(2)}) %collective-permute-start.30) | collective-permute-done | bytes 327712 | tf_op jit(solution)/shard_map/ppermute | solution.py:32
  175.4 2.2 shard_map.135
  178.6 4.8 %collective-permute-done.37.refs_1_ = bf16[128,768]{1,0:T(8,128)(2,1)S(1)} collective-permute-done((bf16[128,768]{1,0:T(8,128)(2,1)S(1)}, bf16[128,768]{1,0:T(8,128)(2,1)S(1)}, u32[]{:S(2)}, u32[]{:S(2)}) %collective-permute-start.37) | collective-permute-done | bytes 196640 | tf_op jit(solution)/shard_map/ppermute | solution.py:32
  183.3 5.1 %collective-permute-done.38.refs_2_ = bf16[128,768]{1,0:T(8,128)(2,1)S(1)} collective-permute-done((bf16[128,768]{1,0:T(8,128)(2,1)S(1)}, bf16[128,768]{1,0:T(8,128)(2,1)S(1)}, u32[]{:S(2)}, u32[]{:S(2)}) %collective-permute-start.38) | collective-permute-done | bytes 196640 | tf_op jit(solution)/shard_map/ppermute | solution.py:32
  194.0 4.2 %collective-permute-done.43.refs_0_ = bf16[128,1664]{1,0:T(8,128)(2,1)S(1)} collective-permute-done((bf16[128,1664]{1,0:T(8,128)(2,1)S(1)}, bf16[128,1664]{1,0:T(8,128)(2,1)S(1)}, u32[]{:S(2)}, u32[]{:S(2)}) %collective-permute-start.43) | collective-permute-done | bytes 426016 | tf_op jit(solution)/shard_map/ppermute | solution.py:32
  198.2 3.4 %shard_map.139 = (bf16[128,1280]{1,0:T(8,128)(2,1)S(1)}, f32[1,1280]{1,0:T(1,128)S(1)}) custom-call(bf16[128,1664]{1,0:T(8,128)(2,1)S(1)} %collective-permute-done.43.refs_0_, f32[128,1]{1,0:T(8,128)S(1)} %get-tuple-element.118.refs_1_, bf16[128,1280]{1,0:T(8,128)(2,1)S(1)} %get-tuple-element.177.refs_2_, ...), custom_call_target="tpu_custom_call" | custom-call | flops 1006632960 | tf_op jit(solution)/shard_map/pallas_call | solution.py:81
  206.0 4.6 %shard_map.140 = (bf16[128,1280]{1,0:T(8,128)(2,1)S(1)}, bf16[128,1280]{1,0:T(8,128)(2,1)S(1)}, bf16[128,1280]{1,0:T(8,128)(2,1)S(1)}, f32[1,1280]{1,0:T(1,128)S(1)}) custom-call(bf16[128,1664]{1,0:T(8,128)(2,1)S(1)} %shard_map.138.refs_0_, bf16[128,1664]{1,0:T(8,128)(2,1)S(1)} %collective-permute-done.41.refs_1_, ...), custom_call_target="tpu_custom_call" | custom-call | flops 1006632960 | tf_op jit(solution)/shard_map/pallas_call | solution.py:81
  210.8 2.1 collective-permute-start.44
  213.5 1.9 collective-permute-start.46
  215.5 4.3 %fusion.3 = bf16[768,1280]{1,0:T(8,128)(2,1)} fusion(bf16[768,1280]{1,0:T(8,128)(2,1)S(1)} %collective-permute-done.49, bf16[768,1280]{1,0:T(8,128)(2,1)} %convolution_convert_fusion, bf16[512,1280]{1,0:T(8,128)(2,1)S(1)} %constant_dynamic-update-slice_fusion.8, bf16[128,768]{1,0:T(8,128)(2,1)S(1)} %get-tuple-element.193, ...), kind=kOutput, calls=%fused_computation.9 | convolution fusion | flops 1013121024 | bytes 7995392 | tf_op jit(solution)/shard_map/dot_general | solution.py:22
  221.4 2.7 %fusion.4 = bf16[1280,768]{1,0:T(8,128)(2,1)} fusion(bf16[1280,768]{1,0:T(8,128)(2,1)S(1)} %collective-permute-done.48, bf16[1280,768]{1,0:T(8,128)(2,1)S(1)} %convolution_convert_fusion.2, bf16[512,1280]{1,0:T(8,128)(2,1)S(1)} %constant_dynamic-update-slice_fusion.10, bf16[512,768]{1,0:T(8,128)(2,1)S(1)} %get-tuple-element.191), kind=kOutput, calls=%fused_computation.10 | convolution fusion | flops 1011548160 | bytes 7995392 | tf_op jit(solution)/shard_map/dot_general | solution.py:22
  224.1 2.7 %fusion.5 = bf16[1280,768]{1,0:T(8,128)(2,1)} fusion(bf16[1280,768]{1,0:T(8,128)(2,1)S(1)} %collective-permute-done.47, bf16[1280,768]{1,0:T(8,128)(2,1)S(1)} %convolution_convert_fusion.3, bf16[512,1280]{1,0:T(8,128)(2,1)S(1)} %constant_dynamic-update-slice_fusion.10, bf16[512,768]{1,0:T(8,128)(2,1)S(1)} %get-tuple-element.190), kind=kOutput, calls=%fused_computation.11 | convolution fusion | flops 1011548160 | bytes 7995392 | tf_op jit(solution)/shard_map/dot_general | solution.py:22
  226.9 1.9 collective-permute-start.53
  (150 shorter events, 59.4 us)
Async XLA Ops:
  0.6 7.5 %collective-permute-start.2 = (bf16[1280,768]{1,0:T(8,128)(2,1)}, bf16[1280,768]{1,0:T(8,128)(2,1)S(1)}, u32[]{:S(2)}, u32[]{:S(2)}) collective-permute-start(bf16[1280,768]{1,0:T(8,128)(2,1)} %bitcast.57), channel_id=1, source_target_pairs={{0,1},{1,0},{2,3},{3,2},{4,5},{5,4},{6,7},{7,6},{8,9},{9,8},{10,11... | collective-permute-start | bytes 5898248 | tf_op jit(solution)/shard_map/ppermute | solution.py:32
  1.2 9.5 %collective-permute-start.4 = (bf16[768,1280]{1,0:T(8,128)(2,1)}, bf16[768,1280]{1,0:T(8,128)(2,1)}, u32[]{:S(2)}, u32[]{:S(2)}) collective-permute-start(bf16[768,1280]{1,0:T(8,128)(2,1)} %bitcast.61), channel_id=1, source_target_pairs={{0,1},{1,0},{2,3},{3,2},{4,5},{5,4},{6,7},{7,6},{8,9},{9,8},{10,11... | collective-permute-start | bytes 5898248 | tf_op jit(solution)/shard_map/ppermute | solution.py:32
  4.0 15.1 %collective-permute-start = (bf16[144,1280]{1,0:T(8,128)(2,1)S(1)}, bf16[144,1280]{1,0:T(8,128)(2,1)S(1)}, u32[]{:S(2)}, u32[]{:S(2)}) collective-permute-start(bf16[144,1280]{1,0:T(8,128)(2,1)S(1)} %get-tuple-element.217), channel_id=1, source_target_pairs={{0,8},{8,0},{16,24},{24,16},{1,9},{9,1},{17,25},{25,17},{2,10},{10... | collective-permute-start | bytes 1105928 | tf_op jit(solution)/shard_map/ppermute | solution.py:32
  6.6 12.5 %collective-permute-start.1 = (bf16[144,1280]{1,0:T(8,128)(2,1)S(1)}, bf16[144,1280]{1,0:T(8,128)(2,1)S(1)}, u32[]{:S(2)}, u32[]{:S(2)}) collective-permute-start(bf16[144,1280]{1,0:T(8,128)(2,1)S(1)} %get-tuple-element.218), channel_id=1, source_target_pairs={{0,16},{8,24},{16,0},{24,8},{1,17},{9,25},{17,1},{25,9},{2,18},{10... | collective-permute-start | bytes 1105928 | tf_op jit(solution)/shard_map/ppermute | solution.py:32
  15.2 13.3 %collective-permute-start.7 = (bf16[144,1280]{1,0:T(8,128)(2,1)S(1)}, bf16[144,1280]{1,0:T(8,128)(2,1)S(1)}, u32[]{:S(2)}, u32[]{:S(2)}) collective-permute-start(bf16[144,1280]{1,0:T(8,128)(2,1)S(1)} %get-tuple-element.115), channel_id=1, source_target_pairs={{0,24},{8,16},{16,8},{24,0},{1,25},{9,17},{17,9},{25,1},{2,26},{10... | collective-permute-start | bytes 1105928 | tf_op jit(solution)/shard_map/ppermute | solution.py:32
  23.7 13.8 %collective-permute-start.5 = (bf16[128,1536]{1,0:T(8,128)(2,1)S(1)}, bf16[128,1536]{1,0:T(8,128)(2,1)S(1)}, u32[]{:S(2)}, u32[]{:S(2)}) collective-permute-start(bf16[128,1536]{1,0:T(8,128)(2,1)S(1)} %get-tuple-element.111), channel_id=1, source_target_pairs={{0,8},{8,0},{16,24},{24,16},{1,9},{9,1},{17,25},{25,17},{2,10},{10... | collective-permute-start | bytes 1179656 | tf_op jit(solution)/shard_map/ppermute | solution.py:32
  24.3 13.2 %collective-permute-start.6 = (bf16[128,1536]{1,0:T(8,128)(2,1)S(1)}, bf16[128,1536]{1,0:T(8,128)(2,1)S(1)}, u32[]{:S(2)}, u32[]{:S(2)}) collective-permute-start(bf16[128,1536]{1,0:T(8,128)(2,1)S(1)} %get-tuple-element.112), channel_id=1, source_target_pairs={{0,16},{8,24},{16,0},{24,8},{1,17},{9,25},{17,1},{25,9},{2,18},{10... | collective-permute-start | bytes 1179656 | tf_op jit(solution)/shard_map/ppermute | solution.py:32
  30.9 13.9 %collective-permute-start.8 = (bf16[128,1536]{1,0:T(8,128)(2,1)S(1)}, bf16[128,1536]{1,0:T(8,128)(2,1)S(1)}, u32[]{:S(2)}, u32[]{:S(2)}) collective-permute-start(bf16[128,1536]{1,0:T(8,128)(2,1)S(1)} %get-tuple-element.116), channel_id=1, source_target_pairs={{0,24},{8,16},{16,8},{24,0},{1,25},{9,17},{17,9},{25,1},{2,26},{10... | collective-permute-start | bytes 1179656 | tf_op jit(solution)/shard_map/ppermute | solution.py:32
  45.4 8.8 %collective-permute-start.9 = (bf16[128,768]{1,0:T(8,128)(2,1)S(1)}, bf16[128,768]{1,0:T(8,128)(2,1)S(1)}, u32[]{:S(2)}, u32[]{:S(2)}) collective-permute-start(bf16[128,768]{1,0:T(8,128)(2,1)S(1)} %get-tuple-element.121.refs_0_), channel_id=1, source_target_pairs={{0,24},{8,16},{16,8},{24,0},{1,25},{9,17},{17,9},{25,1},{2,26},{10... | collective-permute-start | bytes 589832 | tf_op jit(solution)/shard_map/ppermute | solution.py:32
  48.1 8.9 %collective-permute-start.10 = (bf16[128,768]{1,0:T(8,128)(2,1)S(1)}, bf16[128,768]{1,0:T(8,128)(2,1)S(1)}, u32[]{:S(2)}, u32[]{:S(2)}) collective-permute-start(bf16[128,768]{1,0:T(8,128)(2,1)S(1)} %get-tuple-element.121.refs_0_), channel_id=1, source_target_pairs={{0,8},{8,0},{16,24},{24,16},{1,9},{9,1},{17,25},{25,17},{2,10},{10... | collective-permute-start | bytes 589832 | tf_op jit(solution)/shard_map/ppermute | solution.py:32
  48.7 8.3 %collective-permute-start.11 = (bf16[128,768]{1,0:T(8,128)(2,1)S(1)}, bf16[128,768]{1,0:T(8,128)(2,1)S(1)}, u32[]{:S(2)}, u32[]{:S(2)}) collective-permute-start(bf16[128,768]{1,0:T(8,128)(2,1)S(1)} %get-tuple-element.121.refs_0_), channel_id=1, source_target_pairs={{0,16},{8,24},{16,0},{24,8},{1,17},{9,25},{17,1},{25,9},{2,18},{10... | collective-permute-start | bytes 589832 | tf_op jit(solution)/shard_map/ppermute | solution.py:32
  60.0 37.9 %collective-permute-start.12 = (bf16[384,1280]{1,0:T(8,128)(2,1)S(1)}, bf16[384,1280]{1,0:T(8,128)(2,1)S(1)}, u32[]{:S(2)}, u32[]{:S(2)}) collective-permute-start(bf16[384,1280]{1,0:T(8,128)(2,1)S(1)} %get-tuple-element.124), channel_id=1, source_target_pairs={{0,2},{2,4},{4,6},{6,0},{1,3},{3,5},{5,7},{7,1},{8,10},{10,12},{12... | collective-permute-start | bytes 2949128 | tf_op jit(solution)/shard_map/ppermute | solution.py:37
  61.8 11.7 %collective-permute-start.25 = (bf16[128,1280]{1,0:T(8,128)(2,1)S(1)}, bf16[128,1280]{1,0:T(8,128)(2,1)S(1)}, u32[]{:S(2)}, u32[]{:S(2)}) collective-permute-start(bf16[128,1280]{1,0:T(8,128)(2,1)S(1)} %get-tuple-element.208), channel_id=1, source_target_pairs={{0,24},{8,16},{16,8},{24,0},{1,25},{9,17},{17,9},{25,1},{2,26},{10... | collective-permute-start | bytes 983048 | tf_op jit(solution)/shard_map/ppermute | solution.py:32
  64.2 16.2 %collective-permute-start.13 = (bf16[128,1280]{1,0:T(8,128)(2,1)S(1)}, bf16[128,1280]{1,0:T(8,128)(2,1)S(1)}, u32[]{:S(2)}, u32[]{:S(2)}) collective-permute-start(bf16[128,1280]{1,0:T(8,128)(2,1)S(1)} %get-tuple-element.210), channel_id=1, source_target_pairs={{0,8},{8,0},{16,24},{24,16},{1,9},{9,1},{17,25},{25,17},{2,10},{10... | collective-permute-start | bytes 983048 | tf_op jit(solution)/shard_map/ppermute | solution.py:32
  64.7 15.7 %collective-permute-start.14 = (bf16[128,1280]{1,0:T(8,128)(2,1)S(1)}, bf16[128,1280]{1,0:T(8,128)(2,1)S(1)}, u32[]{:S(2)}, u32[]{:S(2)}) collective-permute-start(bf16[128,1280]{1,0:T(8,128)(2,1)S(1)} %get-tuple-element.209), channel_id=1, source_target_pairs={{0,16},{8,24},{16,0},{24,8},{1,17},{9,25},{17,1},{25,9},{2,18},{10... | collective-permute-start | bytes 983048 | tf_op jit(solution)/shard_map/ppermute | solution.py:32
  65.4 26.8 %collective-permute-start.17 = (bf16[128,1280]{1,0:T(8,128)(2,1)S(1)}, bf16[128,1280]{1,0:T(8,128)(2,1)S(1)}, u32[]{:S(2)}, u32[]{:S(2)}) collective-permute-start(bf16[128,1280]{1,0:T(8,128)(2,1)S(1)} %get-tuple-element.120), channel_id=1, source_target_pairs={{0,2},{2,4},{4,6},{6,0},{1,3},{3,5},{5,7},{7,1},{8,10},{10,12},{12... | collective-permute-start | bytes 983048 | tf_op jit(solution)/shard_map/ppermute | solution.py:37
  75.1 43.1 %collective-permute-start.26 = (bf16[128,768]{1,0:T(8,128)(2,1)S(1)}, bf16[128,768]{1,0:T(8,128)(2,1)S(1)}, u32[]{:S(2)}, u32[]{:S(2)}) collective-permute-start(bf16[128,768]{1,0:T(8,128)(2,1)S(1)} %get-tuple-element.145), channel_id=1, source_target_pairs={{0,24},{8,16},{16,8},{24,0},{1,25},{9,17},{17,9},{25,1},{2,26},{10... | collective-permute-start | bytes 589832 | tf_op jit(solution)/shard_map/ppermute | solution.py:32
  80.4 15.2 %collective-permute-start.21 = (f32[128,1]{1,0:T(8,128)S(1)}, f32[128,1]{1,0:T(8,128)S(1)}, u32[]{:S(2)}, u32[]{:S(2)}) collective-permute-start(f32[128,1]{1,0:T(8,128)S(1)} %get-tuple-element.141), channel_id=1, source_target_pairs={{0,24},{8,16},{16,8},{24,0},{1,25},{9,17},{17,9},{25,1},{2,26},{10... | collective-permute-start | bytes 1544 | tf_op jit(solution)/shard_map/ppermute | solution.py:32
  82.6 15.2 %collective-permute-start.20 = (f32[128,1]{1,0:T(8,128)S(1)}, f32[128,1]{1,0:T(8,128)S(1)}, u32[]{:S(2)}, u32[]{:S(2)}) collective-permute-start(f32[128,1]{1,0:T(8,128)S(1)} %get-tuple-element.139), channel_id=1, source_target_pairs={{0,16},{8,24},{16,0},{24,8},{1,17},{9,25},{17,1},{25,9},{2,18},{10... | collective-permute-start | bytes 1544 | tf_op jit(solution)/shard_map/ppermute | solution.py:32
  95.6 13.0 %collective-permute-start.18 = (bf16[128,1536]{1,0:T(8,128)(2,1)S(1)}, bf16[128,1536]{1,0:T(8,128)(2,1)S(1)}, u32[]{:S(2)}, u32[]{:S(2)}) collective-permute-start(bf16[128,1536]{1,0:T(8,128)(2,1)S(1)} %get-tuple-element.133), channel_id=1, source_target_pairs={{0,24},{8,16},{16,8},{24,0},{1,25},{9,17},{17,9},{25,1},{2,26},{10... | collective-permute-start | bytes 1179656 | tf_op jit(solution)/shard_map/ppermute | solution.py:32
  102.3 15.4 %collective-permute-start.15 = (bf16[128,1536]{1,0:T(8,128)(2,1)S(1)}, bf16[128,1536]{1,0:T(8,128)(2,1)S(1)}, u32[]{:S(2)}, u32[]{:S(2)}) collective-permute-start(bf16[128,1536]{1,0:T(8,128)(2,1)S(1)} %get-tuple-element.130), channel_id=1, source_target_pairs={{0,8},{8,0},{16,24},{24,16},{1,9},{9,1},{17,25},{25,17},{2,10},{10... | collective-permute-start | bytes 1179656 | tf_op jit(solution)/shard_map/ppermute | solution.py:32
  103.9 13.9 %collective-permute-start.16 = (bf16[128,1536]{1,0:T(8,128)(2,1)S(1)}, bf16[128,1536]{1,0:T(8,128)(2,1)S(1)}, u32[]{:S(2)}, u32[]{:S(2)}) collective-permute-start(bf16[128,1536]{1,0:T(8,128)(2,1)S(1)} %get-tuple-element.131), channel_id=1, source_target_pairs={{0,16},{8,24},{16,0},{24,8},{1,17},{9,25},{17,1},{25,9},{2,18},{10... | collective-permute-start | bytes 1179656 | tf_op jit(solution)/shard_map/ppermute | solution.py:32
  104.6 15.3 %collective-permute-start.23 = (bf16[128,768]{1,0:T(8,128)(2,1)S(1)}, bf16[128,768]{1,0:T(8,128)(2,1)S(1)}, u32[]{:S(2)}, u32[]{:S(2)}) collective-permute-start(bf16[128,768]{1,0:T(8,128)(2,1)S(1)} %get-tuple-element.143), channel_id=1, source_target_pairs={{0,8},{8,0},{16,24},{24,16},{1,9},{9,1},{17,25},{25,17},{2,10},{10... | collective-permute-start | bytes 589832 | tf_op jit(solution)/shard_map/ppermute | solution.py:32
  108.6 11.2 %collective-permute-start.24 = (bf16[128,768]{1,0:T(8,128)(2,1)S(1)}, bf16[128,768]{1,0:T(8,128)(2,1)S(1)}, u32[]{:S(2)}, u32[]{:S(2)}) collective-permute-start(bf16[128,768]{1,0:T(8,128)(2,1)S(1)} %get-tuple-element.144), channel_id=1, source_target_pairs={{0,16},{8,24},{16,0},{24,8},{1,17},{9,25},{17,1},{25,9},{2,18},{10... | collective-permute-start | bytes 589832 | tf_op jit(solution)/shard_map/ppermute | solution.py:32
  120.4 13.8 %collective-permute-start.27 = (bf16[128,1664]{1,0:T(8,128)(2,1)S(1)}, bf16[128,1664]{1,0:T(8,128)(2,1)S(1)}, u32[]{:S(2)}, u32[]{:S(2)}) collective-permute-start(bf16[128,1664]{1,0:T(8,128)(2,1)S(1)} %shard_map.131.refs_0_), channel_id=1, source_target_pairs={{0,24},{8,16},{16,8},{24,0},{1,25},{9,17},{17,9},{25,1},{2,26},{10... | collective-permute-start | bytes 1277960 | tf_op jit(solution)/shard_map/ppermute | solution.py:32
  121.9 21.4 %collective-permute-start.34 = (bf16[128,1664]{1,0:T(8,128)(2,1)S(1)}, bf16[128,1664]{1,0:T(8,128)(2,1)S(1)}, u32[]{:S(2)}, u32[]{:S(2)}) collective-permute-start(bf16[128,1664]{1,0:T(8,128)(2,1)S(1)} %shard_map.131.refs_0_), channel_id=1, source_target_pairs={{0,8},{8,0},{16,24},{24,16},{1,9},{9,1},{17,25},{25,17},{2,10},{10... | collective-permute-start | bytes 1277960 | tf_op jit(solution)/shard_map/ppermute | solution.py:32
  123.4 21.5 %collective-permute-start.35 = (bf16[128,1664]{1,0:T(8,128)(2,1)S(1)}, bf16[128,1664]{1,0:T(8,128)(2,1)S(1)}, u32[]{:S(2)}, u32[]{:S(2)}) collective-permute-start(bf16[128,1664]{1,0:T(8,128)(2,1)S(1)} %shard_map.131.refs_0_), channel_id=1, source_target_pairs={{0,16},{8,24},{16,0},{24,8},{1,17},{9,25},{17,1},{25,9},{2,18},{10... | collective-permute-start | bytes 1277960 | tf_op jit(solution)/shard_map/ppermute | solution.py:32
  134.1 15.8 %collective-permute-start.28 = (bf16[128,768]{1,0:T(8,128)(2,1)S(1)}, bf16[128,768]{1,0:T(8,128)(2,1)S(1)}, u32[]{:S(2)}, u32[]{:S(2)}) collective-permute-start(bf16[128,768]{1,0:T(8,128)(2,1)S(1)} %get-tuple-element.148.refs_0_), channel_id=1, source_target_pairs={{0,8},{8,0},{16,24},{24,16},{1,9},{9,1},{17,25},{25,17},{2,10},{10... | collective-permute-start | bytes 589832 | tf_op jit(solution)/shard_map/ppermute | solution.py:32
  134.7 15.3 %collective-permute-start.29 = (bf16[128,768]{1,0:T(8,128)(2,1)S(1)}, bf16[128,768]{1,0:T(8,128)(2,1)S(1)}, u32[]{:S(2)}, u32[]{:S(2)}) collective-permute-start(bf16[128,768]{1,0:T(8,128)(2,1)S(1)} %get-tuple-element.148.refs_0_), channel_id=1, source_target_pairs={{0,16},{8,24},{16,0},{24,8},{1,17},{9,25},{17,1},{25,9},{2,18},{10... | collective-permute-start | bytes 589832 | tf_op jit(solution)/shard_map/ppermute | solution.py:32
  136.1 13.8 %collective-permute-start.32 = (bf16[128,768]{1,0:T(8,128)(2,1)S(1)}, bf16[128,768]{1,0:T(8,128)(2,1)S(1)}, u32[]{:S(2)}, u32[]{:S(2)}) collective-permute-start(bf16[128,768]{1,0:T(8,128)(2,1)S(1)} %get-tuple-element.148.refs_0_), channel_id=1, source_target_pairs={{0,24},{8,16},{16,8},{24,0},{1,25},{9,17},{17,9},{25,1},{2,26},{10... | collective-permute-start | bytes 589832 | tf_op jit(solution)/shard_map/ppermute | solution.py:32
  143.3 25.2 %collective-permute-start.39 = (bf16[128,1280]{1,0:T(8,128)(2,1)S(1)}, bf16[128,1280]{1,0:T(8,128)(2,1)S(1)}, u32[]{:S(2)}, u32[]{:S(2)}) collective-permute-start(bf16[128,1280]{1,0:T(8,128)(2,1)S(1)} %get-tuple-element.171), channel_id=1, source_target_pairs={{0,6},{2,0},{4,2},{6,4},{1,7},{3,1},{5,3},{7,5},{8,14},{10,8},{12,... | collective-permute-start | bytes 983048 | tf_op jit(solution)/shard_map/ppermute | solution.py:37
  149.3 26.1 %collective-permute-start.36 = (bf16[384,1280]{1,0:T(8,128)(2,1)S(1)}, bf16[384,1280]{1,0:T(8,128)(2,1)S(1)}, u32[]{:S(2)}, u32[]{:S(2)}) collective-permute-start(bf16[384,1280]{1,0:T(8,128)(2,1)S(1)} %get-tuple-element.154), channel_id=1, source_target_pairs={{0,6},{2,0},{4,2},{6,4},{1,7},{3,1},{5,3},{7,5},{8,14},{10,8},{12,... | collective-permute-start | bytes 2949128 | tf_op jit(solution)/shard_map/ppermute | solution.py:37
  157.4 53.3 %collective-permute-start.33 = (bf16[128,1280]{1,0:T(8,128)(2,1)S(1)}, bf16[128,1280]{1,0:T(8,128)(2,1)S(1)}, u32[]{:S(2)}, u32[]{:S(2)}) collective-permute-start(bf16[128,1280]{1,0:T(8,128)(2,1)S(1)} %get-tuple-element.152), channel_id=1, source_target_pairs={{0,24},{8,16},{16,8},{24,0},{1,25},{9,17},{17,9},{25,1},{2,26},{10... | collective-permute-start | bytes 983048 | tf_op jit(solution)/shard_map/ppermute | solution.py:32
  162.5 12.9 %collective-permute-start.30 = (bf16[128,1280]{1,0:T(8,128)(2,1)S(1)}, bf16[128,1280]{1,0:T(8,128)(2,1)S(1)}, u32[]{:S(2)}, u32[]{:S(2)}) collective-permute-start(bf16[128,1280]{1,0:T(8,128)(2,1)S(1)} %get-tuple-element.150), channel_id=1, source_target_pairs={{0,8},{8,0},{16,24},{24,16},{1,9},{9,1},{17,25},{25,17},{2,10},{10... | collective-permute-start | bytes 983048 | tf_op jit(solution)/shard_map/ppermute | solution.py:32
  164.0 42.0 %collective-permute-start.31 = (bf16[128,1280]{1,0:T(8,128)(2,1)S(1)}, bf16[128,1280]{1,0:T(8,128)(2,1)S(1)}, u32[]{:S(2)}, u32[]{:S(2)}) collective-permute-start(bf16[128,1280]{1,0:T(8,128)(2,1)S(1)} %get-tuple-element.151), channel_id=1, source_target_pairs={{0,16},{8,24},{16,0},{24,8},{1,17},{9,25},{17,1},{25,9},{2,18},{10... | collective-permute-start | bytes 983048 | tf_op jit(solution)/shard_map/ppermute | solution.py:32
  170.1 13.2 %collective-permute-start.40 = (bf16[128,768]{1,0:T(8,128)(2,1)S(1)}, bf16[128,768]{1,0:T(8,128)(2,1)S(1)}, u32[]{:S(2)}, u32[]{:S(2)}) collective-permute-start(bf16[128,768]{1,0:T(8,128)(2,1)S(1)} %get-tuple-element.172), channel_id=1, source_target_pairs={{0,24},{8,16},{16,8},{24,0},{1,25},{9,17},{17,9},{25,1},{2,26},{10... | collective-permute-start | bytes 589832 | tf_op jit(solution)/shard_map/ppermute | solution.py:32
  178.2 10.3 %collective-permute-start.38 = (bf16[128,768]{1,0:T(8,128)(2,1)S(1)}, bf16[128,768]{1,0:T(8,128)(2,1)S(1)}, u32[]{:S(2)}, u32[]{:S(2)}) collective-permute-start(bf16[128,768]{1,0:T(8,128)(2,1)S(1)} %get-tuple-element.170), channel_id=1, source_target_pairs={{0,16},{8,24},{16,0},{24,8},{1,17},{9,25},{17,1},{25,9},{2,18},{10... | collective-permute-start | bytes 589832 | tf_op jit(solution)/shard_map/ppermute | solution.py:32
  189.0 9.2 %collective-permute-start.43 = (bf16[128,1664]{1,0:T(8,128)(2,1)S(1)}, bf16[128,1664]{1,0:T(8,128)(2,1)S(1)}, u32[]{:S(2)}, u32[]{:S(2)}) collective-permute-start(bf16[128,1664]{1,0:T(8,128)(2,1)S(1)} %shard_map.138.refs_0_), channel_id=1, source_target_pairs={{0,24},{8,16},{16,8},{24,0},{1,25},{9,17},{17,9},{25,1},{2,26},{10... | collective-permute-start | bytes 1277960 | tf_op jit(solution)/shard_map/ppermute | solution.py:32
  190.1 12.1 %collective-permute-start.41 = (bf16[128,1664]{1,0:T(8,128)(2,1)S(1)}, bf16[128,1664]{1,0:T(8,128)(2,1)S(1)}, u32[]{:S(2)}, u32[]{:S(2)}) collective-permute-start(bf16[128,1664]{1,0:T(8,128)(2,1)S(1)} %shard_map.138.refs_0_), channel_id=1, source_target_pairs={{0,8},{8,0},{16,24},{24,16},{1,9},{9,1},{17,25},{25,17},{2,10},{10... | collective-permute-start | bytes 1277960 | tf_op jit(solution)/shard_map/ppermute | solution.py:32
  191.2 11.5 %collective-permute-start.42 = (bf16[128,1664]{1,0:T(8,128)(2,1)S(1)}, bf16[128,1664]{1,0:T(8,128)(2,1)S(1)}, u32[]{:S(2)}, u32[]{:S(2)}) collective-permute-start(bf16[128,1664]{1,0:T(8,128)(2,1)S(1)} %shard_map.138.refs_0_), channel_id=1, source_target_pairs={{0,16},{8,24},{16,0},{24,8},{1,17},{9,25},{17,1},{25,9},{2,18},{10... | collective-permute-start | bytes 1277960 | tf_op jit(solution)/shard_map/ppermute | solution.py:32
  198.2 15.3 %collective-permute-start.49 = (bf16[768,1280]{1,0:T(8,128)(2,1)S(1)}, bf16[768,1280]{1,0:T(8,128)(2,1)S(1)}, u32[]{:S(2)}, u32[]{:S(2)}) collective-permute-start(bf16[768,1280]{1,0:T(8,128)(2,1)S(1)} %fusion.8), channel_id=1, source_target_pairs={{0,1},{1,0},{2,3},{3,2},{4,5},{5,4},{6,7},{7,6},{8,9},{9,8},{10,11... | collective-permute-start | bytes 5898248 | tf_op jit(solution)/shard_map/ppermute | solution.py:32
  204.0 15.7 %collective-permute-start.48 = (bf16[1280,768]{1,0:T(8,128)(2,1)S(1)}, bf16[1280,768]{1,0:T(8,128)(2,1)S(1)}, u32[]{:S(2)}, u32[]{:S(2)}) collective-permute-start(bf16[1280,768]{1,0:T(8,128)(2,1)S(1)} %fusion.7), channel_id=1, source_target_pairs={{0,1},{1,0},{2,3},{3,2},{4,5},{5,4},{6,7},{7,6},{8,9},{9,8},{10,11... | collective-permute-start | bytes 5898248 | tf_op jit(solution)/shard_map/ppermute | solution.py:32
  205.4 14.4 %collective-permute-start.47 = (bf16[1280,768]{1,0:T(8,128)(2,1)S(1)}, bf16[1280,768]{1,0:T(8,128)(2,1)S(1)}, u32[]{:S(2)}, u32[]{:S(2)}) collective-permute-start(bf16[1280,768]{1,0:T(8,128)(2,1)S(1)} %fusion.6), channel_id=1, source_target_pairs={{0,1},{1,0},{2,3},{3,2},{4,5},{5,4},{6,7},{7,6},{8,9},{9,8},{10,11... | collective-permute-start | bytes 5898248 | tf_op jit(solution)/shard_map/ppermute | solution.py:32
  210.8 16.0 %collective-permute-start.44 = (bf16[128,1280]{1,0:T(8,128)(2,1)S(1)}, bf16[128,1280]{1,0:T(8,128)(2,1)S(1)}, u32[]{:S(2)}, u32[]{:S(2)}) collective-permute-start(bf16[128,1280]{1,0:T(8,128)(2,1)S(1)} %get-tuple-element.186), channel_id=1, source_target_pairs={{0,8},{8,0},{16,24},{24,16},{1,9},{9,1},{17,25},{25,17},{2,10},{10... | collective-permute-start | bytes 983048 | tf_op jit(solution)/shard_map/ppermute | solution.py:32
  212.9 17.0 %collective-permute-start.45 = (bf16[128,1280]{1,0:T(8,128)(2,1)S(1)}, bf16[128,1280]{1,0:T(8,128)(2,1)S(1)}, u32[]{:S(2)}, u32[]{:S(2)}) collective-permute-start(bf16[128,1280]{1,0:T(8,128)(2,1)S(1)} %get-tuple-element.187), channel_id=1, source_target_pairs={{0,16},{8,24},{16,0},{24,8},{1,17},{9,25},{17,1},{25,9},{2,18},{10... | collective-permute-start | bytes 983048 | tf_op jit(solution)/shard_map/ppermute | solution.py:32
  213.5 16.3 %collective-permute-start.46 = (bf16[128,1280]{1,0:T(8,128)(2,1)S(1)}, bf16[128,1280]{1,0:T(8,128)(2,1)S(1)}, u32[]{:S(2)}, u32[]{:S(2)}) collective-permute-start(bf16[128,1280]{1,0:T(8,128)(2,1)S(1)} %get-tuple-element.178), channel_id=1, source_target_pairs={{0,24},{8,16},{16,8},{24,0},{1,25},{9,17},{17,9},{25,1},{2,26},{10... | collective-permute-start | bytes 983048 | tf_op jit(solution)/shard_map/ppermute | solution.py:32
  219.8 10.4 %collective-permute-start.51 = (f32[1,1280]{1,0:T(1,128)S(1)}, f32[1,1280]{1,0:T(1,128)S(1)}, u32[]{:S(2)}, u32[]{:S(2)}) collective-permute-start(f32[1,1280]{1,0:T(1,128)S(1)} %add.115), channel_id=1, source_target_pairs={{0,8},{8,0},{16,24},{24,16},{1,9},{9,1},{17,25},{25,17},{2,10},{10... | collective-permute-start | bytes 15368 | tf_op jit(solution)/shard_map/ppermute | solution.py:32
  220.8 9.4 %collective-permute-start.52 = (f32[1,1280]{1,0:T(1,128)S(1)}, f32[1,1280]{1,0:T(1,128)S(1)}, u32[]{:S(2)}, u32[]{:S(2)}) collective-permute-start(f32[1,1280]{1,0:T(1,128)S(1)} %add.115), channel_id=1, source_target_pairs={{0,16},{8,24},{16,0},{24,8},{1,17},{9,25},{17,1},{25,9},{2,18},{10... | collective-permute-start | bytes 15368 | tf_op jit(solution)/shard_map/ppermute | solution.py:32
  (14 other events, 80.1 us)

commit v5 on v4

--- a/solution.py
+++ b/solution.py
@@ -489,7 +489,7 @@
         first_rows.insert(0, split)
     hidden = moved(next_hidden, 1)
     grad_blocks = sent([cotangent_quarter(step, next_hidden[0]) for step in range(dp_count)])
-    squares = [after(square, *grad_blocks[1:-1]) for square in squares]
+    squares = [after(square, grad_blocks[-1]) for square in squares]
     inverse = shifted(row_scale(sent(squares), features, True), "pipe", 1)
     act_parts, grad = [], []
     for group, mask in zip(groups, masks[1]):
@@ -502,6 +502,8 @@
 
     parts, gained = [], []
     for rows_in, mask in zip(hidden, masks[1]):
+        if parts:
+            rows_in = after(rows_in, parts[0])
         made, scaled, _ = hidden_parts([rows_in], rows, gain_part, mask, gate_pair, up_pair)
         parts += made
         gained.append(scaled)

time: 232 us -> 235 us (1.013)
  waiting for transfers between devices: 84.3 us -> 87.9 us
    ppermute x49, waiting for transfers between devices: 77.7 us -> 82 us  [swap(): return lax.ppermute(block, axis, partner_route(lax.axis_size(axis), step))]
  transfers between devices with their start and end apart: 54 -> 54, of which waited for: 22 -> 23; matrix products, arithmetic and copies ran while one was open for 11% -> 11% of each run, Pallas kernels for 22% -> 22%
where the time goes in v5:
time: 235 us; the launch traced here: 234 us
  waiting for transfers between devices  87.9 us (37%)
  starting transfers between devices  63.2 us (27%)
  Pallas kernels  55.4 us (24%)
  matrix products  22.1 us (9%)
  local copies, waits for them, and re-layouts  3.66 us (2%)
    ppermute x49, waiting for transfers between devices, swap(): return lax.ppermute(block, axis, partner_route(lax.axis_size(axis), step))  82 us
    ppermute x49, starting transfers between devices, swap(): return lax.ppermute(block, axis, partner_route(lax.axis_size(axis), step))  57.7 us
    pallas_call x22, Pallas kernels, kernel_call(): pl.pallas_call(call, in_specs=[in_vmem] * (count + kept), out_specs=[in_v...  50.9 us
    dot_general x12, matrix products, dot(): lax.dot_general(former, latter, ((contract[:1], contract[1:]), ((), ())),...  22.1 us
    ppermute x5, waiting for transfers between devices, shifted(): lax.ppermute(block, axis, [(i, (i + distance) % size) for i in range(size)])  5.88 us
    ppermute x5, starting transfers between devices, shifted(): lax.ppermute(block, axis, [(i, (i + distance) % size) for i in range(size)])  5.48 us
  transfers between devices with their start and end apart: 54, of which 23 were waited for; matrix products, arithmetic and copies ran while one was open for 11% of the time, Pallas kernels for 22%

profile of v5, /device:TPU:0, one launch (start us, length us, event | category | flops | bytes accessed | tf_op | source)
XLA Modules:
  0.0 234.5 jit_solution(17172147488256986623)
XLA Ops:
  4.0 2.6 %collective-permute-start = (bf16[144,1280]{1,0:T(8,128)(2,1)S(1)}, bf16[144,1280]{1,0:T(8,128)(2,1)S(1)}, u32[]{:S(2)}, u32[]{:S(2)}) collective-permute-start(bf16[144,1280]{1,0:T(8,128)(2,1)S(1)} %get-tuple-element.219), channel_id=1, source_target_pairs={{0,8},{8,0},{16,24},{24,16},{1,9},{9,1},{17,25},{25,17},{2,10},{10... | collective-permute-start | bytes 1105928 | tf_op jit(solution)/shard_map/ppermute | solution.py:32
  8.1 2.6 %collective-permute-done.4.refs_5_ = bf16[768,1280]{1,0:T(8,128)(2,1)} collective-permute-done((bf16[768,1280]{1,0:T(8,128)(2,1)}, bf16[768,1280]{1,0:T(8,128)(2,1)}, u32[]{:S(2)}, u32[]{:S(2)}) %collective-permute-start.4) | collective-permute-done | bytes 1966112 | tf_op jit(solution)/shard_map/ppermute | solution.py:32
  10.7 4.5 %shard_map.118 = (bf16[1280,768]{1,0:T(8,128)(2,1)S(1)}, bf16[1280,768]{1,0:T(8,128)(2,1)S(1)}, bf16[1280,768]{1,0:T(8,128)(2,1)S(1)}, bf16[1280,768]{1,0:T(8,12...) custom-call(bf16[1280,768]{1,0:T(8,128)(2,1)} %bitcast.58, bf16[1280,768]{1,0:T(8,128)(2,1)} %copy-done.3, ...), custom_call_target="tpu_custom_call" | custom-call | bytes 23592960 | tf_op jit(solution)/shard_map/pallas_call | solution.py:109
  15.2 3.9 %collective-permute-start.7 = (bf16[144,1280]{1,0:T(8,128)(2,1)S(1)}, bf16[144,1280]{1,0:T(8,128)(2,1)S(1)}, u32[]{:S(2)}, u32[]{:S(2)}) collective-permute-start(bf16[144,1280]{1,0:T(8,128)(2,1)S(1)} %get-tuple-element.116), channel_id=1, source_target_pairs={{0,24},{8,16},{16,8},{24,0},{1,25},{9,17},{17,9},{25,1},{2,26},{10... | collective-permute-start | bytes 1105928 | tf_op jit(solution)/shard_map/ppermute | solution.py:32
  19.1 4.6 %shard_map.119 = (bf16[128,1536]{1,0:T(8,128)(2,1)S(1)}, bf16[128,1536]{1,0:T(8,128)(2,1)S(1)}, bf16[128,1536]{1,0:T(8,128)(2,1)S(1)}, bf16[384,1280]{1,0:T(8,12...) custom-call(bf16[144,1280]{1,0:T(8,128)(2,1)S(1)} %get-tuple-element, ...), custom_call_target="tpu_custom_call" | custom-call | flops 3019898880 | tf_op jit(solution)/shard_map/pallas_call | solution.py:81
  24.4 4.1 %collective-permute-done.7.refs_0_ = bf16[144,1280]{1,0:T(8,128)(2,1)S(1)} collective-permute-done((bf16[144,1280]{1,0:T(8,128)(2,1)S(1)}, bf16[144,1280]{1,0:T(8,128)(2,1)S(1)}, u32[]{:S(2)}, u32[]{:S(2)}) %collective-permute-start.7) | collective-permute-done | bytes 368672 | tf_op jit(solution)/shard_map/ppermute | solution.py:32
  28.5 2.4 %shard_map.120 = (bf16[128,1536]{1,0:T(8,128)(2,1)S(1)}, bf16[128,1280]{1,0:T(8,128)(2,1)S(1)}, bf16[128,1280]{1,0:T(8,128)(2,1)S(1)}, f32[128,1]{1,0:T(8,128)S(...) custom-call(bf16[144,1280]{1,0:T(8,128)(2,1)S(1)} %collective-permute-done.7.refs_0_, ...), custom_call_target="tpu_custom_call" | custom-call | flops 1006632960 | tf_op jit(solution)/shard_map/pallas_call | solution.py:81
  30.9 3.1 %collective-permute-start.8 = (bf16[128,1536]{1,0:T(8,128)(2,1)S(1)}, bf16[128,1536]{1,0:T(8,128)(2,1)S(1)}, u32[]{:S(2)}, u32[]{:S(2)}) collective-permute-start(bf16[128,1536]{1,0:T(8,128)(2,1)S(1)} %get-tuple-element.117), channel_id=1, source_target_pairs={{0,24},{8,16},{16,8},{24,0},{1,25},{9,17},{17,9},{25,1},{2,26},{10... | collective-permute-start | bytes 1179656 | tf_op jit(solution)/shard_map/ppermute | solution.py:32
  34.3 3.2 %collective-permute-done.5.refs_1_ = bf16[128,1536]{1,0:T(8,128)(2,1)S(1)} collective-permute-done((bf16[128,1536]{1,0:T(8,128)(2,1)S(1)}, bf16[128,1536]{1,0:T(8,128)(2,1)S(1)}, u32[]{:S(2)}, u32[]{:S(2)}) %collective-permute-start.5) | collective-permute-done | bytes 393248 | tf_op jit(solution)/shard_map/ppermute | solution.py:32
  37.5 7.3 %collective-permute-done.8.refs_3_ = bf16[128,1536]{1,0:T(8,128)(2,1)S(1)} collective-permute-done((bf16[128,1536]{1,0:T(8,128)(2,1)S(1)}, bf16[128,1536]{1,0:T(8,128)(2,1)S(1)}, u32[]{:S(2)}, u32[]{:S(2)}) %collective-permute-start.8) | collective-permute-done | bytes 393248 | tf_op jit(solution)/shard_map/ppermute | solution.py:32
  45.4 2.7 %collective-permute-start.9 = (bf16[128,768]{1,0:T(8,128)(2,1)S(1)}, bf16[128,768]{1,0:T(8,128)(2,1)S(1)}, u32[]{:S(2)}, u32[]{:S(2)}) collective-permute-start(bf16[128,768]{1,0:T(8,128)(2,1)S(1)} %get-tuple-element.122.refs_0_), channel_id=1, source_target_pairs={{0,24},{8,16},{16,8},{24,0},{1,25},{9,17},{17,9},{25,1},{2,26},{10... | collective-permute-start | bytes 589832 | tf_op jit(solution)/shard_map/ppermute | solution.py:32
  49.0 5.2 %collective-permute-done.9.refs_0_ = bf16[128,768]{1,0:T(8,128)(2,1)S(1)} collective-permute-done((bf16[128,768]{1,0:T(8,128)(2,1)S(1)}, bf16[128,768]{1,0:T(8,128)(2,1)S(1)}, u32[]{:S(2)}, u32[]{:S(2)}) %collective-permute-start.9) | collective-permute-done | bytes 196640 | tf_op jit(solution)/shard_map/ppermute | solution.py:32
  57.0 3.0 %shard_map.124 = (bf16[384,1280]{1,0:T(8,128)(2,1)S(1)}, f32[128,1]{1,0:T(8,128)S(1)}, f32[128,1]{1,0:T(8,128)S(1)}, f32[128,1]{1,0:T(8,128)S(1)}, bf16[384,768]...) custom-call(bf16[128,768]{1,0:T(8,128)(2,1)S(1)} %get-tuple-element.122.refs_0_, ...), custom_call_target="tpu_custom_call" | custom-call | flops 1509949440 | tf_op jit(solution)/shard_map/pallas_call | solution.py:81
  61.9 2.4 %collective-permute-start.19 = (bf16[128,1280]{1,0:T(8,128)(2,1)S(1)}, bf16[128,1280]{1,0:T(8,128)(2,1)S(1)}, u32[]{:S(2)}, u32[]{:S(2)}) collective-permute-start(bf16[128,1280]{1,0:T(8,128)(2,1)S(1)} %get-tuple-element.210), channel_id=1, source_target_pairs={{0,24},{8,16},{16,8},{24,0},{1,25},{9,17},{17,9},{25,1},{2,26},{10... | collective-permute-start | bytes 983048 | tf_op jit(solution)/shard_map/ppermute | solution.py:32
  67.1 6.4 %collective-permute-done.19.refs_0_ = bf16[128,1280]{1,0:T(8,128)(2,1)S(1)} collective-permute-done((bf16[128,1280]{1,0:T(8,128)(2,1)S(1)}, bf16[128,1280]{1,0:T(8,128)(2,1)S(1)}, u32[]{:S(2)}, u32[]{:S(2)}) %collective-permute-start.19) | collective-permute-done | bytes 327712 | tf_op jit(solution)/shard_map/ppermute | solution.py:32
  75.2 2.3 %collective-permute-start.26 = (bf16[128,768]{1,0:T(8,128)(2,1)S(1)}, bf16[128,768]{1,0:T(8,128)(2,1)S(1)}, u32[]{:S(2)}, u32[]{:S(2)}) collective-permute-start(bf16[128,768]{1,0:T(8,128)(2,1)S(1)} %get-tuple-element.147), channel_id=1, source_target_pairs={{0,24},{8,16},{16,8},{24,0},{1,25},{9,17},{17,9},{25,1},{2,26},{10... | collective-permute-start | bytes 589832 | tf_op jit(solution)/shard_map/ppermute | solution.py:32
  77.6 2.9 %collective-permute-done.13.refs_1_ = bf16[128,1280]{1,0:T(8,128)(2,1)S(1)} collective-permute-done((bf16[128,1280]{1,0:T(8,128)(2,1)S(1)}, bf16[128,1280]{1,0:T(8,128)(2,1)S(1)}, u32[]{:S(2)}, u32[]{:S(2)}) %collective-permute-start.13) | collective-permute-done | bytes 327712 | tf_op jit(solution)/shard_map/ppermute | solution.py:32
  83.4 2.2 shard_map.125
  88.1 4.4 %shard_map.126 = (bf16[128,1536]{1,0:T(8,128)(2,1)S(1)}, bf16[128,1536]{1,0:T(8,128)(2,1)S(1)}, bf16[128,1536]{1,0:T(8,128)(2,1)S(1)}, bf16[384,1280]{1,0:T(8,128)(2,1)S(1)}, bf16[384,1280]{1,0:T(8,128)(2,1)S(1)}) custom-call(bf16[384,1280]{1,0:T(8,128)(2,1)S(1)} %collective-permute-done.12.refs_0_.refs_4_.refs_5_, ...), custom_call_target="tpu_custom_call" | custom-call | flops 3019898880 | tf_op jit(solution)/shard_map/pallas_call | solution.py:81
  92.5 2.2 shard_map.127
  94.7 2.5 %collective-permute-start.18 = (bf16[128,1536]{1,0:T(8,128)(2,1)S(1)}, bf16[128,1536]{1,0:T(8,128)(2,1)S(1)}, u32[]{:S(2)}, u32[]{:S(2)}) collective-permute-start(bf16[128,1536]{1,0:T(8,128)(2,1)S(1)} %get-tuple-element.135), channel_id=1, source_target_pairs={{0,24},{8,16},{16,8},{24,0},{1,25},{9,17},{17,9},{25,1},{2,26},{10... | collective-permute-start | bytes 1179656 | tf_op jit(solution)/shard_map/ppermute | solution.py:32
  98.6 4.9 %collective-permute-done.23.refs_4_.refs_6_ = f32[128,1]{1,0:T(8,128)S(1)} collective-permute-done((f32[128,1]{1,0:T(8,128)S(1)}, f32[128,1]{1,0:T(8,128)S(1)}, u32[]{:S(2)}, u32[]{:S(2)}) %collective-permute-start.23) | collective-permute-done | bytes 544 | tf_op jit(solution)/shard_map/ppermute | solution.py:37
  104.1 3.7 %collective-permute-done.18.refs_3_ = bf16[128,1536]{1,0:T(8,128)(2,1)S(1)} collective-permute-done((bf16[128,1536]{1,0:T(8,128)(2,1)S(1)}, bf16[128,1536]{1,0:T(8,128)(2,1)S(1)}, u32[]{:S(2)}, u32[]{:S(2)}) %collective-permute-start.18) | collective-permute-done | bytes 393248 | tf_op jit(solution)/shard_map/ppermute | solution.py:32
  109.5 6.8 %collective-permute-done.15.refs_1_ = bf16[128,1536]{1,0:T(8,128)(2,1)S(1)} collective-permute-done((bf16[128,1536]{1,0:T(8,128)(2,1)S(1)}, bf16[128,1536]{1,0:T(8,128)(2,1)S(1)}, u32[]{:S(2)}, u32[]{:S(2)}) %collective-permute-start.15) | collective-permute-done | bytes 393248 | tf_op jit(solution)/shard_map/ppermute | solution.py:32
  119.2 2.4 %collective-permute-start.27 = (bf16[128,1664]{1,0:T(8,128)(2,1)S(1)}, bf16[128,1664]{1,0:T(8,128)(2,1)S(1)}, u32[]{:S(2)}, u32[]{:S(2)}) collective-permute-start(bf16[128,1664]{1,0:T(8,128)(2,1)S(1)} %shard_map.131.refs_0_), channel_id=1, source_target_pairs={{0,24},{8,16},{16,8},{24,0},{1,25},{9,17},{17,9},{25,1},{2,26},{10... | collective-permute-start | bytes 1277960 | tf_op jit(solution)/shard_map/ppermute | solution.py:32
  122.8 10.1 %collective-permute-done.27.refs_0_ = bf16[128,1664]{1,0:T(8,128)(2,1)S(1)} collective-permute-done((bf16[128,1664]{1,0:T(8,128)(2,1)S(1)}, bf16[128,1664]{1,0:T(8,128)(2,1)S(1)}, u32[]{:S(2)}, u32[]{:S(2)}) %collective-permute-start.27) | collective-permute-done | bytes 426016 | tf_op jit(solution)/shard_map/ppermute | solution.py:32
  136.4 3.4 %shard_map.136 = (bf16[128,1280]{1,0:T(8,128)(2,1)S(1)}, f32[1,1280]{1,0:T(1,128)S(1)}) custom-call(bf16[128,1664]{1,0:T(8,128)(2,1)S(1)} %collective-permute-done.27.refs_0_, f32[128,1]{1,0:T(8,128)S(1)} %get-tuple-element.134.refs_2_.refs_1_, bf16[128,1280]{1,0:T(8,128)(2,1)S(1)} %get-tuple-element.168.refs_2_, ...), custom_call_target="tpu_custom_call" | custom-call | flops 1006632960 | tf_op jit(solution)/shard_map/pallas_call | solution.py:81
  139.8 2.1 collective-permute-done.34.refs_1_
  143.6 4.4 %shard_map.134 = (bf16[384,1280]{1,0:T(8,128)(2,1)S(1)}, f32[1,1280]{1,0:T(1,128)S(1)}) custom-call(bf16[128,1664]{1,0:T(8,128)(2,1)S(1)} %shard_map.131.refs_0_, bf16[128,1664]{1,0:T(8,128)(2,1)S(1)} %collective-permute-done.34.refs_1_, bf16[128,1664]{1,0:T(8,128)(2,1)S(1)} %collective-permute-done.35.refs_2_, ...), custom_call_target="tpu_custom_call" | custom-call | flops 3019898880 | tf_op jit(solution)/shard_map/pallas_call | solution.py:81
  152.9 2.5 %convolution_convert_fusion.5 = bf16[1280,768]{1,0:T(8,128)(2,1)} fusion(bf16[512,1280]{1,0:T(8,128)(2,1)S(1)} %constant_dynamic-update-slice_fusion, bf16[512,768]{1,0:T(8,128)(2,1)S(1)} %get-tuple-element.159), kind=kOutput, calls=%fused_computation.20 | convolution fusion | flops 1007616000 | bytes 4063232 | tf_op jit(solution)/shard_map/dot_general | solution.py:22
  155.4 2.6 %shard_map.133 = (bf16[128,1280]{1,0:T(8,128)(2,1)S(1)}, f32[128,1]{1,0:T(8,128)}, bf16[128,768]{1,0:T(8,128)(2,1)S(1)}, bf16[128,768]{1,0:T(8,128)(2,1)S(1)}) custom-call(bf16[128,768]{1,0:T(8,128)(2,1)S(1)} %collective-permute-done.32.refs_0_, f32[128,1]{1,0:T(8,128)S(1)} %get-tuple-element.134.refs_2_.refs_1_, ...), custom_call_target="tpu_custom_call" | custom-call | tf_op jit(solution)/shard_map/pallas_call | solution.py:81
  157.9 2.6 %collective-permute-start.33 = (bf16[128,1280]{1,0:T(8,128)(2,1)S(1)}, bf16[128,1280]{1,0:T(8,128)(2,1)S(1)}, u32[]{:S(2)}, u32[]{:S(2)}) collective-permute-start(bf16[128,1280]{1,0:T(8,128)(2,1)S(1)} %get-tuple-element.154), channel_id=1, source_target_pairs={{0,24},{8,16},{16,8},{24,0},{1,25},{9,17},{17,9},{25,1},{2,26},{10... | collective-permute-start | bytes 983048 | tf_op jit(solution)/shard_map/ppermute | solution.py:32
  160.6 3.6 %shard_map.132 = (bf16[128,1280]{1,0:T(8,128)(2,1)S(1)}, bf16[128,1280]{1,0:T(8,128)(2,1)S(1)}, bf16[128,1280]{1,0:T(8,128)(2,1)S(1)}, f32[128,1]{1,0:T(8,128)},...) custom-call(bf16[128,768]{1,0:T(8,128)(2,1)S(1)} %get-tuple-element.150.refs_, ...), custom_call_target="tpu_custom_call" | custom-call | tf_op jit(solution)/shard_map/pallas_call | solution.py:81
  169.4 2.7 %collective-permute-start.40 = (bf16[128,768]{1,0:T(8,128)(2,1)S(1)}, bf16[128,768]{1,0:T(8,128)(2,1)S(1)}, u32[]{:S(2)}, u32[]{:S(2)}) collective-permute-start(bf16[128,768]{1,0:T(8,128)(2,1)S(1)} %get-tuple-element.174), channel_id=1, source_target_pairs={{0,24},{8,16},{16,8},{24,0},{1,25},{9,17},{17,9},{25,1},{2,26},{10... | collective-permute-start | bytes 589832 | tf_op jit(solution)/shard_map/ppermute | solution.py:32
  172.1 4.7 %collective-permute-done.30 = bf16[128,1280]{1,0:T(8,128)(2,1)S(1)} collective-permute-done((bf16[128,1280]{1,0:T(8,128)(2,1)S(1)}, bf16[128,1280]{1,0:T(8,128)(2,1)S(1)}, u32[]{:S(2)}, u32[]{:S(2)}) %collective-permute-start.30) | collective-permute-done | bytes 327712 | tf_op jit(solution)/shard_map/ppermute | solution.py:32
  176.8 2.2 shard_map.135
  180.6 4.1 %collective-permute-done.37.refs_1_ = bf16[128,768]{1,0:T(8,128)(2,1)S(1)} collective-permute-done((bf16[128,768]{1,0:T(8,128)(2,1)S(1)}, bf16[128,768]{1,0:T(8,128)(2,1)S(1)}, u32[]{:S(2)}, u32[]{:S(2)}) %collective-permute-start.37) | collective-permute-done | bytes 196640 | tf_op jit(solution)/shard_map/ppermute | solution.py:32
  184.8 6.5 %collective-permute-done.38.refs_2_ = bf16[128,768]{1,0:T(8,128)(2,1)S(1)} collective-permute-done((bf16[128,768]{1,0:T(8,128)(2,1)S(1)}, bf16[128,768]{1,0:T(8,128)(2,1)S(1)}, u32[]{:S(2)}, u32[]{:S(2)}) %collective-permute-start.38) | collective-permute-done | bytes 196640 | tf_op jit(solution)/shard_map/ppermute | solution.py:32
  192.9 2.5 %collective-permute-start.42 = (bf16[128,1664]{1,0:T(8,128)(2,1)S(1)}, bf16[128,1664]{1,0:T(8,128)(2,1)S(1)}, u32[]{:S(2)}, u32[]{:S(2)}) collective-permute-start(bf16[128,1664]{1,0:T(8,128)(2,1)S(1)} %shard_map.138.refs_0_), channel_id=1, source_target_pairs={{0,16},{8,24},{16,0},{24,8},{1,17},{9,25},{17,1},{25,9},{2,18},{10... | collective-permute-start | bytes 1277960 | tf_op jit(solution)/shard_map/ppermute | solution.py:32
  196.7 4.3 %collective-permute-done.43.refs_0_ = bf16[128,1664]{1,0:T(8,128)(2,1)S(1)} collective-permute-done((bf16[128,1664]{1,0:T(8,128)(2,1)S(1)}, bf16[128,1664]{1,0:T(8,128)(2,1)S(1)}, u32[]{:S(2)}, u32[]{:S(2)}) %collective-permute-start.43) | collective-permute-done | bytes 426016 | tf_op jit(solution)/shard_map/ppermute | solution.py:32
  201.0 3.4 %shard_map.139 = (bf16[128,1280]{1,0:T(8,128)(2,1)S(1)}, f32[1,1280]{1,0:T(1,128)S(1)}) custom-call(bf16[128,1664]{1,0:T(8,128)(2,1)S(1)} %collective-permute-done.43.refs_0_, f32[128,1]{1,0:T(8,128)S(1)} %get-tuple-element.119.refs_1_, bf16[128,1280]{1,0:T(8,128)(2,1)S(1)} %get-tuple-element.179.refs_2_, ...), custom_call_target="tpu_custom_call" | custom-call | flops 1006632960 | tf_op jit(solution)/shard_map/pallas_call | solution.py:81
  206.9 2.8 %fusion.6 = bf16[1280,768]{1,0:T(8,128)(2,1)S(1)} fusion(bf16[1280,768]{1,0:T(8,128)(2,1)} %convolution_convert_fusion.5, bf16[512,1280]{1,0:T(8,128)(2,1)S(1)} %constant_dynamic-update-slice_fusion.6, bf16[512,768]{1,0:T(8,128)(2,1)S(1)} %get-tuple-element.192), kind=kOutput, calls=%fused_computation.12 | convolution fusion | flops 1009582080 | bytes 6029312 | tf_op jit(solution)/shard_map/dot_general | solution.py:22
  210.3 4.6 %shard_map.140 = (bf16[128,1280]{1,0:T(8,128)(2,1)S(1)}, bf16[128,1280]{1,0:T(8,128)(2,1)S(1)}, bf16[128,1280]{1,0:T(8,128)(2,1)S(1)}, f32[1,1280]{1,0:T(1,128)S(1)}) custom-call(bf16[128,1664]{1,0:T(8,128)(2,1)S(1)} %shard_map.138.refs_0_, bf16[128,1664]{1,0:T(8,128)(2,1)S(1)} %collective-permute-done.41.refs_1_, ...), custom_call_target="tpu_custom_call" | custom-call | flops 1006632960 | tf_op jit(solution)/shard_map/pallas_call | solution.py:81
  216.8 1.9 collective-permute-start.46
  218.7 2.7 %fusion.3 = bf16[768,1280]{1,0:T(8,128)(2,1)} fusion(bf16[768,1280]{1,0:T(8,128)(2,1)S(1)} %collective-permute-done.49, bf16[768,1280]{1,0:T(8,128)(2,1)S(1)} %convolution_convert_fusion, bf16[512,1280]{1,0:T(8,128)(2,1)S(1)} %constant_dynamic-update-slice_fusion.8, bf16[128,768]{1,0:T(8,128)(2,1)S(1)} %get-tuple-element.195, ...), kind=kOutput, calls=%fused_computation.9 | convolution fusion | flops 1013121024 | bytes 7995392 | tf_op jit(solution)/shard_map/dot_general | solution.py:22
  223.2 2.7 %fusion.4 = bf16[1280,768]{1,0:T(8,128)(2,1)} fusion(bf16[1280,768]{1,0:T(8,128)(2,1)S(1)} %collective-permute-done.48, bf16[1280,768]{1,0:T(8,128)(2,1)S(1)} %convolution_convert_fusion.2, bf16[512,1280]{1,0:T(8,128)(2,1)S(1)} %constant_dynamic-update-slice_fusion.10, bf16[512,768]{1,0:T(8,128)(2,1)S(1)} %get-tuple-element.193), kind=kOutput, calls=%fused_computation.10 | convolution fusion | flops 1011548160 | bytes 7995392 | tf_op jit(solution)/shard_map/dot_general | solution.py:22
  225.9 2.7 %fusion.5 = bf16[1280,768]{1,0:T(8,128)(2,1)} fusion(bf16[1280,768]{1,0:T(8,128)(2,1)S(1)} %collective-permute-done.47, bf16[1280,768]{1,0:T(8,128)(2,1)S(1)} %convolution_convert_fusion.3, bf16[512,1280]{1,0:T(8,128)(2,1)S(1)} %constant_dynamic-update-slice_fusion.10, bf16[512,768]{1,0:T(8,128)(2,1)S(1)} %get-tuple-element.192), kind=kOutput, calls=%fused_computation.11 | convolution fusion | flops 1011548160 | bytes 7995392 | tf_op jit(solution)/shard_map/dot_general | solution.py:22
  230.5 2.6 %collective-permute-done.45 = bf16[128,1280]{1,0:T(8,128)(2,1)S(1)} collective-permute-done((bf16[128,1280]{1,0:T(8,128)(2,1)S(1)}, bf16[128,1280]{1,0:T(8,128)(2,1)S(1)}, u32[]{:S(2)}, u32[]{:S(2)}) %collective-permute-start.45) | collective-permute-done | bytes 327712 | tf_op jit(solution)/shard_map/ppermute | solution.py:32
  (150 shorter events, 58.8 us)
Async XLA Ops:
  1.2 9.5 %collective-permute-start.4 = (bf16[768,1280]{1,0:T(8,128)(2,1)}, bf16[768,1280]{1,0:T(8,128)(2,1)}, u32[]{:S(2)}, u32[]{:S(2)}) collective-permute-start(bf16[768,1280]{1,0:T(8,128)(2,1)} %bitcast.61), channel_id=1, source_target_pairs={{0,1},{1,0},{2,3},{3,2},{4,5},{5,4},{6,7},{7,6},{8,9},{9,8},{10,11... | collective-permute-start | bytes 5898248 | tf_op jit(solution)/shard_map/ppermute | solution.py:32
  4.0 15.1 %collective-permute-start = (bf16[144,1280]{1,0:T(8,128)(2,1)S(1)}, bf16[144,1280]{1,0:T(8,128)(2,1)S(1)}, u32[]{:S(2)}, u32[]{:S(2)}) collective-permute-start(bf16[144,1280]{1,0:T(8,128)(2,1)S(1)} %get-tuple-element.219), channel_id=1, source_target_pairs={{0,8},{8,0},{16,24},{24,16},{1,9},{9,1},{17,25},{25,17},{2,10},{10... | collective-permute-start | bytes 1105928 | tf_op jit(solution)/shard_map/ppermute | solution.py:32
  6.6 12.5 %collective-permute-start.1 = (bf16[144,1280]{1,0:T(8,128)(2,1)S(1)}, bf16[144,1280]{1,0:T(8,128)(2,1)S(1)}, u32[]{:S(2)}, u32[]{:S(2)}) collective-permute-start(bf16[144,1280]{1,0:T(8,128)(2,1)S(1)} %get-tuple-element.220), channel_id=1, source_target_pairs={{0,16},{8,24},{16,0},{24,8},{1,17},{9,25},{17,1},{25,9},{2,18},{10... | collective-permute-start | bytes 1105928 | tf_op jit(solution)/shard_map/ppermute | solution.py:32
  15.2 13.3 %collective-permute-start.7 = (bf16[144,1280]{1,0:T(8,128)(2,1)S(1)}, bf16[144,1280]{1,0:T(8,128)(2,1)S(1)}, u32[]{:S(2)}, u32[]{:S(2)}) collective-permute-start(bf16[144,1280]{1,0:T(8,128)(2,1)S(1)} %get-tuple-element.116), channel_id=1, source_target_pairs={{0,24},{8,16},{16,8},{24,0},{1,25},{9,17},{17,9},{25,1},{2,26},{10... | collective-permute-start | bytes 1105928 | tf_op jit(solution)/shard_map/ppermute | solution.py:32
  23.7 13.8 %collective-permute-start.5 = (bf16[128,1536]{1,0:T(8,128)(2,1)S(1)}, bf16[128,1536]{1,0:T(8,128)(2,1)S(1)}, u32[]{:S(2)}, u32[]{:S(2)}) collective-permute-start(bf16[128,1536]{1,0:T(8,128)(2,1)S(1)} %get-tuple-element.112), channel_id=1, source_target_pairs={{0,8},{8,0},{16,24},{24,16},{1,9},{9,1},{17,25},{25,17},{2,10},{10... | collective-permute-start | bytes 1179656 | tf_op jit(solution)/shard_map/ppermute | solution.py:32
  24.3 13.2 %collective-permute-start.6 = (bf16[128,1536]{1,0:T(8,128)(2,1)S(1)}, bf16[128,1536]{1,0:T(8,128)(2,1)S(1)}, u32[]{:S(2)}, u32[]{:S(2)}) collective-permute-start(bf16[128,1536]{1,0:T(8,128)(2,1)S(1)} %get-tuple-element.113), channel_id=1, source_target_pairs={{0,16},{8,24},{16,0},{24,8},{1,17},{9,25},{17,1},{25,9},{2,18},{10... | collective-permute-start | bytes 1179656 | tf_op jit(solution)/shard_map/ppermute | solution.py:32
  30.9 13.9 %collective-permute-start.8 = (bf16[128,1536]{1,0:T(8,128)(2,1)S(1)}, bf16[128,1536]{1,0:T(8,128)(2,1)S(1)}, u32[]{:S(2)}, u32[]{:S(2)}) collective-permute-start(bf16[128,1536]{1,0:T(8,128)(2,1)S(1)} %get-tuple-element.117), channel_id=1, source_target_pairs={{0,24},{8,16},{16,8},{24,0},{1,25},{9,17},{17,9},{25,1},{2,26},{10... | collective-permute-start | bytes 1179656 | tf_op jit(solution)/shard_map/ppermute | solution.py:32
  45.4 8.8 %collective-permute-start.9 = (bf16[128,768]{1,0:T(8,128)(2,1)S(1)}, bf16[128,768]{1,0:T(8,128)(2,1)S(1)}, u32[]{:S(2)}, u32[]{:S(2)}) collective-permute-start(bf16[128,768]{1,0:T(8,128)(2,1)S(1)} %get-tuple-element.122.refs_0_), channel_id=1, source_target_pairs={{0,24},{8,16},{16,8},{24,0},{1,25},{9,17},{17,9},{25,1},{2,26},{10... | collective-permute-start | bytes 589832 | tf_op jit(solution)/shard_map/ppermute | solution.py:32
  48.1 8.9 %collective-permute-start.10 = (bf16[128,768]{1,0:T(8,128)(2,1)S(1)}, bf16[128,768]{1,0:T(8,128)(2,1)S(1)}, u32[]{:S(2)}, u32[]{:S(2)}) collective-permute-start(bf16[128,768]{1,0:T(8,128)(2,1)S(1)} %get-tuple-element.122.refs_0_), channel_id=1, source_target_pairs={{0,8},{8,0},{16,24},{24,16},{1,9},{9,1},{17,25},{25,17},{2,10},{10... | collective-permute-start | bytes 589832 | tf_op jit(solution)/shard_map/ppermute | solution.py:32
  48.7 8.3 %collective-permute-start.11 = (bf16[128,768]{1,0:T(8,128)(2,1)S(1)}, bf16[128,768]{1,0:T(8,128)(2,1)S(1)}, u32[]{:S(2)}, u32[]{:S(2)}) collective-permute-start(bf16[128,768]{1,0:T(8,128)(2,1)S(1)} %get-tuple-element.122.refs_0_), channel_id=1, source_target_pairs={{0,16},{8,24},{16,0},{24,8},{1,17},{9,25},{17,1},{25,9},{2,18},{10... | collective-permute-start | bytes 589832 | tf_op jit(solution)/shard_map/ppermute | solution.py:32
  60.0 26.5 %collective-permute-start.12 = (bf16[384,1280]{1,0:T(8,128)(2,1)S(1)}, bf16[384,1280]{1,0:T(8,128)(2,1)S(1)}, u32[]{:S(2)}, u32[]{:S(2)}) collective-permute-start(bf16[384,1280]{1,0:T(8,128)(2,1)S(1)} %get-tuple-element.125), channel_id=1, source_target_pairs={{0,2},{2,4},{4,6},{6,0},{1,3},{3,5},{5,7},{7,1},{8,10},{10,12},{12... | collective-permute-start | bytes 2949128 | tf_op jit(solution)/shard_map/ppermute | solution.py:37
  61.9 11.7 %collective-permute-start.19 = (bf16[128,1280]{1,0:T(8,128)(2,1)S(1)}, bf16[128,1280]{1,0:T(8,128)(2,1)S(1)}, u32[]{:S(2)}, u32[]{:S(2)}) collective-permute-start(bf16[128,1280]{1,0:T(8,128)(2,1)S(1)} %get-tuple-element.210), channel_id=1, source_target_pairs={{0,24},{8,16},{16,8},{24,0},{1,25},{9,17},{17,9},{25,1},{2,26},{10... | collective-permute-start | bytes 983048 | tf_op jit(solution)/shard_map/ppermute | solution.py:32
  64.3 16.2 %collective-permute-start.13 = (bf16[128,1280]{1,0:T(8,128)(2,1)S(1)}, bf16[128,1280]{1,0:T(8,128)(2,1)S(1)}, u32[]{:S(2)}, u32[]{:S(2)}) collective-permute-start(bf16[128,1280]{1,0:T(8,128)(2,1)S(1)} %get-tuple-element.212), channel_id=1, source_target_pairs={{0,8},{8,0},{16,24},{24,16},{1,9},{9,1},{17,25},{25,17},{2,10},{10... | collective-permute-start | bytes 983048 | tf_op jit(solution)/shard_map/ppermute | solution.py:32
  64.8 17.2 %collective-permute-start.14 = (bf16[128,1280]{1,0:T(8,128)(2,1)S(1)}, bf16[128,1280]{1,0:T(8,128)(2,1)S(1)}, u32[]{:S(2)}, u32[]{:S(2)}) collective-permute-start(bf16[128,1280]{1,0:T(8,128)(2,1)S(1)} %get-tuple-element.211), channel_id=1, source_target_pairs={{0,16},{8,24},{16,0},{24,8},{1,17},{9,25},{17,1},{25,9},{2,18},{10... | collective-permute-start | bytes 983048 | tf_op jit(solution)/shard_map/ppermute | solution.py:32
  65.5 27.0 %collective-permute-start.17 = (bf16[128,1280]{1,0:T(8,128)(2,1)S(1)}, bf16[128,1280]{1,0:T(8,128)(2,1)S(1)}, u32[]{:S(2)}, u32[]{:S(2)}) collective-permute-start(bf16[128,1280]{1,0:T(8,128)(2,1)S(1)} %get-tuple-element.121), channel_id=1, source_target_pairs={{0,2},{2,4},{4,6},{6,0},{1,3},{3,5},{5,7},{7,1},{8,10},{10,12},{12... | collective-permute-start | bytes 983048 | tf_op jit(solution)/shard_map/ppermute | solution.py:37
  75.2 41.6 %collective-permute-start.26 = (bf16[128,768]{1,0:T(8,128)(2,1)S(1)}, bf16[128,768]{1,0:T(8,128)(2,1)S(1)}, u32[]{:S(2)}, u32[]{:S(2)}) collective-permute-start(bf16[128,768]{1,0:T(8,128)(2,1)S(1)} %get-tuple-element.147), channel_id=1, source_target_pairs={{0,24},{8,16},{16,8},{24,0},{1,25},{9,17},{17,9},{25,1},{2,26},{10... | collective-permute-start | bytes 589832 | tf_op jit(solution)/shard_map/ppermute | solution.py:32
  80.5 16.9 %collective-permute-start.22 = (f32[128,1]{1,0:T(8,128)S(1)}, f32[128,1]{1,0:T(8,128)S(1)}, u32[]{:S(2)}, u32[]{:S(2)}) collective-permute-start(f32[128,1]{1,0:T(8,128)S(1)} %get-tuple-element.143), channel_id=1, source_target_pairs={{0,24},{8,16},{16,8},{24,0},{1,25},{9,17},{17,9},{25,1},{2,26},{10... | collective-permute-start | bytes 1544 | tf_op jit(solution)/shard_map/ppermute | solution.py:32
  82.0 15.3 %collective-permute-start.21 = (f32[128,1]{1,0:T(8,128)S(1)}, f32[128,1]{1,0:T(8,128)S(1)}, u32[]{:S(2)}, u32[]{:S(2)}) collective-permute-start(f32[128,1]{1,0:T(8,128)S(1)} %get-tuple-element.141), channel_id=1, source_target_pairs={{0,16},{8,24},{16,0},{24,8},{1,17},{9,25},{17,1},{25,9},{2,18},{10... | collective-permute-start | bytes 1544 | tf_op jit(solution)/shard_map/ppermute | solution.py:32
  86.5 10.8 %collective-permute-start.20 = (f32[128,1]{1,0:T(8,128)S(1)}, f32[128,1]{1,0:T(8,128)S(1)}, u32[]{:S(2)}, u32[]{:S(2)}) collective-permute-start(f32[128,1]{1,0:T(8,128)S(1)} %get-tuple-element.139), channel_id=1, source_target_pairs={{0,8},{8,0},{16,24},{24,16},{1,9},{9,1},{17,25},{25,17},{2,10},{10... | collective-permute-start | bytes 1544 | tf_op jit(solution)/shard_map/ppermute | solution.py:32
  94.7 13.1 %collective-permute-start.18 = (bf16[128,1536]{1,0:T(8,128)(2,1)S(1)}, bf16[128,1536]{1,0:T(8,128)(2,1)S(1)}, u32[]{:S(2)}, u32[]{:S(2)}) collective-permute-start(bf16[128,1536]{1,0:T(8,128)(2,1)S(1)} %get-tuple-element.135), channel_id=1, source_target_pairs={{0,24},{8,16},{16,8},{24,0},{1,25},{9,17},{17,9},{25,1},{2,26},{10... | collective-permute-start | bytes 1179656 | tf_op jit(solution)/shard_map/ppermute | solution.py:32
  97.5 18.8 %collective-permute-start.15 = (bf16[128,1536]{1,0:T(8,128)(2,1)S(1)}, bf16[128,1536]{1,0:T(8,128)(2,1)S(1)}, u32[]{:S(2)}, u32[]{:S(2)}) collective-permute-start(bf16[128,1536]{1,0:T(8,128)(2,1)S(1)} %get-tuple-element.131), channel_id=1, source_target_pairs={{0,8},{8,0},{16,24},{24,16},{1,9},{9,1},{17,25},{25,17},{2,10},{10... | collective-permute-start | bytes 1179656 | tf_op jit(solution)/shard_map/ppermute | solution.py:32
  98.1 18.2 %collective-permute-start.16 = (bf16[128,1536]{1,0:T(8,128)(2,1)S(1)}, bf16[128,1536]{1,0:T(8,128)(2,1)S(1)}, u32[]{:S(2)}, u32[]{:S(2)}) collective-permute-start(bf16[128,1536]{1,0:T(8,128)(2,1)S(1)} %get-tuple-element.132), channel_id=1, source_target_pairs={{0,16},{8,24},{16,0},{24,8},{1,17},{9,25},{17,1},{25,9},{2,18},{10... | collective-permute-start | bytes 1179656 | tf_op jit(solution)/shard_map/ppermute | solution.py:32
  103.5 15.2 %collective-permute-start.24 = (bf16[128,768]{1,0:T(8,128)(2,1)S(1)}, bf16[128,768]{1,0:T(8,128)(2,1)S(1)}, u32[]{:S(2)}, u32[]{:S(2)}) collective-permute-start(bf16[128,768]{1,0:T(8,128)(2,1)S(1)} %get-tuple-element.145), channel_id=1, source_target_pairs={{0,8},{8,0},{16,24},{24,16},{1,9},{9,1},{17,25},{25,17},{2,10},{10... | collective-permute-start | bytes 589832 | tf_op jit(solution)/shard_map/ppermute | solution.py:32
  107.8 10.9 %collective-permute-start.25 = (bf16[128,768]{1,0:T(8,128)(2,1)S(1)}, bf16[128,768]{1,0:T(8,128)(2,1)S(1)}, u32[]{:S(2)}, u32[]{:S(2)}) collective-permute-start(bf16[128,768]{1,0:T(8,128)(2,1)S(1)} %get-tuple-element.146), channel_id=1, source_target_pairs={{0,16},{8,24},{16,0},{24,8},{1,17},{9,25},{17,1},{25,9},{2,18},{10... | collective-permute-start | bytes 589832 | tf_op jit(solution)/shard_map/ppermute | solution.py:32
  119.2 13.7 %collective-permute-start.27 = (bf16[128,1664]{1,0:T(8,128)(2,1)S(1)}, bf16[128,1664]{1,0:T(8,128)(2,1)S(1)}, u32[]{:S(2)}, u32[]{:S(2)}) collective-permute-start(bf16[128,1664]{1,0:T(8,128)(2,1)S(1)} %shard_map.131.refs_0_), channel_id=1, source_target_pairs={{0,24},{8,16},{16,8},{24,0},{1,25},{9,17},{17,9},{25,1},{2,26},{10... | collective-permute-start | bytes 1277960 | tf_op jit(solution)/shard_map/ppermute | solution.py:32
  121.6 20.4 %collective-permute-start.34 = (bf16[128,1664]{1,0:T(8,128)(2,1)S(1)}, bf16[128,1664]{1,0:T(8,128)(2,1)S(1)}, u32[]{:S(2)}, u32[]{:S(2)}) collective-permute-start(bf16[128,1664]{1,0:T(8,128)(2,1)S(1)} %shard_map.131.refs_0_), channel_id=1, source_target_pairs={{0,8},{8,0},{16,24},{24,16},{1,9},{9,1},{17,25},{25,17},{2,10},{10... | collective-permute-start | bytes 1277960 | tf_op jit(solution)/shard_map/ppermute | solution.py:32
  122.1 21.5 %collective-permute-start.35 = (bf16[128,1664]{1,0:T(8,128)(2,1)S(1)}, bf16[128,1664]{1,0:T(8,128)(2,1)S(1)}, u32[]{:S(2)}, u32[]{:S(2)}) collective-permute-start(bf16[128,1664]{1,0:T(8,128)(2,1)S(1)} %shard_map.131.refs_0_), channel_id=1, source_target_pairs={{0,16},{8,24},{16,0},{24,8},{1,17},{9,25},{17,1},{25,9},{2,18},{10... | collective-permute-start | bytes 1277960 | tf_op jit(solution)/shard_map/ppermute | solution.py:32
  132.9 15.7 %collective-permute-start.28 = (bf16[128,768]{1,0:T(8,128)(2,1)S(1)}, bf16[128,768]{1,0:T(8,128)(2,1)S(1)}, u32[]{:S(2)}, u32[]{:S(2)}) collective-permute-start(bf16[128,768]{1,0:T(8,128)(2,1)S(1)} %get-tuple-element.150.refs_0_), channel_id=1, source_target_pairs={{0,8},{8,0},{16,24},{24,16},{1,9},{9,1},{17,25},{25,17},{2,10},{10... | collective-permute-start | bytes 589832 | tf_op jit(solution)/shard_map/ppermute | solution.py:32
  134.5 14.2 %collective-permute-start.29 = (bf16[128,768]{1,0:T(8,128)(2,1)S(1)}, bf16[128,768]{1,0:T(8,128)(2,1)S(1)}, u32[]{:S(2)}, u32[]{:S(2)}) collective-permute-start(bf16[128,768]{1,0:T(8,128)(2,1)S(1)} %get-tuple-element.150.refs_0_), channel_id=1, source_target_pairs={{0,16},{8,24},{16,0},{24,8},{1,17},{9,25},{17,1},{25,9},{2,18},{10... | collective-permute-start | bytes 589832 | tf_op jit(solution)/shard_map/ppermute | solution.py:32
  135.8 13.4 %collective-permute-start.32 = (bf16[128,768]{1,0:T(8,128)(2,1)S(1)}, bf16[128,768]{1,0:T(8,128)(2,1)S(1)}, u32[]{:S(2)}, u32[]{:S(2)}) collective-permute-start(bf16[128,768]{1,0:T(8,128)(2,1)S(1)} %get-tuple-element.150.refs_0_), channel_id=1, source_target_pairs={{0,24},{8,16},{16,8},{24,0},{1,25},{9,17},{17,9},{25,1},{2,26},{10... | collective-permute-start | bytes 589832 | tf_op jit(solution)/shard_map/ppermute | solution.py:32
  142.0 25.7 %collective-permute-start.39 = (bf16[128,1280]{1,0:T(8,128)(2,1)S(1)}, bf16[128,1280]{1,0:T(8,128)(2,1)S(1)}, u32[]{:S(2)}, u32[]{:S(2)}) collective-permute-start(bf16[128,1280]{1,0:T(8,128)(2,1)S(1)} %get-tuple-element.173), channel_id=1, source_target_pairs={{0,6},{2,0},{4,2},{6,4},{1,7},{3,1},{5,3},{7,5},{8,14},{10,8},{12,... | collective-permute-start | bytes 983048 | tf_op jit(solution)/shard_map/ppermute | solution.py:37
  148.1 28.7 %collective-permute-start.36 = (bf16[384,1280]{1,0:T(8,128)(2,1)S(1)}, bf16[384,1280]{1,0:T(8,128)(2,1)S(1)}, u32[]{:S(2)}, u32[]{:S(2)}) collective-permute-start(bf16[384,1280]{1,0:T(8,128)(2,1)S(1)} %get-tuple-element.156), channel_id=1, source_target_pairs={{0,6},{2,0},{4,2},{6,4},{1,7},{3,1},{5,3},{7,5},{8,14},{10,8},{12,... | collective-permute-start | bytes 2949128 | tf_op jit(solution)/shard_map/ppermute | solution.py:37
  157.9 57.1 %collective-permute-start.33 = (bf16[128,1280]{1,0:T(8,128)(2,1)S(1)}, bf16[128,1280]{1,0:T(8,128)(2,1)S(1)}, u32[]{:S(2)}, u32[]{:S(2)}) collective-permute-start(bf16[128,1280]{1,0:T(8,128)(2,1)S(1)} %get-tuple-element.154), channel_id=1, source_target_pairs={{0,24},{8,16},{16,8},{24,0},{1,25},{9,17},{17,9},{25,1},{2,26},{10... | collective-permute-start | bytes 983048 | tf_op jit(solution)/shard_map/ppermute | solution.py:32
  164.2 12.6 %collective-permute-start.30 = (bf16[128,1280]{1,0:T(8,128)(2,1)S(1)}, bf16[128,1280]{1,0:T(8,128)(2,1)S(1)}, u32[]{:S(2)}, u32[]{:S(2)}) collective-permute-start(bf16[128,1280]{1,0:T(8,128)(2,1)S(1)} %get-tuple-element.152), channel_id=1, source_target_pairs={{0,8},{8,0},{16,24},{24,16},{1,9},{9,1},{17,25},{25,17},{2,10},{10... | collective-permute-start | bytes 983048 | tf_op jit(solution)/shard_map/ppermute | solution.py:32
  164.8 45.5 %collective-permute-start.31 = (bf16[128,1280]{1,0:T(8,128)(2,1)S(1)}, bf16[128,1280]{1,0:T(8,128)(2,1)S(1)}, u32[]{:S(2)}, u32[]{:S(2)}) collective-permute-start(bf16[128,1280]{1,0:T(8,128)(2,1)S(1)} %get-tuple-element.153), channel_id=1, source_target_pairs={{0,16},{8,24},{16,0},{24,8},{1,17},{9,25},{17,1},{25,9},{2,18},{10... | collective-permute-start | bytes 983048 | tf_op jit(solution)/shard_map/ppermute | solution.py:32
  169.4 15.4 %collective-permute-start.40 = (bf16[128,768]{1,0:T(8,128)(2,1)S(1)}, bf16[128,768]{1,0:T(8,128)(2,1)S(1)}, u32[]{:S(2)}, u32[]{:S(2)}) collective-permute-start(bf16[128,768]{1,0:T(8,128)(2,1)S(1)} %get-tuple-element.174), channel_id=1, source_target_pairs={{0,24},{8,16},{16,8},{24,0},{1,25},{9,17},{17,9},{25,1},{2,26},{10... | collective-permute-start | bytes 589832 | tf_op jit(solution)/shard_map/ppermute | solution.py:32
  180.6 10.7 %collective-permute-start.38 = (bf16[128,768]{1,0:T(8,128)(2,1)S(1)}, bf16[128,768]{1,0:T(8,128)(2,1)S(1)}, u32[]{:S(2)}, u32[]{:S(2)}) collective-permute-start(bf16[128,768]{1,0:T(8,128)(2,1)S(1)} %get-tuple-element.172), channel_id=1, source_target_pairs={{0,16},{8,24},{16,0},{24,8},{1,17},{9,25},{17,1},{25,9},{2,18},{10... | collective-permute-start | bytes 589832 | tf_op jit(solution)/shard_map/ppermute | solution.py:32
  191.8 9.2 %collective-permute-start.43 = (bf16[128,1664]{1,0:T(8,128)(2,1)S(1)}, bf16[128,1664]{1,0:T(8,128)(2,1)S(1)}, u32[]{:S(2)}, u32[]{:S(2)}) collective-permute-start(bf16[128,1664]{1,0:T(8,128)(2,1)S(1)} %shard_map.138.refs_0_), channel_id=1, source_target_pairs={{0,24},{8,16},{16,8},{24,0},{1,25},{9,17},{17,9},{25,1},{2,26},{10... | collective-permute-start | bytes 1277960 | tf_op jit(solution)/shard_map/ppermute | solution.py:32
  191.9 12.5 %collective-permute-start.41 = (bf16[128,1664]{1,0:T(8,128)(2,1)S(1)}, bf16[128,1664]{1,0:T(8,128)(2,1)S(1)}, u32[]{:S(2)}, u32[]{:S(2)}) collective-permute-start(bf16[128,1664]{1,0:T(8,128)(2,1)S(1)} %shard_map.138.refs_0_), channel_id=1, source_target_pairs={{0,8},{8,0},{16,24},{24,16},{1,9},{9,1},{17,25},{25,17},{2,10},{10... | collective-permute-start | bytes 1277960 | tf_op jit(solution)/shard_map/ppermute | solution.py:32
  192.9 12.5 %collective-permute-start.42 = (bf16[128,1664]{1,0:T(8,128)(2,1)S(1)}, bf16[128,1664]{1,0:T(8,128)(2,1)S(1)}, u32[]{:S(2)}, u32[]{:S(2)}) collective-permute-start(bf16[128,1664]{1,0:T(8,128)(2,1)S(1)} %shard_map.138.refs_0_), channel_id=1, source_target_pairs={{0,16},{8,24},{16,0},{24,8},{1,17},{9,25},{17,1},{25,9},{2,18},{10... | collective-permute-start | bytes 1277960 | tf_op jit(solution)/shard_map/ppermute | solution.py:32
  201.0 15.8 %collective-permute-start.49 = (bf16[768,1280]{1,0:T(8,128)(2,1)S(1)}, bf16[768,1280]{1,0:T(8,128)(2,1)S(1)}, u32[]{:S(2)}, u32[]{:S(2)}) collective-permute-start(bf16[768,1280]{1,0:T(8,128)(2,1)S(1)} %fusion.8), channel_id=1, source_target_pairs={{0,1},{1,0},{2,3},{3,2},{4,5},{5,4},{6,7},{7,6},{8,9},{9,8},{10,11... | collective-permute-start | bytes 5898248 | tf_op jit(solution)/shard_map/ppermute | solution.py:32
  206.8 14.7 %collective-permute-start.48 = (bf16[1280,768]{1,0:T(8,128)(2,1)S(1)}, bf16[1280,768]{1,0:T(8,128)(2,1)S(1)}, u32[]{:S(2)}, u32[]{:S(2)}) collective-permute-start(bf16[1280,768]{1,0:T(8,128)(2,1)S(1)} %fusion.7), channel_id=1, source_target_pairs={{0,1},{1,0},{2,3},{3,2},{4,5},{5,4},{6,7},{7,6},{8,9},{9,8},{10,11... | collective-permute-start | bytes 5898248 | tf_op jit(solution)/shard_map/ppermute | solution.py:32
  209.7 11.8 %collective-permute-start.47 = (bf16[1280,768]{1,0:T(8,128)(2,1)S(1)}, bf16[1280,768]{1,0:T(8,128)(2,1)S(1)}, u32[]{:S(2)}, u32[]{:S(2)}) collective-permute-start(bf16[1280,768]{1,0:T(8,128)(2,1)S(1)} %fusion.6), channel_id=1, source_target_pairs={{0,1},{1,0},{2,3},{3,2},{4,5},{5,4},{6,7},{7,6},{8,9},{9,8},{10,11... | collective-permute-start | bytes 5898248 | tf_op jit(solution)/shard_map/ppermute | solution.py:32
  215.1 13.5 %collective-permute-start.44 = (bf16[128,1280]{1,0:T(8,128)(2,1)S(1)}, bf16[128,1280]{1,0:T(8,128)(2,1)S(1)}, u32[]{:S(2)}, u32[]{:S(2)}) collective-permute-start(bf16[128,1280]{1,0:T(8,128)(2,1)S(1)} %get-tuple-element.188), channel_id=1, source_target_pairs={{0,8},{8,0},{16,24},{24,16},{1,9},{9,1},{17,25},{25,17},{2,10},{10... | collective-permute-start | bytes 983048 | tf_op jit(solution)/shard_map/ppermute | solution.py:32
  216.2 16.9 %collective-permute-start.45 = (bf16[128,1280]{1,0:T(8,128)(2,1)S(1)}, bf16[128,1280]{1,0:T(8,128)(2,1)S(1)}, u32[]{:S(2)}, u32[]{:S(2)}) collective-permute-start(bf16[128,1280]{1,0:T(8,128)(2,1)S(1)} %get-tuple-element.189), channel_id=1, source_target_pairs={{0,16},{8,24},{16,0},{24,8},{1,17},{9,25},{17,1},{25,9},{2,18},{10... | collective-permute-start | bytes 983048 | tf_op jit(solution)/shard_map/ppermute | solution.py:32
  216.8 16.3 %collective-permute-start.46 = (bf16[128,1280]{1,0:T(8,128)(2,1)S(1)}, bf16[128,1280]{1,0:T(8,128)(2,1)S(1)}, u32[]{:S(2)}, u32[]{:S(2)}) collective-permute-start(bf16[128,1280]{1,0:T(8,128)(2,1)S(1)} %get-tuple-element.180), channel_id=1, source_target_pairs={{0,24},{8,16},{16,8},{24,0},{1,25},{9,17},{17,9},{25,1},{2,26},{10... | collective-permute-start | bytes 983048 | tf_op jit(solution)/shard_map/ppermute | solution.py:32
  221.5 12.0 %collective-permute-start.51 = (f32[1,1280]{1,0:T(1,128)S(1)}, f32[1,1280]{1,0:T(1,128)S(1)}, u32[]{:S(2)}, u32[]{:S(2)}) collective-permute-start(f32[1,1280]{1,0:T(1,128)S(1)} %add.115), channel_id=1, source_target_pairs={{0,8},{8,0},{16,24},{24,16},{1,9},{9,1},{17,25},{25,17},{2,10},{10... | collective-permute-start | bytes 15368 | tf_op jit(solution)/shard_map/ppermute | solution.py:32
  222.6 10.9 %collective-permute-start.52 = (f32[1,1280]{1,0:T(1,128)S(1)}, f32[1,1280]{1,0:T(1,128)S(1)}, u32[]{:S(2)}, u32[]{:S(2)}) collective-permute-start(f32[1,1280]{1,0:T(1,128)S(1)} %add.115), channel_id=1, source_target_pairs={{0,16},{8,24},{16,0},{24,8},{1,17},{9,25},{17,1},{25,9},{2,18},{10... | collective-permute-start | bytes 15368 | tf_op jit(solution)/shard_map/ppermute | solution.py:32
  (14 other events, 74.6 us)

commit v6 on v5

--- a/solution.py
+++ b/solution.py
@@ -141,6 +141,12 @@
     return pl.ds(pl.multiple_of(tile * size, size), size)
 
 
+def in_lanes(scalar):
+    coarse = scalar.astype(bf16).astype(f32)
+    lane = lax.broadcasted_iota(jnp.int32, (scalar.shape[0], LANES), 1)
+    return jnp.where(lane == 0, coarse, jnp.where(lane == 1, scalar - coarse, 0.0)).astype(bf16)
+
+
 def split_rows(rows_ref, mask_ref, other_ref, own_ref):
     rows = rows_ref[...]
     chosen = mask_ref[...] > 0.5
@@ -164,7 +170,12 @@
         for index, ref in enumerate(block_refs):
             place = slice(index * block_rows, (index + 1) * block_rows)
             block = ref[:block_rows]
-            gained_ref[place] = (block.astype(f32) * gain_ref[...]).astype(bf16)
+            wide = block.astype(f32)
+            gained_ref[place] = (wide * gain_ref[...]).astype(bf16)
+            if not routed:
+                squares = jnp.sum(wide * wide, axis=-1, keepdims=True)
+                tails = [ref.at[:, 2 * units :] for ref in part_refs]
+                store_parts(tails, slice(None), in_lanes(squares))
             if routed:
                 out_refs[-1][place] = block
                 tiles = block_rows // TILE
@@ -194,7 +205,8 @@
         body,
         (*blocks, gain_part, expert if routed else mask),
         (*gate_pair, *up_pair),
-        [jax.ShapeDtypeStruct((part_rows, 2 * units), bf16)] * parts_count
+        [jax.ShapeDtypeStruct((part_rows, 2 * units + LANES * int(not routed)), bf16)]
+        * parts_count
         + [jax.ShapeDtypeStruct((rows, width), bf16)] * 2
         + [jax.ShapeDtypeStruct((rows, 1), f32)] * passes
         + [jax.ShapeDtypeStruct((rows, width), bf16)] * int(routed),
@@ -203,43 +215,44 @@
     return outs[:parts_count], outs[parts_count : parts_count + 2], outs[parts_count + 2 :]
 
 
-def row_scale(blocks, features, summed):
-    rows = blocks[0].shape[0]
+def row_scale(block):
+    rows, features = block.shape
 
     def body(operand_refs, weight_refs, out_refs, scratch):
-        total = jnp.zeros((rows, 1), f32)
-        for ref in operand_refs:
-            wide = ref[...].astype(f32)
-            if not summed:
-                wide = jnp.sum(wide * wide, axis=-1, keepdims=True)
-            total = total + wide
+        wide = operand_refs[0][...].astype(f32)
+        total = jnp.sum(wide * wide, axis=-1, keepdims=True)
         out_refs[0][...] = lax.rsqrt(total / features + epsilon)
 
-    (scale,) = kernel_call(body, blocks, (), [jax.ShapeDtypeStruct((rows, 1), f32)], [])
+    (scale,) = kernel_call(body, (block,), (), [jax.ShapeDtypeStruct((rows, 1), f32)], [])
     return scale
 
 
-def activate(parts, inverse):
-    rows, both = parts[0].shape
-    units = both // 2
+def activate(parts, units, features, inverse=None):
+    rows = parts[0].shape[0]
+    count = len(parts)
 
     def body(operand_refs, weight_refs, out_refs, scratch):
-        *part_refs, inverse_ref = operand_refs
+        part_refs = operand_refs[:count]
         total = part_refs[0][...].astype(f32)
         for ref in part_refs[1:]:
             total = total + ref[...].astype(f32)
-        total = total * inverse_ref[...]
-        gate, up = total[:, :units], total[:, units:]
+        if inverse is None:
+            squares = jnp.sum(total[:, 2 * units :], axis=-1, keepdims=True)
+            scale = lax.rsqrt(squares / features + epsilon)
+        else:
+            scale = operand_refs[-1][...]
+        gate, up = total[:, :units] * scale, total[:, units : 2 * units] * scale
         out_refs[0][...] = gate
         out_refs[1][...] = up
         out_refs[2][...] = (gate / (1.0 + jnp.exp(-gate)) * up).astype(bf16)
+        out_refs[3][...] = scale
 
     return kernel_call(
         body,
-        (*parts, inverse),
+        tuple(parts) + (() if inverse is None else (inverse,)),
         (),
         [jax.ShapeDtypeStruct((rows, units), f32)] * 2
-        + [jax.ShapeDtypeStruct((rows, units), bf16)],
+        + [jax.ShapeDtypeStruct((rows, units), bf16), jax.ShapeDtypeStruct((rows, 1), f32)],
         [],
     )
 
@@ -259,11 +272,10 @@
 
     def body(operand_refs, weight_refs, out_refs, scratch):
         *block_refs, mask_ref, hidden_ref = operand_refs
-        row_refs, square_refs = out_refs[:out_count], out_refs[out_count:-2]
-        joined, square_ref = scratch
+        row_refs = out_refs[:out_count]
+        (joined,) = scratch
         join(joined, block_refs, slice(None))
         split_rows(joined, mask_ref, *out_refs[-2:])
-        square_ref[...] = jnp.zeros_like(square_ref)
         own, other = weight_refs
 
         def visit(columns):
@@ -273,24 +285,20 @@
                 dot(joined[...], other[:, columns], (1, 0)),
             ).astype(bf16)
             out = (hidden_ref[:, columns].astype(f32) + ffn.astype(f32)).astype(bf16)
-            wide = out.astype(f32)
-            square_ref[...] += jnp.sum(wide * wide, axis=-1, keepdims=True)
             store_parts(row_refs, columns, out)
 
         each_tile(width, visit)
-        store_parts(square_refs, slice(None), square_ref[...])
 
     outs = kernel_call(
         body,
         (*blocks, mask, hidden),
         down_pair,
         [jax.ShapeDtypeStruct((rows // out_count, width), bf16)] * out_count
-        + [jax.ShapeDtypeStruct((part_rows, 1), f32)] * count
         + [jax.ShapeDtypeStruct((rows, units), bf16)] * 2,
-        [pltpu.VMEM((rows, units), bf16), pltpu.VMEM((rows, 1), f32)],
+        [pltpu.VMEM((rows, units), bf16)],
         weight_cost=0 if in_parts else 1,
     )
-    return outs[:out_count], outs[out_count:-2], outs[-2:]
+    return outs[:out_count], outs[-2:]
 
 
 def act_grad_parts(blocks, part_rows, mask, down_pair):
@@ -344,11 +352,7 @@
         )
         out_ref[:, :units] = gate_grad.astype(bf16)
         out_ref[:, units : 2 * units] = up_grad.astype(bf16)
-        coarse = shrink.astype(bf16).astype(f32)
-        lane = lax.broadcasted_iota(jnp.int32, (rows, LANES), 1)
-        out_ref[:, 2 * units :] = jnp.where(
-            lane == 0, coarse, jnp.where(lane == 1, shrink - coarse, 0.0)
-        ).astype(bf16)
+        out_ref[:, 2 * units :] = in_lanes(shrink)
 
     (sent,) = kernel_call(
         body,
@@ -463,7 +467,7 @@
     gate_pair, up_pair, down_pair = weights[:2], weights[2:4], weights[4:]
     quarters[-1] = after(quarters[-1], *weights)
     blocks = sent(quarters)
-    inverse = row_scale([own_tokens], features, False)
+    inverse = row_scale(own_tokens)
 
     parts, gained, masks, hidden = [], [], [], []
     for group in groups:
@@ -475,22 +479,19 @@
         masks.append(choices)
         hidden.append(joined)
     masks = list(zip(*masks))
-    gate, up, activated = activate(sent(parts), inverse)
+    gate, up, activated, _ = activate(sent(parts), units, features, inverse)
     kept = [(hidden, gained, inverse, gate, up)]
     first_activated = gather_rows(activated, dp_count)
-    next_hidden, squares, first_rows = [], [], []
+    next_hidden, first_rows = [], []
     for index in reversed(range(len(groups))):
         near = first_activated[groups[index]]
         if next_hidden:
             near = [after(near[0], next_hidden[0]), *near[1:]]
-        (out,), square, split = add_down(near, masks[0][index], down_pair, hidden[index], False)
+        (out,), split = add_down(near, masks[0][index], down_pair, hidden[index], False)
         next_hidden.insert(0, out)
-        squares = [*square, *squares]
         first_rows.insert(0, split)
     hidden = moved(next_hidden, 1)
     grad_blocks = sent([cotangent_quarter(step, next_hidden[0]) for step in range(dp_count)])
-    squares = [after(square, grad_blocks[-1]) for square in squares]
-    inverse = shifted(row_scale(sent(squares), features, True), "pipe", 1)
     act_parts, grad = [], []
     for group, mask in zip(groups, masks[1]):
         made, joined = act_grad_parts(grad_blocks[group], rows, mask, down_pair)
@@ -507,7 +508,7 @@
         made, scaled, _ = hidden_parts([rows_in], rows, gain_part, mask, gate_pair, up_pair)
         parts += made
         gained.append(scaled)
-    gate, up, activated = activate(sent(parts), inverse)
+    gate, up, activated, inverse = activate(sent(parts), units, features)
     kept.append((hidden, gained, inverse, gate, up))
 
     gain_sum = jnp.zeros((1, width), f32)
@@ -554,7 +555,7 @@
             }
             out_parts, last_rows = [], []
             for group, choice, rows_in in zip(groups, masks[1], hidden):
-                made, _, split = add_down(
+                made, split = add_down(
                     last_activated[group], choice, down_pair, rows_in, True
                 )
                 out_parts += made

time: 235 us -> 233 us (level)
  waiting for transfers between devices: 87.9 us -> 93.9 us
  starting transfers between devices: 63.2 us -> 60 us
  matrix products: 22.1 us -> 19.3 us
    ppermute x49 -> x46, waiting for transfers between devices: 82 us -> 90.5 us  [swap(): return lax.ppermute(block, axis, partner_route(lax.axis_size(axis), step))]
    ppermute x49 -> x46, starting transfers between devices: 57.7 us -> 54.6 us  [swap(): return lax.ppermute(block, axis, partner_route(lax.axis_size(axis), step))]
    dot_general x12, matrix products: 22.1 us -> 19.3 us  [dot(): lax.dot_general(former, latter, ((contract[:1], contract[1:]), ((), ())),...]
    ppermute x5 -> x4, waiting for transfers between devices: 5.88 us -> 3.33 us  [shifted(): lax.ppermute(block, axis, [(i, (i + distance) % size) for i in range(size)])]
    pallas_call x22 -> x21, Pallas kernels: 50.9 us -> 48.8 us  [kernel_call(): pl.pallas_call(call, in_specs=[in_vmem] * (count + kept), out_specs=[in_v...]
    ppermute x5 -> x4, starting transfers between devices: 5.48 us -> 5.41 us  [shifted(): lax.ppermute(block, axis, [(i, (i + distance) % size) for i in range(size)])]
  transfers between devices with their start and end apart: 54 -> 50, of which waited for: 23 -> 23; matrix products, arithmetic and copies ran while one was open for 11% -> 10% of each run, Pallas kernels for 22% -> 21%
where the time goes in v6:
time: 233 us; the launch traced here: 232 us
  waiting for transfers between devices  93.9 us (40%)
  starting transfers between devices  60 us (26%)
  Pallas kernels  53.3 us (23%)
  matrix products  19.3 us (8%)
  local copies, waits for them, and re-layouts  3.66 us (2%)
    ppermute x46, waiting for transfers between devices, swap(): return lax.ppermute(block, axis, partner_route(lax.axis_size(axis), step))  90.5 us
    ppermute x46, starting transfers between devices, swap(): return lax.ppermute(block, axis, partner_route(lax.axis_size(axis), step))  54.6 us
    pallas_call x21, Pallas kernels, kernel_call(): pl.pallas_call(call, in_specs=[in_vmem] * (count + kept), out_specs=[in_v...  48.8 us
    dot_general x12, matrix products, dot(): lax.dot_general(former, latter, ((contract[:1], contract[1:]), ((), ())),...  19.3 us
    ppermute x4, starting transfers between devices, shifted(): lax.ppermute(block, axis, [(i, (i + distance) % size) for i in range(size)])  5.41 us
  transfers between devices with their start and end apart: 50, of which 23 were waited for; matrix products, arithmetic and copies ran while one was open for 10% of the time, Pallas kernels for 21%

profile of v6, /device:TPU:0, one launch (start us, length us, event | category | flops | bytes accessed | tf_op | source)
XLA Modules:
  0.0 232.4 jit_solution(15519681390510322159)
XLA Ops:
  4.0 2.6 %collective-permute-start = (bf16[144,1280]{1,0:T(8,128)(2,1)S(1)}, bf16[144,1280]{1,0:T(8,128)(2,1)S(1)}, u32[]{:S(2)}, u32[]{:S(2)}) collective-permute-start(bf16[144,1280]{1,0:T(8,128)(2,1)S(1)} %get-tuple-element.205), channel_id=1, source_target_pairs={{0,8},{8,0},{16,24},{24,16},{1,9},{9,1},{17,25},{25,17},{2,10},{10... | collective-permute-start | bytes 1105928 | tf_op jit(solution)/shard_map/ppermute | solution.py:32
  8.2 2.6 %collective-permute-done.4.refs_5_ = bf16[768,1280]{1,0:T(8,128)(2,1)} collective-permute-done((bf16[768,1280]{1,0:T(8,128)(2,1)}, bf16[768,1280]{1,0:T(8,128)(2,1)}, u32[]{:S(2)}, u32[]{:S(2)}) %collective-permute-start.4) | collective-permute-done | bytes 1966112 | tf_op jit(solution)/shard_map/ppermute | solution.py:32
  10.7 4.5 %shard_map.118 = (bf16[1280,768]{1,0:T(8,128)(2,1)S(1)}, bf16[1280,768]{1,0:T(8,128)(2,1)S(1)}, bf16[1280,768]{1,0:T(8,128)(2,1)S(1)}, bf16[1280,768]{1,0:T(8,12...) custom-call(bf16[1280,768]{1,0:T(8,128)(2,1)} %bitcast.58, bf16[1280,768]{1,0:T(8,128)(2,1)} %copy-done.3, ...), custom_call_target="tpu_custom_call" | custom-call | bytes 23592960 | tf_op jit(solution)/shard_map/pallas_call | solution.py:109
  15.2 3.9 %collective-permute-start.7 = (bf16[144,1280]{1,0:T(8,128)(2,1)S(1)}, bf16[144,1280]{1,0:T(8,128)(2,1)S(1)}, u32[]{:S(2)}, u32[]{:S(2)}) collective-permute-start(bf16[144,1280]{1,0:T(8,128)(2,1)S(1)} %get-tuple-element.109), channel_id=1, source_target_pairs={{0,24},{8,16},{16,8},{24,0},{1,25},{9,17},{17,9},{25,1},{2,26},{10... | collective-permute-start | bytes 1105928 | tf_op jit(solution)/shard_map/ppermute | solution.py:32
  19.1 4.6 %shard_map.119 = (bf16[128,1536]{1,0:T(8,128)(2,1)S(1)}, bf16[128,1536]{1,0:T(8,128)(2,1)S(1)}, bf16[128,1536]{1,0:T(8,128)(2,1)S(1)}, bf16[384,1280]{1,0:T(8,12...) custom-call(bf16[144,1280]{1,0:T(8,128)(2,1)S(1)} %get-tuple-element, ...), custom_call_target="tpu_custom_call" | custom-call | flops 3019898880 | tf_op jit(solution)/shard_map/pallas_call | solution.py:81
  24.4 4.1 %collective-permute-done.7.refs_0_ = bf16[144,1280]{1,0:T(8,128)(2,1)S(1)} collective-permute-done((bf16[144,1280]{1,0:T(8,128)(2,1)S(1)}, bf16[144,1280]{1,0:T(8,128)(2,1)S(1)}, u32[]{:S(2)}, u32[]{:S(2)}) %collective-permute-start.7) | collective-permute-done | bytes 368672 | tf_op jit(solution)/shard_map/ppermute | solution.py:32
  28.5 2.4 %shard_map.120 = (bf16[128,1536]{1,0:T(8,128)(2,1)S(1)}, bf16[128,1280]{1,0:T(8,128)(2,1)S(1)}, bf16[128,1280]{1,0:T(8,128)(2,1)S(1)}, f32[128,1]{1,0:T(8,128)S(...) custom-call(bf16[144,1280]{1,0:T(8,128)(2,1)S(1)} %collective-permute-done.7.refs_0_, ...), custom_call_target="tpu_custom_call" | custom-call | flops 1006632960 | tf_op jit(solution)/shard_map/pallas_call | solution.py:81
  30.9 3.1 %collective-permute-start.8 = (bf16[128,1536]{1,0:T(8,128)(2,1)S(1)}, bf16[128,1536]{1,0:T(8,128)(2,1)S(1)}, u32[]{:S(2)}, u32[]{:S(2)}) collective-permute-start(bf16[128,1536]{1,0:T(8,128)(2,1)S(1)} %get-tuple-element.110), channel_id=1, source_target_pairs={{0,24},{8,16},{16,8},{24,0},{1,25},{9,17},{17,9},{25,1},{2,26},{10... | collective-permute-start | bytes 1179656 | tf_op jit(solution)/shard_map/ppermute | solution.py:32
  34.3 3.2 %collective-permute-done.5.refs_1_ = bf16[128,1536]{1,0:T(8,128)(2,1)S(1)} collective-permute-done((bf16[128,1536]{1,0:T(8,128)(2,1)S(1)}, bf16[128,1536]{1,0:T(8,128)(2,1)S(1)}, u32[]{:S(2)}, u32[]{:S(2)}) %collective-permute-start.5) | collective-permute-done | bytes 393248 | tf_op jit(solution)/shard_map/ppermute | solution.py:32
  37.5 7.3 %collective-permute-done.8.refs_3_ = bf16[128,1536]{1,0:T(8,128)(2,1)S(1)} collective-permute-done((bf16[128,1536]{1,0:T(8,128)(2,1)S(1)}, bf16[128,1536]{1,0:T(8,128)(2,1)S(1)}, u32[]{:S(2)}, u32[]{:S(2)}) %collective-permute-start.8) | collective-permute-done | bytes 393248 | tf_op jit(solution)/shard_map/ppermute | solution.py:32
  45.9 2.7 %collective-permute-start.9 = (bf16[128,768]{1,0:T(8,128)(2,1)S(1)}, bf16[128,768]{1,0:T(8,128)(2,1)S(1)}, u32[]{:S(2)}, u32[]{:S(2)}) collective-permute-start(bf16[128,768]{1,0:T(8,128)(2,1)S(1)} %get-tuple-element.115.refs_0_), channel_id=1, source_target_pairs={{0,24},{8,16},{16,8},{24,0},{1,25},{9,17},{17,9},{25,1},{2,26},{10... | collective-permute-start | bytes 589832 | tf_op jit(solution)/shard_map/ppermute | solution.py:32
  49.5 5.2 %collective-permute-done.9.refs_0_ = bf16[128,768]{1,0:T(8,128)(2,1)S(1)} collective-permute-done((bf16[128,768]{1,0:T(8,128)(2,1)S(1)}, bf16[128,768]{1,0:T(8,128)(2,1)S(1)}, u32[]{:S(2)}, u32[]{:S(2)}) %collective-permute-start.9) | collective-permute-done | bytes 196640 | tf_op jit(solution)/shard_map/ppermute | solution.py:32
  57.5 2.6 %shard_map.124 = (bf16[384,1280]{1,0:T(8,128)(2,1)S(1)}, bf16[384,768]{1,0:T(8,128)(2,1)S(1)}, bf16[384,768]{1,0:T(8,128)(2,1)S(1)}) custom-call(bf16[128,768]{1,0:T(8,128)(2,1)S(1)} %get-tuple-element.115.refs_0_, bf16[128,768]{1,0:T(8,128)(2,1)S(1)} %collective-permute-done.10.refs_1_, bf16[128,768]{1,0:T(8,128)(2,1)S(1)} %collective-permute-done.11.refs_2_, ...), custom_call_target="tpu_custom_call" | custom-call | flops 1509949440 | tf_op jit(solution)/shard_map/pallas_call | solution.py:81
  61.9 2.4 %collective-permute-start.21 = (bf16[128,1280]{1,0:T(8,128)(2,1)S(1)}, bf16[128,1280]{1,0:T(8,128)(2,1)S(1)}, u32[]{:S(2)}, u32[]{:S(2)}) collective-permute-start(bf16[128,1280]{1,0:T(8,128)(2,1)S(1)} %get-tuple-element.196), channel_id=1, source_target_pairs={{0,24},{8,16},{16,8},{24,0},{1,25},{9,17},{17,9},{25,1},{2,26},{10... | collective-permute-start | bytes 983048 | tf_op jit(solution)/shard_map/ppermute | solution.py:32
  67.2 6.4 %collective-permute-done.21.refs_0_ = bf16[128,1280]{1,0:T(8,128)(2,1)S(1)} collective-permute-done((bf16[128,1280]{1,0:T(8,128)(2,1)S(1)}, bf16[128,1280]{1,0:T(8,128)(2,1)S(1)}, u32[]{:S(2)}, u32[]{:S(2)}) %collective-permute-start.21) | collective-permute-done | bytes 327712 | tf_op jit(solution)/shard_map/ppermute | solution.py:32
  75.3 2.4 %collective-permute-start.22 = (bf16[128,768]{1,0:T(8,128)(2,1)S(1)}, bf16[128,768]{1,0:T(8,128)(2,1)S(1)}, u32[]{:S(2)}, u32[]{:S(2)}) collective-permute-start(bf16[128,768]{1,0:T(8,128)(2,1)S(1)} %get-tuple-element.132), channel_id=1, source_target_pairs={{0,24},{8,16},{16,8},{24,0},{1,25},{9,17},{17,9},{25,1},{2,26},{10... | collective-permute-start | bytes 589832 | tf_op jit(solution)/shard_map/ppermute | solution.py:32
  77.7 2.9 %collective-permute-done.13.refs_1_ = bf16[128,1280]{1,0:T(8,128)(2,1)S(1)} collective-permute-done((bf16[128,1280]{1,0:T(8,128)(2,1)S(1)}, bf16[128,1280]{1,0:T(8,128)(2,1)S(1)}, u32[]{:S(2)}, u32[]{:S(2)}) %collective-permute-start.13) | collective-permute-done | bytes 327712 | tf_op jit(solution)/shard_map/ppermute | solution.py:32
  80.5 2.2 shard_map.125
  84.3 2.3 %collective-permute-done.12.refs_0_.refs_4_.refs_5_ = bf16[384,1280]{1,0:T(8,128)(2,1)S(1)} collective-permute-done((bf16[384,1280]{1,0:T(8,128)(2,1)S(1)}, bf16[384,1280]{1,0:T(8,128)(2,1)S(1)}, u32[]{:S(2)}, u32[]{:S(2)}) %collective-permute-start.12) | collective-permute-done | bytes 983072 | tf_op jit(solution)/shard_map/ppermute | solution.py:37
  86.6 4.6 %shard_map.126 = (bf16[128,1664]{1,0:T(8,128)(2,1)S(1)}, bf16[128,1664]{1,0:T(8,128)(2,1)S(1)}, bf16[128,1664]{1,0:T(8,128)(2,1)S(1)}, bf16[384,1280]{1,0:T(8,128)(2,1)S(1)}, bf16[384,1280]{1,0:T(8,128)(2,1)S(1)}) custom-call(bf16[384,1280]{1,0:T(8,128)(2,1)S(1)} %collective-permute-done.12.refs_0_.refs_4_.refs_5_, ...), custom_call_target="tpu_custom_call" | custom-call | flops 3019898880 | tf_op jit(solution)/shard_map/pallas_call | solution.py:81
  92.2 2.3 %shard_map.127 = (bf16[128,1664]{1,0:T(8,128)(2,1)S(1)}, bf16[128,1280]{1,0:T(8,128)(2,1)S(1)}, bf16[128,1280]{1,0:T(8,128)(2,1)S(1)}) custom-call(bf16[128,1280]{1,0:T(8,128)(2,1)S(1)} %collective-permute-done.17.refs_0_.refs_2_.refs_3_, f32[1,1280]{1,0:T(1,128)S(1)} %constant_dynamic-slice_fusion.4.refs_3_.refs_1_.refs_6_.refs_4_, ...), custom_call_target="tpu_custom_call" | custom-call | flops 1006632960 | tf_op jit(solution)/shard_map/pallas_call | solution.py:81
  94.6 2.8 %collective-permute-start.18 = (bf16[128,1664]{1,0:T(8,128)(2,1)S(1)}, bf16[128,1664]{1,0:T(8,128)(2,1)S(1)}, u32[]{:S(2)}, u32[]{:S(2)}) collective-permute-start(bf16[128,1664]{1,0:T(8,128)(2,1)S(1)} %get-tuple-element.128), channel_id=1, source_target_pairs={{0,24},{8,16},{16,8},{24,0},{1,25},{9,17},{17,9},{25,1},{2,26},{10... | collective-permute-start | bytes 1277960 | tf_op jit(solution)/shard_map/ppermute | solution.py:32
  98.3 10.1 %collective-permute-done.18.refs_3_ = bf16[128,1664]{1,0:T(8,128)(2,1)S(1)} collective-permute-done((bf16[128,1664]{1,0:T(8,128)(2,1)S(1)}, bf16[128,1664]{1,0:T(8,128)(2,1)S(1)}, u32[]{:S(2)}, u32[]{:S(2)}) %collective-permute-start.18) | collective-permute-done | bytes 426016 | tf_op jit(solution)/shard_map/ppermute | solution.py:32
  108.3 1.9 collective-permute-start.20
  110.3 5.7 %collective-permute-done.15.refs_1_ = bf16[128,1664]{1,0:T(8,128)(2,1)S(1)} collective-permute-done((bf16[128,1664]{1,0:T(8,128)(2,1)S(1)}, bf16[128,1664]{1,0:T(8,128)(2,1)S(1)}, u32[]{:S(2)}, u32[]{:S(2)}) %collective-permute-start.15) | collective-permute-done | bytes 426016 | tf_op jit(solution)/shard_map/ppermute | solution.py:32
  116.6 3.3 %collective-permute-done.20.refs_2_ = bf16[128,768]{1,0:T(8,128)(2,1)S(1)} collective-permute-done((bf16[128,768]{1,0:T(8,128)(2,1)S(1)}, bf16[128,768]{1,0:T(8,128)(2,1)S(1)}, u32[]{:S(2)}, u32[]{:S(2)}) %collective-permute-start.20) | collective-permute-done | bytes 196640 | tf_op jit(solution)/shard_map/ppermute | solution.py:32
  120.5 2.7 %collective-permute-start.23 = (bf16[128,1664]{1,0:T(8,128)(2,1)S(1)}, bf16[128,1664]{1,0:T(8,128)(2,1)S(1)}, u32[]{:S(2)}, u32[]{:S(2)}) collective-permute-start(bf16[128,1664]{1,0:T(8,128)(2,1)S(1)} %shard_map.130.refs_0_), channel_id=1, source_target_pairs={{0,24},{8,16},{16,8},{24,0},{1,25},{9,17},{17,9},{25,1},{2,26},{10... | collective-permute-start | bytes 1277960 | tf_op jit(solution)/shard_map/ppermute | solution.py:32
  124.1 10.1 %collective-permute-done.23.refs_0_ = bf16[128,1664]{1,0:T(8,128)(2,1)S(1)} collective-permute-done((bf16[128,1664]{1,0:T(8,128)(2,1)S(1)}, bf16[128,1664]{1,0:T(8,128)(2,1)S(1)}, u32[]{:S(2)}, u32[]{:S(2)}) %collective-permute-start.23) | collective-permute-done | bytes 426016 | tf_op jit(solution)/shard_map/ppermute | solution.py:32
  134.9 2.5 %collective-permute-start.25 = (bf16[128,768]{1,0:T(8,128)(2,1)S(1)}, bf16[128,768]{1,0:T(8,128)(2,1)S(1)}, u32[]{:S(2)}, u32[]{:S(2)}) collective-permute-start(bf16[128,768]{1,0:T(8,128)(2,1)S(1)} %get-tuple-element.136.refs_0_), channel_id=1, source_target_pairs={{0,16},{8,24},{16,0},{24,8},{1,17},{9,25},{17,1},{25,9},{2,18},{10... | collective-permute-start | bytes 589832 | tf_op jit(solution)/shard_map/ppermute | solution.py:32
  137.6 3.4 %shard_map.135 = (bf16[128,1280]{1,0:T(8,128)(2,1)S(1)}, f32[1,1280]{1,0:T(1,128)S(1)}) custom-call(bf16[128,1664]{1,0:T(8,128)(2,1)S(1)} %collective-permute-done.23.refs_0_, f32[128,1]{1,0:T(8,128)S(1)} %get-tuple-element.127.refs_2_.refs_1_, bf16[128,1280]{1,0:T(8,128)(2,1)S(1)} %get-tuple-element.154.refs_2_, ...), custom_call_target="tpu_custom_call" | custom-call | flops 1006632960 | tf_op jit(solution)/shard_map/pallas_call | solution.py:81
  141.1 2.4 %collective-permute-done.30.refs_1_ = bf16[128,1664]{1,0:T(8,128)(2,1)S(1)} collective-permute-done((bf16[128,1664]{1,0:T(8,128)(2,1)S(1)}, bf16[128,1664]{1,0:T(8,128)(2,1)S(1)}, u32[]{:S(2)}, u32[]{:S(2)}) %collective-permute-start.30) | collective-permute-done | bytes 426016 | tf_op jit(solution)/shard_map/ppermute | solution.py:32
  145.2 4.4 %shard_map.133 = (bf16[384,1280]{1,0:T(8,128)(2,1)S(1)}, f32[1,1280]{1,0:T(1,128)S(1)}) custom-call(bf16[128,1664]{1,0:T(8,128)(2,1)S(1)} %shard_map.130.refs_0_, bf16[128,1664]{1,0:T(8,128)(2,1)S(1)} %collective-permute-done.30.refs_1_, bf16[128,1664]{1,0:T(8,128)(2,1)S(1)} %collective-permute-done.31.refs_2_, ...), custom_call_target="tpu_custom_call" | custom-call | flops 3019898880 | tf_op jit(solution)/shard_map/pallas_call | solution.py:81
  157.2 2.7 %collective-permute-start.29 = (bf16[128,1280]{1,0:T(8,128)(2,1)S(1)}, bf16[128,1280]{1,0:T(8,128)(2,1)S(1)}, u32[]{:S(2)}, u32[]{:S(2)}) collective-permute-start(bf16[128,1280]{1,0:T(8,128)(2,1)S(1)} %get-tuple-element.140), channel_id=1, source_target_pairs={{0,24},{8,16},{16,8},{24,0},{1,25},{9,17},{17,9},{25,1},{2,26},{10... | collective-permute-start | bytes 983048 | tf_op jit(solution)/shard_map/ppermute | solution.py:32
  159.9 2.6 %shard_map.131 = (bf16[128,1280]{1,0:T(8,128)(2,1)S(1)}, bf16[128,1280]{1,0:T(8,128)(2,1)S(1)}, bf16[128,1280]{1,0:T(8,128)(2,1)S(1)}, bf16[384,768]{1,0:T(8,128)(2,1)S(1)}, bf16[384,768]{1,0:T(8,128)(2,1)S(1)}) custom-call(bf16[128,768]{1,0:T(8,128)(2,1)S(1)} %get-tuple-element.136.refs_0_, bf16[128,768]{1,0:T(8,128)(2,1)S(1)} %collective-permute-done.24.refs_1_, ...), custom_call_target="tpu_custom_call" | custom-call | tf_op jit(solution)/shard_map/pallas_call | solution.py:81
  167.7 2.7 %collective-permute-start.36 = (bf16[128,768]{1,0:T(8,128)(2,1)S(1)}, bf16[128,768]{1,0:T(8,128)(2,1)S(1)}, u32[]{:S(2)}, u32[]{:S(2)}) collective-permute-start(bf16[128,768]{1,0:T(8,128)(2,1)S(1)} %get-tuple-element.160), channel_id=1, source_target_pairs={{0,24},{8,16},{16,8},{24,0},{1,25},{9,17},{17,9},{25,1},{2,26},{10... | collective-permute-start | bytes 589832 | tf_op jit(solution)/shard_map/ppermute | solution.py:32
  170.5 5.7 %collective-permute-done.26 = bf16[128,1280]{1,0:T(8,128)(2,1)S(1)} collective-permute-done((bf16[128,1280]{1,0:T(8,128)(2,1)S(1)}, bf16[128,1280]{1,0:T(8,128)(2,1)S(1)}, u32[]{:S(2)}, u32[]{:S(2)}) %collective-permute-start.26) | collective-permute-done | bytes 327712 | tf_op jit(solution)/shard_map/ppermute | solution.py:32
  176.2 2.2 shard_map.134
  180.0 4.1 %collective-permute-done.33.refs_1_ = bf16[128,768]{1,0:T(8,128)(2,1)S(1)} collective-permute-done((bf16[128,768]{1,0:T(8,128)(2,1)S(1)}, bf16[128,768]{1,0:T(8,128)(2,1)S(1)}, u32[]{:S(2)}, u32[]{:S(2)}) %collective-permute-start.33) | collective-permute-done | bytes 196640 | tf_op jit(solution)/shard_map/ppermute | solution.py:32
  184.1 6.6 %collective-permute-done.34.refs_2_ = bf16[128,768]{1,0:T(8,128)(2,1)S(1)} collective-permute-done((bf16[128,768]{1,0:T(8,128)(2,1)S(1)}, bf16[128,768]{1,0:T(8,128)(2,1)S(1)}, u32[]{:S(2)}, u32[]{:S(2)}) %collective-permute-start.34) | collective-permute-done | bytes 196640 | tf_op jit(solution)/shard_map/ppermute | solution.py:32
  192.4 2.5 %collective-permute-start.38 = (bf16[128,1664]{1,0:T(8,128)(2,1)S(1)}, bf16[128,1664]{1,0:T(8,128)(2,1)S(1)}, u32[]{:S(2)}, u32[]{:S(2)}) collective-permute-start(bf16[128,1664]{1,0:T(8,128)(2,1)S(1)} %shard_map.137.refs_0_), channel_id=1, source_target_pairs={{0,16},{8,24},{16,0},{24,8},{1,17},{9,25},{17,1},{25,9},{2,18},{10... | collective-permute-start | bytes 1277960 | tf_op jit(solution)/shard_map/ppermute | solution.py:32
  196.1 4.3 %collective-permute-done.39.refs_0_ = bf16[128,1664]{1,0:T(8,128)(2,1)S(1)} collective-permute-done((bf16[128,1664]{1,0:T(8,128)(2,1)S(1)}, bf16[128,1664]{1,0:T(8,128)(2,1)S(1)}, u32[]{:S(2)}, u32[]{:S(2)}) %collective-permute-start.39) | collective-permute-done | bytes 426016 | tf_op jit(solution)/shard_map/ppermute | solution.py:32
  200.4 3.4 %shard_map.138 = (bf16[128,1280]{1,0:T(8,128)(2,1)S(1)}, f32[1,1280]{1,0:T(1,128)S(1)}) custom-call(bf16[128,1664]{1,0:T(8,128)(2,1)S(1)} %collective-permute-done.39.refs_0_, f32[128,1]{1,0:T(8,128)S(1)} %get-tuple-element.112.refs_1_, bf16[128,1280]{1,0:T(8,128)(2,1)S(1)} %get-tuple-element.165.refs_2_, ...), custom_call_target="tpu_custom_call" | custom-call | flops 1006632960 | tf_op jit(solution)/shard_map/pallas_call | solution.py:81
  208.2 4.6 %shard_map.139 = (bf16[128,1280]{1,0:T(8,128)(2,1)S(1)}, bf16[128,1280]{1,0:T(8,128)(2,1)S(1)}, bf16[128,1280]{1,0:T(8,128)(2,1)S(1)}, f32[1,1280]{1,0:T(1,128)S(1)}) custom-call(bf16[128,1664]{1,0:T(8,128)(2,1)S(1)} %shard_map.137.refs_0_, bf16[128,1664]{1,0:T(8,128)(2,1)S(1)} %collective-permute-done.37.refs_1_, ...), custom_call_target="tpu_custom_call" | custom-call | flops 1006632960 | tf_op jit(solution)/shard_map/pallas_call | solution.py:81
  214.7 1.9 collective-permute-start.42
  216.7 2.7 %fusion.3 = bf16[768,1280]{1,0:T(8,128)(2,1)} fusion(bf16[768,1280]{1,0:T(8,128)(2,1)S(1)} %collective-permute-done.45, bf16[768,1280]{1,0:T(8,128)(2,1)S(1)} %convolution_convert_fusion, bf16[512,1280]{1,0:T(8,128)(2,1)S(1)} %constant_dynamic-update-slice_fusion.8, bf16[128,768]{1,0:T(8,128)(2,1)S(1)} %get-tuple-element.181, ...), kind=kOutput, calls=%fused_computation.9 | convolution fusion | flops 1013121024 | bytes 7995392 | tf_op jit(solution)/shard_map/dot_general | solution.py:22
  221.1 2.7 %fusion.4 = bf16[1280,768]{1,0:T(8,128)(2,1)} fusion(bf16[1280,768]{1,0:T(8,128)(2,1)S(1)} %collective-permute-done.44, bf16[1280,768]{1,0:T(8,128)(2,1)S(1)} %convolution_convert_fusion.2, bf16[512,1280]{1,0:T(8,128)(2,1)S(1)} %constant_dynamic-update-slice_fusion.10, bf16[512,768]{1,0:T(8,128)(2,1)S(1)} %get-tuple-element.179), kind=kOutput, calls=%fused_computation.10 | convolution fusion | flops 1011548160 | bytes 7995392 | tf_op jit(solution)/shard_map/dot_general | solution.py:22
  223.8 2.7 %fusion.5 = bf16[1280,768]{1,0:T(8,128)(2,1)} fusion(bf16[1280,768]{1,0:T(8,128)(2,1)S(1)} %collective-permute-done.43, bf16[1280,768]{1,0:T(8,128)(2,1)S(1)} %convolution_convert_fusion.3, bf16[512,1280]{1,0:T(8,128)(2,1)S(1)} %constant_dynamic-update-slice_fusion.10, bf16[512,768]{1,0:T(8,128)(2,1)S(1)} %get-tuple-element.178), kind=kOutput, calls=%fused_computation.11 | convolution fusion | flops 1011548160 | bytes 7995392 | tf_op jit(solution)/shard_map/dot_general | solution.py:22
  228.4 2.7 %collective-permute-done.41 = bf16[128,1280]{1,0:T(8,128)(2,1)S(1)} collective-permute-done((bf16[128,1280]{1,0:T(8,128)(2,1)S(1)}, bf16[128,1280]{1,0:T(8,128)(2,1)S(1)}, u32[]{:S(2)}, u32[]{:S(2)}) %collective-permute-start.41) | collective-permute-done | bytes 327712 | tf_op jit(solution)/shard_map/ppermute | solution.py:32
  (141 shorter events, 53.4 us)
Async XLA Ops:
  0.6 7.5 %collective-permute-start.2 = (bf16[1280,768]{1,0:T(8,128)(2,1)}, bf16[1280,768]{1,0:T(8,128)(2,1)S(1)}, u32[]{:S(2)}, u32[]{:S(2)}) collective-permute-start(bf16[1280,768]{1,0:T(8,128)(2,1)} %bitcast.57), channel_id=1, source_target_pairs={{0,1},{1,0},{2,3},{3,2},{4,5},{5,4},{6,7},{7,6},{8,9},{9,8},{10,11... | collective-permute-start | bytes 5898248 | tf_op jit(solution)/shard_map/ppermute | solution.py:32
  1.2 7.0 %collective-permute-start.3 = (bf16[1280,768]{1,0:T(8,128)(2,1)}, bf16[1280,768]{1,0:T(8,128)(2,1)}, u32[]{:S(2)}, u32[]{:S(2)}) collective-permute-start(bf16[1280,768]{1,0:T(8,128)(2,1)} %bitcast.59), channel_id=1, source_target_pairs={{0,1},{1,0},{2,3},{3,2},{4,5},{5,4},{6,7},{7,6},{8,9},{9,8},{10,11... | collective-permute-start | bytes 5898248 | tf_op jit(solution)/shard_map/ppermute | solution.py:32
  1.2 9.5 %collective-permute-start.4 = (bf16[768,1280]{1,0:T(8,128)(2,1)}, bf16[768,1280]{1,0:T(8,128)(2,1)}, u32[]{:S(2)}, u32[]{:S(2)}) collective-permute-start(bf16[768,1280]{1,0:T(8,128)(2,1)} %bitcast.61), channel_id=1, source_target_pairs={{0,1},{1,0},{2,3},{3,2},{4,5},{5,4},{6,7},{7,6},{8,9},{9,8},{10,11... | collective-permute-start | bytes 5898248 | tf_op jit(solution)/shard_map/ppermute | solution.py:32
  4.0 15.1 %collective-permute-start = (bf16[144,1280]{1,0:T(8,128)(2,1)S(1)}, bf16[144,1280]{1,0:T(8,128)(2,1)S(1)}, u32[]{:S(2)}, u32[]{:S(2)}) collective-permute-start(bf16[144,1280]{1,0:T(8,128)(2,1)S(1)} %get-tuple-element.205), channel_id=1, source_target_pairs={{0,8},{8,0},{16,24},{24,16},{1,9},{9,1},{17,25},{25,17},{2,10},{10... | collective-permute-start | bytes 1105928 | tf_op jit(solution)/shard_map/ppermute | solution.py:32
  6.6 12.5 %collective-permute-start.1 = (bf16[144,1280]{1,0:T(8,128)(2,1)S(1)}, bf16[144,1280]{1,0:T(8,128)(2,1)S(1)}, u32[]{:S(2)}, u32[]{:S(2)}) collective-permute-start(bf16[144,1280]{1,0:T(8,128)(2,1)S(1)} %get-tuple-element.206), channel_id=1, source_target_pairs={{0,16},{8,24},{16,0},{24,8},{1,17},{9,25},{17,1},{25,9},{2,18},{10... | collective-permute-start | bytes 1105928 | tf_op jit(solution)/shard_map/ppermute | solution.py:32
  15.2 13.3 %collective-permute-start.7 = (bf16[144,1280]{1,0:T(8,128)(2,1)S(1)}, bf16[144,1280]{1,0:T(8,128)(2,1)S(1)}, u32[]{:S(2)}, u32[]{:S(2)}) collective-permute-start(bf16[144,1280]{1,0:T(8,128)(2,1)S(1)} %get-tuple-element.109), channel_id=1, source_target_pairs={{0,24},{8,16},{16,8},{24,0},{1,25},{9,17},{17,9},{25,1},{2,26},{10... | collective-permute-start | bytes 1105928 | tf_op jit(solution)/shard_map/ppermute | solution.py:32
  23.7 13.8 %collective-permute-start.5 = (bf16[128,1536]{1,0:T(8,128)(2,1)S(1)}, bf16[128,1536]{1,0:T(8,128)(2,1)S(1)}, u32[]{:S(2)}, u32[]{:S(2)}) collective-permute-start(bf16[128,1536]{1,0:T(8,128)(2,1)S(1)} %get-tuple-element.105), channel_id=1, source_target_pairs={{0,8},{8,0},{16,24},{24,16},{1,9},{9,1},{17,25},{25,17},{2,10},{10... | collective-permute-start | bytes 1179656 | tf_op jit(solution)/shard_map/ppermute | solution.py:32
  24.3 13.2 %collective-permute-start.6 = (bf16[128,1536]{1,0:T(8,128)(2,1)S(1)}, bf16[128,1536]{1,0:T(8,128)(2,1)S(1)}, u32[]{:S(2)}, u32[]{:S(2)}) collective-permute-start(bf16[128,1536]{1,0:T(8,128)(2,1)S(1)} %get-tuple-element.106), channel_id=1, source_target_pairs={{0,16},{8,24},{16,0},{24,8},{1,17},{9,25},{17,1},{25,9},{2,18},{10... | collective-permute-start | bytes 1179656 | tf_op jit(solution)/shard_map/ppermute | solution.py:32
  30.9 14.0 %collective-permute-start.8 = (bf16[128,1536]{1,0:T(8,128)(2,1)S(1)}, bf16[128,1536]{1,0:T(8,128)(2,1)S(1)}, u32[]{:S(2)}, u32[]{:S(2)}) collective-permute-start(bf16[128,1536]{1,0:T(8,128)(2,1)S(1)} %get-tuple-element.110), channel_id=1, source_target_pairs={{0,24},{8,16},{16,8},{24,0},{1,25},{9,17},{17,9},{25,1},{2,26},{10... | collective-permute-start | bytes 1179656 | tf_op jit(solution)/shard_map/ppermute | solution.py:32
  45.9 8.7 %collective-permute-start.9 = (bf16[128,768]{1,0:T(8,128)(2,1)S(1)}, bf16[128,768]{1,0:T(8,128)(2,1)S(1)}, u32[]{:S(2)}, u32[]{:S(2)}) collective-permute-start(bf16[128,768]{1,0:T(8,128)(2,1)S(1)} %get-tuple-element.115.refs_0_), channel_id=1, source_target_pairs={{0,24},{8,16},{16,8},{24,0},{1,25},{9,17},{17,9},{25,1},{2,26},{10... | collective-permute-start | bytes 589832 | tf_op jit(solution)/shard_map/ppermute | solution.py:32
  48.6 8.9 %collective-permute-start.10 = (bf16[128,768]{1,0:T(8,128)(2,1)S(1)}, bf16[128,768]{1,0:T(8,128)(2,1)S(1)}, u32[]{:S(2)}, u32[]{:S(2)}) collective-permute-start(bf16[128,768]{1,0:T(8,128)(2,1)S(1)} %get-tuple-element.115.refs_0_), channel_id=1, source_target_pairs={{0,8},{8,0},{16,24},{24,16},{1,9},{9,1},{17,25},{25,17},{2,10},{10... | collective-permute-start | bytes 589832 | tf_op jit(solution)/shard_map/ppermute | solution.py:32
  49.1 8.3 %collective-permute-start.11 = (bf16[128,768]{1,0:T(8,128)(2,1)S(1)}, bf16[128,768]{1,0:T(8,128)(2,1)S(1)}, u32[]{:S(2)}, u32[]{:S(2)}) collective-permute-start(bf16[128,768]{1,0:T(8,128)(2,1)S(1)} %get-tuple-element.115.refs_0_), channel_id=1, source_target_pairs={{0,16},{8,24},{16,0},{24,8},{1,17},{9,25},{17,1},{25,9},{2,18},{10... | collective-permute-start | bytes 589832 | tf_op jit(solution)/shard_map/ppermute | solution.py:32
  60.1 26.5 %collective-permute-start.12 = (bf16[384,1280]{1,0:T(8,128)(2,1)S(1)}, bf16[384,1280]{1,0:T(8,128)(2,1)S(1)}, u32[]{:S(2)}, u32[]{:S(2)}) collective-permute-start(bf16[384,1280]{1,0:T(8,128)(2,1)S(1)} %get-tuple-element.118), channel_id=1, source_target_pairs={{0,2},{2,4},{4,6},{6,0},{1,3},{3,5},{5,7},{7,1},{8,10},{10,12},{12... | collective-permute-start | bytes 2949128 | tf_op jit(solution)/shard_map/ppermute | solution.py:37
  61.9 11.7 %collective-permute-start.21 = (bf16[128,1280]{1,0:T(8,128)(2,1)S(1)}, bf16[128,1280]{1,0:T(8,128)(2,1)S(1)}, u32[]{:S(2)}, u32[]{:S(2)}) collective-permute-start(bf16[128,1280]{1,0:T(8,128)(2,1)S(1)} %get-tuple-element.196), channel_id=1, source_target_pairs={{0,24},{8,16},{16,8},{24,0},{1,25},{9,17},{17,9},{25,1},{2,26},{10... | collective-permute-start | bytes 983048 | tf_op jit(solution)/shard_map/ppermute | solution.py:32
  64.3 16.2 %collective-permute-start.13 = (bf16[128,1280]{1,0:T(8,128)(2,1)S(1)}, bf16[128,1280]{1,0:T(8,128)(2,1)S(1)}, u32[]{:S(2)}, u32[]{:S(2)}) collective-permute-start(bf16[128,1280]{1,0:T(8,128)(2,1)S(1)} %get-tuple-element.198), channel_id=1, source_target_pairs={{0,8},{8,0},{16,24},{24,16},{1,9},{9,1},{17,25},{25,17},{2,10},{10... | collective-permute-start | bytes 983048 | tf_op jit(solution)/shard_map/ppermute | solution.py:32
  64.9 15.7 %collective-permute-start.14 = (bf16[128,1280]{1,0:T(8,128)(2,1)S(1)}, bf16[128,1280]{1,0:T(8,128)(2,1)S(1)}, u32[]{:S(2)}, u32[]{:S(2)}) collective-permute-start(bf16[128,1280]{1,0:T(8,128)(2,1)S(1)} %get-tuple-element.197), channel_id=1, source_target_pairs={{0,16},{8,24},{16,0},{24,8},{1,17},{9,25},{17,1},{25,9},{2,18},{10... | collective-permute-start | bytes 983048 | tf_op jit(solution)/shard_map/ppermute | solution.py:32
  65.6 26.7 %collective-permute-start.17 = (bf16[128,1280]{1,0:T(8,128)(2,1)S(1)}, bf16[128,1280]{1,0:T(8,128)(2,1)S(1)}, u32[]{:S(2)}, u32[]{:S(2)}) collective-permute-start(bf16[128,1280]{1,0:T(8,128)(2,1)S(1)} %get-tuple-element.114), channel_id=1, source_target_pairs={{0,2},{2,4},{4,6},{6,0},{1,3},{3,5},{5,7},{7,1},{8,10},{10,12},{12... | collective-permute-start | bytes 983048 | tf_op jit(solution)/shard_map/ppermute | solution.py:37
  75.3 41.3 %collective-permute-start.22 = (bf16[128,768]{1,0:T(8,128)(2,1)S(1)}, bf16[128,768]{1,0:T(8,128)(2,1)S(1)}, u32[]{:S(2)}, u32[]{:S(2)}) collective-permute-start(bf16[128,768]{1,0:T(8,128)(2,1)S(1)} %get-tuple-element.132), channel_id=1, source_target_pairs={{0,24},{8,16},{16,8},{24,0},{1,25},{9,17},{17,9},{25,1},{2,26},{10... | collective-permute-start | bytes 589832 | tf_op jit(solution)/shard_map/ppermute | solution.py:32
  82.7 33.9 %collective-permute-start.19 = (bf16[128,768]{1,0:T(8,128)(2,1)S(1)}, bf16[128,768]{1,0:T(8,128)(2,1)S(1)}, u32[]{:S(2)}, u32[]{:S(2)}) collective-permute-start(bf16[128,768]{1,0:T(8,128)(2,1)S(1)} %get-tuple-element.130), channel_id=1, source_target_pairs={{0,8},{8,0},{16,24},{24,16},{1,9},{9,1},{17,25},{25,17},{2,10},{10... | collective-permute-start | bytes 589832 | tf_op jit(solution)/shard_map/ppermute | solution.py:32
  94.6 13.8 %collective-permute-start.18 = (bf16[128,1664]{1,0:T(8,128)(2,1)S(1)}, bf16[128,1664]{1,0:T(8,128)(2,1)S(1)}, u32[]{:S(2)}, u32[]{:S(2)}) collective-permute-start(bf16[128,1664]{1,0:T(8,128)(2,1)S(1)} %get-tuple-element.128), channel_id=1, source_target_pairs={{0,24},{8,16},{16,8},{24,0},{1,25},{9,17},{17,9},{25,1},{2,26},{10... | collective-permute-start | bytes 1277960 | tf_op jit(solution)/shard_map/ppermute | solution.py:32
  97.5 18.6 %collective-permute-start.15 = (bf16[128,1664]{1,0:T(8,128)(2,1)S(1)}, bf16[128,1664]{1,0:T(8,128)(2,1)S(1)}, u32[]{:S(2)}, u32[]{:S(2)}) collective-permute-start(bf16[128,1664]{1,0:T(8,128)(2,1)S(1)} %get-tuple-element.124), channel_id=1, source_target_pairs={{0,8},{8,0},{16,24},{24,16},{1,9},{9,1},{17,25},{25,17},{2,10},{10... | collective-permute-start | bytes 1277960 | tf_op jit(solution)/shard_map/ppermute | solution.py:32
  98.1 17.9 %collective-permute-start.16 = (bf16[128,1664]{1,0:T(8,128)(2,1)S(1)}, bf16[128,1664]{1,0:T(8,128)(2,1)S(1)}, u32[]{:S(2)}, u32[]{:S(2)}) collective-permute-start(bf16[128,1664]{1,0:T(8,128)(2,1)S(1)} %get-tuple-element.125), channel_id=1, source_target_pairs={{0,16},{8,24},{16,0},{24,8},{1,17},{9,25},{17,1},{25,9},{2,18},{10... | collective-permute-start | bytes 1277960 | tf_op jit(solution)/shard_map/ppermute | solution.py:32
  108.3 11.6 %collective-permute-start.20 = (bf16[128,768]{1,0:T(8,128)(2,1)S(1)}, bf16[128,768]{1,0:T(8,128)(2,1)S(1)}, u32[]{:S(2)}, u32[]{:S(2)}) collective-permute-start(bf16[128,768]{1,0:T(8,128)(2,1)S(1)} %get-tuple-element.131), channel_id=1, source_target_pairs={{0,16},{8,24},{16,0},{24,8},{1,17},{9,25},{17,1},{25,9},{2,18},{10... | collective-permute-start | bytes 589832 | tf_op jit(solution)/shard_map/ppermute | solution.py:32
  120.5 13.7 %collective-permute-start.23 = (bf16[128,1664]{1,0:T(8,128)(2,1)S(1)}, bf16[128,1664]{1,0:T(8,128)(2,1)S(1)}, u32[]{:S(2)}, u32[]{:S(2)}) collective-permute-start(bf16[128,1664]{1,0:T(8,128)(2,1)S(1)} %shard_map.130.refs_0_), channel_id=1, source_target_pairs={{0,24},{8,16},{16,8},{24,0},{1,25},{9,17},{17,9},{25,1},{2,26},{10... | collective-permute-start | bytes 1277960 | tf_op jit(solution)/shard_map/ppermute | solution.py:32
  123.2 20.4 %collective-permute-start.30 = (bf16[128,1664]{1,0:T(8,128)(2,1)S(1)}, bf16[128,1664]{1,0:T(8,128)(2,1)S(1)}, u32[]{:S(2)}, u32[]{:S(2)}) collective-permute-start(bf16[128,1664]{1,0:T(8,128)(2,1)S(1)} %shard_map.130.refs_0_), channel_id=1, source_target_pairs={{0,8},{8,0},{16,24},{24,16},{1,9},{9,1},{17,25},{25,17},{2,10},{10... | collective-permute-start | bytes 1277960 | tf_op jit(solution)/shard_map/ppermute | solution.py:32
  123.7 21.5 %collective-permute-start.31 = (bf16[128,1664]{1,0:T(8,128)(2,1)S(1)}, bf16[128,1664]{1,0:T(8,128)(2,1)S(1)}, u32[]{:S(2)}, u32[]{:S(2)}) collective-permute-start(bf16[128,1664]{1,0:T(8,128)(2,1)S(1)} %shard_map.130.refs_0_), channel_id=1, source_target_pairs={{0,16},{8,24},{16,0},{24,8},{1,17},{9,25},{17,1},{25,9},{2,18},{10... | collective-permute-start | bytes 1277960 | tf_op jit(solution)/shard_map/ppermute | solution.py:32
  134.1 16.1 %collective-permute-start.24 = (bf16[128,768]{1,0:T(8,128)(2,1)S(1)}, bf16[128,768]{1,0:T(8,128)(2,1)S(1)}, u32[]{:S(2)}, u32[]{:S(2)}) collective-permute-start(bf16[128,768]{1,0:T(8,128)(2,1)S(1)} %get-tuple-element.136.refs_0_), channel_id=1, source_target_pairs={{0,8},{8,0},{16,24},{24,16},{1,9},{9,1},{17,25},{25,17},{2,10},{10... | collective-permute-start | bytes 589832 | tf_op jit(solution)/shard_map/ppermute | solution.py:32
  134.9 15.4 %collective-permute-start.25 = (bf16[128,768]{1,0:T(8,128)(2,1)S(1)}, bf16[128,768]{1,0:T(8,128)(2,1)S(1)}, u32[]{:S(2)}, u32[]{:S(2)}) collective-permute-start(bf16[128,768]{1,0:T(8,128)(2,1)S(1)} %get-tuple-element.136.refs_0_), channel_id=1, source_target_pairs={{0,16},{8,24},{16,0},{24,8},{1,17},{9,25},{17,1},{25,9},{2,18},{10... | collective-permute-start | bytes 589832 | tf_op jit(solution)/shard_map/ppermute | solution.py:32
  137.4 13.4 %collective-permute-start.28 = (bf16[128,768]{1,0:T(8,128)(2,1)S(1)}, bf16[128,768]{1,0:T(8,128)(2,1)S(1)}, u32[]{:S(2)}, u32[]{:S(2)}) collective-permute-start(bf16[128,768]{1,0:T(8,128)(2,1)S(1)} %get-tuple-element.136.refs_0_), channel_id=1, source_target_pairs={{0,24},{8,16},{16,8},{24,0},{1,25},{9,17},{17,9},{25,1},{2,26},{10... | collective-permute-start | bytes 589832 | tf_op jit(solution)/shard_map/ppermute | solution.py:32
  143.5 22.5 %collective-permute-start.35 = (bf16[128,1280]{1,0:T(8,128)(2,1)S(1)}, bf16[128,1280]{1,0:T(8,128)(2,1)S(1)}, u32[]{:S(2)}, u32[]{:S(2)}) collective-permute-start(bf16[128,1280]{1,0:T(8,128)(2,1)S(1)} %get-tuple-element.159), channel_id=1, source_target_pairs={{0,6},{2,0},{4,2},{6,4},{1,7},{3,1},{5,3},{7,5},{8,14},{10,8},{12,... | collective-permute-start | bytes 983048 | tf_op jit(solution)/shard_map/ppermute | solution.py:37
  149.6 26.5 %collective-permute-start.32 = (bf16[384,1280]{1,0:T(8,128)(2,1)S(1)}, bf16[384,1280]{1,0:T(8,128)(2,1)S(1)}, u32[]{:S(2)}, u32[]{:S(2)}) collective-permute-start(bf16[384,1280]{1,0:T(8,128)(2,1)S(1)} %get-tuple-element.142), channel_id=1, source_target_pairs={{0,6},{2,0},{4,2},{6,4},{1,7},{3,1},{5,3},{7,5},{8,14},{10,8},{12,... | collective-permute-start | bytes 2949128 | tf_op jit(solution)/shard_map/ppermute | solution.py:37
  157.2 55.8 %collective-permute-start.29 = (bf16[128,1280]{1,0:T(8,128)(2,1)S(1)}, bf16[128,1280]{1,0:T(8,128)(2,1)S(1)}, u32[]{:S(2)}, u32[]{:S(2)}) collective-permute-start(bf16[128,1280]{1,0:T(8,128)(2,1)S(1)} %get-tuple-element.140), channel_id=1, source_target_pairs={{0,24},{8,16},{16,8},{24,0},{1,25},{9,17},{17,9},{25,1},{2,26},{10... | collective-permute-start | bytes 983048 | tf_op jit(solution)/shard_map/ppermute | solution.py:32
  162.5 13.6 %collective-permute-start.26 = (bf16[128,1280]{1,0:T(8,128)(2,1)S(1)}, bf16[128,1280]{1,0:T(8,128)(2,1)S(1)}, u32[]{:S(2)}, u32[]{:S(2)}) collective-permute-start(bf16[128,1280]{1,0:T(8,128)(2,1)S(1)} %get-tuple-element.138), channel_id=1, source_target_pairs={{0,8},{8,0},{16,24},{24,16},{1,9},{9,1},{17,25},{25,17},{2,10},{10... | collective-permute-start | bytes 983048 | tf_op jit(solution)/shard_map/ppermute | solution.py:32
  163.1 45.1 %collective-permute-start.27 = (bf16[128,1280]{1,0:T(8,128)(2,1)S(1)}, bf16[128,1280]{1,0:T(8,128)(2,1)S(1)}, u32[]{:S(2)}, u32[]{:S(2)}) collective-permute-start(bf16[128,1280]{1,0:T(8,128)(2,1)S(1)} %get-tuple-element.139), channel_id=1, source_target_pairs={{0,16},{8,24},{16,0},{24,8},{1,17},{9,25},{17,1},{25,9},{2,18},{10... | collective-permute-start | bytes 983048 | tf_op jit(solution)/shard_map/ppermute | solution.py:32
  167.7 16.4 %collective-permute-start.36 = (bf16[128,768]{1,0:T(8,128)(2,1)S(1)}, bf16[128,768]{1,0:T(8,128)(2,1)S(1)}, u32[]{:S(2)}, u32[]{:S(2)}) collective-permute-start(bf16[128,768]{1,0:T(8,128)(2,1)S(1)} %get-tuple-element.160), channel_id=1, source_target_pairs={{0,24},{8,16},{16,8},{24,0},{1,25},{9,17},{17,9},{25,1},{2,26},{10... | collective-permute-start | bytes 589832 | tf_op jit(solution)/shard_map/ppermute | solution.py:32
  178.4 5.7 %collective-permute-start.33 = (bf16[128,768]{1,0:T(8,128)(2,1)S(1)}, bf16[128,768]{1,0:T(8,128)(2,1)S(1)}, u32[]{:S(2)}, u32[]{:S(2)}) collective-permute-start(bf16[128,768]{1,0:T(8,128)(2,1)S(1)} %get-tuple-element.151), channel_id=1, source_target_pairs={{0,8},{8,0},{16,24},{24,16},{1,9},{9,1},{17,25},{25,17},{2,10},{10... | collective-permute-start | bytes 589832 | tf_op jit(solution)/shard_map/ppermute | solution.py:32
  179.9 10.8 %collective-permute-start.34 = (bf16[128,768]{1,0:T(8,128)(2,1)S(1)}, bf16[128,768]{1,0:T(8,128)(2,1)S(1)}, u32[]{:S(2)}, u32[]{:S(2)}) collective-permute-start(bf16[128,768]{1,0:T(8,128)(2,1)S(1)} %get-tuple-element.158), channel_id=1, source_target_pairs={{0,16},{8,24},{16,0},{24,8},{1,17},{9,25},{17,1},{25,9},{2,18},{10... | collective-permute-start | bytes 589832 | tf_op jit(solution)/shard_map/ppermute | solution.py:32
  191.2 9.2 %collective-permute-start.39 = (bf16[128,1664]{1,0:T(8,128)(2,1)S(1)}, bf16[128,1664]{1,0:T(8,128)(2,1)S(1)}, u32[]{:S(2)}, u32[]{:S(2)}) collective-permute-start(bf16[128,1664]{1,0:T(8,128)(2,1)S(1)} %shard_map.137.refs_0_), channel_id=1, source_target_pairs={{0,24},{8,16},{16,8},{24,0},{1,25},{9,17},{17,9},{25,1},{2,26},{10... | collective-permute-start | bytes 1277960 | tf_op jit(solution)/shard_map/ppermute | solution.py:32
  191.3 12.5 %collective-permute-start.37 = (bf16[128,1664]{1,0:T(8,128)(2,1)S(1)}, bf16[128,1664]{1,0:T(8,128)(2,1)S(1)}, u32[]{:S(2)}, u32[]{:S(2)}) collective-permute-start(bf16[128,1664]{1,0:T(8,128)(2,1)S(1)} %shard_map.137.refs_0_), channel_id=1, source_target_pairs={{0,8},{8,0},{16,24},{24,16},{1,9},{9,1},{17,25},{25,17},{2,10},{10... | collective-permute-start | bytes 1277960 | tf_op jit(solution)/shard_map/ppermute | solution.py:32
  192.4 12.5 %collective-permute-start.38 = (bf16[128,1664]{1,0:T(8,128)(2,1)S(1)}, bf16[128,1664]{1,0:T(8,128)(2,1)S(1)}, u32[]{:S(2)}, u32[]{:S(2)}) collective-permute-start(bf16[128,1664]{1,0:T(8,128)(2,1)S(1)} %shard_map.137.refs_0_), channel_id=1, source_target_pairs={{0,16},{8,24},{16,0},{24,8},{1,17},{9,25},{17,1},{25,9},{2,18},{10... | collective-permute-start | bytes 1277960 | tf_op jit(solution)/shard_map/ppermute | solution.py:32
  200.4 14.3 %collective-permute-start.45 = (bf16[768,1280]{1,0:T(8,128)(2,1)S(1)}, bf16[768,1280]{1,0:T(8,128)(2,1)S(1)}, u32[]{:S(2)}, u32[]{:S(2)}) collective-permute-start(bf16[768,1280]{1,0:T(8,128)(2,1)S(1)} %fusion.8), channel_id=1, source_target_pairs={{0,1},{1,0},{2,3},{3,2},{4,5},{5,4},{6,7},{7,6},{8,9},{9,8},{10,11... | collective-permute-start | bytes 5898248 | tf_op jit(solution)/shard_map/ppermute | solution.py:32
  206.2 13.1 %collective-permute-start.44 = (bf16[1280,768]{1,0:T(8,128)(2,1)S(1)}, bf16[1280,768]{1,0:T(8,128)(2,1)S(1)}, u32[]{:S(2)}, u32[]{:S(2)}) collective-permute-start(bf16[1280,768]{1,0:T(8,128)(2,1)S(1)} %fusion.7), channel_id=1, source_target_pairs={{0,1},{1,0},{2,3},{3,2},{4,5},{5,4},{6,7},{7,6},{8,9},{9,8},{10,11... | collective-permute-start | bytes 5898248 | tf_op jit(solution)/shard_map/ppermute | solution.py:32
  207.6 11.8 %collective-permute-start.43 = (bf16[1280,768]{1,0:T(8,128)(2,1)S(1)}, bf16[1280,768]{1,0:T(8,128)(2,1)S(1)}, u32[]{:S(2)}, u32[]{:S(2)}) collective-permute-start(bf16[1280,768]{1,0:T(8,128)(2,1)S(1)} %fusion.6), channel_id=1, source_target_pairs={{0,1},{1,0},{2,3},{3,2},{4,5},{5,4},{6,7},{7,6},{8,9},{9,8},{10,11... | collective-permute-start | bytes 5898248 | tf_op jit(solution)/shard_map/ppermute | solution.py:32
  213.0 13.5 %collective-permute-start.40 = (bf16[128,1280]{1,0:T(8,128)(2,1)S(1)}, bf16[128,1280]{1,0:T(8,128)(2,1)S(1)}, u32[]{:S(2)}, u32[]{:S(2)}) collective-permute-start(bf16[128,1280]{1,0:T(8,128)(2,1)S(1)} %get-tuple-element.174), channel_id=1, source_target_pairs={{0,8},{8,0},{16,24},{24,16},{1,9},{9,1},{17,25},{25,17},{2,10},{10... | collective-permute-start | bytes 983048 | tf_op jit(solution)/shard_map/ppermute | solution.py:32
  214.1 16.9 %collective-permute-start.41 = (bf16[128,1280]{1,0:T(8,128)(2,1)S(1)}, bf16[128,1280]{1,0:T(8,128)(2,1)S(1)}, u32[]{:S(2)}, u32[]{:S(2)}) collective-permute-start(bf16[128,1280]{1,0:T(8,128)(2,1)S(1)} %get-tuple-element.175), channel_id=1, source_target_pairs={{0,16},{8,24},{16,0},{24,8},{1,17},{9,25},{17,1},{25,9},{2,18},{10... | collective-permute-start | bytes 983048 | tf_op jit(solution)/shard_map/ppermute | solution.py:32
  214.7 16.3 %collective-permute-start.42 = (bf16[128,1280]{1,0:T(8,128)(2,1)S(1)}, bf16[128,1280]{1,0:T(8,128)(2,1)S(1)}, u32[]{:S(2)}, u32[]{:S(2)}) collective-permute-start(bf16[128,1280]{1,0:T(8,128)(2,1)S(1)} %get-tuple-element.166), channel_id=1, source_target_pairs={{0,24},{8,16},{16,8},{24,0},{1,25},{9,17},{17,9},{25,1},{2,26},{10... | collective-permute-start | bytes 983048 | tf_op jit(solution)/shard_map/ppermute | solution.py:32
  219.4 12.0 %collective-permute-start.47 = (f32[1,1280]{1,0:T(1,128)S(1)}, f32[1,1280]{1,0:T(1,128)S(1)}, u32[]{:S(2)}, u32[]{:S(2)}) collective-permute-start(f32[1,1280]{1,0:T(1,128)S(1)} %add.115), channel_id=1, source_target_pairs={{0,8},{8,0},{16,24},{24,16},{1,9},{9,1},{17,25},{25,17},{2,10},{10... | collective-permute-start | bytes 15368 | tf_op jit(solution)/shard_map/ppermute | solution.py:32
  220.5 10.9 %collective-permute-start.48 = (f32[1,1280]{1,0:T(1,128)S(1)}, f32[1,1280]{1,0:T(1,128)S(1)}, u32[]{:S(2)}, u32[]{:S(2)}) collective-permute-start(f32[1,1280]{1,0:T(1,128)S(1)} %add.115), channel_id=1, source_target_pairs={{0,16},{8,24},{16,0},{24,8},{1,17},{9,25},{17,1},{25,9},{2,18},{10... | collective-permute-start | bytes 15368 | tf_op jit(solution)/shard_map/ppermute | solution.py:32
  (10 other events, 48.3 us)

commit v7 on v6

--- a/solution.py
+++ b/solution.py
@@ -504,11 +504,13 @@
     parts, gained = [], []
     for rows_in, mask in zip(hidden, masks[1]):
         if parts:
-            rows_in = after(rows_in, parts[0])
+            parts = sent(parts)
+            rows_in = after(rows_in, parts[1])
         made, scaled, _ = hidden_parts([rows_in], rows, gain_part, mask, gate_pair, up_pair)
         parts += made
         gained.append(scaled)
-    gate, up, activated, inverse = activate(sent(parts), units, features)
+    parts[-1] = swap(parts[-1], "dp", dp_count - 1)
+    gate, up, activated, inverse = activate(parts, units, features)
     kept.append((hidden, gained, inverse, gate, up))
 
     gain_sum = jnp.zeros((1, width), f32)

time: 233 us -> 236 us (1.013)
  matrix products: 19.3 us -> 22.1 us
    dot_general x12, matrix products: 19.3 us -> 22.1 us  [dot(): lax.dot_general(former, latter, ((contract[:1], contract[1:]), ((), ())),...]
    ppermute x4, waiting for transfers between devices: 3.33 us -> 5.95 us  [shifted(): lax.ppermute(block, axis, [(i, (i + distance) % size) for i in range(size)])]
  transfers between devices with their start and end apart: 50 -> 50, of which waited for: 23 -> 21; matrix products, arithmetic and copies ran while one was open for 10% -> 11% of each run, Pallas kernels for 21% -> 21%
where the time goes in v7:
time: 236 us; the launch traced here: 235 us
  waiting for transfers between devices  94.5 us (40%)
  starting transfers between devices  59.6 us (25%)
  Pallas kernels  53.3 us (23%)
  matrix products  22.1 us (9%)
  local copies, waits for them, and re-layouts  3.79 us (2%)
    ppermute x46, waiting for transfers between devices, swap(): return lax.ppermute(block, axis, partner_route(lax.axis_size(axis), step))  88.5 us
    ppermute x46, starting transfers between devices, swap(): return lax.ppermute(block, axis, partner_route(lax.axis_size(axis), step))  54.3 us
    pallas_call x21, Pallas kernels, kernel_call(): pl.pallas_call(call, in_specs=[in_vmem] * (count + kept), out_specs=[in_v...  48.8 us
    dot_general x12, matrix products, dot(): lax.dot_general(former, latter, ((contract[:1], contract[1:]), ((), ())),...  22.1 us
    ppermute x4, waiting for transfers between devices, shifted(): lax.ppermute(block, axis, [(i, (i + distance) % size) for i in range(size)])  5.95 us
    ppermute x4, starting transfers between devices, shifted(): lax.ppermute(block, axis, [(i, (i + distance) % size) for i in range(size)])  5.27 us
  transfers between devices with their start and end apart: 50, of which 21 were waited for; matrix products, arithmetic and copies ran while one was open for 11% of the time, Pallas kernels for 21%

profile of v7, /device:TPU:0, one launch (start us, length us, event | category | flops | bytes accessed | tf_op | source)
XLA Modules:
  0.0 235.5 jit_solution(1896547916687947841)
XLA Ops:
  4.0 2.6 %collective-permute-start = (bf16[144,1280]{1,0:T(8,128)(2,1)S(1)}, bf16[144,1280]{1,0:T(8,128)(2,1)S(1)}, u32[]{:S(2)}, u32[]{:S(2)}) collective-permute-start(bf16[144,1280]{1,0:T(8,128)(2,1)S(1)} %get-tuple-element.205), channel_id=1, source_target_pairs={{0,8},{8,0},{16,24},{24,16},{1,9},{9,1},{17,25},{25,17},{2,10},{10... | collective-permute-start | bytes 1105928 | tf_op jit(solution)/shard_map/ppermute | solution.py:32
  8.1 2.6 %collective-permute-done.4.refs_5_ = bf16[768,1280]{1,0:T(8,128)(2,1)} collective-permute-done((bf16[768,1280]{1,0:T(8,128)(2,1)}, bf16[768,1280]{1,0:T(8,128)(2,1)}, u32[]{:S(2)}, u32[]{:S(2)}) %collective-permute-start.4) | collective-permute-done | bytes 1966112 | tf_op jit(solution)/shard_map/ppermute | solution.py:32
  10.7 4.5 %shard_map.118 = (bf16[1280,768]{1,0:T(8,128)(2,1)S(1)}, bf16[1280,768]{1,0:T(8,128)(2,1)S(1)}, bf16[1280,768]{1,0:T(8,128)(2,1)S(1)}, bf16[1280,768]{1,0:T(8,12...) custom-call(bf16[1280,768]{1,0:T(8,128)(2,1)} %bitcast.58, bf16[1280,768]{1,0:T(8,128)(2,1)} %copy-done.3, ...), custom_call_target="tpu_custom_call" | custom-call | bytes 23592960 | tf_op jit(solution)/shard_map/pallas_call | solution.py:109
  15.2 3.9 %collective-permute-start.7 = (bf16[144,1280]{1,0:T(8,128)(2,1)S(1)}, bf16[144,1280]{1,0:T(8,128)(2,1)S(1)}, u32[]{:S(2)}, u32[]{:S(2)}) collective-permute-start(bf16[144,1280]{1,0:T(8,128)(2,1)S(1)} %get-tuple-element.109), channel_id=1, source_target_pairs={{0,24},{8,16},{16,8},{24,0},{1,25},{9,17},{17,9},{25,1},{2,26},{10... | collective-permute-start | bytes 1105928 | tf_op jit(solution)/shard_map/ppermute | solution.py:32
  19.1 4.6 %shard_map.119 = (bf16[128,1536]{1,0:T(8,128)(2,1)S(1)}, bf16[128,1536]{1,0:T(8,128)(2,1)S(1)}, bf16[128,1536]{1,0:T(8,128)(2,1)S(1)}, bf16[384,1280]{1,0:T(8,12...) custom-call(bf16[144,1280]{1,0:T(8,128)(2,1)S(1)} %get-tuple-element, ...), custom_call_target="tpu_custom_call" | custom-call | flops 3019898880 | tf_op jit(solution)/shard_map/pallas_call | solution.py:81
  24.4 4.1 %collective-permute-done.7.refs_0_ = bf16[144,1280]{1,0:T(8,128)(2,1)S(1)} collective-permute-done((bf16[144,1280]{1,0:T(8,128)(2,1)S(1)}, bf16[144,1280]{1,0:T(8,128)(2,1)S(1)}, u32[]{:S(2)}, u32[]{:S(2)}) %collective-permute-start.7) | collective-permute-done | bytes 368672 | tf_op jit(solution)/shard_map/ppermute | solution.py:32
  28.5 2.4 %shard_map.120 = (bf16[128,1536]{1,0:T(8,128)(2,1)S(1)}, bf16[128,1280]{1,0:T(8,128)(2,1)S(1)}, bf16[128,1280]{1,0:T(8,128)(2,1)S(1)}, f32[128,1]{1,0:T(8,128)S(...) custom-call(bf16[144,1280]{1,0:T(8,128)(2,1)S(1)} %collective-permute-done.7.refs_0_, ...), custom_call_target="tpu_custom_call" | custom-call | flops 1006632960 | tf_op jit(solution)/shard_map/pallas_call | solution.py:81
  30.9 3.1 %collective-permute-start.8 = (bf16[128,1536]{1,0:T(8,128)(2,1)S(1)}, bf16[128,1536]{1,0:T(8,128)(2,1)S(1)}, u32[]{:S(2)}, u32[]{:S(2)}) collective-permute-start(bf16[128,1536]{1,0:T(8,128)(2,1)S(1)} %get-tuple-element.110), channel_id=1, source_target_pairs={{0,24},{8,16},{16,8},{24,0},{1,25},{9,17},{17,9},{25,1},{2,26},{10... | collective-permute-start | bytes 1179656 | tf_op jit(solution)/shard_map/ppermute | solution.py:32
  34.3 3.2 %collective-permute-done.5.refs_1_ = bf16[128,1536]{1,0:T(8,128)(2,1)S(1)} collective-permute-done((bf16[128,1536]{1,0:T(8,128)(2,1)S(1)}, bf16[128,1536]{1,0:T(8,128)(2,1)S(1)}, u32[]{:S(2)}, u32[]{:S(2)}) %collective-permute-start.5) | collective-permute-done | bytes 393248 | tf_op jit(solution)/shard_map/ppermute | solution.py:32
  37.5 7.3 %collective-permute-done.8.refs_3_ = bf16[128,1536]{1,0:T(8,128)(2,1)S(1)} collective-permute-done((bf16[128,1536]{1,0:T(8,128)(2,1)S(1)}, bf16[128,1536]{1,0:T(8,128)(2,1)S(1)}, u32[]{:S(2)}, u32[]{:S(2)}) %collective-permute-start.8) | collective-permute-done | bytes 393248 | tf_op jit(solution)/shard_map/ppermute | solution.py:32
  45.9 2.7 %collective-permute-start.9 = (bf16[128,768]{1,0:T(8,128)(2,1)S(1)}, bf16[128,768]{1,0:T(8,128)(2,1)S(1)}, u32[]{:S(2)}, u32[]{:S(2)}) collective-permute-start(bf16[128,768]{1,0:T(8,128)(2,1)S(1)} %get-tuple-element.115.refs_0_), channel_id=1, source_target_pairs={{0,24},{8,16},{16,8},{24,0},{1,25},{9,17},{17,9},{25,1},{2,26},{10... | collective-permute-start | bytes 589832 | tf_op jit(solution)/shard_map/ppermute | solution.py:32
  49.4 5.2 %collective-permute-done.9.refs_0_ = bf16[128,768]{1,0:T(8,128)(2,1)S(1)} collective-permute-done((bf16[128,768]{1,0:T(8,128)(2,1)S(1)}, bf16[128,768]{1,0:T(8,128)(2,1)S(1)}, u32[]{:S(2)}, u32[]{:S(2)}) %collective-permute-start.9) | collective-permute-done | bytes 196640 | tf_op jit(solution)/shard_map/ppermute | solution.py:32
  57.5 2.6 %shard_map.124 = (bf16[384,1280]{1,0:T(8,128)(2,1)S(1)}, bf16[384,768]{1,0:T(8,128)(2,1)S(1)}, bf16[384,768]{1,0:T(8,128)(2,1)S(1)}) custom-call(bf16[128,768]{1,0:T(8,128)(2,1)S(1)} %get-tuple-element.115.refs_0_, bf16[128,768]{1,0:T(8,128)(2,1)S(1)} %collective-permute-done.10.refs_1_, bf16[128,768]{1,0:T(8,128)(2,1)S(1)} %collective-permute-done.11.refs_2_, ...), custom_call_target="tpu_custom_call" | custom-call | flops 1509949440 | tf_op jit(solution)/shard_map/pallas_call | solution.py:81
  60.1 1.6 collective-permute-start.12
  67.2 5.4 %collective-permute-done.13.refs_1_ = bf16[128,1280]{1,0:T(8,128)(2,1)S(1)} collective-permute-done((bf16[128,1280]{1,0:T(8,128)(2,1)S(1)}, bf16[128,1280]{1,0:T(8,128)(2,1)S(1)}, u32[]{:S(2)}, u32[]{:S(2)}) %collective-permute-start.13) | collective-permute-done | bytes 327712 | tf_op jit(solution)/shard_map/ppermute | solution.py:32
  72.6 5.8 %collective-permute-done.14.refs_2_ = bf16[128,1280]{1,0:T(8,128)(2,1)S(1)} collective-permute-done((bf16[128,1280]{1,0:T(8,128)(2,1)S(1)}, bf16[128,1280]{1,0:T(8,128)(2,1)S(1)}, u32[]{:S(2)}, u32[]{:S(2)}) %collective-permute-start.14) | collective-permute-done | bytes 327712 | tf_op jit(solution)/shard_map/ppermute | solution.py:32
  78.5 2.2 shard_map.125
  80.7 5.9 %collective-permute-done.12.refs_0_.refs_4_.refs_5_ = bf16[384,1280]{1,0:T(8,128)(2,1)S(1)} collective-permute-done((bf16[384,1280]{1,0:T(8,128)(2,1)S(1)}, bf16[384,1280]{1,0:T(8,128)(2,1)S(1)}, u32[]{:S(2)}, u32[]{:S(2)}) %collective-permute-start.12) | collective-permute-done | bytes 983072 | tf_op jit(solution)/shard_map/ppermute | solution.py:37
  86.6 4.6 %shard_map.126 = (bf16[128,1664]{1,0:T(8,128)(2,1)S(1)}, bf16[128,1664]{1,0:T(8,128)(2,1)S(1)}, bf16[128,1664]{1,0:T(8,128)(2,1)S(1)}, bf16[384,1280]{1,0:T(8,128)(2,1)S(1)}, bf16[384,1280]{1,0:T(8,128)(2,1)S(1)}) custom-call(bf16[384,1280]{1,0:T(8,128)(2,1)S(1)} %collective-permute-done.12.refs_0_.refs_4_.refs_5_, ...), custom_call_target="tpu_custom_call" | custom-call | flops 3019898880 | tf_op jit(solution)/shard_map/pallas_call | solution.py:81
  92.8 1.7 shard_map.129
  99.6 4.5 %collective-permute-done.15.refs_1_ = bf16[128,1664]{1,0:T(8,128)(2,1)S(1)} collective-permute-done((bf16[128,1664]{1,0:T(8,128)(2,1)S(1)}, bf16[128,1664]{1,0:T(8,128)(2,1)S(1)}, u32[]{:S(2)}, u32[]{:S(2)}) %collective-permute-start.15) | collective-permute-done | bytes 426016 | tf_op jit(solution)/shard_map/ppermute | solution.py:32
  104.0 2.4 %shard_map.127 = (bf16[128,1664]{1,0:T(8,128)(2,1)S(1)}, bf16[128,1280]{1,0:T(8,128)(2,1)S(1)}, bf16[128,1280]{1,0:T(8,128)(2,1)S(1)}) custom-call(bf16[128,1280]{1,0:T(8,128)(2,1)S(1)} %collective-permute-done.17.refs_0_.refs_2_.refs_3_, f32[1,1280]{1,0:T(1,128)S(1)} %constant_dynamic-slice_fusion.4.refs_3_.refs_1_.refs_6_.refs_4_, ...), custom_call_target="tpu_custom_call" | custom-call | flops 1006632960 | tf_op jit(solution)/shard_map/pallas_call | solution.py:81
  106.4 2.3 collective-permute-start.18
  109.0 15.1 %collective-permute-done.16.refs_2_ = bf16[128,1664]{1,0:T(8,128)(2,1)S(1)} collective-permute-done((bf16[128,1664]{1,0:T(8,128)(2,1)S(1)}, bf16[128,1664]{1,0:T(8,128)(2,1)S(1)}, u32[]{:S(2)}, u32[]{:S(2)}) %collective-permute-start.16) | collective-permute-done | bytes 426016 | tf_op jit(solution)/shard_map/ppermute | solution.py:32
  127.0 1.7 collective-permute-start.31
  128.8 10.1 %collective-permute-done.23.refs_0_ = bf16[128,1664]{1,0:T(8,128)(2,1)S(1)} collective-permute-done((bf16[128,1664]{1,0:T(8,128)(2,1)S(1)}, bf16[128,1664]{1,0:T(8,128)(2,1)S(1)}, u32[]{:S(2)}, u32[]{:S(2)}) %collective-permute-start.23) | collective-permute-done | bytes 426016 | tf_op jit(solution)/shard_map/ppermute | solution.py:32
  139.8 2.6 %collective-permute-start.28 = (bf16[128,768]{1,0:T(8,128)(2,1)S(1)}, bf16[128,768]{1,0:T(8,128)(2,1)S(1)}, u32[]{:S(2)}, u32[]{:S(2)}) collective-permute-start(bf16[128,768]{1,0:T(8,128)(2,1)S(1)} %get-tuple-element.136.refs_0_), channel_id=1, source_target_pairs={{0,24},{8,16},{16,8},{24,0},{1,25},{9,17},{17,9},{25,1},{2,26},{10... | collective-permute-start | bytes 589832 | tf_op jit(solution)/shard_map/ppermute | solution.py:32
  142.4 3.4 %shard_map.135 = (bf16[128,1280]{1,0:T(8,128)(2,1)S(1)}, f32[1,1280]{1,0:T(1,128)S(1)}) custom-call(bf16[128,1664]{1,0:T(8,128)(2,1)S(1)} %collective-permute-done.23.refs_0_, f32[128,1]{1,0:T(8,128)S(1)} %get-tuple-element.127.refs_2_.refs_1_, bf16[128,1280]{1,0:T(8,128)(2,1)S(1)} %get-tuple-element.154.refs_2_, ...), custom_call_target="tpu_custom_call" | custom-call | flops 1006632960 | tf_op jit(solution)/shard_map/pallas_call | solution.py:81
  148.4 4.4 %shard_map.133 = (bf16[384,1280]{1,0:T(8,128)(2,1)S(1)}, f32[1,1280]{1,0:T(1,128)S(1)}) custom-call(bf16[128,1664]{1,0:T(8,128)(2,1)S(1)} %shard_map.130.refs_0_, bf16[128,1664]{1,0:T(8,128)(2,1)S(1)} %collective-permute-done.30.refs_1_, bf16[128,1664]{1,0:T(8,128)(2,1)S(1)} %collective-permute-done.31.refs_2_, ...), custom_call_target="tpu_custom_call" | custom-call | flops 3019898880 | tf_op jit(solution)/shard_map/pallas_call | solution.py:81
  157.2 2.5 %convolution_convert_fusion.5 = bf16[1280,768]{1,0:T(8,128)(2,1)} fusion(bf16[512,1280]{1,0:T(8,128)(2,1)S(1)} %constant_dynamic-update-slice_fusion, bf16[512,768]{1,0:T(8,128)(2,1)S(1)} %get-tuple-element.145), kind=kOutput, calls=%fused_computation.20 | convolution fusion | flops 1007616000 | bytes 4063232 | tf_op jit(solution)/shard_map/dot_general | solution.py:22
  161.2 1.9 collective-permute-start.29
  163.1 2.6 %shard_map.131 = (bf16[128,1280]{1,0:T(8,128)(2,1)S(1)}, bf16[128,1280]{1,0:T(8,128)(2,1)S(1)}, bf16[128,1280]{1,0:T(8,128)(2,1)S(1)}, bf16[384,768]{1,0:T(8,128)(2,1)S(1)}, bf16[384,768]{1,0:T(8,128)(2,1)S(1)}) custom-call(bf16[128,768]{1,0:T(8,128)(2,1)S(1)} %get-tuple-element.136.refs_0_, bf16[128,768]{1,0:T(8,128)(2,1)S(1)} %collective-permute-done.24.refs_1_, ...), custom_call_target="tpu_custom_call" | custom-call | tf_op jit(solution)/shard_map/pallas_call | solution.py:81
  170.0 1.7 shard_map.136
  171.7 1.9 collective-permute-start.36
  173.6 4.1 %collective-permute-done.26 = bf16[128,1280]{1,0:T(8,128)(2,1)S(1)} collective-permute-done((bf16[128,1280]{1,0:T(8,128)(2,1)S(1)}, bf16[128,1280]{1,0:T(8,128)(2,1)S(1)}, u32[]{:S(2)}, u32[]{:S(2)}) %collective-permute-start.26) | collective-permute-done | bytes 327712 | tf_op jit(solution)/shard_map/ppermute | solution.py:32
  177.8 2.2 shard_map.134
  182.4 3.4 %collective-permute-done.33.refs_1_ = bf16[128,768]{1,0:T(8,128)(2,1)S(1)} collective-permute-done((bf16[128,768]{1,0:T(8,128)(2,1)S(1)}, bf16[128,768]{1,0:T(8,128)(2,1)S(1)}, u32[]{:S(2)}, u32[]{:S(2)}) %collective-permute-start.33) | collective-permute-done | bytes 196640 | tf_op jit(solution)/shard_map/ppermute | solution.py:32
  185.8 6.5 %collective-permute-done.34.refs_2_ = bf16[128,768]{1,0:T(8,128)(2,1)S(1)} collective-permute-done((bf16[128,768]{1,0:T(8,128)(2,1)S(1)}, bf16[128,768]{1,0:T(8,128)(2,1)S(1)}, u32[]{:S(2)}, u32[]{:S(2)}) %collective-permute-start.34) | collective-permute-done | bytes 196640 | tf_op jit(solution)/shard_map/ppermute | solution.py:32
  197.7 4.3 %collective-permute-done.39.refs_0_ = bf16[128,1664]{1,0:T(8,128)(2,1)S(1)} collective-permute-done((bf16[128,1664]{1,0:T(8,128)(2,1)S(1)}, bf16[128,1664]{1,0:T(8,128)(2,1)S(1)}, u32[]{:S(2)}, u32[]{:S(2)}) %collective-permute-start.39) | collective-permute-done | bytes 426016 | tf_op jit(solution)/shard_map/ppermute | solution.py:32
  202.0 3.4 %shard_map.138 = (bf16[128,1280]{1,0:T(8,128)(2,1)S(1)}, f32[1,1280]{1,0:T(1,128)S(1)}) custom-call(bf16[128,1664]{1,0:T(8,128)(2,1)S(1)} %collective-permute-done.39.refs_0_, f32[128,1]{1,0:T(8,128)S(1)} %get-tuple-element.112.refs_1_, bf16[128,1280]{1,0:T(8,128)(2,1)S(1)} %get-tuple-element.165.refs_2_, ...), custom_call_target="tpu_custom_call" | custom-call | flops 1006632960 | tf_op jit(solution)/shard_map/pallas_call | solution.py:81
  207.9 2.8 %fusion.6 = bf16[1280,768]{1,0:T(8,128)(2,1)S(1)} fusion(bf16[1280,768]{1,0:T(8,128)(2,1)} %convolution_convert_fusion.5, bf16[512,1280]{1,0:T(8,128)(2,1)S(1)} %constant_dynamic-update-slice_fusion.6, bf16[512,768]{1,0:T(8,128)(2,1)S(1)} %get-tuple-element.178), kind=kOutput, calls=%fused_computation.12 | convolution fusion | flops 1009582080 | bytes 6029312 | tf_op jit(solution)/shard_map/dot_general | solution.py:22
  211.3 4.6 %shard_map.139 = (bf16[128,1280]{1,0:T(8,128)(2,1)S(1)}, bf16[128,1280]{1,0:T(8,128)(2,1)S(1)}, bf16[128,1280]{1,0:T(8,128)(2,1)S(1)}, f32[1,1280]{1,0:T(1,128)S(1)}) custom-call(bf16[128,1664]{1,0:T(8,128)(2,1)S(1)} %shard_map.137.refs_0_, bf16[128,1664]{1,0:T(8,128)(2,1)S(1)} %collective-permute-done.37.refs_1_, ...), custom_call_target="tpu_custom_call" | custom-call | flops 1006632960 | tf_op jit(solution)/shard_map/pallas_call | solution.py:81
  217.8 1.9 collective-permute-start.42
  219.7 2.7 %fusion.3 = bf16[768,1280]{1,0:T(8,128)(2,1)} fusion(bf16[768,1280]{1,0:T(8,128)(2,1)S(1)} %collective-permute-done.45, bf16[768,1280]{1,0:T(8,128)(2,1)S(1)} %convolution_convert_fusion, bf16[512,1280]{1,0:T(8,128)(2,1)S(1)} %constant_dynamic-update-slice_fusion.8, bf16[128,768]{1,0:T(8,128)(2,1)S(1)} %get-tuple-element.181, ...), kind=kOutput, calls=%fused_computation.9 | convolution fusion | flops 1013121024 | bytes 7995392 | tf_op jit(solution)/shard_map/dot_general | solution.py:22
  224.2 2.7 %fusion.4 = bf16[1280,768]{1,0:T(8,128)(2,1)} fusion(bf16[1280,768]{1,0:T(8,128)(2,1)S(1)} %collective-permute-done.44, bf16[1280,768]{1,0:T(8,128)(2,1)S(1)} %convolution_convert_fusion.2, bf16[512,1280]{1,0:T(8,128)(2,1)S(1)} %constant_dynamic-update-slice_fusion.10, bf16[512,768]{1,0:T(8,128)(2,1)S(1)} %get-tuple-element.179), kind=kOutput, calls=%fused_computation.10 | convolution fusion | flops 1011548160 | bytes 7995392 | tf_op jit(solution)/shard_map/dot_general | solution.py:22
  226.9 2.7 %fusion.5 = bf16[1280,768]{1,0:T(8,128)(2,1)} fusion(bf16[1280,768]{1,0:T(8,128)(2,1)S(1)} %collective-permute-done.43, bf16[1280,768]{1,0:T(8,128)(2,1)S(1)} %convolution_convert_fusion.3, bf16[512,1280]{1,0:T(8,128)(2,1)S(1)} %constant_dynamic-update-slice_fusion.10, bf16[512,768]{1,0:T(8,128)(2,1)S(1)} %get-tuple-element.178), kind=kOutput, calls=%fused_computation.11 | convolution fusion | flops 1011548160 | bytes 7995392 | tf_op jit(solution)/shard_map/dot_general | solution.py:22
  229.6 1.9 collective-permute-start.49
  231.5 2.6 %collective-permute-done.41 = bf16[128,1280]{1,0:T(8,128)(2,1)S(1)} collective-permute-done((bf16[128,1280]{1,0:T(8,128)(2,1)S(1)}, bf16[128,1280]{1,0:T(8,128)(2,1)S(1)}, u32[]{:S(2)}, u32[]{:S(2)}) %collective-permute-start.41) | collective-permute-done | bytes 327712 | tf_op jit(solution)/shard_map/ppermute | solution.py:32
  (141 shorter events, 55.0 us)
Async XLA Ops:
  0.6 7.5 %collective-permute-start.2 = (bf16[1280,768]{1,0:T(8,128)(2,1)}, bf16[1280,768]{1,0:T(8,128)(2,1)S(1)}, u32[]{:S(2)}, u32[]{:S(2)}) collective-permute-start(bf16[1280,768]{1,0:T(8,128)(2,1)} %bitcast.57), channel_id=1, source_target_pairs={{0,1},{1,0},{2,3},{3,2},{4,5},{5,4},{6,7},{7,6},{8,9},{9,8},{10,11... | collective-permute-start | bytes 5898248 | tf_op jit(solution)/shard_map/ppermute | solution.py:32
  1.2 7.0 %collective-permute-start.3 = (bf16[1280,768]{1,0:T(8,128)(2,1)}, bf16[1280,768]{1,0:T(8,128)(2,1)}, u32[]{:S(2)}, u32[]{:S(2)}) collective-permute-start(bf16[1280,768]{1,0:T(8,128)(2,1)} %bitcast.59), channel_id=1, source_target_pairs={{0,1},{1,0},{2,3},{3,2},{4,5},{5,4},{6,7},{7,6},{8,9},{9,8},{10,11... | collective-permute-start | bytes 5898248 | tf_op jit(solution)/shard_map/ppermute | solution.py:32
  1.2 9.5 %collective-permute-start.4 = (bf16[768,1280]{1,0:T(8,128)(2,1)}, bf16[768,1280]{1,0:T(8,128)(2,1)}, u32[]{:S(2)}, u32[]{:S(2)}) collective-permute-start(bf16[768,1280]{1,0:T(8,128)(2,1)} %bitcast.61), channel_id=1, source_target_pairs={{0,1},{1,0},{2,3},{3,2},{4,5},{5,4},{6,7},{7,6},{8,9},{9,8},{10,11... | collective-permute-start | bytes 5898248 | tf_op jit(solution)/shard_map/ppermute | solution.py:32
  4.0 15.1 %collective-permute-start = (bf16[144,1280]{1,0:T(8,128)(2,1)S(1)}, bf16[144,1280]{1,0:T(8,128)(2,1)S(1)}, u32[]{:S(2)}, u32[]{:S(2)}) collective-permute-start(bf16[144,1280]{1,0:T(8,128)(2,1)S(1)} %get-tuple-element.205), channel_id=1, source_target_pairs={{0,8},{8,0},{16,24},{24,16},{1,9},{9,1},{17,25},{25,17},{2,10},{10... | collective-permute-start | bytes 1105928 | tf_op jit(solution)/shard_map/ppermute | solution.py:32
  6.6 12.5 %collective-permute-start.1 = (bf16[144,1280]{1,0:T(8,128)(2,1)S(1)}, bf16[144,1280]{1,0:T(8,128)(2,1)S(1)}, u32[]{:S(2)}, u32[]{:S(2)}) collective-permute-start(bf16[144,1280]{1,0:T(8,128)(2,1)S(1)} %get-tuple-element.206), channel_id=1, source_target_pairs={{0,16},{8,24},{16,0},{24,8},{1,17},{9,25},{17,1},{25,9},{2,18},{10... | collective-permute-start | bytes 1105928 | tf_op jit(solution)/shard_map/ppermute | solution.py:32
  15.2 13.3 %collective-permute-start.7 = (bf16[144,1280]{1,0:T(8,128)(2,1)S(1)}, bf16[144,1280]{1,0:T(8,128)(2,1)S(1)}, u32[]{:S(2)}, u32[]{:S(2)}) collective-permute-start(bf16[144,1280]{1,0:T(8,128)(2,1)S(1)} %get-tuple-element.109), channel_id=1, source_target_pairs={{0,24},{8,16},{16,8},{24,0},{1,25},{9,17},{17,9},{25,1},{2,26},{10... | collective-permute-start | bytes 1105928 | tf_op jit(solution)/shard_map/ppermute | solution.py:32
  23.7 13.8 %collective-permute-start.5 = (bf16[128,1536]{1,0:T(8,128)(2,1)S(1)}, bf16[128,1536]{1,0:T(8,128)(2,1)S(1)}, u32[]{:S(2)}, u32[]{:S(2)}) collective-permute-start(bf16[128,1536]{1,0:T(8,128)(2,1)S(1)} %get-tuple-element.105), channel_id=1, source_target_pairs={{0,8},{8,0},{16,24},{24,16},{1,9},{9,1},{17,25},{25,17},{2,10},{10... | collective-permute-start | bytes 1179656 | tf_op jit(solution)/shard_map/ppermute | solution.py:32
  24.3 13.2 %collective-permute-start.6 = (bf16[128,1536]{1,0:T(8,128)(2,1)S(1)}, bf16[128,1536]{1,0:T(8,128)(2,1)S(1)}, u32[]{:S(2)}, u32[]{:S(2)}) collective-permute-start(bf16[128,1536]{1,0:T(8,128)(2,1)S(1)} %get-tuple-element.106), channel_id=1, source_target_pairs={{0,16},{8,24},{16,0},{24,8},{1,17},{9,25},{17,1},{25,9},{2,18},{10... | collective-permute-start | bytes 1179656 | tf_op jit(solution)/shard_map/ppermute | solution.py:32
  30.9 13.9 %collective-permute-start.8 = (bf16[128,1536]{1,0:T(8,128)(2,1)S(1)}, bf16[128,1536]{1,0:T(8,128)(2,1)S(1)}, u32[]{:S(2)}, u32[]{:S(2)}) collective-permute-start(bf16[128,1536]{1,0:T(8,128)(2,1)S(1)} %get-tuple-element.110), channel_id=1, source_target_pairs={{0,24},{8,16},{16,8},{24,0},{1,25},{9,17},{17,9},{25,1},{2,26},{10... | collective-permute-start | bytes 1179656 | tf_op jit(solution)/shard_map/ppermute | solution.py:32
  45.9 8.7 %collective-permute-start.9 = (bf16[128,768]{1,0:T(8,128)(2,1)S(1)}, bf16[128,768]{1,0:T(8,128)(2,1)S(1)}, u32[]{:S(2)}, u32[]{:S(2)}) collective-permute-start(bf16[128,768]{1,0:T(8,128)(2,1)S(1)} %get-tuple-element.115.refs_0_), channel_id=1, source_target_pairs={{0,24},{8,16},{16,8},{24,0},{1,25},{9,17},{17,9},{25,1},{2,26},{10... | collective-permute-start | bytes 589832 | tf_op jit(solution)/shard_map/ppermute | solution.py:32
  48.6 8.9 %collective-permute-start.10 = (bf16[128,768]{1,0:T(8,128)(2,1)S(1)}, bf16[128,768]{1,0:T(8,128)(2,1)S(1)}, u32[]{:S(2)}, u32[]{:S(2)}) collective-permute-start(bf16[128,768]{1,0:T(8,128)(2,1)S(1)} %get-tuple-element.115.refs_0_), channel_id=1, source_target_pairs={{0,8},{8,0},{16,24},{24,16},{1,9},{9,1},{17,25},{25,17},{2,10},{10... | collective-permute-start | bytes 589832 | tf_op jit(solution)/shard_map/ppermute | solution.py:32
  49.1 8.3 %collective-permute-start.11 = (bf16[128,768]{1,0:T(8,128)(2,1)S(1)}, bf16[128,768]{1,0:T(8,128)(2,1)S(1)}, u32[]{:S(2)}, u32[]{:S(2)}) collective-permute-start(bf16[128,768]{1,0:T(8,128)(2,1)S(1)} %get-tuple-element.115.refs_0_), channel_id=1, source_target_pairs={{0,16},{8,24},{16,0},{24,8},{1,17},{9,25},{17,1},{25,9},{2,18},{10... | collective-permute-start | bytes 589832 | tf_op jit(solution)/shard_map/ppermute | solution.py:32
  60.1 26.5 %collective-permute-start.12 = (bf16[384,1280]{1,0:T(8,128)(2,1)S(1)}, bf16[384,1280]{1,0:T(8,128)(2,1)S(1)}, u32[]{:S(2)}, u32[]{:S(2)}) collective-permute-start(bf16[384,1280]{1,0:T(8,128)(2,1)S(1)} %get-tuple-element.118), channel_id=1, source_target_pairs={{0,2},{2,4},{4,6},{6,0},{1,3},{3,5},{5,7},{7,1},{8,10},{10,12},{12... | collective-permute-start | bytes 2949128 | tf_op jit(solution)/shard_map/ppermute | solution.py:37
  61.9 10.7 %collective-permute-start.13 = (bf16[128,1280]{1,0:T(8,128)(2,1)S(1)}, bf16[128,1280]{1,0:T(8,128)(2,1)S(1)}, u32[]{:S(2)}, u32[]{:S(2)}) collective-permute-start(bf16[128,1280]{1,0:T(8,128)(2,1)S(1)} %get-tuple-element.198), channel_id=1, source_target_pairs={{0,8},{8,0},{16,24},{24,16},{1,9},{9,1},{17,25},{25,17},{2,10},{10... | collective-permute-start | bytes 983048 | tf_op jit(solution)/shard_map/ppermute | solution.py:32
  63.5 15.0 %collective-permute-start.14 = (bf16[128,1280]{1,0:T(8,128)(2,1)S(1)}, bf16[128,1280]{1,0:T(8,128)(2,1)S(1)}, u32[]{:S(2)}, u32[]{:S(2)}) collective-permute-start(bf16[128,1280]{1,0:T(8,128)(2,1)S(1)} %get-tuple-element.197), channel_id=1, source_target_pairs={{0,16},{8,24},{16,0},{24,8},{1,17},{9,25},{17,1},{25,9},{2,18},{10... | collective-permute-start | bytes 983048 | tf_op jit(solution)/shard_map/ppermute | solution.py:32
  65.0 33.2 %collective-permute-start.17 = (bf16[128,1280]{1,0:T(8,128)(2,1)S(1)}, bf16[128,1280]{1,0:T(8,128)(2,1)S(1)}, u32[]{:S(2)}, u32[]{:S(2)}) collective-permute-start(bf16[128,1280]{1,0:T(8,128)(2,1)S(1)} %get-tuple-element.114), channel_id=1, source_target_pairs={{0,2},{2,4},{4,6},{6,0},{1,3},{3,5},{5,7},{7,1},{8,10},{10,12},{12... | collective-permute-start | bytes 983048 | tf_op jit(solution)/shard_map/ppermute | solution.py:37
  66.6 26.2 %collective-permute-start.21 = (bf16[128,1280]{1,0:T(8,128)(2,1)S(1)}, bf16[128,1280]{1,0:T(8,128)(2,1)S(1)}, u32[]{:S(2)}, u32[]{:S(2)}) collective-permute-start(bf16[128,1280]{1,0:T(8,128)(2,1)S(1)} %get-tuple-element.196), channel_id=1, source_target_pairs={{0,24},{8,16},{16,8},{24,0},{1,25},{9,17},{17,9},{25,1},{2,26},{10... | collective-permute-start | bytes 983048 | tf_op jit(solution)/shard_map/ppermute | solution.py:32
  91.2 12.8 %collective-permute-start.15 = (bf16[128,1664]{1,0:T(8,128)(2,1)S(1)}, bf16[128,1664]{1,0:T(8,128)(2,1)S(1)}, u32[]{:S(2)}, u32[]{:S(2)}) collective-permute-start(bf16[128,1664]{1,0:T(8,128)(2,1)S(1)} %get-tuple-element.124), channel_id=1, source_target_pairs={{0,8},{8,0},{16,24},{24,16},{1,9},{9,1},{17,25},{25,17},{2,10},{10... | collective-permute-start | bytes 1277960 | tf_op jit(solution)/shard_map/ppermute | solution.py:32
  94.5 30.2 %collective-permute-start.22 = (bf16[128,768]{1,0:T(8,128)(2,1)S(1)}, bf16[128,768]{1,0:T(8,128)(2,1)S(1)}, u32[]{:S(2)}, u32[]{:S(2)}) collective-permute-start(bf16[128,768]{1,0:T(8,128)(2,1)S(1)} %get-tuple-element.132), channel_id=1, source_target_pairs={{0,24},{8,16},{16,8},{24,0},{1,25},{9,17},{17,9},{25,1},{2,26},{10... | collective-permute-start | bytes 589832 | tf_op jit(solution)/shard_map/ppermute | solution.py:32
  95.9 28.8 %collective-permute-start.19 = (bf16[128,768]{1,0:T(8,128)(2,1)S(1)}, bf16[128,768]{1,0:T(8,128)(2,1)S(1)}, u32[]{:S(2)}, u32[]{:S(2)}) collective-permute-start(bf16[128,768]{1,0:T(8,128)(2,1)S(1)} %get-tuple-element.130), channel_id=1, source_target_pairs={{0,8},{8,0},{16,24},{24,16},{1,9},{9,1},{17,25},{25,17},{2,10},{10... | collective-permute-start | bytes 589832 | tf_op jit(solution)/shard_map/ppermute | solution.py:32
  97.4 27.3 %collective-permute-start.20 = (bf16[128,768]{1,0:T(8,128)(2,1)S(1)}, bf16[128,768]{1,0:T(8,128)(2,1)S(1)}, u32[]{:S(2)}, u32[]{:S(2)}) collective-permute-start(bf16[128,768]{1,0:T(8,128)(2,1)S(1)} %get-tuple-element.131), channel_id=1, source_target_pairs={{0,16},{8,24},{16,0},{24,8},{1,17},{9,25},{17,1},{25,9},{2,18},{10... | collective-permute-start | bytes 589832 | tf_op jit(solution)/shard_map/ppermute | solution.py:32
  98.2 26.0 %collective-permute-start.16 = (bf16[128,1664]{1,0:T(8,128)(2,1)S(1)}, bf16[128,1664]{1,0:T(8,128)(2,1)S(1)}, u32[]{:S(2)}, u32[]{:S(2)}) collective-permute-start(bf16[128,1664]{1,0:T(8,128)(2,1)S(1)} %get-tuple-element.125), channel_id=1, source_target_pairs={{0,16},{8,24},{16,0},{24,8},{1,17},{9,25},{17,1},{25,9},{2,18},{10... | collective-permute-start | bytes 1277960 | tf_op jit(solution)/shard_map/ppermute | solution.py:32
  106.4 17.8 %collective-permute-start.18 = (bf16[128,1664]{1,0:T(8,128)(2,1)S(1)}, bf16[128,1664]{1,0:T(8,128)(2,1)S(1)}, u32[]{:S(2)}, u32[]{:S(2)}) collective-permute-start(bf16[128,1664]{1,0:T(8,128)(2,1)S(1)} %get-tuple-element.128), channel_id=1, source_target_pairs={{0,24},{8,16},{16,8},{24,0},{1,25},{9,17},{17,9},{25,1},{2,26},{10... | collective-permute-start | bytes 1277960 | tf_op jit(solution)/shard_map/ppermute | solution.py:32
  125.2 13.7 %collective-permute-start.23 = (bf16[128,1664]{1,0:T(8,128)(2,1)S(1)}, bf16[128,1664]{1,0:T(8,128)(2,1)S(1)}, u32[]{:S(2)}, u32[]{:S(2)}) collective-permute-start(bf16[128,1664]{1,0:T(8,128)(2,1)S(1)} %shard_map.130.refs_0_), channel_id=1, source_target_pairs={{0,24},{8,16},{16,8},{24,0},{1,25},{9,17},{17,9},{25,1},{2,26},{10... | collective-permute-start | bytes 1277960 | tf_op jit(solution)/shard_map/ppermute | solution.py:32
  125.6 21.3 %collective-permute-start.30 = (bf16[128,1664]{1,0:T(8,128)(2,1)S(1)}, bf16[128,1664]{1,0:T(8,128)(2,1)S(1)}, u32[]{:S(2)}, u32[]{:S(2)}) collective-permute-start(bf16[128,1664]{1,0:T(8,128)(2,1)S(1)} %shard_map.130.refs_0_), channel_id=1, source_target_pairs={{0,8},{8,0},{16,24},{24,16},{1,9},{9,1},{17,25},{25,17},{2,10},{10... | collective-permute-start | bytes 1277960 | tf_op jit(solution)/shard_map/ppermute | solution.py:32
  127.0 21.4 %collective-permute-start.31 = (bf16[128,1664]{1,0:T(8,128)(2,1)S(1)}, bf16[128,1664]{1,0:T(8,128)(2,1)S(1)}, u32[]{:S(2)}, u32[]{:S(2)}) collective-permute-start(bf16[128,1664]{1,0:T(8,128)(2,1)S(1)} %shard_map.130.refs_0_), channel_id=1, source_target_pairs={{0,16},{8,24},{16,0},{24,8},{1,17},{9,25},{17,1},{25,9},{2,18},{10... | collective-permute-start | bytes 1277960 | tf_op jit(solution)/shard_map/ppermute | solution.py:32
  138.9 14.5 %collective-permute-start.24 = (bf16[128,768]{1,0:T(8,128)(2,1)S(1)}, bf16[128,768]{1,0:T(8,128)(2,1)S(1)}, u32[]{:S(2)}, u32[]{:S(2)}) collective-permute-start(bf16[128,768]{1,0:T(8,128)(2,1)S(1)} %get-tuple-element.136.refs_0_), channel_id=1, source_target_pairs={{0,8},{8,0},{16,24},{24,16},{1,9},{9,1},{17,25},{25,17},{2,10},{10... | collective-permute-start | bytes 589832 | tf_op jit(solution)/shard_map/ppermute | solution.py:32
  139.5 14.0 %collective-permute-start.25 = (bf16[128,768]{1,0:T(8,128)(2,1)S(1)}, bf16[128,768]{1,0:T(8,128)(2,1)S(1)}, u32[]{:S(2)}, u32[]{:S(2)}) collective-permute-start(bf16[128,768]{1,0:T(8,128)(2,1)S(1)} %get-tuple-element.136.refs_0_), channel_id=1, source_target_pairs={{0,16},{8,24},{16,0},{24,8},{1,17},{9,25},{17,1},{25,9},{2,18},{10... | collective-permute-start | bytes 589832 | tf_op jit(solution)/shard_map/ppermute | solution.py:32
  139.8 13.7 %collective-permute-start.28 = (bf16[128,768]{1,0:T(8,128)(2,1)S(1)}, bf16[128,768]{1,0:T(8,128)(2,1)S(1)}, u32[]{:S(2)}, u32[]{:S(2)}) collective-permute-start(bf16[128,768]{1,0:T(8,128)(2,1)S(1)} %get-tuple-element.136.refs_0_), channel_id=1, source_target_pairs={{0,24},{8,16},{16,8},{24,0},{1,25},{9,17},{17,9},{25,1},{2,26},{10... | collective-permute-start | bytes 589832 | tf_op jit(solution)/shard_map/ppermute | solution.py:32
  146.9 23.1 %collective-permute-start.35 = (bf16[128,1280]{1,0:T(8,128)(2,1)S(1)}, bf16[128,1280]{1,0:T(8,128)(2,1)S(1)}, u32[]{:S(2)}, u32[]{:S(2)}) collective-permute-start(bf16[128,1280]{1,0:T(8,128)(2,1)S(1)} %get-tuple-element.159), channel_id=1, source_target_pairs={{0,6},{2,0},{4,2},{6,4},{1,7},{3,1},{5,3},{7,5},{8,14},{10,8},{12,... | collective-permute-start | bytes 983048 | tf_op jit(solution)/shard_map/ppermute | solution.py:37
  152.9 24.9 %collective-permute-start.32 = (bf16[384,1280]{1,0:T(8,128)(2,1)S(1)}, bf16[384,1280]{1,0:T(8,128)(2,1)S(1)}, u32[]{:S(2)}, u32[]{:S(2)}) collective-permute-start(bf16[384,1280]{1,0:T(8,128)(2,1)S(1)} %get-tuple-element.142), channel_id=1, source_target_pairs={{0,6},{2,0},{4,2},{6,4},{1,7},{3,1},{5,3},{7,5},{8,14},{10,8},{12,... | collective-permute-start | bytes 2949128 | tf_op jit(solution)/shard_map/ppermute | solution.py:37
  161.2 54.8 %collective-permute-start.29 = (bf16[128,1280]{1,0:T(8,128)(2,1)S(1)}, bf16[128,1280]{1,0:T(8,128)(2,1)S(1)}, u32[]{:S(2)}, u32[]{:S(2)}) collective-permute-start(bf16[128,1280]{1,0:T(8,128)(2,1)S(1)} %get-tuple-element.140), channel_id=1, source_target_pairs={{0,24},{8,16},{16,8},{24,0},{1,25},{9,17},{17,9},{25,1},{2,26},{10... | collective-permute-start | bytes 983048 | tf_op jit(solution)/shard_map/ppermute | solution.py:32
  165.7 12.1 %collective-permute-start.26 = (bf16[128,1280]{1,0:T(8,128)(2,1)S(1)}, bf16[128,1280]{1,0:T(8,128)(2,1)S(1)}, u32[]{:S(2)}, u32[]{:S(2)}) collective-permute-start(bf16[128,1280]{1,0:T(8,128)(2,1)S(1)} %get-tuple-element.138), channel_id=1, source_target_pairs={{0,8},{8,0},{16,24},{24,16},{1,9},{9,1},{17,25},{25,17},{2,10},{10... | collective-permute-start | bytes 983048 | tf_op jit(solution)/shard_map/ppermute | solution.py:32
  167.3 44.0 %collective-permute-start.27 = (bf16[128,1280]{1,0:T(8,128)(2,1)S(1)}, bf16[128,1280]{1,0:T(8,128)(2,1)S(1)}, u32[]{:S(2)}, u32[]{:S(2)}) collective-permute-start(bf16[128,1280]{1,0:T(8,128)(2,1)S(1)} %get-tuple-element.139), channel_id=1, source_target_pairs={{0,16},{8,24},{16,0},{24,8},{1,17},{9,25},{17,1},{25,9},{2,18},{10... | collective-permute-start | bytes 983048 | tf_op jit(solution)/shard_map/ppermute | solution.py:32
  171.7 14.0 %collective-permute-start.36 = (bf16[128,768]{1,0:T(8,128)(2,1)S(1)}, bf16[128,768]{1,0:T(8,128)(2,1)S(1)}, u32[]{:S(2)}, u32[]{:S(2)}) collective-permute-start(bf16[128,768]{1,0:T(8,128)(2,1)S(1)} %get-tuple-element.160), channel_id=1, source_target_pairs={{0,24},{8,16},{16,8},{24,0},{1,25},{9,17},{17,9},{25,1},{2,26},{10... | collective-permute-start | bytes 589832 | tf_op jit(solution)/shard_map/ppermute | solution.py:32
  180.0 5.7 %collective-permute-start.33 = (bf16[128,768]{1,0:T(8,128)(2,1)S(1)}, bf16[128,768]{1,0:T(8,128)(2,1)S(1)}, u32[]{:S(2)}, u32[]{:S(2)}) collective-permute-start(bf16[128,768]{1,0:T(8,128)(2,1)S(1)} %get-tuple-element.151), channel_id=1, source_target_pairs={{0,8},{8,0},{16,24},{24,16},{1,9},{9,1},{17,25},{25,17},{2,10},{10... | collective-permute-start | bytes 589832 | tf_op jit(solution)/shard_map/ppermute | solution.py:32
  181.5 10.8 %collective-permute-start.34 = (bf16[128,768]{1,0:T(8,128)(2,1)S(1)}, bf16[128,768]{1,0:T(8,128)(2,1)S(1)}, u32[]{:S(2)}, u32[]{:S(2)}) collective-permute-start(bf16[128,768]{1,0:T(8,128)(2,1)S(1)} %get-tuple-element.158), channel_id=1, source_target_pairs={{0,16},{8,24},{16,0},{24,8},{1,17},{9,25},{17,1},{25,9},{2,18},{10... | collective-permute-start | bytes 589832 | tf_op jit(solution)/shard_map/ppermute | solution.py:32
  192.8 9.2 %collective-permute-start.39 = (bf16[128,1664]{1,0:T(8,128)(2,1)S(1)}, bf16[128,1664]{1,0:T(8,128)(2,1)S(1)}, u32[]{:S(2)}, u32[]{:S(2)}) collective-permute-start(bf16[128,1664]{1,0:T(8,128)(2,1)S(1)} %shard_map.137.refs_0_), channel_id=1, source_target_pairs={{0,24},{8,16},{16,8},{24,0},{1,25},{9,17},{17,9},{25,1},{2,26},{10... | collective-permute-start | bytes 1277960 | tf_op jit(solution)/shard_map/ppermute | solution.py:32
  193.8 11.9 %collective-permute-start.37 = (bf16[128,1664]{1,0:T(8,128)(2,1)S(1)}, bf16[128,1664]{1,0:T(8,128)(2,1)S(1)}, u32[]{:S(2)}, u32[]{:S(2)}) collective-permute-start(bf16[128,1664]{1,0:T(8,128)(2,1)S(1)} %shard_map.137.refs_0_), channel_id=1, source_target_pairs={{0,8},{8,0},{16,24},{24,16},{1,9},{9,1},{17,25},{25,17},{2,10},{10... | collective-permute-start | bytes 1277960 | tf_op jit(solution)/shard_map/ppermute | solution.py:32
  195.0 11.4 %collective-permute-start.38 = (bf16[128,1664]{1,0:T(8,128)(2,1)S(1)}, bf16[128,1664]{1,0:T(8,128)(2,1)S(1)}, u32[]{:S(2)}, u32[]{:S(2)}) collective-permute-start(bf16[128,1664]{1,0:T(8,128)(2,1)S(1)} %shard_map.137.refs_0_), channel_id=1, source_target_pairs={{0,16},{8,24},{16,0},{24,8},{1,17},{9,25},{17,1},{25,9},{2,18},{10... | collective-permute-start | bytes 1277960 | tf_op jit(solution)/shard_map/ppermute | solution.py:32
  202.0 15.8 %collective-permute-start.45 = (bf16[768,1280]{1,0:T(8,128)(2,1)S(1)}, bf16[768,1280]{1,0:T(8,128)(2,1)S(1)}, u32[]{:S(2)}, u32[]{:S(2)}) collective-permute-start(bf16[768,1280]{1,0:T(8,128)(2,1)S(1)} %fusion.8), channel_id=1, source_target_pairs={{0,1},{1,0},{2,3},{3,2},{4,5},{5,4},{6,7},{7,6},{8,9},{9,8},{10,11... | collective-permute-start | bytes 5898248 | tf_op jit(solution)/shard_map/ppermute | solution.py:32
  207.8 14.7 %collective-permute-start.44 = (bf16[1280,768]{1,0:T(8,128)(2,1)S(1)}, bf16[1280,768]{1,0:T(8,128)(2,1)S(1)}, u32[]{:S(2)}, u32[]{:S(2)}) collective-permute-start(bf16[1280,768]{1,0:T(8,128)(2,1)S(1)} %fusion.7), channel_id=1, source_target_pairs={{0,1},{1,0},{2,3},{3,2},{4,5},{5,4},{6,7},{7,6},{8,9},{9,8},{10,11... | collective-permute-start | bytes 5898248 | tf_op jit(solution)/shard_map/ppermute | solution.py:32
  210.7 11.8 %collective-permute-start.43 = (bf16[1280,768]{1,0:T(8,128)(2,1)S(1)}, bf16[1280,768]{1,0:T(8,128)(2,1)S(1)}, u32[]{:S(2)}, u32[]{:S(2)}) collective-permute-start(bf16[1280,768]{1,0:T(8,128)(2,1)S(1)} %fusion.6), channel_id=1, source_target_pairs={{0,1},{1,0},{2,3},{3,2},{4,5},{5,4},{6,7},{7,6},{8,9},{9,8},{10,11... | collective-permute-start | bytes 5898248 | tf_op jit(solution)/shard_map/ppermute | solution.py:32
  216.1 13.5 %collective-permute-start.40 = (bf16[128,1280]{1,0:T(8,128)(2,1)S(1)}, bf16[128,1280]{1,0:T(8,128)(2,1)S(1)}, u32[]{:S(2)}, u32[]{:S(2)}) collective-permute-start(bf16[128,1280]{1,0:T(8,128)(2,1)S(1)} %get-tuple-element.174), channel_id=1, source_target_pairs={{0,8},{8,0},{16,24},{24,16},{1,9},{9,1},{17,25},{25,17},{2,10},{10... | collective-permute-start | bytes 983048 | tf_op jit(solution)/shard_map/ppermute | solution.py:32
  217.2 16.9 %collective-permute-start.41 = (bf16[128,1280]{1,0:T(8,128)(2,1)S(1)}, bf16[128,1280]{1,0:T(8,128)(2,1)S(1)}, u32[]{:S(2)}, u32[]{:S(2)}) collective-permute-start(bf16[128,1280]{1,0:T(8,128)(2,1)S(1)} %get-tuple-element.175), channel_id=1, source_target_pairs={{0,16},{8,24},{16,0},{24,8},{1,17},{9,25},{17,1},{25,9},{2,18},{10... | collective-permute-start | bytes 983048 | tf_op jit(solution)/shard_map/ppermute | solution.py:32
  217.8 16.3 %collective-permute-start.42 = (bf16[128,1280]{1,0:T(8,128)(2,1)S(1)}, bf16[128,1280]{1,0:T(8,128)(2,1)S(1)}, u32[]{:S(2)}, u32[]{:S(2)}) collective-permute-start(bf16[128,1280]{1,0:T(8,128)(2,1)S(1)} %get-tuple-element.166), channel_id=1, source_target_pairs={{0,24},{8,16},{16,8},{24,0},{1,25},{9,17},{17,9},{25,1},{2,26},{10... | collective-permute-start | bytes 983048 | tf_op jit(solution)/shard_map/ppermute | solution.py:32
  222.5 12.0 %collective-permute-start.47 = (f32[1,1280]{1,0:T(1,128)S(1)}, f32[1,1280]{1,0:T(1,128)S(1)}, u32[]{:S(2)}, u32[]{:S(2)}) collective-permute-start(f32[1,1280]{1,0:T(1,128)S(1)} %add.115), channel_id=1, source_target_pairs={{0,8},{8,0},{16,24},{24,16},{1,9},{9,1},{17,25},{25,17},{2,10},{10... | collective-permute-start | bytes 15368 | tf_op jit(solution)/shard_map/ppermute | solution.py:32
  223.6 10.9 %collective-permute-start.48 = (f32[1,1280]{1,0:T(1,128)S(1)}, f32[1,1280]{1,0:T(1,128)S(1)}, u32[]{:S(2)}, u32[]{:S(2)}) collective-permute-start(f32[1,1280]{1,0:T(1,128)S(1)} %add.115), channel_id=1, source_target_pairs={{0,16},{8,24},{16,0},{24,8},{1,17},{9,25},{17,1},{25,9},{2,18},{10... | collective-permute-start | bytes 15368 | tf_op jit(solution)/shard_map/ppermute | solution.py:32
  (10 other events, 48.3 us)
